TPU v7x, 32 devices: a whole 2x2x4 slice. The times are simulated.
32 devices in a mesh: groups: 2 (over y), gx: 4 (over x, core), gy: 4 (over z).
Axes of the slice: x: 2, y: 2, z: 4, core: 2. Of those that a mesh axis runs over, the one named last changes fastest.
Arguments:
- field: bfloat16 [64, 16, 16, 512], P(None, ('groups', 'gx'), 'gy'), parts along dimension 1, may hold values from -100 to 100
- cotangent: bfloat16 [64, 16, 16, 512], P(None, ('groups', 'gx'), 'gy'), parts along dimension 1, may hold values from -6 to 6
- qk_weight: float32 [3, 2, 64, 64], replicated, may hold values from -0.75 to 0.75
- w_value: bfloat16 [64, 64], replicated, may hold values from -0.75 to 0.75
- w_out: bfloat16 [64, 64], replicated, may hold values from -0.75 to 0.75
Outputs:
- layer_output: bfloat16 [64, 16, 16, 512], P(None, ('groups', 'gx'), 'gy'), parts along dimension 1
- field_grad: bfloat16 [64, 16, 16, 512], P(None, ('groups', 'gx'), 'gy'), parts along dimension 1
There are 2 independent parts, one for each index of `groups`. A program takes and returns all parts, laid end to end along the dimension named above; an argument that names none is the same for every part. Nothing has to cross between parts.
All inputs are finite; a program needn't handle non-finite values.
Results may differ from a plain program's by a relative error of at most 0.0075.
Values may be sent and summed in bfloat16 or wider, within the bound.
No kernel may reach another device: no remote copies, remote signals or barrier semaphores. Data moves between devices by JAX's collectives and lax.ppermute only.
A program may use at most 64 MiB of HBM per device.

v0:
```python
import math

import jax
import jax.numpy as jnp
from jax import lax
from jax.sharding import PartitionSpec as P

WIDTH = 64
HEADS = 8
HEAD_DIM = 8


EPSILON = 1e-06
PRECISE = lax.Precision.HIGHEST


def axis_features(pooled, weights):
    inverse = lax.rsqrt(jnp.mean(pooled * pooled, axis=0, keepdims=True) + EPSILON)
    normed = pooled * inverse
    length = pooled.shape[1]
    factor = 1.0 / math.sqrt(HEAD_DIM * length)
    queries = jnp.dot(weights[0].T, normed, precision=PRECISE).reshape(HEADS, HEAD_DIM, length)
    keyset = jnp.dot(weights[1].T, normed, precision=PRECISE).reshape(HEADS, HEAD_DIM, length)
    kernel = (jnp.einsum("hdm,hdn->hmn", queries, keyset, precision=PRECISE) * factor).astype(
        jnp.bfloat16
    )
    return (kernel, normed, inverse, queries, keyset, factor)


def kernel_backward(gram, queries, keyset, factor):
    grad_query = factor * jnp.einsum("hmn,hdn->hdm", gram, keyset, precision=PRECISE)
    grad_keyset = factor * jnp.einsum("hmn,hdm->hdn", gram, queries, precision=PRECISE)
    return (grad_query, grad_keyset)


def pooled_grad(normed, inverse, weights, grad_query, grad_keyset):
    length = normed.shape[1]
    grad_normed = jnp.dot(weights[0], grad_query.reshape(WIDTH, length), precision=PRECISE)
    grad_normed = grad_normed + jnp.dot(
        weights[1], grad_keyset.reshape(WIDTH, length), precision=PRECISE
    )
    return inverse * (grad_normed - normed * jnp.mean(grad_normed * normed, axis=0, keepdims=True))


def head_table(position, block_size):
    channels = position * block_size + jnp.arange(block_size, dtype=jnp.int32)
    heads_all = jnp.arange(HEADS, dtype=jnp.int32)
    return (channels[:, None] // HEAD_DIM == heads_all[None, :]).astype(jnp.bfloat16)


def per_device(field, cotangent, qk_weight, w_value, w_out):
    span_x = lax.axis_size("gx")
    span_y = lax.axis_size("gy")
    rows_x = field.shape[1]
    rows_y = field.shape[2]
    grid_depth = field.shape[3]
    grid_x = rows_x * span_x
    grid_y = rows_y * span_y
    cell_count = rows_x * rows_y * grid_depth
    start_x = lax.axis_index("gx") * rows_x
    start_y = lax.axis_index("gy") * rows_y
    sum_x = jnp.sum(field, axis=(2, 3), dtype=jnp.float32)
    sum_y = jnp.sum(field, axis=(1, 3), dtype=jnp.float32)
    sum_z = jnp.sum(field, axis=(1, 2), dtype=jnp.float32)
    part_x = lax.psum(sum_x, "gy")
    total_x = lax.all_gather(part_x, "gx", axis=1, tiled=True)
    part_y = lax.psum(sum_y, "gx")
    total_y = lax.all_gather(part_y, "gy", axis=1, tiled=True)
    total_z = lax.psum(sum_z, ("gx", "gy"))
    kernel_x, normed_x, inverse_x, query_x, keyset_x, factor_x = axis_features(
        total_x / (grid_y * grid_depth), qk_weight[0]
    )
    kernel_y, normed_y, inverse_y, query_y, keyset_y, factor_y = axis_features(
        total_y / (grid_x * grid_depth), qk_weight[1]
    )
    kernel_z, normed_z, inverse_z, query_z, keyset_z, factor_z = axis_features(
        total_z / (grid_x * grid_y), qk_weight[2]
    )
    values = jnp.dot(
        w_value.T, field.reshape(WIDTH, cell_count), preferred_element_type=jnp.float32
    ).astype(jnp.bfloat16)
    values = values.reshape(HEADS, HEAD_DIM, rows_x, rows_y, grid_depth)
    after_z = jnp.einsum(
        "hzk,hdxyk->hdxyz", kernel_z, values, preferred_element_type=jnp.float32
    ).astype(jnp.bfloat16)
    after_z = after_z.reshape(WIDTH, rows_x, rows_y, grid_depth)
    table_y = head_table(lax.axis_index("gy"), WIDTH // span_y)
    channel_y = jnp.einsum(
        "eh,hmn->emn", table_y, kernel_y, preferred_element_type=jnp.float32
    ).astype(jnp.bfloat16)
    pencil_z = lax.all_to_all(after_z, "gy", split_axis=0, concat_axis=2, tiled=True)
    mixed_y = jnp.einsum(
        "eyj,exjz->exyz", channel_y, pencil_z, preferred_element_type=jnp.float32
    ).astype(jnp.bfloat16)
    after_y = lax.all_to_all(mixed_y, "gy", split_axis=2, concat_axis=0, tiled=True)
    table_x = head_table(lax.axis_index("gx"), WIDTH // span_x)
    channel_x = jnp.einsum(
        "eh,hmn->emn", table_x, kernel_x, preferred_element_type=jnp.float32
    ).astype(jnp.bfloat16)
    pencil_y = lax.all_to_all(after_y, "gx", split_axis=0, concat_axis=1, tiled=True)
    mixed_x = jnp.einsum(
        "exi,eiyz->exyz", channel_x, pencil_y, preferred_element_type=jnp.float32
    ).astype(jnp.bfloat16)
    after_x = lax.all_to_all(mixed_x, "gx", split_axis=1, concat_axis=0, tiled=True)
    projected = jnp.dot(
        w_out.T, after_x.reshape(WIDTH, cell_count), preferred_element_type=jnp.float32
    )
    layer_output = (
        (projected + field.reshape(WIDTH, cell_count))
        .astype(jnp.bfloat16)
        .reshape(WIDTH, rows_x, rows_y, grid_depth)
    )
    upstream = jnp.dot(
        w_out, cotangent.reshape(WIDTH, cell_count), preferred_element_type=jnp.float32
    ).astype(jnp.bfloat16)
    upstream = upstream.reshape(WIDTH, rows_x, rows_y, grid_depth)
    pencil_grad = lax.all_to_all(upstream, "gx", split_axis=0, concat_axis=1, tiled=True)
    back_x = jnp.einsum(
        "exi,exyz->eiyz", channel_x, pencil_grad, preferred_element_type=jnp.float32
    ).astype(jnp.bfloat16)
    channel_gram = jnp.einsum(
        "emyz,enyz->emn", pencil_grad, pencil_y, preferred_element_type=jnp.float32
    )
    gram_x = jnp.einsum("eh,emn->hmn", table_x.astype(jnp.float32), channel_gram, precision=PRECISE)
    down_y = lax.all_to_all(back_x, "gx", split_axis=1, concat_axis=0, tiled=True)
    pencil_down = lax.all_to_all(down_y, "gy", split_axis=0, concat_axis=2, tiled=True)
    back_y = jnp.einsum(
        "eyj,exyz->exjz", channel_y, pencil_down, preferred_element_type=jnp.float32
    ).astype(jnp.bfloat16)
    channel_gram_y = jnp.einsum(
        "exmz,exnz->emn", pencil_down, pencil_z, preferred_element_type=jnp.float32
    )
    gram_y = jnp.einsum(
        "eh,emn->hmn", table_y.astype(jnp.float32), channel_gram_y, precision=PRECISE
    )
    down_z = lax.all_to_all(back_y, "gy", split_axis=2, concat_axis=0, tiled=True).reshape(
        HEADS, HEAD_DIM, rows_x, rows_y, grid_depth
    )
    grad_values = jnp.einsum(
        "hzk,hdxyz->hdxyk", kernel_z, down_z, preferred_element_type=jnp.float32
    ).astype(jnp.bfloat16)
    gram_z = jnp.einsum("hdxym,hdxyn->hmn", down_z, values, preferred_element_type=jnp.float32)
    grads_x = kernel_backward(gram_x, query_x, keyset_x, factor_x)
    grads_y = kernel_backward(gram_y, query_y, keyset_y, factor_y)
    grads_z = kernel_backward(gram_z, query_z, keyset_z, factor_z)
    summed = lax.psum(
        (grads_x[0], grads_x[1], grads_y[0], grads_y[1], grads_z[0], grads_z[1]), ("gx", "gy")
    )
    pull_x = pooled_grad(normed_x, inverse_x, qk_weight[0], summed[0], summed[1])
    pull_y = pooled_grad(normed_y, inverse_y, qk_weight[1], summed[2], summed[3])
    pull_z = pooled_grad(normed_z, inverse_z, qk_weight[2], summed[4], summed[5])
    local_x = lax.dynamic_slice_in_dim(pull_x, start_x, rows_x, 1) / (grid_y * grid_depth)
    local_y = lax.dynamic_slice_in_dim(pull_y, start_y, rows_y, 1) / (grid_x * grid_depth)
    local_z = pull_z / (grid_x * grid_y)
    through_values = jnp.dot(
        w_value, grad_values.reshape(WIDTH, cell_count), preferred_element_type=jnp.float32
    )
    through_values = through_values.reshape(WIDTH, rows_x, rows_y, grid_depth)
    field_grad = (
        cotangent.astype(jnp.float32)
        + through_values
        + local_x[:, :, None, None]
        + local_y[:, None, :, None]
        + local_z[:, None, None, :]
    ).astype(jnp.bfloat16)
    return (layer_output, field_grad)


def solution(mesh):
    placed = (
        P(None, ("groups", "gx"), "gy", None),
        P(None, ("groups", "gx"), "gy", None),
        P(),
        P(),
        P(),
    )
    return jax.shard_map(
        per_device,
        mesh=mesh,
        in_specs=placed,
        out_specs=(P(None, ("groups", "gx"), "gy", None), P(None, ("groups", "gx"), "gy", None)),
        check_vma=False,
    )
```

profile of v0, /device:TPU:0, one launch (start us, length us, event | category | flops | bytes accessed | tf_op | source)
XLA Modules:
  0.0 405.8 jit_solution(15734663713839999378)
XLA Ops:
  7.2 2.5 convert_reduce_fusion.1
  9.7 1.4 reshape.209
  13.3 4.2 %all-to-all-start.4 = ((bf16[64,2,4,512]{3,2,1,0:T(4,128)(2,1)}), bf16[64,2,4,512]{3,2,1,0:T(4,128)(2,1)S(1)}, u32[]{:S(2)}, u32[]{:S(2)}) async-start(bf16[64,2,4,512]{3,2,1,0:T(4,128)(2,1)} %reshape.210), calls=%async_computation.4 | async-start | bytes 1048576 | tf_op jit(solution)/shard_map/all_to_all | solution.py:117
  17.5 20.0 %psum.63 = f32[64,2]{1,0:T(8,128)S(1)} all-reduce(f32[64,2]{1,0:T(8,128)S(1)} %get-tuple-element.4), channel_id=1, replica_groups=mesh['groups'=2,'gx'=4,'gy'=4] {'gy'}, use_global_device_ids=true, to_apply=%region_1.0 | all-reduce | flops 128 | bytes 1024 | tf_op jit(solution)/shard_map/psum | solution.py:65
  37.6 5.1 %all-gather = f32[4,2,64]{2,1,0:T(2,128)S(1)} all-gather(f32[1,2,64]{2,1,0:T(2,128)S(1)} %bitcast.267), channel_id=1, replica_groups=mesh['groups'=2,'gx'=4,'gy'=4] {'gx'}, dimensions={0}, use_global_device_ids=true | all-gather | bytes 2560 | tf_op jit(solution)/shard_map/all_gather | solution.py:66
  45.3 1.4 reshape.200
  47.9 54.1 %all-reduce.5.cloned.1.call-done = f32[64,512]{1,0:T(8,128)} async-done(((f32[64,512]{1,0:T(8,128)}), f32[64,512]{1,0:T(8,128)}) %all-reduce.5.cloned.1.call-update) | async-done | bytes 131088 | tf_op jit(solution)/shard_map/psum | solution.py:69
  108.1 3.5 all-to-all-start.5
  111.6 7.0 %fusion.6 = bf16[8,512,512,1,1]{2,1,4,3,0:T(8,128)(2,1)S(1)} fusion(f32[8,8,512]{2,1,0:T(8,128)S(1)} %convolution_bitcast_fusion.4, f32[8,8,512]{2,1,0:T(8,128)S(1)} %convolution_bitcast_fusion.3), kind=kOutput, calls=%fused_computation.11 | convolution fusion | flops 205520896 | bytes 4456448 | tf_op jit(solution)/shard_map/hdm,hdn->hmn/dot_general | solution.py:24
  118.6 1.9 copy-done.1
  120.6 1.4 convolution_convert_fusion.3
  123.2 6.2 %all-to-all-start = ((bf16[64,2,4,512]{3,2,1,0:T(4,128)(2,1)}), bf16[64,2,4,512]{3,2,1,0:T(4,128)(2,1)S(1)}, u32[]{:S(2)}, u32[]{:S(2)}) async-start(bf16[64,2,4,512]{3,2,1,0:T(4,128)(2,1)} %copy.94), calls=%async_computation | async-start | bytes 1048576 | tf_op jit(solution)/shard_map/all_to_all | solution.py:91
  129.4 11.9 %psum.65 = f32[64,4]{1,0:T(8,128)S(1)} all-reduce(f32[64,4]{1,0:T(8,128)S(1)} %get-tuple-element.3), channel_id=1, replica_groups=mesh['groups'=2,'gx'=4,'gy'=4] {'gx'}, use_global_device_ids=true, to_apply=%region_7.0 | all-reduce | flops 256 | bytes 2048 | tf_op jit(solution)/shard_map/psum | solution.py:67
  141.4 12.4 %all-gather.1 = f32[4,4,64]{2,1,0:T(4,128)S(1)} all-gather(f32[1,4,64]{2,1,0:T(4,128)S(1)} %copy.97), channel_id=1, replica_groups=mesh['groups'=2,'gx'=4,'gy'=4] {'gy'}, dimensions={0}, use_global_device_ids=true | all-gather | bytes 5120 | tf_op jit(solution)/shard_map/all_gather | solution.py:68
  156.4 3.7 all-to-all-start.6
  162.9 1.3 copy.102
  164.2 7.1 %all-to-all-done.6 = bf16[64,2,4,512]{3,2,1,0:T(4,128)(2,1)S(1)} async-done(((bf16[64,2,4,512]{3,2,1,0:T(4,128)(2,1)}), bf16[64,2,4,512]{3,2,1,0:T(4,128)(2,1)S(1)}, u32[]{:S(2)}, u32[]{:S(2)}) %all-to-all-start.6) | async-done | bytes 524320 | tf_op jit(solution)/shard_map/all_to_all | solution.py:126
  171.3 3.5 all-to-all-start.1
  178.2 1.3 copy.120
  179.9 7.1 %all-to-all-done.1 = bf16[16,2,16,512]{3,1,0,2:T(2,128)(2,1)S(1)} async-done(((bf16[16,2,16,512]{3,1,0,2:T(2,128)(2,1)}), bf16[16,2,16,512]{3,1,0,2:T(2,128)(2,1)S(1)}, u32[]{:S(2)}, u32[]{:S(2)}) %all-to-all-start.1) | async-done | bytes 524320 | tf_op jit(solution)/shard_map/all_to_all | solution.py:95
  188.3 3.5 all-to-all-start.2
  194.5 6.1 %all-to-all-done.2 = bf16[64,2,4,512]{3,2,1,0:T(4,128)(2,1)S(1)} async-done(((bf16[64,2,4,512]{3,2,1,0:T(4,128)(2,1)}), bf16[64,2,4,512]{3,2,1,0:T(4,128)(2,1)S(1)}, u32[]{:S(2)}, u32[]{:S(2)}) %all-to-all-start.2) | async-done | bytes 524320 | tf_op jit(solution)/shard_map/all_to_all | solution.py:100
  200.6 3.5 all-to-all-start.7
  210.4 62.1 %all-reduce = (f32[64,16]{1,0:T(8,128)S(1)}, f32[64,16]{1,0:T(8,128)S(1)}, f32[64,8]{1,0:T(8,128)S(1)}, f32[64,8]{1,0:T(8,128)S(1)}) all-reduce(f32[64,16]{1,0:T(8,128)S(1)} %fusion.25, f32[64,16]{1,0:T(8,128)S(1)} %fusion.24, f32[64,8]{1,0:T(8,128)S(1)} %fusion.27, ...), channel_id=1, replica_groups=mesh['groups'=2,'gx'=4,'gy'=4] {'gx','gy'}, use_global_device_ids=true, to_apply=%region_12.13 | all-reduce | flops 3072 | bytes 24576 | tf_op jit(solution)/shard_map/psum | solution.py:146
  279.2 3.5 all-to-all-start.3
  282.8 3.0 convolution_convert_fusion.2
  285.9 4.5 %fusion.33 = f32[8,512,512,1,1]{2,1,0,4,3:T(8,128)} fusion(bf16[8,8,2,4,512]{4,1,0,3,2:T(8,128)(2,1)S(1)} %bitcast.242, bf16[8,8,2,4,512]{4,1,3,2,0:T(8,128)(2,1)S(1)} %bitcast.240), kind=kOutput, calls=%fused_computation.59 | convolution fusion | flops 268435456 | bytes 9437184 | tf_op jit(solution)/shard_map/hdxym,hdxyn->hmn/dot_general | solution.py:142
  291.4 7.4 %fusion.18 = f32[64,512]{1,0:T(8,128)} fusion(f32[8,8,512]{2,1,0:T(8,128)S(1)} %convolution_bitcast_fusion.4, f32[8,512,512,1,1]{2,1,0,4,3:T(8,128)} %fusion.33), kind=kOutput, calls=%fused_computation.26 | convolution fusion | flops 201359360 | bytes 8650752 | tf_op jit(solution)/shard_map/hmn,hdm->hdn/dot_general | solution.py:32
  298.8 7.6 %fusion.12 = f32[64,512]{1,0:T(8,128)} fusion(f32[8,8,512]{2,1,0:T(8,128)S(1)} %convolution_bitcast_fusion.3, f32[8,512,512,1,1]{2,1,0,4,3:T(8,128)S(1)} %copy-done.2), kind=kOutput, calls=%fused_computation.24 | convolution fusion | flops 201359360 | bytes 8650752 | tf_op jit(solution)/shard_map/hmn,hdn->hdm/dot_general | solution.py:31
  307.4 1.4 reshape.207
  310.4 83.7 %all-reduce.7.cloned.1.call-done = (f32[64,512]{1,0:T(8,128)}, f32[64,512]{1,0:T(8,128)}) async-done(((f32[64,512]{1,0:T(8,128)}, f32[64,512]{1,0:T(8,128)}), (f32[64,512]{1,0:T(8,128)}, f32[64,512]{1,0:T(8,128)})) %all-reduce.7.cloned.1.call-update) | async-done | bytes 262160 | tf_op jit(solution)/shard_map/psum | solution.py:146
  396.6 2.4 add_convert_fusion
  (133 shorter events, 45.3 us)
Async XLA Ops:
  7.2 40.1 %copy-start = (bf16[64,64]{1,0:T(8,128)(2,1)S(1)}, bf16[64,64]{1,0:T(8,128)(2,1)}, u32[]{:S(2)}) copy-start(bf16[64,64]{1,0:T(8,128)(2,1)} %param.8) | copy-start | bytes 24580
  7.2 94.8 %all-reduce.5.cloned.1.call-start = ((), (), s32[]{:S(2)}) async-start(), calls=%async_computation.8 | async-start | bytes 262144 | tf_op jit(solution)/shard_map/psum | solution.py:69
  13.3 92.6 %all-to-all-start.4 = ((bf16[64,2,4,512]{3,2,1,0:T(4,128)(2,1)}), bf16[64,2,4,512]{3,2,1,0:T(4,128)(2,1)S(1)}, u32[]{:S(2)}, u32[]{:S(2)}) async-start(bf16[64,2,4,512]{3,2,1,0:T(4,128)(2,1)} %reshape.210), calls=%async_computation.4 | async-start | bytes 1048576 | tf_op jit(solution)/shard_map/all_to_all | solution.py:117
  42.7 1.6 copy-start.11
  43.3 3.4 copy-start.17
  46.8 59.2 %copy-start.5 = (f32[64,8]{1,0:T(8,128)}, f32[64,8]{1,0:T(8,128)S(1)}, u32[]{:S(2)}) copy-start(f32[64,8]{1,0:T(8,128)S(1)} %copy.152) | copy-start | bytes 6148
  46.9 59.1 %copy-start.6 = (f32[64,8]{1,0:T(8,128)}, f32[64,8]{1,0:T(8,128)S(1)}, u32[]{:S(2)}) copy-start(f32[64,8]{1,0:T(8,128)S(1)} %copy.151) | copy-start | bytes 6148
  47.3 58.7 %copy-start.15 = (s32[16]{0:T(128)}, s32[16]{0:T(128)S(1)}, u32[]{:S(2)}) copy-start(s32[16]{0:T(128)S(1)} %get-tuple-element.24) | copy-start | bytes 196
  47.3 114.2 %copy-start.16 = (s32[16]{0:T(128)}, s32[16]{0:T(128)S(1)}, u32[]{:S(2)}) copy-start(s32[16]{0:T(128)S(1)} %get-tuple-element.23) | copy-start | bytes 196
  47.8 60.2 %copy-start.4 = (bf16[16,8,8,1]{1,2,3,0:T(8,128)(2,1)}, bf16[16,8,8,1]{1,2,3,0:T(8,128)(2,1)S(1)}, u32[]{:S(2)}) copy-start(bf16[16,8,8,1]{1,2,3,0:T(8,128)(2,1)S(1)} %copy.138) | copy-start | bytes 6148
  103.5 2.5 copy-start.12
  108.1 15.1 %all-to-all-start.5 = ((bf16[16,8,4,512]{3,2,0,1:T(4,128)(2,1)}), bf16[16,8,4,512]{3,2,0,1:T(4,128)(2,1)S(1)}, u32[]{:S(2)}, u32[]{:S(2)}) async-start(bf16[16,8,4,512]{3,2,0,1:T(4,128)(2,1)} %copy.113), calls=%async_computation.5 | async-start | bytes 1048576 | tf_op jit(solution)/shard_map/all_to_all | solution.py:125
  118.6 1.9 copy-start.1
  123.2 33.2 %all-to-all-start = ((bf16[64,2,4,512]{3,2,1,0:T(4,128)(2,1)}), bf16[64,2,4,512]{3,2,1,0:T(4,128)(2,1)S(1)}, u32[]{:S(2)}, u32[]{:S(2)}) async-start(bf16[64,2,4,512]{3,2,1,0:T(4,128)(2,1)} %copy.94), calls=%async_computation | async-start | bytes 1048576 | tf_op jit(solution)/shard_map/all_to_all | solution.py:91
  153.8 6.2 %copy-start.9 = (f32[4,4,64]{2,1,0:T(4,128)}, f32[4,4,64]{2,1,0:T(4,128)S(1)}, u32[]{:S(2)}) copy-start(f32[4,4,64]{2,1,0:T(4,128)S(1)} %all-gather.1) | copy-start | bytes 12292
  154.0 6.1 %copy-start.18 = (f32[16]{0:T(128)}, f32[16]{0:T(128)S(1)}, u32[]{:S(2)}) copy-start(f32[16]{0:T(128)S(1)} %get-tuple-element.18) | copy-start | bytes 196
  155.0 7.0 %copy-start.7 = (f32[64,16]{1,0:T(8,128)}, f32[64,16]{1,0:T(8,128)S(1)}, u32[]{:S(2)}) copy-start(f32[64,16]{1,0:T(8,128)S(1)} %copy.98) | copy-start | bytes 12292
  156.4 15.0 %all-to-all-start.6 = ((bf16[64,2,4,512]{3,2,1,0:T(4,128)(2,1)}), bf16[64,2,4,512]{3,2,1,0:T(4,128)(2,1)S(1)}, u32[]{:S(2)}, u32[]{:S(2)}) async-start(bf16[64,2,4,512]{3,2,1,0:T(4,128)(2,1)} %copy.116), calls=%async_computation.6 | async-start | bytes 1048576 | tf_op jit(solution)/shard_map/all_to_all | solution.py:126
  161.1 0.9 copy-start.8
  171.3 15.7 %all-to-all-start.1 = ((bf16[16,2,16,512]{3,1,0,2:T(2,128)(2,1)}), bf16[16,2,16,512]{3,1,0,2:T(2,128)(2,1)S(1)}, u32[]{:S(2)}, u32[]{:S(2)}) async-start(bf16[16,2,16,512]{3,1,0,2:T(2,128)(2,1)} %copy.102), calls=%async_computation.1 | async-start | bytes 1048576 | tf_op jit(solution)/shard_map/all_to_all | solution.py:95
  188.3 12.3 %all-to-all-start.2 = ((bf16[64,2,4,512]{3,2,1,0:T(4,128)(2,1)}), bf16[64,2,4,512]{3,2,1,0:T(4,128)(2,1)S(1)}, u32[]{:S(2)}, u32[]{:S(2)}) async-start(bf16[64,2,4,512]{3,2,1,0:T(4,128)(2,1)} %copy.105), calls=%async_computation.2 | async-start | bytes 1048576 | tf_op jit(solution)/shard_map/all_to_all | solution.py:100
  200.6 78.5 %all-to-all-start.7 = ((bf16[16,2,16,512]{3,1,0,2:T(2,128)(2,1)}), bf16[16,2,16,512]{3,1,0,2:T(2,128)(2,1)S(1)}, u32[]{:S(2)}, u32[]{:S(2)}) async-start(bf16[16,2,16,512]{3,1,0,2:T(2,128)(2,1)} %copy.120), calls=%async_computation.7 | async-start | bytes 1048576 | tf_op jit(solution)/shard_map/all_to_all | solution.py:136
  279.2 27.3 %all-to-all-start.3 = ((bf16[16,8,4,512]{3,2,0,1:T(4,128)(2,1)}), bf16[16,8,4,512]{3,2,0,1:T(4,128)(2,1)S(1)}, u32[]{:S(2)}, u32[]{:S(2)}) async-start(bf16[16,8,4,512]{3,2,0,1:T(4,128)(2,1)} %copy.109), calls=%async_computation.3 | async-start | bytes 1048576 | tf_op jit(solution)/shard_map/all_to_all | solution.py:104
  282.7 111.5 %all-reduce.7.cloned.1.call-start = ((), (), s32[]{:S(2)}) async-start(), calls=%async_computation.9 | async-start | bytes 524288 | tf_op jit(solution)/shard_map/psum | solution.py:146
  291.4 7.4 %copy-start.2 = (f32[8,512,512,1,1]{2,1,0,4,3:T(8,128)S(1)}, f32[8,512,512,1,1]{2,1,0,4,3:T(8,128)}, u32[]{:S(2)}) copy-start(f32[8,512,512,1,1]{2,1,0,4,3:T(8,128)} %fusion.33) | copy-start | bytes 25165828
  291.4 17.5 %copy-start.10 = (bf16[64,64]{1,0:T(8,128)(2,1)S(1)}, bf16[64,64]{1,0:T(8,128)(2,1)}, u32[]{:S(2)}) copy-start(bf16[64,64]{1,0:T(8,128)(2,1)} %param.9) | copy-start | bytes 24580
  298.8 96.5 %copy-start.3 = (f32[64,512]{1,0:T(8,128)S(1)}, f32[64,512]{1,0:T(8,128)}, u32[]{:S(2)}) copy-start(f32[64,512]{1,0:T(8,128)} %all-reduce.5.cloned.1.call-done) | copy-start | bytes 393220
  298.8 96.5 %copy-start.13 = (f32[512]{0:T(512)S(1)}, f32[512]{0:T(512)}, u32[]{:S(2)}) copy-start(f32[512]{0:T(512)} %copy-done.12) | copy-start | bytes 6148
  298.8 97.7 %copy-start.14 = (f32[512]{0:T(512)S(1)}, f32[512]{0:T(512)}, u32[]{:S(2)}) copy-start(f32[512]{0:T(512)} %get-tuple-element.13) | copy-start | bytes 6148
Sparse Core Ops, SparseCore 0:
  12.0 89.8 all-reduce.4
  306.5 87.5 all-reduce.6
where the time goes:
time: 408 us; the launch traced here: 406 us
  waiting for transfers between devices  158 us (39%)
  blocking collectives  112 us (27%)
  matrix products  54.6 us (13%)
  starting transfers between devices  31.5 us (8%)
  local copies, waits for them, and re-layouts  25.7 us (6%)
  between operations  14.7 us (4%)
  other arithmetic  9.58 us (2%)
    psum x1, waiting for transfers between devices, per_device(): lax.psum((grads_x[0], grads_x[1], grads_y[0], grads_y[1], grads_z[0], gra...  83.7 us
    psum x1, blocking collectives, per_device(): lax.psum((grads_x[0], grads_x[1], grads_y[0], grads_y[1], grads_z[0], gra...  62.1 us
    psum x1, waiting for transfers between devices, per_device(): total_z = lax.psum(sum_z, ('gx', 'gy'))  54.1 us
    psum x1, blocking collectives, per_device(): part_x = lax.psum(sum_x, 'gy')  20 us
    all_gather x1, blocking collectives, per_device(): total_y = lax.all_gather(part_y, 'gy', axis=1, tiled=True)  12.4 us
    psum x1, blocking collectives, per_device(): part_y = lax.psum(sum_y, 'gx')  11.9 us
    dot_general x3, matrix products, kernel_backward(): jnp.einsum('hmn,hdn->hdm', gram, keyset, precision=PRECISE)  9.51 us
    dot_general x3, matrix products, kernel_backward(): jnp.einsum('hmn,hdm->hdn', gram, queries, precision=PRECISE)  9.29 us
  transfers between devices with their start and end apart: 10, of which 5 were waited for; matrix products, arithmetic and copies ran while one was open for 19% of the time, Pallas kernels for 0%

commit v1 on v0

v1 whole, which is shorter than its diff:
```python
import math

import jax
import jax.numpy as jnp
from jax import lax
from jax.sharding import PartitionSpec as P

WIDTH = 64
HEADS = 8
HEAD_DIM = 8
LANES = 128

EPSILON = 1e-06
PRECISE = lax.Precision.HIGHEST
AXES = ("gx", "gy")


def swap(part, axis, size, step):
    return lax.ppermute(part, axis, [(i, i ^ step) for i in range(size)])


def swap_gather(part, axis, size):
    found = jnp.stack([part] + [swap(part, axis, size, step) for step in range(1, size)])
    return found[jnp.arange(size) ^ lax.axis_index(axis)]


def swap_scatter(parts, axis, size):
    me = lax.axis_index(axis)
    total = parts[me]
    for step in range(1, size):
        total = total + swap(parts[me ^ step], axis, size, step)
    return total


def gather(part, count, flat=True):
    if flat:
        return swap_gather(part, AXES, count)
    size_x, size_y = lax.axis_size("gx"), lax.axis_size("gy")
    found = swap_gather(swap_gather(part, "gy", size_y), "gx", size_x)
    return found.reshape((count,) + part.shape)


def reduce_blocks(total, count):
    width, depth = total.shape
    blocks = total.reshape(width, depth // LANES, LANES).transpose(1, 0, 2)
    blocks = blocks.reshape(count, width * depth // LANES // count, LANES)
    size_x, size_y = lax.axis_size("gx"), lax.axis_size("gy")
    mine = swap_scatter(blocks.reshape((size_x, size_y) + blocks.shape[1:]), "gx", size_x)
    mine = swap_scatter(mine, "gy", size_y)
    whole = gather(mine, count).reshape(depth // LANES, width, LANES)
    return whole.transpose(1, 0, 2).reshape(width, depth)


def axis_features(pooled, weights):
    inverse = lax.rsqrt(jnp.mean(pooled * pooled, axis=0, keepdims=True) + EPSILON)
    normed = pooled * inverse
    length = pooled.shape[1]
    factor = 1.0 / math.sqrt(HEAD_DIM * length)
    queries = jnp.dot(weights[0].T, normed, precision=PRECISE).reshape(HEADS, HEAD_DIM, length)
    keyset = jnp.dot(weights[1].T, normed, precision=PRECISE).reshape(HEADS, HEAD_DIM, length)
    return (normed, inverse, queries, keyset, factor)


def axis_kernel(queries, keyset, factor):
    scores = jnp.einsum("hdm,hdn->hmn", queries, keyset, precision=PRECISE)
    return (scores * factor).astype(jnp.bfloat16)


def kernel_backward(gram, queries, keyset, factor):
    grad_query = factor * jnp.einsum("hmn,hdn->hdm", gram, keyset, precision=PRECISE)
    grad_keyset = factor * jnp.einsum("hmn,hdm->hdn", gram, queries, precision=PRECISE)
    return (grad_query, grad_keyset)


def grad_of_normed(weights, grad_query, grad_keyset):
    length = grad_query.shape[-1]
    grad_normed = jnp.dot(weights[0], grad_query.reshape(WIDTH, length), precision=PRECISE)
    return grad_normed + jnp.dot(
        weights[1], grad_keyset.reshape(WIDTH, length), precision=PRECISE
    )


def pooled_grad(normed, inverse, grad_normed):
    return inverse * (grad_normed - normed * jnp.mean(grad_normed * normed, axis=0, keepdims=True))


def f32_einsum(pattern, left, right):
    return jnp.einsum(pattern, left, right, preferred_element_type=jnp.float32)


def per_device(field, cotangent, qk_weight, w_value, w_out):
    span_x = lax.axis_size("gx")
    span_y = lax.axis_size("gy")
    count = span_x * span_y
    rows_x, rows_y, depth = field.shape[1:]
    cells = rows_x * rows_y
    grid_x = rows_x * span_x
    grid_y = rows_y * span_y
    start_x = lax.axis_index("gx") * rows_x
    start_y = lax.axis_index("gy") * rows_y
    bf16 = jnp.bfloat16

    cols = field.reshape(WIDTH, cells, depth)
    cots = cotangent.reshape(WIDTH, cells, depth)

    sum_z = jnp.sum(cols, axis=1, dtype=jnp.float32)
    sum_rows = jnp.sum(cols, axis=2, dtype=jnp.float32)
    rows_all = gather(sum_rows.T, count).reshape(span_x, span_y, rows_x, rows_y, WIDTH)
    total_x = jnp.sum(rows_all, axis=(1, 3)).reshape(grid_x, WIDTH).T
    total_y = jnp.sum(rows_all, axis=(0, 2)).reshape(grid_y, WIDTH).T
    total_z = reduce_blocks(sum_z, count)

    normed_x, inverse_x, query_x, keyset_x, factor_x = axis_features(
        total_x / (grid_y * depth), qk_weight[0]
    )
    normed_y, inverse_y, query_y, keyset_y, factor_y = axis_features(
        total_y / (grid_x * depth), qk_weight[1]
    )
    normed_z, inverse_z, query_z, keyset_z, factor_z = axis_features(
        total_z / (grid_x * grid_y), qk_weight[2]
    )
    kernel_x = axis_kernel(query_x, keyset_x, factor_x)
    kernel_y = axis_kernel(query_y, keyset_y, factor_y)
    query_b = query_z.astype(bf16)
    keyset_b = keyset_z.astype(bf16)

    wv = w_value.reshape(WIDTH, HEADS, HEAD_DIM)
    wo = w_out.reshape(HEADS, HEAD_DIM, WIDTH)
    coef_f = f32_einsum("cpk,hgk->cphg", cols, keyset_b)
    coef_c = f32_einsum("cpz,hgz->cphg", cots, query_b)
    low_f = jnp.einsum("chd,cphg->phdg", wv.astype(jnp.float32), coef_f, precision=PRECISE)
    low_c = jnp.einsum("hdc,cphg->phdg", wo.astype(jnp.float32), coef_c, precision=PRECISE)
    squares = HEAD_DIM * HEAD_DIM
    both = jnp.stack([low_f, low_c]).astype(bf16).reshape(2, cells, HEADS * squares)
    both = gather(both, count, False).reshape(span_x, span_y, 2, rows_x, rows_y, HEADS * squares)
    both = both.transpose(2, 0, 3, 1, 4, 5).reshape(2, grid_x, grid_y, HEADS, squares)
    low_f, low_c = both[0], both[1]

    mid_f = f32_einsum("hyj,xjhq->xyhq", kernel_y, low_f).astype(bf16)
    top_f = f32_einsum("hxi,iyhq->xyhq", kernel_x, mid_f)
    mid_c = f32_einsum("hxi,xyhq->iyhq", kernel_x, low_c).astype(bf16)
    top_c = f32_einsum("hyj,xyhq->xjhq", kernel_y, mid_c)
    gram_x = factor_z * f32_einsum("myhq,nyhq->hmn", low_c, mid_f)
    gram_y = factor_z * f32_einsum("xmhq,xnhq->hmn", mid_c, low_f)

    def here(top):
        top = lax.dynamic_slice_in_dim(top, start_x, rows_x, 0)
        top = lax.dynamic_slice_in_dim(top, start_y, rows_y, 1)
        return top.reshape(cells, HEADS, HEAD_DIM, HEAD_DIM)

    left_f = factor_z * jnp.einsum(
        "hdc,phdg->cphg", wo.astype(jnp.float32), here(top_f), precision=PRECISE
    )
    left_c = factor_z * jnp.einsum(
        "chd,phdg->cphg", wv.astype(jnp.float32), here(top_c), precision=PRECISE
    )
    left_f = left_f.astype(bf16)
    left_c = left_c.astype(bf16)

    grad_query_z = f32_einsum("cphg,cpz->hgz", left_f, cots)
    grad_keyset_z = f32_einsum("cphg,cpz->hgz", left_c, cols)
    gn_z = reduce_blocks(grad_of_normed(qk_weight[2], grad_query_z, grad_keyset_z), count)

    layer_output = (cols.astype(jnp.float32) + f32_einsum("cphg,hgz->cpz", left_f, query_b)).astype(bf16)
    through = f32_einsum("cphg,hgz->cpz", left_c, keyset_b)

    gn_x = grad_of_normed(qk_weight[0], *kernel_backward(gram_x, query_x, keyset_x, factor_x))
    gn_y = grad_of_normed(qk_weight[1], *kernel_backward(gram_y, query_y, keyset_y, factor_y))
    pull_x = pooled_grad(normed_x, inverse_x, gn_x)
    pull_y = pooled_grad(normed_y, inverse_y, gn_y)
    pull_z = pooled_grad(normed_z, inverse_z, gn_z)
    local_x = lax.dynamic_slice_in_dim(pull_x, start_x, rows_x, 1) / (grid_y * depth)
    local_y = lax.dynamic_slice_in_dim(pull_y, start_y, rows_y, 1) / (grid_x * depth)
    local_xy = (local_x[:, :, None] + local_y[:, None, :]).reshape(WIDTH, cells)
    local_z = pull_z / (grid_x * grid_y)
    field_grad = (
        cots.astype(jnp.float32) + through + local_xy[:, :, None] + local_z[:, None, :]
    ).astype(bf16)
    return (layer_output.reshape(field.shape), field_grad.reshape(field.shape))


def solution(mesh):
    placed = P(None, ("groups", "gx"), "gy", None)
    return jax.shard_map(
        per_device,
        mesh=mesh,
        in_specs=(placed, placed, P(), P(), P()),
        out_specs=(placed, placed),
        check_vma=False,
    )
```

time: 408 us -> 205 us (0.50)
  blocking collectives: 112 us -> 0 us
  waiting for transfers between devices: 158 us -> 109 us
  matrix products: 54.6 us -> 9.39 us
  starting transfers between devices: 31.5 us -> 69.6 us
  between operations: 14.7 us -> 1.52 us
  local copies, waits for them, and re-layouts: 25.7 us -> 12.6 us
  other arithmetic: 9.58 us -> 2.52 us
    psum x2 -> x0, waiting for transfers between devices: 138 us -> none  [the longest x1 83.7 us: per_device(): lax.psum((grads_x[0], grads_x[1], grads_y[0], grads_y[1], grads_z[0], gra...]
    ppermute x0 -> x63, waiting for transfers between devices: none -> 109 us  [swap(): return lax.ppermute(part, axis, [(i, i ^ step) for i in range(size)])]
    psum x3 -> x0, blocking collectives: 94.1 us -> none  [the longest x1 62.1 us: per_device(): lax.psum((grads_x[0], grads_x[1], grads_y[0], grads_y[1], grads_z[0], gra...]
    ppermute x0 -> x63, starting transfers between devices: none -> 69.6 us  [swap(): return lax.ppermute(part, axis, [(i, i ^ step) for i in range(size)])]
    all_to_all x8 -> x0, starting transfers between devices: 31.4 us -> none  [the longest x1 6.22 us: per_device(): lax.all_to_all(after_z, 'gy', split_axis=0, concat_axis=2, tiled=True)]
    dot_general x25 -> x24, matrix products: 29.4 us -> 7.15 us  [the longest x12 3.79 us: f32_einsum(): return jnp.einsum(pattern, left, right, preferred_element_type=jnp.float32)]
    all_to_all x8 -> x0, waiting for transfers between devices: 20.3 us -> none  [the longest x1 7.13 us: per_device(): lax.all_to_all(mixed_y, 'gy', split_axis=2, concat_axis=0, tiled=True)]
    all_gather x2 -> x0, blocking collectives: 17.5 us -> none  [the longest x1 12.4 us: per_device(): total_y = lax.all_gather(part_y, 'gy', axis=1, tiled=True)]
  transfers between devices with their start and end apart: 10 -> 63, of which waited for: 5 -> 40; matrix products, arithmetic and copies ran while one was open for 19% -> 4% of each run, Pallas kernels for 0% -> 0%
where the time goes in v1:
time: 205 us
  waiting for transfers between devices  109 us (53%)
  starting transfers between devices  69.6 us (34%)
  local copies, waits for them, and re-layouts  12.6 us (6%)
  matrix products  9.39 us (5%)
  other arithmetic  2.52 us (1%)
    ppermute x63, waiting for transfers between devices, swap(): return lax.ppermute(part, axis, [(i, i ^ step) for i in range(size)])  109 us
    ppermute x63, starting transfers between devices, swap(): return lax.ppermute(part, axis, [(i, i ^ step) for i in range(size)])  69.6 us
  transfers between devices with their start and end apart: 63, of which 40 were waited for; matrix products, arithmetic and copies ran while one was open for 4% of the time, Pallas kernels for 0%

profile of v1, /device:TPU:0, one launch (start us, length us, event | category | flops | bytes accessed | tf_op | source)
XLA Modules:
  0.0 205.0 jit_solution(11872246099821922474)
XLA Ops:
  2.4 4.4 %collective-permute-start.40 = (f32[8,64]{1,0:T(8,128)S(1)}, f32[8,64]{1,0:T(8,128)S(1)}, u32[]{:S(2)}, u32[]{:S(2)}) collective-permute-start(f32[8,64]{1,0:T(8,128)S(1)} %bitcast.473), channel_id=1, source_target_pairs={{0,14},{1,15},{2,12},{3,13},{4,10},{5,11},{6,8},{7,9},{8,6},{9,7},... | collective-permute-start | bytes 6152 | tf_op jit(solution)/shard_map/ppermute | solution.py:19
  15.6 2.6 %collective-permute-done.28 = f32[8,64]{1,0:T(8,128)S(1)} collective-permute-done((f32[8,64]{1,0:T(8,128)S(1)}, f32[8,64]{1,0:T(8,128)S(1)}, u32[]{:S(2)}, u32[]{:S(2)}) %collective-permute-start.28) | collective-permute-done | bytes 2080 | tf_op jit(solution)/shard_map/ppermute | solution.py:19
  18.2 3.3 %collective-permute-start.29 = (f32[8,64]{1,0:T(8,128)S(1)}, f32[8,64]{1,0:T(8,128)S(1)}, u32[]{:S(2)}, u32[]{:S(2)}) collective-permute-start(f32[8,64]{1,0:T(8,128)S(1)} %bitcast.480), channel_id=1, source_target_pairs={{0,3},{1,2},{2,1},{3,0},{4,7},{5,6},{6,5},{7,4},{8,11},{9,10},{10,... | collective-permute-start | bytes 6152 | tf_op jit(solution)/shard_map/ppermute | solution.py:19
  24.8 3.0 %collective-permute-done.31 = f32[8,64]{1,0:T(8,128)S(1)} collective-permute-done((f32[8,64]{1,0:T(8,128)S(1)}, f32[8,64]{1,0:T(8,128)S(1)}, u32[]{:S(2)}, u32[]{:S(2)}) %collective-permute-start.31) | collective-permute-done | bytes 2080 | tf_op jit(solution)/shard_map/ppermute | solution.py:19
  31.7 3.1 %collective-permute-start.33 = (f32[8,64]{1,0:T(8,128)S(1)}, f32[8,64]{1,0:T(8,128)S(1)}, u32[]{:S(2)}, u32[]{:S(2)}) collective-permute-start(f32[8,64]{1,0:T(8,128)S(1)} %bitcast.484), channel_id=1, source_target_pairs={{0,7},{1,6},{2,5},{3,4},{4,3},{5,2},{6,1},{7,0},{8,15},{9,14},{10,... | collective-permute-start | bytes 6152 | tf_op jit(solution)/shard_map/ppermute | solution.py:19
  40.3 4.4 %collective-permute-done.35 = f32[8,64]{1,0:T(8,128)S(1)} collective-permute-done((f32[8,64]{1,0:T(8,128)S(1)}, f32[8,64]{1,0:T(8,128)S(1)}, u32[]{:S(2)}, u32[]{:S(2)}) %collective-permute-start.35) | collective-permute-done | bytes 2080 | tf_op jit(solution)/shard_map/ppermute | solution.py:19
  46.5 3.5 %collective-permute-done.36 = f32[8,64]{1,0:T(8,128)S(1)} collective-permute-done((f32[8,64]{1,0:T(8,128)S(1)}, f32[8,64]{1,0:T(8,128)S(1)}, u32[]{:S(2)}, u32[]{:S(2)}) %collective-permute-start.36) | collective-permute-done | bytes 2080 | tf_op jit(solution)/shard_map/ppermute | solution.py:19
  50.6 4.0 %collective-permute-start.2 = (f32[4,16,128]{2,1,0:T(8,128)S(1)}, f32[4,16,128]{2,1,0:T(8,128)S(1)}, u32[]{:S(2)}, u32[]{:S(2)}) collective-permute-start(f32[4,16,128]{2,1,0:T(8,128)S(1)} %bitcast.468), channel_id=1, source_target_pairs={{0,12},{4,8},{8,4},{12,0},{1,13},{5,9},{9,5},{13,1},{2,14},{6,10},... | collective-permute-start | bytes 98312 | tf_op jit(solution)/shard_map/ppermute | solution.py:19
  66.9 2.9 %collective-permute-start.18 = (f32[16,128]{1,0:T(8,128)S(1)}, f32[16,128]{1,0:T(8,128)S(1)}, u32[]{:S(2)}, u32[]{:S(2)}) collective-permute-start(f32[16,128]{1,0:T(8,128)S(1)} %get-tuple-element.11), channel_id=1, source_target_pairs={{0,13},{1,12},{2,15},{3,14},{4,9},{5,8},{6,11},{7,10},{8,5},{9,4},... | collective-permute-start | bytes 24584 | tf_op jit(solution)/shard_map/ppermute | solution.py:19
  69.9 2.9 %collective-permute-start.16 = (f32[16,128]{1,0:T(8,128)S(1)}, f32[16,128]{1,0:T(8,128)S(1)}, u32[]{:S(2)}, u32[]{:S(2)}) collective-permute-start(f32[16,128]{1,0:T(8,128)S(1)} %get-tuple-element.11), channel_id=1, source_target_pairs={{0,11},{1,10},{2,9},{3,8},{4,15},{5,14},{6,13},{7,12},{8,3},{9,2},... | collective-permute-start | bytes 24584 | tf_op jit(solution)/shard_map/ppermute | solution.py:19
  73.2 4.2 %collective-permute-done.7 = f32[16,128]{1,0:T(8,128)S(1)} collective-permute-done((f32[16,128]{1,0:T(8,128)S(1)}, f32[16,128]{1,0:T(8,128)S(1)}, u32[]{:S(2)}, u32[]{:S(2)}) %collective-permute-start.7) | collective-permute-done | bytes 8224 | tf_op jit(solution)/shard_map/ppermute | solution.py:19
  79.2 3.6 %collective-permute-done.8 = f32[16,128]{1,0:T(8,128)S(1)} collective-permute-done((f32[16,128]{1,0:T(8,128)S(1)}, f32[16,128]{1,0:T(8,128)S(1)}, u32[]{:S(2)}, u32[]{:S(2)}) %collective-permute-start.8) | collective-permute-done | bytes 8224 | tf_op jit(solution)/shard_map/ppermute | solution.py:19
  84.0 3.1 %collective-permute-done.10 = f32[16,128]{1,0:T(8,128)S(1)} collective-permute-done((f32[16,128]{1,0:T(8,128)S(1)}, f32[16,128]{1,0:T(8,128)S(1)}, u32[]{:S(2)}, u32[]{:S(2)}) %collective-permute-start.10) | collective-permute-done | bytes 8224 | tf_op jit(solution)/shard_map/ppermute | solution.py:19
  87.5 3.6 %collective-permute-done.11 = f32[16,128]{1,0:T(8,128)S(1)} collective-permute-done((f32[16,128]{1,0:T(8,128)S(1)}, f32[16,128]{1,0:T(8,128)S(1)}, u32[]{:S(2)}, u32[]{:S(2)}) %collective-permute-start.11) | collective-permute-done | bytes 8224 | tf_op jit(solution)/shard_map/ppermute | solution.py:19
  92.7 3.3 %collective-permute-done.12 = f32[16,128]{1,0:T(8,128)S(1)} collective-permute-done((f32[16,128]{1,0:T(8,128)S(1)}, f32[16,128]{1,0:T(8,128)S(1)}, u32[]{:S(2)}, u32[]{:S(2)}) %collective-permute-start.12) | collective-permute-done | bytes 8224 | tf_op jit(solution)/shard_map/ppermute | solution.py:19
  96.5 3.1 %collective-permute-done.13 = f32[16,128]{1,0:T(8,128)S(1)} collective-permute-done((f32[16,128]{1,0:T(8,128)S(1)}, f32[16,128]{1,0:T(8,128)S(1)}, u32[]{:S(2)}, u32[]{:S(2)}) %collective-permute-start.13) | collective-permute-done | bytes 8224 | tf_op jit(solution)/shard_map/ppermute | solution.py:19
  99.6 4.5 %collective-permute-done.14 = f32[16,128]{1,0:T(8,128)S(1)} collective-permute-done((f32[16,128]{1,0:T(8,128)S(1)}, f32[16,128]{1,0:T(8,128)S(1)}, u32[]{:S(2)}, u32[]{:S(2)}) %collective-permute-start.14) | collective-permute-done | bytes 8224 | tf_op jit(solution)/shard_map/ppermute | solution.py:19
  104.5 5.1 %collective-permute-done.15 = f32[16,128]{1,0:T(8,128)S(1)} collective-permute-done((f32[16,128]{1,0:T(8,128)S(1)}, f32[16,128]{1,0:T(8,128)S(1)}, u32[]{:S(2)}, u32[]{:S(2)}) %collective-permute-start.15) | collective-permute-done | bytes 8224 | tf_op jit(solution)/shard_map/ppermute | solution.py:19
  109.7 5.7 %collective-permute-done.20 = f32[16,128]{1,0:T(8,128)S(1)} collective-permute-done((f32[16,128]{1,0:T(8,128)S(1)}, f32[16,128]{1,0:T(8,128)S(1)}, u32[]{:S(2)}, u32[]{:S(2)}) %collective-permute-start.20) | collective-permute-done | bytes 8224 | tf_op jit(solution)/shard_map/ppermute | solution.py:19
  120.5 2.5 %collective-permute-start.21 = (bf16[2,8,512]{2,1,0:T(8,128)(2,1)S(1)}, bf16[2,8,512]{2,1,0:T(8,128)(2,1)S(1)}, u32[]{:S(2)}, u32[]{:S(2)}) collective-permute-start(bf16[2,8,512]{2,1,0:T(8,128)(2,1)S(1)} %constant_dynamic-update-slice_fusion.32), channel_id=1, source_target_pairs={{0,1},{1,0},{2,3},{3,2},{4,5},{5,4},{6,7},{7,6},{8,9},{9,8},{10,11... | collective-permute-start | bytes 49160 | tf_op jit(solution)/shard_map/ppermute | solution.py:19
  127.9 2.8 %collective-permute-done.25 = bf16[4,2,8,512]{3,2,1,0:T(8,128)(2,1)S(1)} collective-permute-done((bf16[4,2,8,512]{3,2,1,0:T(8,128)(2,1)S(1)}, bf16[4,2,8,512]{3,2,1,0:T(8,128)(2,1)S(1)}, u32[]{:S(2)}, u32[]{:S(2)}) %collective-permute-start.25) | collective-permute-done | bytes 65568 | tf_op jit(solution)/shard_map/ppermute | solution.py:19
  147.1 3.4 %collective-permute-done.47 = f32[16,128]{1,0:T(8,128)S(1)} collective-permute-done((f32[16,128]{1,0:T(8,128)S(1)}, f32[16,128]{1,0:T(8,128)S(1)}, u32[]{:S(2)}, u32[]{:S(2)}) %collective-permute-start.47) | collective-permute-done | bytes 8224 | tf_op jit(solution)/shard_map/ppermute | solution.py:19
  154.5 2.9 %collective-permute-start.60 = (f32[16,128]{1,0:T(8,128)S(1)}, f32[16,128]{1,0:T(8,128)S(1)}, u32[]{:S(2)}, u32[]{:S(2)}) collective-permute-start(f32[16,128]{1,0:T(8,128)S(1)} %get-tuple-element.9), channel_id=1, source_target_pairs={{0,13},{1,12},{2,15},{3,14},{4,9},{5,8},{6,11},{7,10},{8,5},{9,4},... | collective-permute-start | bytes 24584 | tf_op jit(solution)/shard_map/ppermute | solution.py:19
  161.5 3.4 %collective-permute-done.49 = f32[16,128]{1,0:T(8,128)S(1)} collective-permute-done((f32[16,128]{1,0:T(8,128)S(1)}, f32[16,128]{1,0:T(8,128)S(1)}, u32[]{:S(2)}, u32[]{:S(2)}) %collective-permute-start.49) | collective-permute-done | bytes 8224 | tf_op jit(solution)/shard_map/ppermute | solution.py:19
  167.0 3.3 %collective-permute-done.50 = f32[16,128]{1,0:T(8,128)S(1)} collective-permute-done((f32[16,128]{1,0:T(8,128)S(1)}, f32[16,128]{1,0:T(8,128)S(1)}, u32[]{:S(2)}, u32[]{:S(2)}) %collective-permute-start.50) | collective-permute-done | bytes 8224 | tf_op jit(solution)/shard_map/ppermute | solution.py:19
  171.6 3.1 %collective-permute-done.52 = f32[16,128]{1,0:T(8,128)S(1)} collective-permute-done((f32[16,128]{1,0:T(8,128)S(1)}, f32[16,128]{1,0:T(8,128)S(1)}, u32[]{:S(2)}, u32[]{:S(2)}) %collective-permute-start.52) | collective-permute-done | bytes 8224 | tf_op jit(solution)/shard_map/ppermute | solution.py:19
  175.3 3.3 %collective-permute-done.53 = f32[16,128]{1,0:T(8,128)S(1)} collective-permute-done((f32[16,128]{1,0:T(8,128)S(1)}, f32[16,128]{1,0:T(8,128)S(1)}, u32[]{:S(2)}, u32[]{:S(2)}) %collective-permute-start.53) | collective-permute-done | bytes 8224 | tf_op jit(solution)/shard_map/ppermute | solution.py:19
  180.5 3.0 %collective-permute-done.54 = f32[16,128]{1,0:T(8,128)S(1)} collective-permute-done((f32[16,128]{1,0:T(8,128)S(1)}, f32[16,128]{1,0:T(8,128)S(1)}, u32[]{:S(2)}, u32[]{:S(2)}) %collective-permute-start.54) | collective-permute-done | bytes 8224 | tf_op jit(solution)/shard_map/ppermute | solution.py:19
  184.5 2.6 %collective-permute-done.55 = f32[16,128]{1,0:T(8,128)S(1)} collective-permute-done((f32[16,128]{1,0:T(8,128)S(1)}, f32[16,128]{1,0:T(8,128)S(1)}, u32[]{:S(2)}, u32[]{:S(2)}) %collective-permute-start.55) | collective-permute-done | bytes 8224 | tf_op jit(solution)/shard_map/ppermute | solution.py:19
  187.1 4.5 %collective-permute-done.56 = f32[16,128]{1,0:T(8,128)S(1)} collective-permute-done((f32[16,128]{1,0:T(8,128)S(1)}, f32[16,128]{1,0:T(8,128)S(1)}, u32[]{:S(2)}, u32[]{:S(2)}) %collective-permute-start.56) | collective-permute-done | bytes 8224 | tf_op jit(solution)/shard_map/ppermute | solution.py:19
  192.3 4.8 %collective-permute-done.57 = f32[16,128]{1,0:T(8,128)S(1)} collective-permute-done((f32[16,128]{1,0:T(8,128)S(1)}, f32[16,128]{1,0:T(8,128)S(1)}, u32[]{:S(2)}, u32[]{:S(2)}) %collective-permute-start.57) | collective-permute-done | bytes 8224 | tf_op jit(solution)/shard_map/ppermute | solution.py:19
  197.2 5.7 %collective-permute-done.62 = f32[16,128]{1,0:T(8,128)S(1)} collective-permute-done((f32[16,128]{1,0:T(8,128)S(1)}, f32[16,128]{1,0:T(8,128)S(1)}, u32[]{:S(2)}, u32[]{:S(2)}) %collective-permute-start.62) | collective-permute-done | bytes 8224 | tf_op jit(solution)/shard_map/ppermute | solution.py:19
  (263 shorter events, 87.8 us)
Async XLA Ops:
  2.4 53.8 %collective-permute-start.40 = (f32[8,64]{1,0:T(8,128)S(1)}, f32[8,64]{1,0:T(8,128)S(1)}, u32[]{:S(2)}, u32[]{:S(2)}) collective-permute-start(f32[8,64]{1,0:T(8,128)S(1)} %bitcast.473), channel_id=1, source_target_pairs={{0,14},{1,15},{2,12},{3,13},{4,10},{5,11},{6,8},{7,9},{8,6},{9,7},... | collective-permute-start | bytes 6152 | tf_op jit(solution)/shard_map/ppermute | solution.py:19
  6.8 47.8 %collective-permute-start.39 = (f32[8,64]{1,0:T(8,128)S(1)}, f32[8,64]{1,0:T(8,128)S(1)}, u32[]{:S(2)}, u32[]{:S(2)}) collective-permute-start(f32[8,64]{1,0:T(8,128)S(1)} %bitcast.474), channel_id=1, source_target_pairs={{0,13},{1,12},{2,15},{3,14},{4,9},{5,8},{6,11},{7,10},{8,5},{9,4},... | collective-permute-start | bytes 6152 | tf_op jit(solution)/shard_map/ppermute | solution.py:19
  8.6 46.0 %collective-permute-start.38 = (f32[8,64]{1,0:T(8,128)S(1)}, f32[8,64]{1,0:T(8,128)S(1)}, u32[]{:S(2)}, u32[]{:S(2)}) collective-permute-start(f32[8,64]{1,0:T(8,128)S(1)} %bitcast.475), channel_id=1, source_target_pairs={{0,12},{1,13},{2,14},{3,15},{4,8},{5,9},{6,10},{7,11},{8,4},{9,5},... | collective-permute-start | bytes 6152 | tf_op jit(solution)/shard_map/ppermute | solution.py:19
  9.5 41.1 %collective-permute-start.37 = (f32[8,64]{1,0:T(8,128)S(1)}, f32[8,64]{1,0:T(8,128)S(1)}, u32[]{:S(2)}, u32[]{:S(2)}) collective-permute-start(f32[8,64]{1,0:T(8,128)S(1)} %bitcast.476), channel_id=1, source_target_pairs={{0,11},{1,10},{2,9},{3,8},{4,15},{5,14},{6,13},{7,12},{8,3},{9,2},... | collective-permute-start | bytes 6152 | tf_op jit(solution)/shard_map/ppermute | solution.py:19
  18.2 5.4 %collective-permute-start.29 = (f32[8,64]{1,0:T(8,128)S(1)}, f32[8,64]{1,0:T(8,128)S(1)}, u32[]{:S(2)}, u32[]{:S(2)}) collective-permute-start(f32[8,64]{1,0:T(8,128)S(1)} %bitcast.480), channel_id=1, source_target_pairs={{0,3},{1,2},{2,1},{3,0},{4,7},{5,6},{6,5},{7,4},{8,11},{9,10},{10,... | collective-permute-start | bytes 6152 | tf_op jit(solution)/shard_map/ppermute | solution.py:19
  31.7 4.8 %collective-permute-start.33 = (f32[8,64]{1,0:T(8,128)S(1)}, f32[8,64]{1,0:T(8,128)S(1)}, u32[]{:S(2)}, u32[]{:S(2)}) collective-permute-start(f32[8,64]{1,0:T(8,128)S(1)} %bitcast.484), channel_id=1, source_target_pairs={{0,7},{1,6},{2,5},{3,4},{4,3},{5,2},{6,1},{7,0},{8,15},{9,14},{10,... | collective-permute-start | bytes 6152 | tf_op jit(solution)/shard_map/ppermute | solution.py:19
  44.7 5.4 %collective-permute-start.36 = (f32[8,64]{1,0:T(8,128)S(1)}, f32[8,64]{1,0:T(8,128)S(1)}, u32[]{:S(2)}, u32[]{:S(2)}) collective-permute-start(f32[8,64]{1,0:T(8,128)S(1)} %bitcast.487), channel_id=1, source_target_pairs={{0,10},{1,11},{2,8},{3,9},{4,14},{5,15},{6,12},{7,13},{8,2},{9,3},... | collective-permute-start | bytes 6152 | tf_op jit(solution)/shard_map/ppermute | solution.py:19
  50.1 6.1 %collective-permute-start.41 = (f32[8,64]{1,0:T(8,128)S(1)}, f32[8,64]{1,0:T(8,128)S(1)}, u32[]{:S(2)}, u32[]{:S(2)}) collective-permute-start(f32[8,64]{1,0:T(8,128)S(1)} %bitcast.488), channel_id=1, source_target_pairs={{0,15},{1,14},{2,13},{3,12},{4,11},{5,10},{6,9},{7,8},{8,7},{9,6},... | collective-permute-start | bytes 6152 | tf_op jit(solution)/shard_map/ppermute | solution.py:19
  50.6 7.1 %collective-permute-start.2 = (f32[4,16,128]{2,1,0:T(8,128)S(1)}, f32[4,16,128]{2,1,0:T(8,128)S(1)}, u32[]{:S(2)}, u32[]{:S(2)}) collective-permute-start(f32[4,16,128]{2,1,0:T(8,128)S(1)} %bitcast.468), channel_id=1, source_target_pairs={{0,12},{4,8},{8,4},{12,0},{1,13},{5,9},{9,5},{13,1},{2,14},{6,10},... | collective-permute-start | bytes 98312 | tf_op jit(solution)/shard_map/ppermute | solution.py:19
  58.7 5.5 %collective-permute-start.5 = (f32[16,128]{1,0:T(8,128)S(1)}, f32[16,128]{1,0:T(8,128)S(1)}, u32[]{:S(2)}, u32[]{:S(2)}) collective-permute-start(f32[16,128]{1,0:T(8,128)S(1)} %get-tuple-element.26), channel_id=1, source_target_pairs={{0,3},{1,2},{2,1},{3,0},{4,7},{5,6},{6,5},{7,4},{8,11},{9,10},{10,... | collective-permute-start | bytes 24584 | tf_op jit(solution)/shard_map/ppermute | solution.py:19
  65.4 7.4 %collective-permute-start.6 = (f32[16,128]{1,0:T(8,128)S(1)}, f32[16,128]{1,0:T(8,128)S(1)}, u32[]{:S(2)}, u32[]{:S(2)}) collective-permute-start(f32[16,128]{1,0:T(8,128)S(1)} %get-tuple-element.11), channel_id=1, source_target_pairs={{0,1},{1,0},{2,3},{3,2},{4,5},{5,4},{6,7},{7,6},{8,9},{9,8},{10,11... | collective-permute-start | bytes 24584 | tf_op jit(solution)/shard_map/ppermute | solution.py:19
  66.9 42.7 %collective-permute-start.19 = (f32[16,128]{1,0:T(8,128)S(1)}, f32[16,128]{1,0:T(8,128)S(1)}, u32[]{:S(2)}, u32[]{:S(2)}) collective-permute-start(f32[16,128]{1,0:T(8,128)S(1)} %get-tuple-element.11), channel_id=1, source_target_pairs={{0,14},{1,15},{2,12},{3,13},{4,10},{5,11},{6,8},{7,9},{8,6},{9,7},... | collective-permute-start | bytes 24584 | tf_op jit(solution)/shard_map/ppermute | solution.py:19
  66.9 42.7 %collective-permute-start.18 = (f32[16,128]{1,0:T(8,128)S(1)}, f32[16,128]{1,0:T(8,128)S(1)}, u32[]{:S(2)}, u32[]{:S(2)}) collective-permute-start(f32[16,128]{1,0:T(8,128)S(1)} %get-tuple-element.11), channel_id=1, source_target_pairs={{0,13},{1,12},{2,15},{3,14},{4,9},{5,8},{6,11},{7,10},{8,5},{9,4},... | collective-permute-start | bytes 24584 | tf_op jit(solution)/shard_map/ppermute | solution.py:19
  69.9 39.7 %collective-permute-start.17 = (f32[16,128]{1,0:T(8,128)S(1)}, f32[16,128]{1,0:T(8,128)S(1)}, u32[]{:S(2)}, u32[]{:S(2)}) collective-permute-start(f32[16,128]{1,0:T(8,128)S(1)} %get-tuple-element.11), channel_id=1, source_target_pairs={{0,12},{1,13},{2,14},{3,15},{4,8},{5,9},{6,10},{7,11},{8,4},{9,5},... | collective-permute-start | bytes 24584 | tf_op jit(solution)/shard_map/ppermute | solution.py:19
  69.9 39.7 %collective-permute-start.16 = (f32[16,128]{1,0:T(8,128)S(1)}, f32[16,128]{1,0:T(8,128)S(1)}, u32[]{:S(2)}, u32[]{:S(2)}) collective-permute-start(f32[16,128]{1,0:T(8,128)S(1)} %get-tuple-element.11), channel_id=1, source_target_pairs={{0,11},{1,10},{2,9},{3,8},{4,15},{5,14},{6,13},{7,12},{8,3},{9,2},... | collective-permute-start | bytes 24584 | tf_op jit(solution)/shard_map/ppermute | solution.py:19
  77.4 5.4 %collective-permute-start.8 = (f32[16,128]{1,0:T(8,128)S(1)}, f32[16,128]{1,0:T(8,128)S(1)}, u32[]{:S(2)}, u32[]{:S(2)}) collective-permute-start(f32[16,128]{1,0:T(8,128)S(1)} %get-tuple-element.11), channel_id=1, source_target_pairs={{0,3},{1,2},{2,1},{3,0},{4,7},{5,6},{6,5},{7,4},{8,11},{9,10},{10,... | collective-permute-start | bytes 24584 | tf_op jit(solution)/shard_map/ppermute | solution.py:19
  91.0 4.9 %collective-permute-start.12 = (f32[16,128]{1,0:T(8,128)S(1)}, f32[16,128]{1,0:T(8,128)S(1)}, u32[]{:S(2)}, u32[]{:S(2)}) collective-permute-start(f32[16,128]{1,0:T(8,128)S(1)} %get-tuple-element.11), channel_id=1, source_target_pairs={{0,7},{1,6},{2,5},{3,4},{4,3},{5,2},{6,1},{7,0},{8,15},{9,14},{10,... | collective-permute-start | bytes 24584 | tf_op jit(solution)/shard_map/ppermute | solution.py:19
  104.1 5.4 %collective-permute-start.15 = (f32[16,128]{1,0:T(8,128)S(1)}, f32[16,128]{1,0:T(8,128)S(1)}, u32[]{:S(2)}, u32[]{:S(2)}) collective-permute-start(f32[16,128]{1,0:T(8,128)S(1)} %get-tuple-element.11), channel_id=1, source_target_pairs={{0,10},{1,11},{2,8},{3,9},{4,14},{5,15},{6,12},{7,13},{8,2},{9,3},... | collective-permute-start | bytes 24584 | tf_op jit(solution)/shard_map/ppermute | solution.py:19
  109.6 5.8 %collective-permute-start.20 = (f32[16,128]{1,0:T(8,128)S(1)}, f32[16,128]{1,0:T(8,128)S(1)}, u32[]{:S(2)}, u32[]{:S(2)}) collective-permute-start(f32[16,128]{1,0:T(8,128)S(1)} %get-tuple-element.11), channel_id=1, source_target_pairs={{0,15},{1,14},{2,13},{3,12},{4,11},{5,10},{6,9},{7,8},{8,7},{9,6},... | collective-permute-start | bytes 24584 | tf_op jit(solution)/shard_map/ppermute | solution.py:19
  118.6 5.6 %collective-permute-start.23 = (bf16[2,8,512]{2,1,0:T(8,128)(2,1)S(1)}, bf16[2,8,512]{2,1,0:T(8,128)(2,1)S(1)}, u32[]{:S(2)}, u32[]{:S(2)}) collective-permute-start(bf16[2,8,512]{2,1,0:T(8,128)(2,1)S(1)} %constant_dynamic-update-slice_fusion.32), channel_id=1, source_target_pairs={{0,3},{1,2},{2,1},{3,0},{4,7},{5,6},{6,5},{7,4},{8,11},{9,10},{10,... | collective-permute-start | bytes 49160 | tf_op jit(solution)/shard_map/ppermute | solution.py:19
  120.5 4.6 %collective-permute-start.21 = (bf16[2,8,512]{2,1,0:T(8,128)(2,1)S(1)}, bf16[2,8,512]{2,1,0:T(8,128)(2,1)S(1)}, u32[]{:S(2)}, u32[]{:S(2)}) collective-permute-start(bf16[2,8,512]{2,1,0:T(8,128)(2,1)S(1)} %constant_dynamic-update-slice_fusion.32), channel_id=1, source_target_pairs={{0,1},{1,0},{2,3},{3,2},{4,5},{5,4},{6,7},{7,6},{8,9},{9,8},{10,11... | collective-permute-start | bytes 49160 | tf_op jit(solution)/shard_map/ppermute | solution.py:19
  125.7 5.0 %collective-permute-start.25 = (bf16[4,2,8,512]{3,2,1,0:T(8,128)(2,1)S(1)}, bf16[4,2,8,512]{3,2,1,0:T(8,128)(2,1)S(1)}, u32[]{:S(2)}, u32[]{:S(2)}) collective-permute-start(bf16[4,2,8,512]{3,2,1,0:T(8,128)(2,1)S(1)} %gather_fusion.1), channel_id=1, source_target_pairs={{0,8},{4,12},{8,0},{12,4},{1,9},{5,13},{9,1},{13,5},{2,10},{6,14},... | collective-permute-start | bytes 196616 | tf_op jit(solution)/shard_map/ppermute | solution.py:19
  145.1 5.4 %collective-permute-start.47 = (f32[16,128]{1,0:T(8,128)S(1)}, f32[16,128]{1,0:T(8,128)S(1)}, u32[]{:S(2)}, u32[]{:S(2)}) collective-permute-start(f32[16,128]{1,0:T(8,128)S(1)} %get-tuple-element.23), channel_id=1, source_target_pairs={{0,3},{1,2},{2,1},{3,0},{4,7},{5,6},{6,5},{7,4},{8,11},{9,10},{10,... | collective-permute-start | bytes 24584 | tf_op jit(solution)/shard_map/ppermute | solution.py:19
  151.5 8.9 %collective-permute-start.48 = (f32[16,128]{1,0:T(8,128)S(1)}, f32[16,128]{1,0:T(8,128)S(1)}, u32[]{:S(2)}, u32[]{:S(2)}) collective-permute-start(f32[16,128]{1,0:T(8,128)S(1)} %get-tuple-element.9), channel_id=1, source_target_pairs={{0,1},{1,0},{2,3},{3,2},{4,5},{5,4},{6,7},{7,6},{8,9},{9,8},{10,11... | collective-permute-start | bytes 24584 | tf_op jit(solution)/shard_map/ppermute | solution.py:19
  154.1 43.1 %collective-permute-start.61 = (f32[16,128]{1,0:T(8,128)S(1)}, f32[16,128]{1,0:T(8,128)S(1)}, u32[]{:S(2)}, u32[]{:S(2)}) collective-permute-start(f32[16,128]{1,0:T(8,128)S(1)} %get-tuple-element.9), channel_id=1, source_target_pairs={{0,14},{1,15},{2,12},{3,13},{4,10},{5,11},{6,8},{7,9},{8,6},{9,7},... | collective-permute-start | bytes 24584 | tf_op jit(solution)/shard_map/ppermute | solution.py:19
  154.5 42.7 %collective-permute-start.60 = (f32[16,128]{1,0:T(8,128)S(1)}, f32[16,128]{1,0:T(8,128)S(1)}, u32[]{:S(2)}, u32[]{:S(2)}) collective-permute-start(f32[16,128]{1,0:T(8,128)S(1)} %get-tuple-element.9), channel_id=1, source_target_pairs={{0,13},{1,12},{2,15},{3,14},{4,9},{5,8},{6,11},{7,10},{8,5},{9,4},... | collective-permute-start | bytes 24584 | tf_op jit(solution)/shard_map/ppermute | solution.py:19
  157.3 39.8 %collective-permute-start.59 = (f32[16,128]{1,0:T(8,128)S(1)}, f32[16,128]{1,0:T(8,128)S(1)}, u32[]{:S(2)}, u32[]{:S(2)}) collective-permute-start(f32[16,128]{1,0:T(8,128)S(1)} %get-tuple-element.9), channel_id=1, source_target_pairs={{0,12},{1,13},{2,14},{3,15},{4,8},{5,9},{6,10},{7,11},{8,4},{9,5},... | collective-permute-start | bytes 24584 | tf_op jit(solution)/shard_map/ppermute | solution.py:19
  157.9 39.2 %collective-permute-start.58 = (f32[16,128]{1,0:T(8,128)S(1)}, f32[16,128]{1,0:T(8,128)S(1)}, u32[]{:S(2)}, u32[]{:S(2)}) collective-permute-start(f32[16,128]{1,0:T(8,128)S(1)} %get-tuple-element.9), channel_id=1, source_target_pairs={{0,11},{1,10},{2,9},{3,8},{4,15},{5,14},{6,13},{7,12},{8,3},{9,2},... | collective-permute-start | bytes 24584 | tf_op jit(solution)/shard_map/ppermute | solution.py:19
  164.9 5.4 %collective-permute-start.50 = (f32[16,128]{1,0:T(8,128)S(1)}, f32[16,128]{1,0:T(8,128)S(1)}, u32[]{:S(2)}, u32[]{:S(2)}) collective-permute-start(f32[16,128]{1,0:T(8,128)S(1)} %get-tuple-element.9), channel_id=1, source_target_pairs={{0,3},{1,2},{2,1},{3,0},{4,7},{5,6},{6,5},{7,4},{8,11},{9,10},{10,... | collective-permute-start | bytes 24584 | tf_op jit(solution)/shard_map/ppermute | solution.py:19
  178.6 4.9 %collective-permute-start.54 = (f32[16,128]{1,0:T(8,128)S(1)}, f32[16,128]{1,0:T(8,128)S(1)}, u32[]{:S(2)}, u32[]{:S(2)}) collective-permute-start(f32[16,128]{1,0:T(8,128)S(1)} %get-tuple-element.9), channel_id=1, source_target_pairs={{0,7},{1,6},{2,5},{3,4},{4,3},{5,2},{6,1},{7,0},{8,15},{9,14},{10,... | collective-permute-start | bytes 24584 | tf_op jit(solution)/shard_map/ppermute | solution.py:19
  191.7 5.4 %collective-permute-start.57 = (f32[16,128]{1,0:T(8,128)S(1)}, f32[16,128]{1,0:T(8,128)S(1)}, u32[]{:S(2)}, u32[]{:S(2)}) collective-permute-start(f32[16,128]{1,0:T(8,128)S(1)} %get-tuple-element.9), channel_id=1, source_target_pairs={{0,10},{1,11},{2,8},{3,9},{4,14},{5,15},{6,12},{7,13},{8,2},{9,3},... | collective-permute-start | bytes 24584 | tf_op jit(solution)/shard_map/ppermute | solution.py:19
  197.1 5.8 %collective-permute-start.62 = (f32[16,128]{1,0:T(8,128)S(1)}, f32[16,128]{1,0:T(8,128)S(1)}, u32[]{:S(2)}, u32[]{:S(2)}) collective-permute-start(f32[16,128]{1,0:T(8,128)S(1)} %get-tuple-element.9), channel_id=1, source_target_pairs={{0,15},{1,14},{2,13},{3,12},{4,11},{5,10},{6,9},{7,8},{8,7},{9,6},... | collective-permute-start | bytes 24584 | tf_op jit(solution)/shard_map/ppermute | solution.py:19
  (36 other events, 287.3 us)

commit v2 on v1

--- a/solution.py
+++ b/solution.py
@@ -1,8 +1,12 @@
+import functools
 import math
 
 import jax
 import jax.numpy as jnp
+import numpy as np
 from jax import lax
+from jax.experimental import pallas as pl
+from jax.experimental.pallas import tpu as pltpu
 from jax.sharding import PartitionSpec as P
 
 WIDTH = 64
@@ -15,38 +19,19 @@
 AXES = ("gx", "gy")
 
 
-def swap(part, axis, size, step):
-    return lax.ppermute(part, axis, [(i, i ^ step) for i in range(size)])
-
-
-def swap_gather(part, axis, size):
-    found = jnp.stack([part] + [swap(part, axis, size, step) for step in range(1, size)])
-    return found[jnp.arange(size) ^ lax.axis_index(axis)]
-
-
-def swap_scatter(parts, axis, size):
-    me = lax.axis_index(axis)
-    total = parts[me]
-    for step in range(1, size):
-        total = total + swap(parts[me ^ step], axis, size, step)
-    return total
-
-
-def gather(part, count, flat=True):
-    if flat:
-        return swap_gather(part, AXES, count)
-    size_x, size_y = lax.axis_size("gx"), lax.axis_size("gy")
-    found = swap_gather(swap_gather(part, "gy", size_y), "gx", size_x)
-    return found.reshape((count,) + part.shape)
+def exchange(parts):
+    return lax.all_to_all(parts, AXES, split_axis=0, concat_axis=0, tiled=True)
+
+
+def gather(part, count):
+    return exchange(jnp.broadcast_to(part[None], (count,) + part.shape))
 
 
 def reduce_blocks(total, count):
     width, depth = total.shape
     blocks = total.reshape(width, depth // LANES, LANES).transpose(1, 0, 2)
     blocks = blocks.reshape(count, width * depth // LANES // count, LANES)
-    size_x, size_y = lax.axis_size("gx"), lax.axis_size("gy")
-    mine = swap_scatter(blocks.reshape((size_x, size_y) + blocks.shape[1:]), "gx", size_x)
-    mine = swap_scatter(mine, "gy", size_y)
+    mine = jnp.sum(exchange(blocks), axis=0)
     whole = gather(mine, count).reshape(depth // LANES, width, LANES)
     return whole.transpose(1, 0, 2).reshape(width, depth)
 
@@ -132,7 +117,7 @@
     low_c = jnp.einsum("hdc,cphg->phdg", wo.astype(jnp.float32), coef_c, precision=PRECISE)
     squares = HEAD_DIM * HEAD_DIM
     both = jnp.stack([low_f, low_c]).astype(bf16).reshape(2, cells, HEADS * squares)
-    both = gather(both, count, False).reshape(span_x, span_y, 2, rows_x, rows_y, HEADS * squares)
+    both = gather(both, count).reshape(span_x, span_y, 2, rows_x, rows_y, HEADS * squares)
     both = both.transpose(2, 0, 3, 1, 4, 5).reshape(2, grid_x, grid_y, HEADS, squares)
     low_f, low_c = both[0], both[1]
 
@@ -179,12 +164,377 @@
     return (layer_output.reshape(field.shape), field_grad.reshape(field.shape))
 
 
+def split(x):
+    high = x.astype(jnp.bfloat16)
+    return high, (x - high.astype(jnp.float32)).astype(jnp.bfloat16)
+
+
+NN = (((1,), (0,)), ((), ()))
+NT = (((1,), (1,)), ((), ()))
+TN = (((0,), (0,)), ((), ()))
+
+
+def mul(left, right, dims=NN):
+    return lax.dot_general(left, right, dims, preferred_element_type=jnp.float32)
+
+
+def mul_near(left, right, dims=NN):
+    left_high, left_low = split(left)
+    right_high, right_low = split(right)
+    return (
+        mul(left_high, right_high, dims)
+        + mul(left_low, right_high, dims)
+        + mul(left_high, right_low, dims)
+    )
+
+
+def mul_left(left, right, dims=NN):
+    high, low = split(left)
+    return mul(high, right, dims) + mul(low, right, dims)
+
+
+def number(shape, dim):
+    return lax.broadcasted_iota(jnp.int32, shape, dim)
+
+
+def put_blocks(ref, total):
+    count = ref.shape[0]
+    columns = total.shape[1] // LANES
+    groups = count // columns
+    rows = WIDTH // groups
+    for block in range(count):
+        column, group = block // groups, block % groups
+        ref[block, 0:rows, :] = total[
+            group * rows : (group + 1) * rows, column * LANES : (column + 1) * LANES
+        ]
+
+
+def whole_blocks(ref, depth):
+    columns = depth // LANES
+    blocks = ref[...].reshape(columns, WIDTH, LANES)
+    return jnp.concatenate([blocks[i] for i in range(columns)], axis=1)
+
+
+def prepare_kernel(wv_ref, wo_ref, qk_ref, wv_out, wo_out, wq_out, wk_out, wz_out):
+    wide = HEADS * HEAD_DIM * HEAD_DIM
+    row = number((WIDTH, wide), 0)
+    lane = number((WIDTH, wide), 1)
+    by_channel = ((lane >> 3) == row).astype(jnp.bfloat16)
+    by_factor = (((lane >> 6) * HEAD_DIM + (lane & 7)) == row).astype(jnp.bfloat16)
+    wv_out[...] = mul(wv_ref[...], by_channel)
+    wo_out[...] = mul(wo_ref[...], by_channel, TN)
+    for index, out in ((0, wq_out), (1, wk_out)):
+        high, low = split(qk_ref[2, index])
+        out[0:WIDTH, :] = mul(high, by_factor).astype(jnp.bfloat16)
+        out[WIDTH : 2 * WIDTH, :] = mul(low, by_factor).astype(jnp.bfloat16)
+        wz_out[index * WIDTH : (index + 1) * WIDTH, :] = qk_ref[2, index].T
+
+
+def sums_kernel(field_ref, out_ref):
+    data = field_ref[...]
+    rows, depth = data.shape
+    cells = rows // WIDTH
+    pick = (number((WIDTH, rows), 1) // cells == number((WIDTH, rows), 0)).astype(jnp.bfloat16)
+    part = mul(pick, data)
+    row_sums = mul(data, jnp.ones((depth, LANES), jnp.bfloat16)).reshape(WIDTH, cells, LANES)
+    shape = row_sums.shape
+    own = jnp.sum(jnp.where(number(shape, 0) == number(shape, 2), row_sums, 0.0), axis=0)
+    put_blocks(out_ref, part)
+    for block in range(out_ref.shape[0]):
+        out_ref[block, out_ref.shape[1] - cells :, :] = own
+
+
+def add_kernel(recv_ref, out_ref):
+    rows = out_ref.shape[1]
+    total = jnp.sum(recv_ref[:, 0:rows, :], axis=0)
+    out_ref[...] = jnp.broadcast_to(total[None], out_ref.shape)
+
+
+def plane_kernel(cells, lengths, me_ref, recv_ref, same_ref, qk_ref, mix_ref, feat_ref):
+    places = recv_ref.shape[0] * cells
+    totals = recv_ref[:, recv_ref.shape[1] - cells :, :].reshape(places, LANES)[:, :WIDTH]
+    here = pl.ds(pl.multiple_of(me_ref[0] * cells, cells), cells)
+    head = (number((HEADS * cells, WIDTH), 0) // cells) == (number((HEADS * cells, WIDTH), 1) >> 3)
+    high, low = split(totals)
+    forward = backward = None
+    for axis in range(2):
+        same = same_ref[axis]
+        pooled = (mul(same, high) + mul(same, low)) * (1.0 / lengths[axis][1])
+        inverse = lax.rsqrt(jnp.mean(pooled * pooled, axis=1, keepdims=True) + EPSILON)
+        normed = pooled * inverse
+        query = mul_near(normed, qk_ref[axis, 0])
+        keyset = mul_near(normed, qk_ref[axis, 1])
+        feat_ref[4 * axis] = normed
+        feat_ref[4 * axis + 1] = query
+        feat_ref[4 * axis + 2] = keyset
+        feat_ref[4 * axis + 3] = jnp.broadcast_to(inverse, (places, WIDTH))
+        factor = 1.0 / math.sqrt(HEAD_DIM * lengths[axis][0])
+
+        def local(index, other):
+            rows = feat_ref[4 * axis + index, here, :]
+            rows = jnp.broadcast_to(rows[None], (HEADS, cells, WIDTH)).reshape(-1, WIDTH)
+            scores = mul_near(jnp.where(head, rows, 0.0), other, NT) * factor
+            return scores.astype(jnp.bfloat16).astype(jnp.float32)
+
+        one, two = local(1, keyset), local(2, query)
+        forward = one if forward is None else forward * one
+        backward = two if backward is None else backward * two
+    mix_ref[0] = forward
+    mix_ref[1] = backward
+
+
+def coef_kernel(places, recv_ref, wz_ref, field_ref, cot_ref, wv_ref, wo_ref,
+                send_ref, feat_ref, query_ref, keyset_ref):
+    rows, depth = field_ref.shape
+    cells = rows // WIDTH
+    wide = HEADS * HEAD_DIM * HEAD_DIM
+    pooled = whole_blocks(recv_ref, depth) * (1.0 / places)
+    inverse = lax.rsqrt(jnp.mean(pooled * pooled, axis=0, keepdims=True) + EPSILON)
+    normed = pooled * inverse
+    feat_ref[0:WIDTH, :] = normed
+    feat_ref[WIDTH:, :] = jnp.broadcast_to(inverse, (HEAD_DIM, depth))
+    both = mul_near(wz_ref[...], normed)
+
+    def expand(part):
+        part = part.reshape(HEADS, 1, HEAD_DIM, depth)
+        part = jnp.broadcast_to(part, (HEADS, HEAD_DIM, HEAD_DIM, depth))
+        return part.reshape(wide, depth).astype(jnp.bfloat16)
+
+    query = expand(both[:WIDTH])
+    keyset = expand(both[WIDTH:])
+    query_ref[...] = query
+    keyset_ref[...] = keyset
+    low_f = mul(field_ref[...], keyset, NT).reshape(WIDTH, cells, wide)
+    low_f = jnp.sum(wv_ref[...][:, None, :] * low_f, axis=0)
+    low_c = mul(cot_ref[...], query, NT).reshape(WIDTH, cells, wide)
+    low_c = jnp.sum(wo_ref[...][:, None, :] * low_c, axis=0)
+    low = jnp.concatenate([low_f, low_c], axis=0).astype(jnp.bfloat16)
+    send_ref[...] = jnp.broadcast_to(low[None], send_ref.shape)
+
+
+def mix_kernel(factor, recv_ref, mix_ref, wv_ref, wo_ref, wq_ref, wk_ref, field_ref, cot_ref,
+               send_ref, left_f_ref, left_c_ref):
+    rows = field_ref.shape[0]
+    cells = rows // WIDTH
+    places = recv_ref.shape[0] * cells
+    wide = recv_ref.shape[2]
+    both = recv_ref[...].astype(jnp.float32)
+    shape = (HEADS, cells, wide)
+    head = number(shape, 0) == (number(shape, 2) >> 6)
+
+    def top(mix, low):
+        low = low.reshape(places, wide).astype(jnp.bfloat16)
+        found = mul_left(mix, low).reshape(shape)
+        return jnp.sum(jnp.where(head, found, 0.0), axis=0) * factor
+
+    left_f = wo_ref[...][:, None, :] * top(mix_ref[0], both[:, :cells])[None]
+    left_f = left_f.reshape(rows, wide).astype(jnp.bfloat16)
+    left_c = wv_ref[...][:, None, :] * top(mix_ref[1], both[:, cells:])[None]
+    left_c = left_c.reshape(rows, wide).astype(jnp.bfloat16)
+    left_f_ref[...] = left_f
+    left_c_ref[...] = left_c
+
+    def pull(weights, left, right):
+        found = mul(weights, left, NT)
+        return mul_left(found[:WIDTH] + found[WIDTH:], right)
+
+    put_blocks(
+        send_ref,
+        pull(wq_ref[...], left_f, cot_ref[...]) + pull(wk_ref[...], left_c, field_ref[...]),
+    )
+
+
+def output_kernel(left_ref, query_ref, field_ref, out_ref):
+    found = mul(left_ref[...], query_ref[...]) + field_ref[...].astype(jnp.float32)
+    out_ref[...] = found.astype(jnp.bfloat16)
+
+
+def gram_kernel(cells, lengths, factor_z, me_ref, recv_ref, feat_ref, same_ref, qk_ref, out_ref,
+                found_ref):
+    places = recv_ref.shape[0] * cells
+    wide = recv_ref.shape[2]
+    squares = HEAD_DIM * HEAD_DIM
+    both = recv_ref[...].astype(jnp.float32)
+    low_f = both[:, :cells].reshape(places, wide).astype(jnp.bfloat16)
+    low_c = both[:, cells:].reshape(places, wide).astype(jnp.bfloat16)
+    here = pl.ds(pl.multiple_of(me_ref[0] * cells, cells), cells)
+    lane = number((places, LANES), 1)
+    products = []
+    for pair in range(wide // LANES):
+        part_f = low_f[:, pair * LANES : (pair + 1) * LANES]
+        part_c = low_c[:, pair * LANES : (pair + 1) * LANES]
+        for half in range(LANES // squares):
+            mine = (lane >> 6) == half
+            products.append(mul(jnp.where(mine, part_c, jnp.zeros_like(part_c)), part_f, NT))
+    product = jnp.concatenate(products, axis=0)
+    heads = number((HEADS * places, WIDTH), 0) // places == number((HEADS * places, WIDTH), 1) >> 3
+
+    def stack(part):
+        part = jnp.broadcast_to(part[None], (HEADS, places, WIDTH)).reshape(-1, WIDTH)
+        return jnp.where(heads, part, 0.0)
+
+    factors = [1.0 / math.sqrt(HEAD_DIM * lengths[axis][0]) for axis in range(2)]
+    queries = [stack(feat_ref[4 * axis + 1]) for axis in range(2)]
+    keysets = [stack(feat_ref[4 * axis + 2]) for axis in range(2)]
+    kernels = []
+    for axis in range(2):
+        scores = mul_near(queries[axis], feat_ref[4 * axis + 2], NT) * factors[axis]
+        kernels.append(scores.astype(jnp.bfloat16).astype(jnp.float32))
+    total = jnp.zeros((cells, WIDTH), jnp.float32)
+    for axis in range(2):
+        gram = (product * kernels[1 - axis]).astype(jnp.bfloat16)
+        across = jnp.concatenate(
+            [gram[h * places : (h + 1) * places] for h in range(HEADS)], axis=1
+        )
+        scale = factors[axis] * factor_z
+        grad_query = mul(across, keysets[axis].astype(jnp.bfloat16)) * scale
+        grad_keyset = mul(gram, queries[axis].astype(jnp.bfloat16), TN) * scale
+        found = mul_near(grad_query, qk_ref[axis, 0], NT) + mul_near(grad_keyset, qk_ref[axis, 1], NT)
+        high, low = split(found)
+        found_ref[...] = mul(same_ref[axis], high) + mul(same_ref[axis], low)
+        found = found_ref[here, :]
+        normed = feat_ref[4 * axis, here, :]
+        inverse = feat_ref[4 * axis + 3, here, :]
+        found = found - normed * jnp.mean(found * normed, axis=1, keepdims=True)
+        total = total + inverse * found * (1.0 / lengths[axis][1])
+    out_ref[...] = total
+
+
+def base_kernel(left_ref, keyset_ref, cot_ref, plane_ref, out_ref):
+    rows = cot_ref.shape[0]
+    cells = rows // WIDTH
+    shape = (WIDTH, cells, WIDTH)
+    own = jnp.where(number(shape, 0) == number(shape, 2), plane_ref[...][None], 0.0)
+    plane = mul_left(own.reshape(rows, WIDTH), jnp.ones((WIDTH, LANES), jnp.bfloat16))
+    found = mul(left_ref[...], keyset_ref[...]) + cot_ref[...].astype(jnp.float32)
+    columns = found.shape[1] // LANES
+    out_ref[...] = found + jnp.concatenate([plane] * columns, axis=1)
+
+
+def final_kernel(places, recv_ref, feat_ref, base_ref, out_ref):
+    rows, depth = base_ref.shape
+    cells = rows // WIDTH
+    found = whole_blocks(recv_ref, depth)
+    normed = feat_ref[0:WIDTH, :]
+    inverse = feat_ref[WIDTH : WIDTH + 1, :]
+    found = inverse * (found - normed * jnp.mean(found * normed, axis=0, keepdims=True))
+    found = found * (1.0 / places)
+    total = base_ref[...].reshape(WIDTH, cells, depth) + found[:, None, :]
+    out_ref[...] = total.reshape(rows, depth).astype(jnp.bfloat16)
+
+
+def run(kernel, outs, operands, scalars=0, flops=0, scratch=()):
+    vmem = pl.BlockSpec(memory_space=pltpu.VMEM)
+    smem = pl.BlockSpec(memory_space=pltpu.SMEM)
+    moved = sum(x.size * x.dtype.itemsize for x in tuple(operands) + tuple(outs))
+    found = pl.pallas_call(
+        kernel,
+        out_shape=tuple(outs),
+        in_specs=[smem] * scalars + [vmem] * (len(operands) - scalars),
+        out_specs=tuple(vmem for _ in outs),
+        scratch_shapes=list(scratch),
+        compiler_params=pltpu.CompilerParams(vmem_limit_bytes=48 * 1024 * 1024),
+        cost_estimate=pl.CostEstimate(flops=flops, bytes_accessed=moved, transcendentals=0),
+    )(*operands)
+    return found[0] if len(outs) == 1 else found
+
+
+def per_device_kernels(field, cotangent, qk_weight, w_value, w_out):
+    span_x = lax.axis_size("gx")
+    span_y = lax.axis_size("gy")
+    count = span_x * span_y
+    rows_x, rows_y, depth = field.shape[1:]
+    cells = rows_x * rows_y
+    places = count * cells
+    grid_x = rows_x * span_x
+    grid_y = rows_y * span_y
+    rows = WIDTH * cells
+    wide = WIDTH * HEAD_DIM
+    f32, bf16 = jnp.float32, jnp.bfloat16
+    like = jax.ShapeDtypeStruct
+    lengths = ((grid_x, grid_y * depth), (grid_y, grid_x * depth))
+    me = (lax.axis_index("gx") * span_y + lax.axis_index("gy")).astype(jnp.int32).reshape(1)
+
+    place = np.arange(places)
+    at_x = place // cells // span_y * rows_x + place % cells // rows_y
+    at_y = place // cells % span_y * rows_y + place % rows_y
+    same = jnp.asarray(
+        np.stack([at_x[:, None] == at_x[None], at_y[:, None] == at_y[None]]), dtype=bf16
+    )
+
+    cols = field.reshape(rows, depth)
+    cots = cotangent.reshape(rows, depth)
+    share = WIDTH * depth // LANES // count
+    block = like((count, share, LANES), f32)
+    factor_z = 1.0 / math.sqrt(HEAD_DIM * depth)
+    cube = rows * wide * depth * 2
+
+    sums = run(sums_kernel, [like((count, share + cells, LANES), f32)], (cols,), flops=cube // 4)
+    recv = exchange(sums)
+    wv, wo, wq, wk, wz = run(
+        prepare_kernel,
+        [like((WIDTH, wide), f32)] * 2 + [like((2 * WIDTH, wide), bf16)] * 2
+        + [like((2 * WIDTH, WIDTH), f32)],
+        (w_value, w_out, qk_weight),
+        flops=cube // 8,
+    )
+    pooled = exchange(run(add_kernel, [block], (recv,)))
+    mix, feat = run(
+        functools.partial(plane_kernel, cells, lengths),
+        [like((2, HEADS * cells, places), f32), like((8, places, WIDTH), f32)],
+        (me, recv, same, qk_weight),
+        scalars=1,
+        flops=cube // 2,
+    )
+    send, feat_z, query, keyset = run(
+        functools.partial(coef_kernel, grid_x * grid_y),
+        [like((count, 2 * cells, wide), bf16), like((WIDTH + HEAD_DIM, depth), f32)]
+        + [like((wide, depth), bf16)] * 2,
+        (pooled, wz, cols, cots, wv, wo),
+        flops=2 * cube,
+    )
+    low = exchange(send)
+    send, left_f, left_c = run(
+        functools.partial(mix_kernel, factor_z),
+        [block, like((rows, wide), bf16), like((rows, wide), bf16)],
+        (low, mix, wv, wo, wq, wk, cols, cots),
+        flops=cube,
+    )
+    recv = exchange(send)
+    layer_output = run(output_kernel, [like((rows, depth), bf16)], (left_f, query, cols), flops=cube)
+    plane = run(
+        functools.partial(gram_kernel, cells, lengths, factor_z),
+        [like((cells, WIDTH), f32)],
+        (me, low, feat, same, qk_weight),
+        scalars=1,
+        flops=2 * cube,
+        scratch=[pltpu.VMEM((places, WIDTH), f32)],
+    )
+    pulled = exchange(run(add_kernel, [block], (recv,)))
+    base = run(base_kernel, [like((rows, depth), f32)], (left_c, keyset, cots, plane), flops=cube)
+    field_grad = run(
+        functools.partial(final_kernel, grid_x * grid_y),
+        [like((rows, depth), bf16)],
+        (pulled, feat_z, base),
+    )
+    return (layer_output.reshape(field.shape), field_grad.reshape(field.shape))
+
+
 def solution(mesh):
     placed = P(None, ("groups", "gx"), "gy", None)
-    return jax.shard_map(
-        per_device,
-        mesh=mesh,
-        in_specs=(placed, placed, P(), P(), P()),
-        out_specs=(placed, placed),
-        check_vma=False,
-    )
+    count = mesh.shape["gx"] * mesh.shape["gy"]
+
+    def program(*arrays):
+        _, grid_x, grid_y, depth = arrays[0].shape
+        places = grid_x // mesh.shape["groups"] * grid_y
+        small = places == LANES and places == 8 * count and depth % LANES == 0
+        small = small and count % (depth // LANES) == 0
+        return jax.shard_map(
+            per_device_kernels if small else per_device,
+            mesh=mesh,
+            in_specs=(placed, placed, P(), P(), P()),
+            out_specs=(placed, placed),
+            check_vma=False,
+        )(*arrays)
+
+    return program

time: 205 us -> 72.5 us (0.35)
  waiting for transfers between devices: 109 us -> 15.4 us
  starting transfers between devices: 69.6 us -> 11 us
  blocking collectives: 0 us -> 25.9 us
  matrix products: 9.39 us -> 0 us
  Pallas kernels: 0 us -> 9.18 us
  local copies, waits for them, and re-layouts: 12.6 us -> 9.5 us
  other arithmetic: 2.52 us -> 0 us
    ppermute x63 -> x0, waiting for transfers between devices: 109 us -> none  [swap(): return lax.ppermute(part, axis, [(i, i ^ step) for i in range(size)])]
    ppermute x63 -> x0, starting transfers between devices: 69.6 us -> none  [swap(): return lax.ppermute(part, axis, [(i, i ^ step) for i in range(size)])]
    all_to_all x0 -> x2, blocking collectives: none -> 25.9 us  [exchange(): return lax.all_to_all(parts, AXES, split_axis=0, concat_axis=0, tiled=True)]
    all_to_all x0 -> x3, waiting for transfers between devices: none -> 15.4 us  [exchange(): return lax.all_to_all(parts, AXES, split_axis=0, concat_axis=0, tiled=True)]
    all_to_all x0 -> x3, starting transfers between devices: none -> 11 us  [exchange(): return lax.all_to_all(parts, AXES, split_axis=0, concat_axis=0, tiled=True)]
    dot_general x34 -> x0, matrix products: 9.39 us -> none  [the longest x12 3.79 us: f32_einsum(): return jnp.einsum(pattern, left, right, preferred_element_type=jnp.float32)]
    pallas_call x0 -> x11, Pallas kernels: none -> 9.18 us  [run(): pl.pallas_call(kernel, out_shape=tuple(outs), in_specs=[smem] * scalars +...]
    unnamed x55 -> x28, local copies, waits for them, and re-layouts: 1.02 us -> 6.37 us
  transfers between devices with their start and end apart: 63 -> 3, of which waited for: 40 -> 3; matrix products, arithmetic and copies ran while one was open for 4% -> 1% of each run, Pallas kernels for 0% -> 6%
where the time goes in v2:
time: 72.5 us; the launch traced here: 71.8 us
  blocking collectives  25.9 us (36%)
  waiting for transfers between devices  15.4 us (21%)
  starting transfers between devices  11 us (15%)
  local copies, waits for them, and re-layouts  9.5 us (13%)
  Pallas kernels  9.18 us (13%)
  between operations  0.83 us (1%)
    all_to_all x2, blocking collectives, exchange(): return lax.all_to_all(parts, AXES, split_axis=0, concat_axis=0, tiled=True)  25.9 us
    all_to_all x3, waiting for transfers between devices, exchange(): return lax.all_to_all(parts, AXES, split_axis=0, concat_axis=0, tiled=True)  15.4 us
    all_to_all x3, starting transfers between devices, exchange(): return lax.all_to_all(parts, AXES, split_axis=0, concat_axis=0, tiled=True)  11 us
    pallas_call x11, Pallas kernels, run(): pl.pallas_call(kernel, out_shape=tuple(outs), in_specs=[smem] * scalars +...  9.18 us
    unnamed x28, local copies, waits for them, and re-layouts  6.37 us
    reshape x2, local copies, waits for them, and re-layouts, per_device_kernels(): return (layer_output.reshape(field.shape), field_grad.reshape(field.shape))  1.83 us
  transfers between devices with their start and end apart: 3, of which 3 were waited for; matrix products, arithmetic and copies ran while one was open for 1% of the time, Pallas kernels for 6%

profile of v2, /device:TPU:0, one launch (start us, length us, event | category | flops | bytes accessed | tf_op | source)
XLA Modules:
  0.0 71.8 jit_solution(5108431444100580202)
XLA Ops:
  0.6 1.2 %reshape.19.field_ref = bf16[512,512]{1,0:T(8,128)(2,1)S(1)} reshape(bf16[64,2,4,512]{3,2,1,0:T(4,128)(2,1)} %param.6) | data formatting | bytes 1048576 | tf_op jit(solution)/shard_map/reshape | solution.py:465
  1.8 0.4 shard_map.77
  2.2 15.4 %all_to_all.25.recv_ref = f32[16,24,128]{2,1,0:T(8,128)S(1)} all-to-all(f32[16,24,128]{2,1,0:T(8,128)S(1)} %shard_map.77), channel_id=1, replica_groups=mesh['groups'=2,'gx'=4,'gy'=4] {'gx','gy'}, dimensions={0} | all-to-all | bytes 393216 | tf_op jit(solution)/shard_map/all_to_all | solution.py:23
  17.6 0.7 shard_map.78
  18.3 3.8 %all-to-all-start.1 = ((f32[16,16,128]{2,1,0:T(8,128)}), f32[16,16,128]{2,1,0:T(8,128)S(1)}, u32[]{:S(2)}, u32[]{:S(2)}) async-start(f32[16,16,128]{2,1,0:T(8,128)} %shard_map.78), calls=%async_computation.1 | async-start | bytes 262144 | tf_op jit(solution)/shard_map/all_to_all | solution.py:23
  22.2 0.1 reshape.20.cot_ref
  22.3 0.8 %copy-done.4 = f32[3,2,64,64]{3,2,1,0:T(8,128)S(1)} copy-done((f32[3,2,64,64]{3,2,1,0:T(8,128)S(1)}, f32[3,2,64,64]{3,2,1,0:T(8,128)}, u32[]{:S(2)}) %copy-start.4) | copy-done | bytes 98328
  23.1 0.3 shard_map.79
  23.4 6.1 %all-to-all-done.1.recv_ref = f32[16,16,128]{2,1,0:T(8,128)S(1)} async-done(((f32[16,16,128]{2,1,0:T(8,128)}), f32[16,16,128]{2,1,0:T(8,128)S(1)}, u32[]{:S(2)}, u32[]{:S(2)}) %all-to-all-start.1) | async-done | bytes 131104 | tf_op jit(solution)/shard_map/all_to_all | solution.py:23
  29.5 1.7 %shard_map.80 = (bf16[16,16,512]{2,1,0:T(8,128)(2,1)}, f32[72,512]{1,0:T(8,128)S(1)}, bf16[512,512]{1,0:T(8,128)(2,1)S(1)}, bf16[512,512]{1,0:T(8,128)(2,1)S(1)}) custom-call(f32[16,16,128]{2,1,0:T(8,128)S(1)} %all-to-all-done.1.recv_ref, f32[128,64]{1,0:T(8,128)S(1)} %get-tuple-element.16.wz_ref, bf16[512,512]{1,0:T(8,128)(2,1)S(1)} %reshape.19.field_ref, ...), custom_call_target="tpu_custom_call" | custom-call | flops 536870912 | bytes 2932736 | tf_op jit(solution)/shard_map/pallas_call | solution.py:430
  31.3 0.8 %copy-done = bf16[512,512]{1,0:T(8,128)(2,1)} copy-done((bf16[512,512]{1,0:T(8,128)(2,1)}, bf16[512,512]{1,0:T(8,128)(2,1)S(1)}, u32[]{:S(2)}) %copy-start) | copy-done | bytes 524312
  32.1 3.7 %all-to-all-start.2 = ((bf16[16,16,512]{2,1,0:T(8,128)(2,1)}), bf16[16,16,512]{2,1,0:T(8,128)(2,1)S(1)}, u32[]{:S(2)}, u32[]{:S(2)}) async-start(bf16[16,16,512]{2,1,0:T(8,128)(2,1)} %get-tuple-element.19), calls=%async_computation.2 | async-start | bytes 524288 | tf_op jit(solution)/shard_map/all_to_all | solution.py:23
  35.8 1.2 %shard_map.81 = (f32[2,64,128]{2,1,0:T(8,128)S(1)}, f32[8,128,64]{2,1,0:T(8,128)S(1)}) custom-call(s32[1]{0:T(128)} %bitcast.me_ref, f32[16,24,128]{2,1,0:T(8,128)S(1)} %all_to_all.25.recv_ref, bf16[2,128,128]{2,1,0:T(8,128)(2,1)S(1)} %copy-done.9, f32[3,2,64,64]{3,2,1,0:T(8,128)S(1)} %copy-done.4), custom_call_target="tpu_custom_call" | custom-call | flops 134217728 | bytes 688132 | tf_op jit(solution)/shard_map/pallas_call | solution.py:430
  37.0 0.8 %copy-done.11 = f32[8,128,64]{2,1,0:T(8,128)} copy-done((f32[8,128,64]{2,1,0:T(8,128)}, f32[8,128,64]{2,1,0:T(8,128)S(1)}, u32[]{:S(2)}) %copy-start.11) | copy-done | bytes 262168
  37.8 8.0 %all-to-all-done.2.recv_ref = bf16[16,16,512]{2,1,0:T(8,128)(2,1)S(1)} async-done(((bf16[16,16,512]{2,1,0:T(8,128)(2,1)}), bf16[16,16,512]{2,1,0:T(8,128)(2,1)S(1)}, u32[]{:S(2)}, u32[]{:S(2)}) %all-to-all-start.2) | async-done | bytes 262176 | tf_op jit(solution)/shard_map/all_to_all | solution.py:23
  45.8 0.9 %copy-done.6 = bf16[128,512]{1,0:T(8,128)(2,1)S(1)} copy-done((bf16[128,512]{1,0:T(8,128)(2,1)S(1)}, bf16[128,512]{1,0:T(8,128)(2,1)}, u32[]{:S(2)}) %copy-start.6) | copy-done | bytes 131096
  46.7 1.3 %shard_map.82 = (f32[16,16,128]{2,1,0:T(8,128)S(1)}, bf16[512,512]{1,0:T(8,128)(2,1)S(1)}, bf16[512,512]{1,0:T(8,128)(2,1)S(1)}) custom-call(bf16[16,16,512]{2,1,0:T(8,128)(2,1)S(1)} %all-to-all-done.2.recv_ref, f32[2,64,128]{2,1,0:T(8,128)S(1)} %get-tuple-element.20.mix_ref, f32[64,512]{1,0:T(8,128)S(1)} %get-tuple-element.17.wv_ref, ...), custom_call_target="tpu_custom_call" | custom-call | flops 268435456 | bytes 3080192 | tf_op jit(solution)/shard_map/pallas_call | solution.py:430
  47.9 0.8 %copy-done.2 = bf16[512,512]{1,0:T(8,128)(2,1)} copy-done((bf16[512,512]{1,0:T(8,128)(2,1)}, bf16[512,512]{1,0:T(8,128)(2,1)S(1)}, u32[]{:S(2)}) %copy-start.2) | copy-done | bytes 524312
  48.7 10.5 %all_to_all.26.recv_ref = f32[16,16,128]{2,1,0:T(8,128)S(1)} all-to-all(f32[16,16,128]{2,1,0:T(8,128)S(1)} %get-tuple-element.25), channel_id=1, replica_groups=mesh['groups'=2,'gx'=4,'gy'=4] {'gx','gy'}, dimensions={0} | all-to-all | bytes 262144 | tf_op jit(solution)/shard_map/all_to_all | solution.py:23
  59.2 0.7 shard_map.84
  59.9 3.5 %all-to-all-start.4 = ((f32[16,16,128]{2,1,0:T(8,128)}), f32[16,16,128]{2,1,0:T(8,128)S(1)}, u32[]{:S(2)}, u32[]{:S(2)}) async-start(f32[16,16,128]{2,1,0:T(8,128)} %shard_map.84), calls=%async_computation.4 | async-start | bytes 262144 | tf_op jit(solution)/shard_map/all_to_all | solution.py:23
  63.4 1.0 %copy-done.1 = bf16[512,512]{1,0:T(8,128)(2,1)S(1)} copy-done((bf16[512,512]{1,0:T(8,128)(2,1)S(1)}, bf16[512,512]{1,0:T(8,128)(2,1)}, u32[]{:S(2)}) %copy-start.1) | copy-done | bytes 524312
  64.5 1.0 %copy-done.3 = bf16[512,512]{1,0:T(8,128)(2,1)S(1)} copy-done((bf16[512,512]{1,0:T(8,128)(2,1)S(1)}, bf16[512,512]{1,0:T(8,128)(2,1)}, u32[]{:S(2)}) %copy-start.3) | copy-done | bytes 524312
  65.5 0.4 shard_map.83
  66.0 0.0 copy-start.10
  66.0 0.9 %reshape.22 = bf16[64,2,4,512]{3,2,1,0:T(4,128)(2,1)} reshape(bf16[512,512]{1,0:T(8,128)(2,1)S(1)} %shard_map.83) | data formatting | bytes 1048576 | tf_op jit(solution)/shard_map/reshape | solution.py:520
  66.9 0.2 copy-done.12
  67.1 1.9 %shard_map.85.plane_ref = f32[8,64]{1,0:T(8,128)S(1)} custom-call(s32[1]{0:T(128)} %bitcast.me_ref, bf16[16,16,512]{2,1,0:T(8,128)(2,1)S(1)} %all-to-all-done.2.recv_ref, f32[8,128,64]{2,1,0:T(8,128)S(1)} %copy-done.12, bf16[2,128,128]{2,1,0:T(8,128)(2,1)S(1)} %copy-done.10, f32[3,2,64,64]{3,2,1,0:T(8,128)S(1)} %copy-done.4), custom_call_target="tpu_custom_call" | custom-call | flops 536870912 | bytes 690180 | tf_op jit(solution)/shard_map/pallas_call | solution.py:430
  69.0 0.5 shard_map.86.base_ref
  69.5 1.2 %all-to-all-done.4.recv_ref = f32[16,16,128]{2,1,0:T(8,128)S(1)} async-done(((f32[16,16,128]{2,1,0:T(8,128)}), f32[16,16,128]{2,1,0:T(8,128)S(1)}, u32[]{:S(2)}, u32[]{:S(2)}) %all-to-all-start.4) | async-done | bytes 131104 | tf_op jit(solution)/shard_map/all_to_all | solution.py:23
  70.7 0.1 shard_map.87
  70.9 0.9 %reshape.23 = bf16[64,2,4,512]{3,2,1,0:T(4,128)(2,1)} reshape(bf16[512,512]{1,0:T(8,128)(2,1)S(1)} %shard_map.87) | data formatting | bytes 1048576 | tf_op jit(solution)/shard_map/reshape | solution.py:520
  (19 shorter events, 0.1 us)
Async XLA Ops:
  2.2 20.0 %copy-start.13 = (bf16[64,2,4,512]{3,2,1,0:T(4,128)(2,1)S(1)}, bf16[64,2,4,512]{3,2,1,0:T(4,128)(2,1)}, u32[]{:S(2)}) copy-start(bf16[64,2,4,512]{3,2,1,0:T(4,128)(2,1)} %param.7) | copy-start | bytes 1572868
  18.3 11.2 %all-to-all-start.1 = ((f32[16,16,128]{2,1,0:T(8,128)}), f32[16,16,128]{2,1,0:T(8,128)S(1)}, u32[]{:S(2)}, u32[]{:S(2)}) async-start(f32[16,16,128]{2,1,0:T(8,128)} %shard_map.78), calls=%async_computation.1 | async-start | bytes 262144 | tf_op jit(solution)/shard_map/all_to_all | solution.py:23
  22.2 0.9 %copy-start.4 = (f32[3,2,64,64]{3,2,1,0:T(8,128)S(1)}, f32[3,2,64,64]{3,2,1,0:T(8,128)}, u32[]{:S(2)}) copy-start(f32[3,2,64,64]{3,2,1,0:T(8,128)} %qk_ref.5) | copy-start | bytes 294916
  22.2 0.9 %copy-start.7 = (bf16[64,64]{1,0:T(8,128)(2,1)S(1)}, bf16[64,64]{1,0:T(8,128)(2,1)}, u32[]{:S(2)}) copy-start(bf16[64,64]{1,0:T(8,128)(2,1)} %wv_ref.1) | copy-start | bytes 24580
  22.2 0.9 %copy-start.8 = (bf16[64,64]{1,0:T(8,128)(2,1)S(1)}, bf16[64,64]{1,0:T(8,128)(2,1)}, u32[]{:S(2)}) copy-start(bf16[64,64]{1,0:T(8,128)(2,1)} %wo_ref.1) | copy-start | bytes 24580
  23.4 7.9 %copy-start.5 = (bf16[128,512]{1,0:T(8,128)(2,1)}, bf16[128,512]{1,0:T(8,128)(2,1)S(1)}, u32[]{:S(2)}) copy-start(bf16[128,512]{1,0:T(8,128)(2,1)S(1)} %get-tuple-element.22.wk_ref) | copy-start | bytes 393220
  31.3 0.8 %copy-start = (bf16[512,512]{1,0:T(8,128)(2,1)}, bf16[512,512]{1,0:T(8,128)(2,1)S(1)}, u32[]{:S(2)}) copy-start(bf16[512,512]{1,0:T(8,128)(2,1)S(1)} %get-tuple-element.24.query_ref) | copy-start | bytes 1572868
  32.1 3.7 %copy-start.9 = (bf16[2,128,128]{2,1,0:T(8,128)(2,1)S(1)}, bf16[2,128,128]{2,1,0:T(8,128)(2,1)}, u32[]{:S(2)}) copy-start(bf16[2,128,128]{2,1,0:T(8,128)(2,1)} %constant.11.clone.same_ref) | copy-start | bytes 196612
  32.1 13.7 %all-to-all-start.2 = ((bf16[16,16,512]{2,1,0:T(8,128)(2,1)}), bf16[16,16,512]{2,1,0:T(8,128)(2,1)S(1)}, u32[]{:S(2)}, u32[]{:S(2)}) async-start(bf16[16,16,512]{2,1,0:T(8,128)(2,1)} %get-tuple-element.19), calls=%async_computation.2 | async-start | bytes 524288 | tf_op jit(solution)/shard_map/all_to_all | solution.py:23
  37.0 0.8 %copy-start.11 = (f32[8,128,64]{2,1,0:T(8,128)}, f32[8,128,64]{2,1,0:T(8,128)S(1)}, u32[]{:S(2)}) copy-start(f32[8,128,64]{2,1,0:T(8,128)S(1)} %get-tuple-element.29.feat_ref) | copy-start | bytes 786436
  45.8 0.9 %copy-start.6 = (bf16[128,512]{1,0:T(8,128)(2,1)S(1)}, bf16[128,512]{1,0:T(8,128)(2,1)}, u32[]{:S(2)}) copy-start(bf16[128,512]{1,0:T(8,128)(2,1)} %copy-done.5) | copy-start | bytes 393220
  47.9 0.8 %copy-start.2 = (bf16[512,512]{1,0:T(8,128)(2,1)}, bf16[512,512]{1,0:T(8,128)(2,1)S(1)}, u32[]{:S(2)}) copy-start(bf16[512,512]{1,0:T(8,128)(2,1)S(1)} %get-tuple-element.23.left_ref) | copy-start | bytes 1572868
  59.9 10.8 %all-to-all-start.4 = ((f32[16,16,128]{2,1,0:T(8,128)}), f32[16,16,128]{2,1,0:T(8,128)S(1)}, u32[]{:S(2)}, u32[]{:S(2)}) async-start(f32[16,16,128]{2,1,0:T(8,128)} %shard_map.84), calls=%async_computation.4 | async-start | bytes 262144 | tf_op jit(solution)/shard_map/all_to_all | solution.py:23
  63.4 1.0 %copy-start.1 = (bf16[512,512]{1,0:T(8,128)(2,1)S(1)}, bf16[512,512]{1,0:T(8,128)(2,1)}, u32[]{:S(2)}) copy-start(bf16[512,512]{1,0:T(8,128)(2,1)} %copy-done) | copy-start | bytes 1572868
  64.5 1.0 %copy-start.3 = (bf16[512,512]{1,0:T(8,128)(2,1)S(1)}, bf16[512,512]{1,0:T(8,128)(2,1)}, u32[]{:S(2)}) copy-start(bf16[512,512]{1,0:T(8,128)(2,1)} %copy-done.2) | copy-start | bytes 1572868
  66.0 0.9 %copy-start.10 = (bf16[2,128,128]{2,1,0:T(8,128)(2,1)S(1)}, bf16[2,128,128]{2,1,0:T(8,128)(2,1)}, u32[]{:S(2)}) copy-start(bf16[2,128,128]{2,1,0:T(8,128)(2,1)} %constant.11.clone.same_ref) | copy-start | bytes 196612
  66.0 1.1 %copy-start.12 = (f32[8,128,64]{2,1,0:T(8,128)S(1)}, f32[8,128,64]{2,1,0:T(8,128)}, u32[]{:S(2)}) copy-start(f32[8,128,64]{2,1,0:T(8,128)} %copy-done.11) | copy-start | bytes 786436

commit v3 on v2

--- a/solution.py
+++ b/solution.py
@@ -433,7 +433,7 @@
         in_specs=[smem] * scalars + [vmem] * (len(operands) - scalars),
         out_specs=tuple(vmem for _ in outs),
         scratch_shapes=list(scratch),
-        compiler_params=pltpu.CompilerParams(vmem_limit_bytes=48 * 1024 * 1024),
+        compiler_params=pltpu.CompilerParams(vmem_limit_bytes=16 * 1024 * 1024),
         cost_estimate=pl.CostEstimate(flops=flops, bytes_accessed=moved, transcendentals=0),
     )(*operands)
     return found[0] if len(outs) == 1 else found

time: 72.5 us -> 72.5 us (level)
  no operation moved by 1% of the time
where the time goes in v3:
time: 72.5 us; the launch traced here: 71.8 us
  blocking collectives  25.9 us (36%)
  waiting for transfers between devices  15.4 us (21%)
  starting transfers between devices  11 us (15%)
  local copies, waits for them, and re-layouts  9.5 us (13%)
  Pallas kernels  9.18 us (13%)
  between operations  0.83 us (1%)
    all_to_all x2, blocking collectives, exchange(): return lax.all_to_all(parts, AXES, split_axis=0, concat_axis=0, tiled=True)  25.9 us
    all_to_all x3, waiting for transfers between devices, exchange(): return lax.all_to_all(parts, AXES, split_axis=0, concat_axis=0, tiled=True)  15.4 us
    all_to_all x3, starting transfers between devices, exchange(): return lax.all_to_all(parts, AXES, split_axis=0, concat_axis=0, tiled=True)  11 us
    pallas_call x11, Pallas kernels, run(): pl.pallas_call(kernel, out_shape=tuple(outs), in_specs=[smem] * scalars +...  9.18 us
    unnamed x28, local copies, waits for them, and re-layouts  6.37 us
    reshape x2, local copies, waits for them, and re-layouts, per_device_kernels(): return (layer_output.reshape(field.shape), field_grad.reshape(field.shape))  1.83 us
  transfers between devices with their start and end apart: 3, of which 3 were waited for; matrix products, arithmetic and copies ran while one was open for 1% of the time, Pallas kernels for 6%

profile of v3, /device:TPU:0, one launch (start us, length us, event | category | flops | bytes accessed | tf_op | source)
XLA Modules:
  0.0 71.8 jit_solution(6340166182422690416)
XLA Ops:
  0.6 1.2 %reshape.19.field_ref = bf16[512,512]{1,0:T(8,128)(2,1)S(1)} reshape(bf16[64,2,4,512]{3,2,1,0:T(4,128)(2,1)} %param.6) | data formatting | bytes 1048576 | tf_op jit(solution)/shard_map/reshape | solution.py:465
  1.8 0.4 shard_map.77
  2.2 15.4 %all_to_all.25.recv_ref = f32[16,24,128]{2,1,0:T(8,128)S(1)} all-to-all(f32[16,24,128]{2,1,0:T(8,128)S(1)} %shard_map.77), channel_id=1, replica_groups=mesh['groups'=2,'gx'=4,'gy'=4] {'gx','gy'}, dimensions={0} | all-to-all | bytes 393216 | tf_op jit(solution)/shard_map/all_to_all | solution.py:23
  17.6 0.7 shard_map.78
  18.3 3.8 %all-to-all-start.1 = ((f32[16,16,128]{2,1,0:T(8,128)}), f32[16,16,128]{2,1,0:T(8,128)S(1)}, u32[]{:S(2)}, u32[]{:S(2)}) async-start(f32[16,16,128]{2,1,0:T(8,128)} %shard_map.78), calls=%async_computation.1 | async-start | bytes 262144 | tf_op jit(solution)/shard_map/all_to_all | solution.py:23
  22.2 0.1 reshape.20.cot_ref
  22.3 0.8 %copy-done.4 = f32[3,2,64,64]{3,2,1,0:T(8,128)S(1)} copy-done((f32[3,2,64,64]{3,2,1,0:T(8,128)S(1)}, f32[3,2,64,64]{3,2,1,0:T(8,128)}, u32[]{:S(2)}) %copy-start.4) | copy-done | bytes 98328
  23.1 0.3 shard_map.79
  23.4 6.1 %all-to-all-done.1.recv_ref = f32[16,16,128]{2,1,0:T(8,128)S(1)} async-done(((f32[16,16,128]{2,1,0:T(8,128)}), f32[16,16,128]{2,1,0:T(8,128)S(1)}, u32[]{:S(2)}, u32[]{:S(2)}) %all-to-all-start.1) | async-done | bytes 131104 | tf_op jit(solution)/shard_map/all_to_all | solution.py:23
  29.5 1.7 %shard_map.80 = (bf16[16,16,512]{2,1,0:T(8,128)(2,1)}, f32[72,512]{1,0:T(8,128)S(1)}, bf16[512,512]{1,0:T(8,128)(2,1)S(1)}, bf16[512,512]{1,0:T(8,128)(2,1)S(1)}) custom-call(f32[16,16,128]{2,1,0:T(8,128)S(1)} %all-to-all-done.1.recv_ref, f32[128,64]{1,0:T(8,128)S(1)} %get-tuple-element.16.wz_ref, bf16[512,512]{1,0:T(8,128)(2,1)S(1)} %reshape.19.field_ref, ...), custom_call_target="tpu_custom_call" | custom-call | flops 536870912 | bytes 2932736 | tf_op jit(solution)/shard_map/pallas_call | solution.py:430
  31.3 0.8 %copy-done = bf16[512,512]{1,0:T(8,128)(2,1)} copy-done((bf16[512,512]{1,0:T(8,128)(2,1)}, bf16[512,512]{1,0:T(8,128)(2,1)S(1)}, u32[]{:S(2)}) %copy-start) | copy-done | bytes 524312
  32.1 3.7 %all-to-all-start.2 = ((bf16[16,16,512]{2,1,0:T(8,128)(2,1)}), bf16[16,16,512]{2,1,0:T(8,128)(2,1)S(1)}, u32[]{:S(2)}, u32[]{:S(2)}) async-start(bf16[16,16,512]{2,1,0:T(8,128)(2,1)} %get-tuple-element.19), calls=%async_computation.2 | async-start | bytes 524288 | tf_op jit(solution)/shard_map/all_to_all | solution.py:23
  35.8 1.2 %shard_map.81 = (f32[2,64,128]{2,1,0:T(8,128)S(1)}, f32[8,128,64]{2,1,0:T(8,128)S(1)}) custom-call(s32[1]{0:T(128)} %bitcast.me_ref, f32[16,24,128]{2,1,0:T(8,128)S(1)} %all_to_all.25.recv_ref, bf16[2,128,128]{2,1,0:T(8,128)(2,1)S(1)} %copy-done.9, f32[3,2,64,64]{3,2,1,0:T(8,128)S(1)} %copy-done.4), custom_call_target="tpu_custom_call" | custom-call | flops 134217728 | bytes 688132 | tf_op jit(solution)/shard_map/pallas_call | solution.py:430
  37.0 0.8 %copy-done.11 = f32[8,128,64]{2,1,0:T(8,128)} copy-done((f32[8,128,64]{2,1,0:T(8,128)}, f32[8,128,64]{2,1,0:T(8,128)S(1)}, u32[]{:S(2)}) %copy-start.11) | copy-done | bytes 262168
  37.8 8.0 %all-to-all-done.2.recv_ref = bf16[16,16,512]{2,1,0:T(8,128)(2,1)S(1)} async-done(((bf16[16,16,512]{2,1,0:T(8,128)(2,1)}), bf16[16,16,512]{2,1,0:T(8,128)(2,1)S(1)}, u32[]{:S(2)}, u32[]{:S(2)}) %all-to-all-start.2) | async-done | bytes 262176 | tf_op jit(solution)/shard_map/all_to_all | solution.py:23
  45.8 0.9 %copy-done.6 = bf16[128,512]{1,0:T(8,128)(2,1)S(1)} copy-done((bf16[128,512]{1,0:T(8,128)(2,1)S(1)}, bf16[128,512]{1,0:T(8,128)(2,1)}, u32[]{:S(2)}) %copy-start.6) | copy-done | bytes 131096
  46.7 1.3 %shard_map.82 = (f32[16,16,128]{2,1,0:T(8,128)S(1)}, bf16[512,512]{1,0:T(8,128)(2,1)S(1)}, bf16[512,512]{1,0:T(8,128)(2,1)S(1)}) custom-call(bf16[16,16,512]{2,1,0:T(8,128)(2,1)S(1)} %all-to-all-done.2.recv_ref, f32[2,64,128]{2,1,0:T(8,128)S(1)} %get-tuple-element.20.mix_ref, f32[64,512]{1,0:T(8,128)S(1)} %get-tuple-element.17.wv_ref, ...), custom_call_target="tpu_custom_call" | custom-call | flops 268435456 | bytes 3080192 | tf_op jit(solution)/shard_map/pallas_call | solution.py:430
  47.9 0.8 %copy-done.2 = bf16[512,512]{1,0:T(8,128)(2,1)} copy-done((bf16[512,512]{1,0:T(8,128)(2,1)}, bf16[512,512]{1,0:T(8,128)(2,1)S(1)}, u32[]{:S(2)}) %copy-start.2) | copy-done | bytes 524312
  48.7 10.5 %all_to_all.26.recv_ref = f32[16,16,128]{2,1,0:T(8,128)S(1)} all-to-all(f32[16,16,128]{2,1,0:T(8,128)S(1)} %get-tuple-element.25), channel_id=1, replica_groups=mesh['groups'=2,'gx'=4,'gy'=4] {'gx','gy'}, dimensions={0} | all-to-all | bytes 262144 | tf_op jit(solution)/shard_map/all_to_all | solution.py:23
  59.2 0.7 shard_map.84
  59.9 3.5 %all-to-all-start.4 = ((f32[16,16,128]{2,1,0:T(8,128)}), f32[16,16,128]{2,1,0:T(8,128)S(1)}, u32[]{:S(2)}, u32[]{:S(2)}) async-start(f32[16,16,128]{2,1,0:T(8,128)} %shard_map.84), calls=%async_computation.4 | async-start | bytes 262144 | tf_op jit(solution)/shard_map/all_to_all | solution.py:23
  63.4 1.0 %copy-done.1 = bf16[512,512]{1,0:T(8,128)(2,1)S(1)} copy-done((bf16[512,512]{1,0:T(8,128)(2,1)S(1)}, bf16[512,512]{1,0:T(8,128)(2,1)}, u32[]{:S(2)}) %copy-start.1) | copy-done | bytes 524312
  64.5 1.0 %copy-done.3 = bf16[512,512]{1,0:T(8,128)(2,1)S(1)} copy-done((bf16[512,512]{1,0:T(8,128)(2,1)S(1)}, bf16[512,512]{1,0:T(8,128)(2,1)}, u32[]{:S(2)}) %copy-start.3) | copy-done | bytes 524312
  65.5 0.4 shard_map.83
  66.0 0.0 copy-start.10
  66.0 0.9 %reshape.22 = bf16[64,2,4,512]{3,2,1,0:T(4,128)(2,1)} reshape(bf16[512,512]{1,0:T(8,128)(2,1)S(1)} %shard_map.83) | data formatting | bytes 1048576 | tf_op jit(solution)/shard_map/reshape | solution.py:520
  66.9 0.2 copy-done.12
  67.1 1.9 %shard_map.85.plane_ref = f32[8,64]{1,0:T(8,128)S(1)} custom-call(s32[1]{0:T(128)} %bitcast.me_ref, bf16[16,16,512]{2,1,0:T(8,128)(2,1)S(1)} %all-to-all-done.2.recv_ref, f32[8,128,64]{2,1,0:T(8,128)S(1)} %copy-done.12, bf16[2,128,128]{2,1,0:T(8,128)(2,1)S(1)} %copy-done.10, f32[3,2,64,64]{3,2,1,0:T(8,128)S(1)} %copy-done.4), custom_call_target="tpu_custom_call" | custom-call | flops 536870912 | bytes 690180 | tf_op jit(solution)/shard_map/pallas_call | solution.py:430
  69.0 0.5 shard_map.86.base_ref
  69.5 1.2 %all-to-all-done.4.recv_ref = f32[16,16,128]{2,1,0:T(8,128)S(1)} async-done(((f32[16,16,128]{2,1,0:T(8,128)}), f32[16,16,128]{2,1,0:T(8,128)S(1)}, u32[]{:S(2)}, u32[]{:S(2)}) %all-to-all-start.4) | async-done | bytes 131104 | tf_op jit(solution)/shard_map/all_to_all | solution.py:23
  70.7 0.1 shard_map.87
  70.9 0.9 %reshape.23 = bf16[64,2,4,512]{3,2,1,0:T(4,128)(2,1)} reshape(bf16[512,512]{1,0:T(8,128)(2,1)S(1)} %shard_map.87) | data formatting | bytes 1048576 | tf_op jit(solution)/shard_map/reshape | solution.py:520
  (19 shorter events, 0.1 us)
Async XLA Ops:
  2.2 20.0 %copy-start.13 = (bf16[64,2,4,512]{3,2,1,0:T(4,128)(2,1)S(1)}, bf16[64,2,4,512]{3,2,1,0:T(4,128)(2,1)}, u32[]{:S(2)}) copy-start(bf16[64,2,4,512]{3,2,1,0:T(4,128)(2,1)} %param.7) | copy-start | bytes 1572868
  18.3 11.2 %all-to-all-start.1 = ((f32[16,16,128]{2,1,0:T(8,128)}), f32[16,16,128]{2,1,0:T(8,128)S(1)}, u32[]{:S(2)}, u32[]{:S(2)}) async-start(f32[16,16,128]{2,1,0:T(8,128)} %shard_map.78), calls=%async_computation.1 | async-start | bytes 262144 | tf_op jit(solution)/shard_map/all_to_all | solution.py:23
  22.2 0.9 %copy-start.4 = (f32[3,2,64,64]{3,2,1,0:T(8,128)S(1)}, f32[3,2,64,64]{3,2,1,0:T(8,128)}, u32[]{:S(2)}) copy-start(f32[3,2,64,64]{3,2,1,0:T(8,128)} %qk_ref.5) | copy-start | bytes 294916
  22.2 0.9 %copy-start.7 = (bf16[64,64]{1,0:T(8,128)(2,1)S(1)}, bf16[64,64]{1,0:T(8,128)(2,1)}, u32[]{:S(2)}) copy-start(bf16[64,64]{1,0:T(8,128)(2,1)} %wv_ref.1) | copy-start | bytes 24580
  22.2 0.9 %copy-start.8 = (bf16[64,64]{1,0:T(8,128)(2,1)S(1)}, bf16[64,64]{1,0:T(8,128)(2,1)}, u32[]{:S(2)}) copy-start(bf16[64,64]{1,0:T(8,128)(2,1)} %wo_ref.1) | copy-start | bytes 24580
  23.4 7.9 %copy-start.5 = (bf16[128,512]{1,0:T(8,128)(2,1)}, bf16[128,512]{1,0:T(8,128)(2,1)S(1)}, u32[]{:S(2)}) copy-start(bf16[128,512]{1,0:T(8,128)(2,1)S(1)} %get-tuple-element.22.wk_ref) | copy-start | bytes 393220
  31.3 0.8 %copy-start = (bf16[512,512]{1,0:T(8,128)(2,1)}, bf16[512,512]{1,0:T(8,128)(2,1)S(1)}, u32[]{:S(2)}) copy-start(bf16[512,512]{1,0:T(8,128)(2,1)S(1)} %get-tuple-element.24.query_ref) | copy-start | bytes 1572868
  32.1 3.7 %copy-start.9 = (bf16[2,128,128]{2,1,0:T(8,128)(2,1)S(1)}, bf16[2,128,128]{2,1,0:T(8,128)(2,1)}, u32[]{:S(2)}) copy-start(bf16[2,128,128]{2,1,0:T(8,128)(2,1)} %constant.11.clone.same_ref) | copy-start | bytes 196612
  32.1 13.7 %all-to-all-start.2 = ((bf16[16,16,512]{2,1,0:T(8,128)(2,1)}), bf16[16,16,512]{2,1,0:T(8,128)(2,1)S(1)}, u32[]{:S(2)}, u32[]{:S(2)}) async-start(bf16[16,16,512]{2,1,0:T(8,128)(2,1)} %get-tuple-element.19), calls=%async_computation.2 | async-start | bytes 524288 | tf_op jit(solution)/shard_map/all_to_all | solution.py:23
  37.0 0.8 %copy-start.11 = (f32[8,128,64]{2,1,0:T(8,128)}, f32[8,128,64]{2,1,0:T(8,128)S(1)}, u32[]{:S(2)}) copy-start(f32[8,128,64]{2,1,0:T(8,128)S(1)} %get-tuple-element.29.feat_ref) | copy-start | bytes 786436
  45.8 0.9 %copy-start.6 = (bf16[128,512]{1,0:T(8,128)(2,1)S(1)}, bf16[128,512]{1,0:T(8,128)(2,1)}, u32[]{:S(2)}) copy-start(bf16[128,512]{1,0:T(8,128)(2,1)} %copy-done.5) | copy-start | bytes 393220
  47.9 0.8 %copy-start.2 = (bf16[512,512]{1,0:T(8,128)(2,1)}, bf16[512,512]{1,0:T(8,128)(2,1)S(1)}, u32[]{:S(2)}) copy-start(bf16[512,512]{1,0:T(8,128)(2,1)S(1)} %get-tuple-element.23.left_ref) | copy-start | bytes 1572868
  59.9 10.8 %all-to-all-start.4 = ((f32[16,16,128]{2,1,0:T(8,128)}), f32[16,16,128]{2,1,0:T(8,128)S(1)}, u32[]{:S(2)}, u32[]{:S(2)}) async-start(f32[16,16,128]{2,1,0:T(8,128)} %shard_map.84), calls=%async_computation.4 | async-start | bytes 262144 | tf_op jit(solution)/shard_map/all_to_all | solution.py:23
  63.4 1.0 %copy-start.1 = (bf16[512,512]{1,0:T(8,128)(2,1)S(1)}, bf16[512,512]{1,0:T(8,128)(2,1)}, u32[]{:S(2)}) copy-start(bf16[512,512]{1,0:T(8,128)(2,1)} %copy-done) | copy-start | bytes 1572868
  64.5 1.0 %copy-start.3 = (bf16[512,512]{1,0:T(8,128)(2,1)S(1)}, bf16[512,512]{1,0:T(8,128)(2,1)}, u32[]{:S(2)}) copy-start(bf16[512,512]{1,0:T(8,128)(2,1)} %copy-done.2) | copy-start | bytes 1572868
  66.0 0.9 %copy-start.10 = (bf16[2,128,128]{2,1,0:T(8,128)(2,1)S(1)}, bf16[2,128,128]{2,1,0:T(8,128)(2,1)}, u32[]{:S(2)}) copy-start(bf16[2,128,128]{2,1,0:T(8,128)(2,1)} %constant.11.clone.same_ref) | copy-start | bytes 196612
  66.0 1.1 %copy-start.12 = (f32[8,128,64]{2,1,0:T(8,128)S(1)}, f32[8,128,64]{2,1,0:T(8,128)}, u32[]{:S(2)}) copy-start(f32[8,128,64]{2,1,0:T(8,128)} %copy-done.11) | copy-start | bytes 786436

commit v4 on v3

--- a/solution.py
+++ b/solution.py
@@ -21,6 +21,10 @@
 
 def exchange(parts):
     return lax.all_to_all(parts, AXES, split_axis=0, concat_axis=0, tiled=True)
+
+
+def swap(part, axis, size, step):
+    return lax.ppermute(part, axis, [(i, i ^ step) for i in range(size)])
 
 
 def gather(part, count):
@@ -197,22 +201,29 @@
     return lax.broadcasted_iota(jnp.int32, shape, dim)
 
 
-def put_blocks(ref, total):
-    count = ref.shape[0]
-    columns = total.shape[1] // LANES
-    groups = count // columns
-    rows = WIDTH // groups
-    for block in range(count):
-        column, group = block // groups, block % groups
-        ref[block, 0:rows, :] = total[
-            group * rows : (group + 1) * rows, column * LANES : (column + 1) * LANES
-        ]
-
-
-def whole_blocks(ref, depth):
-    columns = depth // LANES
-    blocks = ref[...].reshape(columns, WIDTH, LANES)
-    return jnp.concatenate([blocks[i] for i in range(columns)], axis=1)
+def put_quarters(place_ref, part_ref, total, outs):
+    for index in range(part_ref.shape[0]):
+        part_ref[index] = total[:, index * LANES : (index + 1) * LANES]
+    for step, out in enumerate(outs):
+        out[0:WIDTH, :] = part_ref[place_ref[0] ^ step]
+
+
+def join_quarters(place_ref, part_ref, quarters):
+    for step, quarter in enumerate(quarters):
+        part_ref[place_ref[0] ^ step] = quarter[...]
+    return jnp.concatenate([part_ref[index] for index in range(part_ref.shape[0])], axis=1)
+
+
+def expand(part):
+    depth = part.shape[1]
+    part = part.reshape(HEADS, 1, HEAD_DIM, depth)
+    part = jnp.broadcast_to(part, (HEADS, HEAD_DIM, HEAD_DIM, depth))
+    return part.reshape(WIDTH * HEAD_DIM, depth).astype(jnp.bfloat16)
+
+
+def spread(weights, top):
+    left = weights[:, None, :] * top[None]
+    return left.reshape(-1, left.shape[2]).astype(jnp.bfloat16)
 
 
 def prepare_kernel(wv_ref, wo_ref, qk_ref, wv_out, wo_out, wq_out, wk_out, wz_out):
@@ -230,7 +241,8 @@
         wz_out[index * WIDTH : (index + 1) * WIDTH, :] = qk_ref[2, index].T
 
 
-def sums_kernel(field_ref, out_ref):
+def sums_kernel(place_ref, field_ref, *refs):
+    outs, part_ref = refs[:-1], refs[-1]
     data = field_ref[...]
     rows, depth = data.shape
     cells = rows // WIDTH
@@ -239,21 +251,60 @@
     row_sums = mul(data, jnp.ones((depth, LANES), jnp.bfloat16)).reshape(WIDTH, cells, LANES)
     shape = row_sums.shape
     own = jnp.sum(jnp.where(number(shape, 0) == number(shape, 2), row_sums, 0.0), axis=0)
-    put_blocks(out_ref, part)
-    for block in range(out_ref.shape[0]):
-        out_ref[block, out_ref.shape[1] - cells :, :] = own
-
-
-def add_kernel(recv_ref, out_ref):
-    rows = out_ref.shape[1]
-    total = jnp.sum(recv_ref[:, 0:rows, :], axis=0)
-    out_ref[...] = jnp.broadcast_to(total[None], out_ref.shape)
-
-
-def plane_kernel(cells, lengths, me_ref, recv_ref, same_ref, qk_ref, mix_ref, feat_ref):
-    places = recv_ref.shape[0] * cells
-    totals = recv_ref[:, recv_ref.shape[1] - cells :, :].reshape(places, LANES)[:, :WIDTH]
-    here = pl.ds(pl.multiple_of(me_ref[0] * cells, cells), cells)
+    put_quarters(place_ref, part_ref, part, outs)
+    for out in outs:
+        out[WIDTH:, :] = own
+
+
+def add_kernel(*refs):
+    parts, out_ref = refs[:-1], refs[-1]
+    total = parts[0][0:WIDTH, :]
+    for part in parts[1:]:
+        total = total + part[0:WIDTH, :]
+    out_ref[0:WIDTH, :] = total
+    cells = parts[0].shape[0] - WIDTH
+    for step, part in enumerate(parts):
+        start = WIDTH + step * cells
+        out_ref[start : start + cells, :] = part[WIDTH:, :]
+
+
+def factor_kernel(places, *refs):
+    parts, (wz_ref, both_ref, feat_ref) = refs[:-3], refs[-3:]
+    total = parts[0][0:WIDTH, :]
+    for part in parts[1:]:
+        total = total + part[0:WIDTH, :]
+    pooled = total * (1.0 / places)
+    inverse = lax.rsqrt(jnp.mean(pooled * pooled, axis=0, keepdims=True) + EPSILON)
+    normed = pooled * inverse
+    feat_ref[0:WIDTH, :] = normed
+    feat_ref[WIDTH:, :] = jnp.broadcast_to(inverse, (HEAD_DIM, LANES))
+    both_ref[...] = mul_near(wz_ref[...], normed).astype(jnp.bfloat16)
+
+
+def pull_kernel(places, *refs):
+    parts, (feat_ref, out_ref) = refs[:-2], refs[-2:]
+    found = parts[0][...]
+    for part in parts[1:]:
+        found = found + part[...]
+    normed = feat_ref[0:WIDTH, :]
+    inverse = feat_ref[WIDTH : WIDTH + 1, :]
+    found = inverse * (found - normed * jnp.mean(found * normed, axis=0, keepdims=True))
+    out_ref[...] = found * (1.0 / places)
+
+
+def plane_kernel(cells, lengths, place_ref, *refs):
+    parts, (same_ref, qk_ref, mix_ref, feat_ref, total_ref) = refs[:-5], refs[-5:]
+    span_y = len(parts)
+    count = total_ref.shape[0]
+    places = count * cells
+    for block in range(count):
+        step_x, step_y = block // span_y, block % span_y
+        start = WIDTH + step_x * cells
+        index = (place_ref[0] ^ step_x) * span_y + (place_ref[1] ^ step_y)
+        total_ref[index] = parts[step_y][start : start + cells, :]
+    totals = total_ref[...].reshape(places, LANES)[:, :WIDTH]
+    me = place_ref[0] * span_y + place_ref[1]
+    here = pl.ds(pl.multiple_of(me * cells, cells), cells)
     head = (number((HEADS * cells, WIDTH), 0) // cells) == (number((HEADS * cells, WIDTH), 1) >> 3)
     high, low = split(totals)
     forward = backward = None
@@ -283,27 +334,17 @@
     mix_ref[1] = backward
 
 
-def coef_kernel(places, recv_ref, wz_ref, field_ref, cot_ref, wv_ref, wo_ref,
-                send_ref, feat_ref, query_ref, keyset_ref):
+def coef_kernel(place_ref, *refs):
+    quarters, rest = refs[:-8], refs[-8:]
+    field_ref, cot_ref, wv_ref, wo_ref, send_ref, both_ref, part_ref = rest[1:]
+    quarters = quarters + rest[:1]
     rows, depth = field_ref.shape
     cells = rows // WIDTH
     wide = HEADS * HEAD_DIM * HEAD_DIM
-    pooled = whole_blocks(recv_ref, depth) * (1.0 / places)
-    inverse = lax.rsqrt(jnp.mean(pooled * pooled, axis=0, keepdims=True) + EPSILON)
-    normed = pooled * inverse
-    feat_ref[0:WIDTH, :] = normed
-    feat_ref[WIDTH:, :] = jnp.broadcast_to(inverse, (HEAD_DIM, depth))
-    both = mul_near(wz_ref[...], normed)
-
-    def expand(part):
-        part = part.reshape(HEADS, 1, HEAD_DIM, depth)
-        part = jnp.broadcast_to(part, (HEADS, HEAD_DIM, HEAD_DIM, depth))
-        return part.reshape(wide, depth).astype(jnp.bfloat16)
-
+    both = join_quarters(place_ref, part_ref, [q[...].astype(jnp.float32) for q in quarters])
+    both_ref[...] = both.astype(jnp.bfloat16)
     query = expand(both[:WIDTH])
     keyset = expand(both[WIDTH:])
-    query_ref[...] = query
-    keyset_ref[...] = keyset
     low_f = mul(field_ref[...], keyset, NT).reshape(WIDTH, cells, wide)
     low_f = jnp.sum(wv_ref[...][:, None, :] * low_f, axis=0)
     low_c = mul(cot_ref[...], query, NT).reshape(WIDTH, cells, wide)
@@ -312,8 +353,9 @@
     send_ref[...] = jnp.broadcast_to(low[None], send_ref.shape)
 
 
-def mix_kernel(factor, recv_ref, mix_ref, wv_ref, wo_ref, wq_ref, wk_ref, field_ref, cot_ref,
-               send_ref, left_f_ref, left_c_ref):
+def mix_kernel(factor, place_ref, recv_ref, mix_ref, wv_ref, wo_ref, wq_ref, wk_ref, field_ref,
+               cot_ref, top_ref, *refs):
+    outs, part_ref = refs[:-1], refs[-1]
     rows = field_ref.shape[0]
     cells = rows // WIDTH
     places = recv_ref.shape[0] * cells
@@ -327,29 +369,28 @@
         found = mul_left(mix, low).reshape(shape)
         return jnp.sum(jnp.where(head, found, 0.0), axis=0) * factor
 
-    left_f = wo_ref[...][:, None, :] * top(mix_ref[0], both[:, :cells])[None]
-    left_f = left_f.reshape(rows, wide).astype(jnp.bfloat16)
-    left_c = wv_ref[...][:, None, :] * top(mix_ref[1], both[:, cells:])[None]
-    left_c = left_c.reshape(rows, wide).astype(jnp.bfloat16)
-    left_f_ref[...] = left_f
-    left_c_ref[...] = left_c
+    top_f = top(mix_ref[0], both[:, :cells])
+    top_c = top(mix_ref[1], both[:, cells:])
+    top_ref[0] = top_f
+    top_ref[1] = top_c
+    left_f = spread(wo_ref[...], top_f)
+    left_c = spread(wv_ref[...], top_c)
 
     def pull(weights, left, right):
         found = mul(weights, left, NT)
         return mul_left(found[:WIDTH] + found[WIDTH:], right)
 
-    put_blocks(
-        send_ref,
-        pull(wq_ref[...], left_f, cot_ref[...]) + pull(wk_ref[...], left_c, field_ref[...]),
-    )
-
-
-def output_kernel(left_ref, query_ref, field_ref, out_ref):
-    found = mul(left_ref[...], query_ref[...]) + field_ref[...].astype(jnp.float32)
-    out_ref[...] = found.astype(jnp.bfloat16)
-
-
-def gram_kernel(cells, lengths, factor_z, me_ref, recv_ref, feat_ref, same_ref, qk_ref, out_ref,
+    found = pull(wq_ref[...], left_f, cot_ref[...]) + pull(wk_ref[...], left_c, field_ref[...])
+    put_quarters(place_ref, part_ref, found, outs)
+
+
+def output_kernel(top_ref, wo_ref, both_ref, field_ref, out_ref):
+    query = expand(both_ref[...].astype(jnp.float32)[:WIDTH])
+    left = spread(wo_ref[...], top_ref[0])
+    out_ref[...] = (mul(left, query) + field_ref[...].astype(jnp.float32)).astype(jnp.bfloat16)
+
+
+def gram_kernel(cells, span_y, lengths, factor_z, place_ref, recv_ref, feat_ref, same_ref, qk_ref, out_ref,
                 found_ref):
     places = recv_ref.shape[0] * cells
     wide = recv_ref.shape[2]
@@ -357,7 +398,8 @@
     both = recv_ref[...].astype(jnp.float32)
     low_f = both[:, :cells].reshape(places, wide).astype(jnp.bfloat16)
     low_c = both[:, cells:].reshape(places, wide).astype(jnp.bfloat16)
-    here = pl.ds(pl.multiple_of(me_ref[0] * cells, cells), cells)
+    me = place_ref[0] * span_y + place_ref[1]
+    here = pl.ds(pl.multiple_of(me * cells, cells), cells)
     lane = number((places, LANES), 1)
     products = []
     for pair in range(wide // LANES):
@@ -400,25 +442,24 @@
     out_ref[...] = total
 
 
-def base_kernel(left_ref, keyset_ref, cot_ref, plane_ref, out_ref):
+def base_kernel(top_ref, wv_ref, both_ref, cot_ref, plane_ref, out_ref):
     rows = cot_ref.shape[0]
     cells = rows // WIDTH
     shape = (WIDTH, cells, WIDTH)
     own = jnp.where(number(shape, 0) == number(shape, 2), plane_ref[...][None], 0.0)
     plane = mul_left(own.reshape(rows, WIDTH), jnp.ones((WIDTH, LANES), jnp.bfloat16))
-    found = mul(left_ref[...], keyset_ref[...]) + cot_ref[...].astype(jnp.float32)
+    keyset = expand(both_ref[...].astype(jnp.float32)[WIDTH:])
+    left = spread(wv_ref[...], top_ref[1])
+    found = mul(left, keyset) + cot_ref[...].astype(jnp.float32)
     columns = found.shape[1] // LANES
     out_ref[...] = found + jnp.concatenate([plane] * columns, axis=1)
 
 
-def final_kernel(places, recv_ref, feat_ref, base_ref, out_ref):
+def final_kernel(place_ref, *refs):
+    quarters, (base_ref, out_ref, part_ref) = refs[:-3], refs[-3:]
     rows, depth = base_ref.shape
     cells = rows // WIDTH
-    found = whole_blocks(recv_ref, depth)
-    normed = feat_ref[0:WIDTH, :]
-    inverse = feat_ref[WIDTH : WIDTH + 1, :]
-    found = inverse * (found - normed * jnp.mean(found * normed, axis=0, keepdims=True))
-    found = found * (1.0 / places)
+    found = join_quarters(place_ref, part_ref, quarters)
     total = base_ref[...].reshape(WIDTH, cells, depth) + found[:, None, :]
     out_ref[...] = total.reshape(rows, depth).astype(jnp.bfloat16)
 
@@ -453,24 +494,33 @@
     f32, bf16 = jnp.float32, jnp.bfloat16
     like = jax.ShapeDtypeStruct
     lengths = ((grid_x, grid_y * depth), (grid_y, grid_x * depth))
-    me = (lax.axis_index("gx") * span_y + lax.axis_index("gy")).astype(jnp.int32).reshape(1)
-
-    place = np.arange(places)
-    at_x = place // cells // span_y * rows_x + place % cells // rows_y
-    at_y = place // cells % span_y * rows_y + place % rows_y
+    place = jnp.stack([lax.axis_index("gx"), lax.axis_index("gy")]).astype(jnp.int32)
+
+    cell = np.arange(places)
+    at_x = cell // cells // span_y * rows_x + cell % cells // rows_y
+    at_y = cell // cells % span_y * rows_y + cell % rows_y
     same = jnp.asarray(
         np.stack([at_x[:, None] == at_x[None], at_y[:, None] == at_y[None]]), dtype=bf16
     )
 
     cols = field.reshape(rows, depth)
     cots = cotangent.reshape(rows, depth)
-    share = WIDTH * depth // LANES // count
-    block = like((count, share, LANES), f32)
+    block = like((WIDTH, LANES), f32)
+    parts = pltpu.VMEM((span_x, WIDTH, LANES), f32)
     factor_z = 1.0 / math.sqrt(HEAD_DIM * depth)
     cube = rows * wide * depth * 2
 
-    sums = run(sums_kernel, [like((count, share + cells, LANES), f32)], (cols,), flops=cube // 4)
-    recv = exchange(sums)
+    def swaps(sent, axis, size):
+        if not isinstance(sent, (tuple, list)):
+            sent = [sent] * size
+        return tuple(sent[:1]) + tuple(
+            swap(sent[step], axis, size, step) for step in range(1, size)
+        )
+
+    sums = run(
+        sums_kernel, [like((WIDTH + cells, LANES), f32)] * span_x, (place, cols),
+        scalars=1, flops=cube // 4, scratch=[parts],
+    )
     wv, wo, wq, wk, wz = run(
         prepare_kernel,
         [like((WIDTH, wide), f32)] * 2 + [like((2 * WIDTH, wide), bf16)] * 2
@@ -478,44 +528,64 @@
         (w_value, w_out, qk_weight),
         flops=cube // 8,
     )
-    pooled = exchange(run(add_kernel, [block], (recv,)))
+    total = run(
+        add_kernel, [like((WIDTH + span_x * cells, LANES), f32)], swaps(sums, "gx", span_x)
+    )
+    totals = swaps(total, "gy", span_y)
+    mine, feat_z = run(
+        functools.partial(factor_kernel, grid_x * grid_y),
+        [like((2 * WIDTH, LANES), bf16), like((WIDTH + HEAD_DIM, LANES), f32)],
+        totals + (wz,),
+    )
     mix, feat = run(
         functools.partial(plane_kernel, cells, lengths),
         [like((2, HEADS * cells, places), f32), like((8, places, WIDTH), f32)],
-        (me, recv, same, qk_weight),
+        (place,) + totals + (same, qk_weight),
         scalars=1,
         flops=cube // 2,
-    )
-    send, feat_z, query, keyset = run(
-        functools.partial(coef_kernel, grid_x * grid_y),
-        [like((count, 2 * cells, wide), bf16), like((WIDTH + HEAD_DIM, depth), f32)]
-        + [like((wide, depth), bf16)] * 2,
-        (pooled, wz, cols, cots, wv, wo),
+        scratch=[pltpu.VMEM((count, cells, LANES), f32)],
+    )
+    send, both = run(
+        coef_kernel,
+        [like((count, 2 * cells, wide), bf16), like((2 * WIDTH, depth), bf16)],
+        (place,) + swaps(mine, "gx", span_x) + (cols, cots, wv, wo),
+        scalars=1,
         flops=2 * cube,
+        scratch=[pltpu.VMEM((span_x, 2 * WIDTH, LANES), f32)],
     )
     low = exchange(send)
-    send, left_f, left_c = run(
+    top, *pulls = run(
         functools.partial(mix_kernel, factor_z),
-        [block, like((rows, wide), bf16), like((rows, wide), bf16)],
-        (low, mix, wv, wo, wq, wk, cols, cots),
+        [like((2, cells, wide), f32)] + [block] * span_x,
+        (place, low, mix, wv, wo, wq, wk, cols, cots),
+        scalars=1,
         flops=cube,
-    )
-    recv = exchange(send)
-    layer_output = run(output_kernel, [like((rows, depth), bf16)], (left_f, query, cols), flops=cube)
+        scratch=[parts],
+    )
+    total = sum(swaps(pulls, "gx", span_x))
+    layer_output = run(
+        output_kernel, [like((rows, depth), bf16)], (top, wo, both, cols), flops=cube
+    )
     plane = run(
-        functools.partial(gram_kernel, cells, lengths, factor_z),
+        functools.partial(gram_kernel, cells, span_y, lengths, factor_z),
         [like((cells, WIDTH), f32)],
-        (me, low, feat, same, qk_weight),
+        (place, low, feat, same, qk_weight),
         scalars=1,
         flops=2 * cube,
         scratch=[pltpu.VMEM((places, WIDTH), f32)],
     )
-    pulled = exchange(run(add_kernel, [block], (recv,)))
-    base = run(base_kernel, [like((rows, depth), f32)], (left_c, keyset, cots, plane), flops=cube)
+    mine = run(
+        functools.partial(pull_kernel, grid_x * grid_y),
+        [block],
+        swaps(total, "gy", span_y) + (feat_z,),
+    )
+    base = run(base_kernel, [like((rows, depth), f32)], (top, wv, both, cots, plane), flops=cube)
     field_grad = run(
-        functools.partial(final_kernel, grid_x * grid_y),
+        final_kernel,
         [like((rows, depth), bf16)],
-        (pulled, feat_z, base),
+        (place,) + swaps(mine, "gx", span_x) + (base,),
+        scalars=1,
+        scratch=[parts],
     )
     return (layer_output.reshape(field.shape), field_grad.reshape(field.shape))
 
@@ -527,8 +597,8 @@
     def program(*arrays):
         _, grid_x, grid_y, depth = arrays[0].shape
         places = grid_x // mesh.shape["groups"] * grid_y
-        small = places == LANES and places == 8 * count and depth % LANES == 0
-        small = small and count % (depth // LANES) == 0
+        small = places == LANES and places == 8 * count
+        small = small and depth == LANES * mesh.shape["gx"] and count & (count - 1) == 0
         return jax.shard_map(
             per_device_kernels if small else per_device,
             mesh=mesh,

time: 72.5 us -> 58.4 us (0.81)
  blocking collectives: 25.9 us -> 0 us
  starting transfers between devices: 11 us -> 21.8 us
  local copies, waits for them, and re-layouts: 9.5 us -> 3.2 us
  waiting for transfers between devices: 15.4 us -> 21.2 us
  Pallas kernels: 9.18 us -> 11.1 us
    all_to_all x2 -> x0, blocking collectives: 25.9 us -> none  [exchange(): return lax.all_to_all(parts, AXES, split_axis=0, concat_axis=0, tiled=True)]
    ppermute x0 -> x18, starting transfers between devices: none -> 17.8 us  [swap(): return lax.ppermute(part, axis, [(i, i ^ step) for i in range(size)])]
    ppermute x0 -> x18, waiting for transfers between devices: none -> 12.9 us  [swap(): return lax.ppermute(part, axis, [(i, i ^ step) for i in range(size)])]
    all_to_all x3 -> x1, starting transfers between devices: 11 us -> 3.91 us  [exchange(): return lax.all_to_all(parts, AXES, split_axis=0, concat_axis=0, tiled=True)]
    all_to_all x3 -> x1, waiting for transfers between devices: 15.4 us -> 8.29 us  [exchange(): return lax.all_to_all(parts, AXES, split_axis=0, concat_axis=0, tiled=True)]
    unnamed x28 -> x10, local copies, waits for them, and re-layouts: 6.37 us -> 0.02 us
    pallas_call x11 -> x12, Pallas kernels: 9.18 us -> 11.1 us  [run(): pl.pallas_call(kernel, out_shape=tuple(outs), in_specs=[smem] * scalars +...]
  transfers between devices with their start and end apart: 3 -> 19, of which waited for: 3 -> 10; matrix products, arithmetic and copies ran while one was open for 1% -> 2% of each run, Pallas kernels for 6% -> 9%
where the time goes in v4:
time: 58.4 us; the launch traced here: 58.1 us
  starting transfers between devices  21.8 us (37%)
  waiting for transfers between devices  21.2 us (36%)
  Pallas kernels  11.1 us (19%)
  local copies, waits for them, and re-layouts  3.2 us (5%)
  between operations  0.79 us (1%)
    ppermute x18, starting transfers between devices, swap(): return lax.ppermute(part, axis, [(i, i ^ step) for i in range(size)])  17.8 us
    ppermute x18, waiting for transfers between devices, swap(): return lax.ppermute(part, axis, [(i, i ^ step) for i in range(size)])  12.9 us
    pallas_call x12, Pallas kernels, run(): pl.pallas_call(kernel, out_shape=tuple(outs), in_specs=[smem] * scalars +...  11.1 us
    all_to_all x1, waiting for transfers between devices, exchange(): return lax.all_to_all(parts, AXES, split_axis=0, concat_axis=0, tiled=True)  8.29 us
    all_to_all x1, starting transfers between devices, exchange(): return lax.all_to_all(parts, AXES, split_axis=0, concat_axis=0, tiled=True)  3.91 us
    reshape x2, local copies, waits for them, and re-layouts, per_device_kernels(): return (layer_output.reshape(field.shape), field_grad.reshape(field.shape))  1.84 us
    reshape x1, local copies, waits for them, and re-layouts, per_device_kernels(): cols = field.reshape(rows, depth)  1.22 us
  transfers between devices with their start and end apart: 19, of which 10 were waited for; matrix products, arithmetic and copies ran while one was open for 2% of the time, Pallas kernels for 9%

profile of v4, /device:TPU:0, one launch (start us, length us, event | category | flops | bytes accessed | tf_op | source)
XLA Modules:
  0.0 58.1 jit_solution(4508352366514527009)
XLA Ops:
  0.6 1.2 %reshape.16.field_ref.refs_4_ = bf16[512,512]{1,0:T(8,128)(2,1)S(1)} reshape(bf16[64,2,4,512]{3,2,1,0:T(4,128)(2,1)} %param.6) | data formatting | bytes 1048576 | tf_op jit(solution)/shard_map/reshape | solution.py:506
  2.0 0.9 %shard_map.77 = (f32[72,128]{1,0:T(8,128)S(1)}, f32[72,128]{1,0:T(8,128)S(1)}, f32[72,128]{1,0:T(8,128)S(1)}, f32[72,128]{1,0:T(8,128)S(1)}) custom-call(s32[2]{0:T(128)S(1)} %pad_add_fusion.place_ref, bf16[512,512]{1,0:T(8,128)(2,1)S(1)} %reshape.16.field_ref.refs_4_), custom_call_target="tpu_custom_call" | custom-call | flops 67108864 | bytes 671752 | tf_op jit(solution)/shard_map/pallas_call | solution.py:471
  2.9 0.5 collective-permute-start
  3.4 2.6 %collective-permute-start.1 = (f32[72,128]{1,0:T(8,128)S(1)}, f32[72,128]{1,0:T(8,128)S(1)}, u32[]{:S(2)}, u32[]{:S(2)}) collective-permute-start(f32[72,128]{1,0:T(8,128)S(1)} %get-tuple-element.24), channel_id=1, source_target_pairs={{0,8},{4,12},{8,0},{12,4},{1,9},{5,13},{9,1},{13,5},{2,10},{6,14},... | collective-permute-start | bytes 110600 | tf_op jit(solution)/shard_map/ppermute | solution.py:27
  6.1 2.0 %collective-permute-done.1.refs_2_ = f32[72,128]{1,0:T(8,128)S(1)} collective-permute-done((f32[72,128]{1,0:T(8,128)S(1)}, f32[72,128]{1,0:T(8,128)S(1)}, u32[]{:S(2)}, u32[]{:S(2)}) %collective-permute-start.1) | collective-permute-done | bytes 36896 | tf_op jit(solution)/shard_map/ppermute | solution.py:27
  8.1 1.4 %collective-permute-done.2.refs_3_ = f32[72,128]{1,0:T(8,128)S(1)} collective-permute-done((f32[72,128]{1,0:T(8,128)S(1)}, f32[72,128]{1,0:T(8,128)S(1)}, u32[]{:S(2)}, u32[]{:S(2)}) %collective-permute-start.2) | collective-permute-done | bytes 36896 | tf_op jit(solution)/shard_map/ppermute | solution.py:27
  9.4 3.7 %collective-permute-start.5 = (f32[96,128]{1,0:T(8,128)S(1)}, f32[96,128]{1,0:T(8,128)S(1)}, u32[]{:S(2)}, u32[]{:S(2)}) collective-permute-start(f32[96,128]{1,0:T(8,128)S(1)} %shard_map.78.refs_0_), channel_id=1, source_target_pairs={{0,3},{1,2},{2,1},{3,0},{4,7},{5,6},{6,5},{7,4},{8,11},{9,10},{10,... | collective-permute-start | bytes 147464 | tf_op jit(solution)/shard_map/ppermute | solution.py:27
  13.1 0.8 %collective-permute-start.3 = (f32[96,128]{1,0:T(8,128)S(1)}, f32[96,128]{1,0:T(8,128)S(1)}, u32[]{:S(2)}, u32[]{:S(2)}) collective-permute-start(f32[96,128]{1,0:T(8,128)S(1)} %shard_map.78.refs_0_), channel_id=1, source_target_pairs={{0,1},{1,0},{2,3},{3,2},{4,5},{5,4},{6,7},{7,6},{8,9},{9,8},{10,11... | collective-permute-start | bytes 147464 | tf_op jit(solution)/shard_map/ppermute | solution.py:27
  14.2 1.3 %collective-permute-done.5.refs_3_ = f32[96,128]{1,0:T(8,128)S(1)} collective-permute-done((f32[96,128]{1,0:T(8,128)S(1)}, f32[96,128]{1,0:T(8,128)S(1)}, u32[]{:S(2)}, u32[]{:S(2)}) %collective-permute-start.5) | collective-permute-done | bytes 49184 | tf_op jit(solution)/shard_map/ppermute | solution.py:27
  15.4 2.6 %collective-permute-done.4.refs_2_ = f32[96,128]{1,0:T(8,128)S(1)} collective-permute-done((f32[96,128]{1,0:T(8,128)S(1)}, f32[96,128]{1,0:T(8,128)S(1)}, u32[]{:S(2)}, u32[]{:S(2)}) %collective-permute-start.4) | collective-permute-done | bytes 49184 | tf_op jit(solution)/shard_map/ppermute | solution.py:27
  18.4 0.9 %collective-permute-start.7 = (bf16[128,128]{1,0:T(8,128)(2,1)S(1)}, bf16[128,128]{1,0:T(8,128)(2,1)S(1)}, u32[]{:S(2)}, u32[]{:S(2)}) collective-permute-start(bf16[128,128]{1,0:T(8,128)(2,1)S(1)} %get-tuple-element.27.refs_0_), channel_id=1, source_target_pairs={{0,8},{4,12},{8,0},{12,4},{1,9},{5,13},{9,1},{13,5},{2,10},{6,14},... | collective-permute-start | bytes 98312 | tf_op jit(solution)/shard_map/ppermute | solution.py:27
  19.3 0.9 %collective-permute-start.6 = (bf16[128,128]{1,0:T(8,128)(2,1)S(1)}, bf16[128,128]{1,0:T(8,128)(2,1)S(1)}, u32[]{:S(2)}, u32[]{:S(2)}) collective-permute-start(bf16[128,128]{1,0:T(8,128)(2,1)S(1)} %get-tuple-element.27.refs_0_), channel_id=1, source_target_pairs={{0,4},{4,0},{8,12},{12,8},{1,5},{5,1},{9,13},{13,9},{2,6},{6,2},{1... | collective-permute-start | bytes 98312 | tf_op jit(solution)/shard_map/ppermute | solution.py:27
  20.3 1.3 %collective-permute-done.8.refs_3_ = bf16[128,128]{1,0:T(8,128)(2,1)S(1)} collective-permute-done((bf16[128,128]{1,0:T(8,128)(2,1)S(1)}, bf16[128,128]{1,0:T(8,128)(2,1)S(1)}, u32[]{:S(2)}, u32[]{:S(2)}) %collective-permute-start.8) | collective-permute-done | bytes 32800 | tf_op jit(solution)/shard_map/ppermute | solution.py:27
  21.7 1.0 %collective-permute-done.7.refs_2_ = bf16[128,128]{1,0:T(8,128)(2,1)S(1)} collective-permute-done((bf16[128,128]{1,0:T(8,128)(2,1)S(1)}, bf16[128,128]{1,0:T(8,128)(2,1)S(1)}, u32[]{:S(2)}, u32[]{:S(2)}) %collective-permute-start.7) | collective-permute-done | bytes 32800 | tf_op jit(solution)/shard_map/ppermute | solution.py:27
  22.7 2.0 %shard_map.81 = (bf16[16,16,512]{2,1,0:T(8,128)(2,1)}, bf16[128,512]{1,0:T(8,128)(2,1)S(1)}) custom-call(s32[2]{0:T(128)S(1)} %pad_add_fusion.place_ref, bf16[128,128]{1,0:T(8,128)(2,1)S(1)} %get-tuple-element.27.refs_0_, bf16[128,128]{1,0:T(8,128)(2,1)S(1)} %collective-permute-done.6.refs_1_, bf16[128,128]{1,0:T(8,128)(2,1)S(1)} %collective-permute-done.7.refs_2_, ...), custom_call_target="tpu_custom_call" | custom-call | flops 536870912 | bytes 1835016 | tf_op jit(solution)/shard_map/pallas_call | solution.py:471
  24.7 3.9 %all-to-all-start = ((bf16[16,16,512]{2,1,0:T(8,128)(2,1)}), bf16[16,16,512]{2,1,0:T(8,128)(2,1)S(1)}, u32[]{:S(2)}, u32[]{:S(2)}) async-start(bf16[16,16,512]{2,1,0:T(8,128)(2,1)} %get-tuple-element.30), calls=%async_computation | async-start | bytes 524288 | tf_op jit(solution)/shard_map/all_to_all | solution.py:23
  28.6 1.8 %shard_map.82 = (f32[2,64,128]{2,1,0:T(8,128)S(1)}, f32[8,128,64]{2,1,0:T(8,128)S(1)}) custom-call(s32[2]{0:T(128)S(1)} %pad_add_fusion.place_ref, f32[96,128]{1,0:T(8,128)S(1)} %shard_map.78.refs_0_, f32[96,128]{1,0:T(8,128)S(1)} %collective-permute-done.3.refs_1_, f32[96,128]{1,0:T(8,128)S(1)} %collective-permute-done.4.refs_2_, ...), custom_call_target="tpu_custom_call" | custom-call | flops 134217728 | bytes 688136 | tf_op jit(solution)/shard_map/pallas_call | solution.py:471
  30.4 8.3 %all-to-all-done.recv_ref = bf16[16,16,512]{2,1,0:T(8,128)(2,1)S(1)} async-done(((bf16[16,16,512]{2,1,0:T(8,128)(2,1)}), bf16[16,16,512]{2,1,0:T(8,128)(2,1)S(1)}, u32[]{:S(2)}, u32[]{:S(2)}) %all-to-all-start) | async-done | bytes 262176 | tf_op jit(solution)/shard_map/all_to_all | solution.py:23
  38.7 1.8 %shard_map.83 = (f32[2,8,512]{2,1,0:T(8,128)S(1)}, f32[64,128]{1,0:T(8,128)S(1)}, f32[64,128]{1,0:T(8,128)S(1)}, f32[64,128]{1,0:T(8,128)S(1)}, f32[64,128]{1,0:T(8,128)S(1)}) custom-call(s32[2]{0:T(128)S(1)} %pad_add_fusion.place_ref, bf16[16,16,512]{2,1,0:T(8,128)(2,1)S(1)} %all-to-all-done.recv_ref, f32[2,64,128]{2,1,0:T(8,128)S(1)} %get-tuple-element.31.mix_ref, ...), custom_call_target="tpu_custom_call" | custom-call | flops 268435456 | bytes 2064392 | tf_op jit(solution)/shard_map/pallas_call | solution.py:471
  40.5 0.8 %collective-permute-start.10 = (f32[64,128]{1,0:T(8,128)S(1)}, f32[64,128]{1,0:T(8,128)S(1)}, u32[]{:S(2)}, u32[]{:S(2)}) collective-permute-start(f32[64,128]{1,0:T(8,128)S(1)} %get-tuple-element.38), channel_id=1, source_target_pairs={{0,8},{4,12},{8,0},{12,4},{1,9},{5,13},{9,1},{13,5},{2,10},{6,14},... | collective-permute-start | bytes 98312 | tf_op jit(solution)/shard_map/ppermute | solution.py:27
  41.4 1.0 %collective-permute-start.11 = (f32[64,128]{1,0:T(8,128)S(1)}, f32[64,128]{1,0:T(8,128)S(1)}, u32[]{:S(2)}, u32[]{:S(2)}) collective-permute-start(f32[64,128]{1,0:T(8,128)S(1)} %get-tuple-element.39), channel_id=1, source_target_pairs={{0,12},{4,8},{8,4},{12,0},{1,13},{5,9},{9,5},{13,1},{2,14},{6,10},... | collective-permute-start | bytes 98312 | tf_op jit(solution)/shard_map/ppermute | solution.py:27
  42.4 2.3 %collective-permute-done.10 = f32[64,128]{1,0:T(8,128)S(1)} collective-permute-done((f32[64,128]{1,0:T(8,128)S(1)}, f32[64,128]{1,0:T(8,128)S(1)}, u32[]{:S(2)}, u32[]{:S(2)}) %collective-permute-start.10) | collective-permute-done | bytes 32800 | tf_op jit(solution)/shard_map/ppermute | solution.py:27
  45.1 1.5 %collective-permute-start.14 = (f32[64,128]{1,0:T(8,128)S(1)}, f32[64,128]{1,0:T(8,128)S(1)}, u32[]{:S(2)}, u32[]{:S(2)}) collective-permute-start(f32[64,128]{1,0:T(8,128)S(1)} %add_add_fusion.refs_0_), channel_id=1, source_target_pairs={{0,3},{1,2},{2,1},{3,0},{4,7},{5,6},{6,5},{7,4},{8,11},{9,10},{10,... | collective-permute-start | bytes 98312 | tf_op jit(solution)/shard_map/ppermute | solution.py:27
  46.9 2.6 %collective-permute-start.12 = (f32[64,128]{1,0:T(8,128)S(1)}, f32[64,128]{1,0:T(8,128)S(1)}, u32[]{:S(2)}, u32[]{:S(2)}) collective-permute-start(f32[64,128]{1,0:T(8,128)S(1)} %add_add_fusion.refs_0_), channel_id=1, source_target_pairs={{0,1},{1,0},{2,3},{3,2},{4,5},{5,4},{6,7},{7,6},{8,9},{9,8},{10,11... | collective-permute-start | bytes 98312 | tf_op jit(solution)/shard_map/ppermute | solution.py:27
  49.5 2.4 %shard_map.86.plane_ref = f32[8,64]{1,0:T(8,128)S(1)} custom-call(s32[2]{0:T(128)S(1)} %pad_add_fusion.place_ref, bf16[16,16,512]{2,1,0:T(8,128)(2,1)S(1)} %all-to-all-done.recv_ref, f32[8,128,64]{2,1,0:T(8,128)S(1)} %get-tuple-element.41.feat_ref, bf16[2,128,128]{2,1,0:T(8,128)(2,1)S(1)} %copy-done.3, f32[3,2,64,64]{3,2,1,0:T(8,128)S(1)} %copy-done), custom_call_target="tpu_custom_call" | custom-call | flops 536870912 | bytes 690184 | tf_op jit(solution)/shard_map/pallas_call | solution.py:471
  52.4 1.0 %collective-permute-start.16 = (f32[64,128]{1,0:T(8,128)S(1)}, f32[64,128]{1,0:T(8,128)S(1)}, u32[]{:S(2)}, u32[]{:S(2)}) collective-permute-start(f32[64,128]{1,0:T(8,128)S(1)} %shard_map.85.refs_0_), channel_id=1, source_target_pairs={{0,8},{4,12},{8,0},{12,4},{1,9},{5,13},{9,1},{13,5},{2,10},{6,14},... | collective-permute-start | bytes 98312 | tf_op jit(solution)/shard_map/ppermute | solution.py:27
  53.5 0.5 collective-permute-start.15
  54.4 0.9 %reshape.18 = bf16[64,2,4,512]{3,2,1,0:T(4,128)(2,1)} reshape(bf16[512,512]{1,0:T(8,128)(2,1)S(1)} %shard_map.84) | data formatting | bytes 1048576 | tf_op jit(solution)/shard_map/reshape | solution.py:590
  55.3 0.5 shard_map.87.refs_4_
  55.9 0.6 collective-permute-done.16.refs_2_
  56.4 0.7 %shard_map.88 = bf16[512,512]{1,0:T(8,128)(2,1)S(1)} custom-call(s32[2]{0:T(128)S(1)} %pad_add_fusion.place_ref, f32[64,128]{1,0:T(8,128)S(1)} %shard_map.85.refs_0_, f32[64,128]{1,0:T(8,128)S(1)} %collective-permute-done.15.refs_1_, f32[64,128]{1,0:T(8,128)S(1)} %collective-permute-done.16.refs_2_, f32[64,128]{1,0:T(8,128)S(1)} %collective-permute-done.17.refs_3_, ...), custom_call_target="tpu_custom_call" | custom-call | bytes 1703944 | tf_op jit(solution)/shard_map/pallas_call | solution.py:471
  57.2 0.9 %reshape.19 = bf16[64,2,4,512]{3,2,1,0:T(4,128)(2,1)} reshape(bf16[512,512]{1,0:T(8,128)(2,1)S(1)} %shard_map.88) | data formatting | bytes 1048576 | tf_op jit(solution)/shard_map/reshape | solution.py:590
  (34 shorter events, 2.7 us)
Async XLA Ops:
  0.6 19.6 %copy-start.4 = (bf16[64,2,4,512]{3,2,1,0:T(4,128)(2,1)S(1)}, bf16[64,2,4,512]{3,2,1,0:T(4,128)(2,1)}, u32[]{:S(2)}) copy-start(bf16[64,2,4,512]{3,2,1,0:T(4,128)(2,1)} %param.7) | copy-start | bytes 1572868
  2.0 11.9 %copy-start.1 = (bf16[64,64]{1,0:T(8,128)(2,1)S(1)}, bf16[64,64]{1,0:T(8,128)(2,1)}, u32[]{:S(2)}) copy-start(bf16[64,64]{1,0:T(8,128)(2,1)} %wv_ref.1) | copy-start | bytes 24580
  2.0 11.9 %copy-start.2 = (bf16[64,64]{1,0:T(8,128)(2,1)S(1)}, bf16[64,64]{1,0:T(8,128)(2,1)}, u32[]{:S(2)}) copy-start(bf16[64,64]{1,0:T(8,128)(2,1)} %wo_ref.1) | copy-start | bytes 24580
  2.9 11.0 %copy-start = (f32[3,2,64,64]{3,2,1,0:T(8,128)S(1)}, f32[3,2,64,64]{3,2,1,0:T(8,128)}, u32[]{:S(2)}) copy-start(f32[3,2,64,64]{3,2,1,0:T(8,128)} %qk_ref.3) | copy-start | bytes 294916
  2.9 3.2 %collective-permute-start = (f32[72,128]{1,0:T(8,128)S(1)}, f32[72,128]{1,0:T(8,128)S(1)}, u32[]{:S(2)}, u32[]{:S(2)}) collective-permute-start(f32[72,128]{1,0:T(8,128)S(1)} %get-tuple-element.23), channel_id=1, source_target_pairs={{0,4},{4,0},{8,12},{12,8},{1,5},{5,1},{9,13},{13,9},{2,6},{6,2},{1... | collective-permute-start | bytes 110600 | tf_op jit(solution)/shard_map/ppermute | solution.py:27
  3.4 4.6 %collective-permute-start.1 = (f32[72,128]{1,0:T(8,128)S(1)}, f32[72,128]{1,0:T(8,128)S(1)}, u32[]{:S(2)}, u32[]{:S(2)}) collective-permute-start(f32[72,128]{1,0:T(8,128)S(1)} %get-tuple-element.24), channel_id=1, source_target_pairs={{0,8},{4,12},{8,0},{12,4},{1,9},{5,13},{9,1},{13,5},{2,10},{6,14},... | collective-permute-start | bytes 110600 | tf_op jit(solution)/shard_map/ppermute | solution.py:27
  6.0 3.4 %collective-permute-start.2 = (f32[72,128]{1,0:T(8,128)S(1)}, f32[72,128]{1,0:T(8,128)S(1)}, u32[]{:S(2)}, u32[]{:S(2)}) collective-permute-start(f32[72,128]{1,0:T(8,128)S(1)} %get-tuple-element.25), channel_id=1, source_target_pairs={{0,12},{4,8},{8,4},{12,0},{1,13},{5,9},{9,5},{13,1},{2,14},{6,10},... | collective-permute-start | bytes 110600 | tf_op jit(solution)/shard_map/ppermute | solution.py:27
  9.4 6.0 %collective-permute-start.5 = (f32[96,128]{1,0:T(8,128)S(1)}, f32[96,128]{1,0:T(8,128)S(1)}, u32[]{:S(2)}, u32[]{:S(2)}) collective-permute-start(f32[96,128]{1,0:T(8,128)S(1)} %shard_map.78.refs_0_), channel_id=1, source_target_pairs={{0,3},{1,2},{2,1},{3,0},{4,7},{5,6},{6,5},{7,4},{8,11},{9,10},{10,... | collective-permute-start | bytes 147464 | tf_op jit(solution)/shard_map/ppermute | solution.py:27
  13.1 5.0 %collective-permute-start.4 = (f32[96,128]{1,0:T(8,128)S(1)}, f32[96,128]{1,0:T(8,128)S(1)}, u32[]{:S(2)}, u32[]{:S(2)}) collective-permute-start(f32[96,128]{1,0:T(8,128)S(1)} %shard_map.78.refs_0_), channel_id=1, source_target_pairs={{0,2},{1,3},{2,0},{3,1},{4,6},{5,7},{6,4},{7,5},{8,10},{9,11},{10,... | collective-permute-start | bytes 147464 | tf_op jit(solution)/shard_map/ppermute | solution.py:27
  13.1 5.0 %collective-permute-start.3 = (f32[96,128]{1,0:T(8,128)S(1)}, f32[96,128]{1,0:T(8,128)S(1)}, u32[]{:S(2)}, u32[]{:S(2)}) collective-permute-start(f32[96,128]{1,0:T(8,128)S(1)} %shard_map.78.refs_0_), channel_id=1, source_target_pairs={{0,1},{1,0},{2,3},{3,2},{4,5},{5,4},{6,7},{7,6},{8,9},{9,8},{10,11... | collective-permute-start | bytes 147464 | tf_op jit(solution)/shard_map/ppermute | solution.py:27
  18.3 3.4 %collective-permute-start.8 = (bf16[128,128]{1,0:T(8,128)(2,1)S(1)}, bf16[128,128]{1,0:T(8,128)(2,1)S(1)}, u32[]{:S(2)}, u32[]{:S(2)}) collective-permute-start(bf16[128,128]{1,0:T(8,128)(2,1)S(1)} %get-tuple-element.27.refs_0_), channel_id=1, source_target_pairs={{0,12},{4,8},{8,4},{12,0},{1,13},{5,9},{9,5},{13,1},{2,14},{6,10},... | collective-permute-start | bytes 98312 | tf_op jit(solution)/shard_map/ppermute | solution.py:27
  18.4 4.2 %collective-permute-start.7 = (bf16[128,128]{1,0:T(8,128)(2,1)S(1)}, bf16[128,128]{1,0:T(8,128)(2,1)S(1)}, u32[]{:S(2)}, u32[]{:S(2)}) collective-permute-start(bf16[128,128]{1,0:T(8,128)(2,1)S(1)} %get-tuple-element.27.refs_0_), channel_id=1, source_target_pairs={{0,8},{4,12},{8,0},{12,4},{1,9},{5,13},{9,1},{13,5},{2,10},{6,14},... | collective-permute-start | bytes 98312 | tf_op jit(solution)/shard_map/ppermute | solution.py:27
  19.3 3.3 %collective-permute-start.6 = (bf16[128,128]{1,0:T(8,128)(2,1)S(1)}, bf16[128,128]{1,0:T(8,128)(2,1)S(1)}, u32[]{:S(2)}, u32[]{:S(2)}) collective-permute-start(bf16[128,128]{1,0:T(8,128)(2,1)S(1)} %get-tuple-element.27.refs_0_), channel_id=1, source_target_pairs={{0,4},{4,0},{8,12},{12,8},{1,5},{5,1},{9,13},{13,9},{2,6},{6,2},{1... | collective-permute-start | bytes 98312 | tf_op jit(solution)/shard_map/ppermute | solution.py:27
  24.7 3.9 %copy-start.3 = (bf16[2,128,128]{2,1,0:T(8,128)(2,1)S(1)}, bf16[2,128,128]{2,1,0:T(8,128)(2,1)}, u32[]{:S(2)}) copy-start(bf16[2,128,128]{2,1,0:T(8,128)(2,1)} %constant.9.clone.refs_4_.same_ref) | copy-start | bytes 196612
  24.7 14.0 %all-to-all-start = ((bf16[16,16,512]{2,1,0:T(8,128)(2,1)}), bf16[16,16,512]{2,1,0:T(8,128)(2,1)S(1)}, u32[]{:S(2)}, u32[]{:S(2)}) async-start(bf16[16,16,512]{2,1,0:T(8,128)(2,1)} %get-tuple-element.30), calls=%async_computation | async-start | bytes 524288 | tf_op jit(solution)/shard_map/all_to_all | solution.py:23
  40.5 1.9 %collective-permute-start.9 = (f32[64,128]{1,0:T(8,128)S(1)}, f32[64,128]{1,0:T(8,128)S(1)}, u32[]{:S(2)}, u32[]{:S(2)}) collective-permute-start(f32[64,128]{1,0:T(8,128)S(1)} %get-tuple-element.37), channel_id=1, source_target_pairs={{0,4},{4,0},{8,12},{12,8},{1,5},{5,1},{9,13},{13,9},{2,6},{6,2},{1... | collective-permute-start | bytes 98312 | tf_op jit(solution)/shard_map/ppermute | solution.py:27
  40.5 4.1 %collective-permute-start.10 = (f32[64,128]{1,0:T(8,128)S(1)}, f32[64,128]{1,0:T(8,128)S(1)}, u32[]{:S(2)}, u32[]{:S(2)}) collective-permute-start(f32[64,128]{1,0:T(8,128)S(1)} %get-tuple-element.38), channel_id=1, source_target_pairs={{0,8},{4,12},{8,0},{12,4},{1,9},{5,13},{9,1},{13,5},{2,10},{6,14},... | collective-permute-start | bytes 98312 | tf_op jit(solution)/shard_map/ppermute | solution.py:27
  41.4 3.7 %collective-permute-start.11 = (f32[64,128]{1,0:T(8,128)S(1)}, f32[64,128]{1,0:T(8,128)S(1)}, u32[]{:S(2)}, u32[]{:S(2)}) collective-permute-start(f32[64,128]{1,0:T(8,128)S(1)} %get-tuple-element.39), channel_id=1, source_target_pairs={{0,12},{4,8},{8,4},{12,0},{1,13},{5,9},{9,5},{13,1},{2,14},{6,10},... | collective-permute-start | bytes 98312 | tf_op jit(solution)/shard_map/ppermute | solution.py:27
  45.1 6.9 %collective-permute-start.14 = (f32[64,128]{1,0:T(8,128)S(1)}, f32[64,128]{1,0:T(8,128)S(1)}, u32[]{:S(2)}, u32[]{:S(2)}) collective-permute-start(f32[64,128]{1,0:T(8,128)S(1)} %add_add_fusion.refs_0_), channel_id=1, source_target_pairs={{0,3},{1,2},{2,1},{3,0},{4,7},{5,6},{6,5},{7,4},{8,11},{9,10},{10,... | collective-permute-start | bytes 98312 | tf_op jit(solution)/shard_map/ppermute | solution.py:27
  46.6 5.4 %collective-permute-start.13 = (f32[64,128]{1,0:T(8,128)S(1)}, f32[64,128]{1,0:T(8,128)S(1)}, u32[]{:S(2)}, u32[]{:S(2)}) collective-permute-start(f32[64,128]{1,0:T(8,128)S(1)} %add_add_fusion.refs_0_), channel_id=1, source_target_pairs={{0,2},{1,3},{2,0},{3,1},{4,6},{5,7},{6,4},{7,5},{8,10},{9,11},{10,... | collective-permute-start | bytes 98312 | tf_op jit(solution)/shard_map/ppermute | solution.py:27
  46.9 5.1 %collective-permute-start.12 = (f32[64,128]{1,0:T(8,128)S(1)}, f32[64,128]{1,0:T(8,128)S(1)}, u32[]{:S(2)}, u32[]{:S(2)}) collective-permute-start(f32[64,128]{1,0:T(8,128)S(1)} %add_add_fusion.refs_0_), channel_id=1, source_target_pairs={{0,1},{1,0},{2,3},{3,2},{4,5},{5,4},{6,7},{7,6},{8,9},{9,8},{10,11... | collective-permute-start | bytes 98312 | tf_op jit(solution)/shard_map/ppermute | solution.py:27
  52.0 3.8 %collective-permute-start.17 = (f32[64,128]{1,0:T(8,128)S(1)}, f32[64,128]{1,0:T(8,128)S(1)}, u32[]{:S(2)}, u32[]{:S(2)}) collective-permute-start(f32[64,128]{1,0:T(8,128)S(1)} %shard_map.85.refs_0_), channel_id=1, source_target_pairs={{0,12},{4,8},{8,4},{12,0},{1,13},{5,9},{9,5},{13,1},{2,14},{6,10},... | collective-permute-start | bytes 98312 | tf_op jit(solution)/shard_map/ppermute | solution.py:27
  52.4 4.0 %collective-permute-start.16 = (f32[64,128]{1,0:T(8,128)S(1)}, f32[64,128]{1,0:T(8,128)S(1)}, u32[]{:S(2)}, u32[]{:S(2)}) collective-permute-start(f32[64,128]{1,0:T(8,128)S(1)} %shard_map.85.refs_0_), channel_id=1, source_target_pairs={{0,8},{4,12},{8,0},{12,4},{1,9},{5,13},{9,1},{13,5},{2,10},{6,14},... | collective-permute-start | bytes 98312 | tf_op jit(solution)/shard_map/ppermute | solution.py:27
  53.5 3.0 %collective-permute-start.15 = (f32[64,128]{1,0:T(8,128)S(1)}, f32[64,128]{1,0:T(8,128)S(1)}, u32[]{:S(2)}, u32[]{:S(2)}) collective-permute-start(f32[64,128]{1,0:T(8,128)S(1)} %shard_map.85.refs_0_), channel_id=1, source_target_pairs={{0,4},{4,0},{8,12},{12,8},{1,5},{5,1},{9,13},{13,9},{2,6},{6,2},{1... | collective-permute-start | bytes 98312 | tf_op jit(solution)/shard_map/ppermute | solution.py:27

commit v5 on v4

--- a/solution.py
+++ b/solution.py
@@ -193,8 +193,9 @@
 
 
 def mul_left(left, right, dims=NN):
-    high, low = split(left)
-    return mul(high, right, dims) + mul(low, right, dims)
+    rows = left.shape[0]
+    both = mul(jnp.concatenate(split(left), axis=0), right, dims)
+    return both[:rows] + both[rows:]
 
 
 def number(shape, dim):
@@ -243,17 +244,20 @@
 
 def sums_kernel(place_ref, field_ref, *refs):
     outs, part_ref = refs[:-1], refs[-1]
-    data = field_ref[...]
-    rows, depth = data.shape
-    cells = rows // WIDTH
-    pick = (number((WIDTH, rows), 1) // cells == number((WIDTH, rows), 0)).astype(jnp.bfloat16)
-    part = mul(pick, data)
-    row_sums = mul(data, jnp.ones((depth, LANES), jnp.bfloat16)).reshape(WIDTH, cells, LANES)
-    shape = row_sums.shape
-    own = jnp.sum(jnp.where(number(shape, 0) == number(shape, 2), row_sums, 0.0), axis=0)
+    data = field_ref[...].astype(jnp.float32)
+    _, rows_x, rows_y, depth = data.shape
+    part = jnp.sum(jnp.sum(data, axis=1), axis=1)
+    lanes = data[..., :LANES]
+    for start in range(LANES, depth, LANES):
+        lanes = lanes + data[..., start : start + LANES]
+    row_sums = jnp.sum(lanes, axis=3, keepdims=True)
+    shape = lanes.shape
+    own = jnp.sum(jnp.where(number(shape, 0) == number(shape, 3), row_sums, 0.0), axis=0)
     put_quarters(place_ref, part_ref, part, outs)
     for out in outs:
-        out[WIDTH:, :] = own
+        for index in range(rows_x):
+            start = WIDTH + index * rows_y
+            out[start : start + rows_y, :] = own[index]
 
 
 def add_kernel(*refs):
@@ -292,20 +296,23 @@
     out_ref[...] = found * (1.0 / places)
 
 
-def plane_kernel(cells, lengths, place_ref, *refs):
-    parts, (same_ref, qk_ref, mix_ref, feat_ref, total_ref) = refs[:-5], refs[-5:]
-    span_y = len(parts)
-    count = total_ref.shape[0]
-    places = count * cells
-    for block in range(count):
-        step_x, step_y = block // span_y, block % span_y
-        start = WIDTH + step_x * cells
-        index = (place_ref[0] ^ step_x) * span_y + (place_ref[1] ^ step_y)
-        total_ref[index] = parts[step_y][start : start + cells, :]
-    totals = total_ref[...].reshape(places, LANES)[:, :WIDTH]
-    me = place_ref[0] * span_y + place_ref[1]
-    here = pl.ds(pl.multiple_of(me * cells, cells), cells)
-    head = (number((HEADS * cells, WIDTH), 0) // cells) == (number((HEADS * cells, WIDTH), 1) >> 3)
+def by_head(part):
+    shape = (HEADS, part.shape[0], WIDTH)
+    mine = number(shape, 0) == (number(shape, 2) >> 3)
+    return jnp.where(mine, part[None], 0.0).reshape(-1, WIDTH)
+
+
+def plane_kernel(cells, lengths, *refs):
+    parts, (same_ref, qk_ref, mix_ref, feat_ref, full_ref) = refs[:-5], refs[-5:]
+    totals = jnp.concatenate(
+        [
+            part[WIDTH + step * cells : WIDTH + (step + 1) * cells, :]
+            for step in range((parts[0].shape[0] - WIDTH) // cells)
+            for part in parts
+        ],
+        axis=0,
+    )[:, :WIDTH]
+    places = totals.shape[0]
     high, low = split(totals)
     forward = backward = None
     for axis in range(2):
@@ -321,13 +328,14 @@
         feat_ref[4 * axis + 3] = jnp.broadcast_to(inverse, (places, WIDTH))
         factor = 1.0 / math.sqrt(HEAD_DIM * lengths[axis][0])
 
-        def local(index, other):
-            rows = feat_ref[4 * axis + index, here, :]
-            rows = jnp.broadcast_to(rows[None], (HEADS, cells, WIDTH)).reshape(-1, WIDTH)
-            scores = mul_near(jnp.where(head, rows, 0.0), other, NT) * factor
-            return scores.astype(jnp.bfloat16).astype(jnp.float32)
-
-        one, two = local(1, keyset), local(2, query)
+        def scores(rows, other):
+            found = mul_near(by_head(rows), other, NT) * factor
+            return found.astype(jnp.bfloat16).astype(jnp.float32)
+
+        full = scores(query, keyset)
+        full_ref[axis] = full
+        one = full.reshape(HEADS, places, places)[:, :cells].reshape(-1, places)
+        two = scores(keyset[:cells], query)
         forward = one if forward is None else forward * one
         backward = two if backward is None else backward * two
     mix_ref[0] = forward
@@ -350,27 +358,35 @@
     low_c = mul(cot_ref[...], query, NT).reshape(WIDTH, cells, wide)
     low_c = jnp.sum(wo_ref[...][:, None, :] * low_c, axis=0)
     low = jnp.concatenate([low_f, low_c], axis=0).astype(jnp.bfloat16)
-    send_ref[...] = jnp.broadcast_to(low[None], send_ref.shape)
-
-
-def mix_kernel(factor, place_ref, recv_ref, mix_ref, wv_ref, wo_ref, wq_ref, wk_ref, field_ref,
-               cot_ref, top_ref, *refs):
-    outs, part_ref = refs[:-1], refs[-1]
-    rows = field_ref.shape[0]
-    cells = rows // WIDTH
-    places = recv_ref.shape[0] * cells
-    wide = recv_ref.shape[2]
-    both = recv_ref[...].astype(jnp.float32)
+    send_ref[...] = low
+
+
+def join_low(refs, cells):
+    low = jnp.concatenate([ref[...].astype(jnp.float32) for ref in refs], axis=0)
+    wide = low.shape[1]
+    low = low.reshape(-1, 2 * cells, wide)
+    return [
+        low[:, start : start + cells].reshape(-1, wide).astype(jnp.bfloat16)
+        for start in (0, cells)
+    ]
+
+
+def mix_kernel(factor, spans, place_ref, *refs):
+    lows, refs = refs[:spans], refs[spans:]
+    mix_ref, wv_ref, wo_ref, wq_ref, wk_ref, field_ref, cot_ref, top_ref = refs[:8]
+    outs, part_ref = refs[8:-1], refs[-1]
+    cells = field_ref.shape[0] // WIDTH
+    low_f, low_c = join_low(lows, cells)
+    wide = low_f.shape[1]
     shape = (HEADS, cells, wide)
     head = number(shape, 0) == (number(shape, 2) >> 6)
 
     def top(mix, low):
-        low = low.reshape(places, wide).astype(jnp.bfloat16)
         found = mul_left(mix, low).reshape(shape)
         return jnp.sum(jnp.where(head, found, 0.0), axis=0) * factor
 
-    top_f = top(mix_ref[0], both[:, :cells])
-    top_c = top(mix_ref[1], both[:, cells:])
+    top_f = top(mix_ref[0], low_f)
+    top_c = top(mix_ref[1], low_c)
     top_ref[0] = top_f
     top_ref[1] = top_c
     left_f = spread(wo_ref[...], top_f)
@@ -384,22 +400,25 @@
     put_quarters(place_ref, part_ref, found, outs)
 
 
+def put_cells(ref, total):
+    _, rows_x, rows_y, depth = ref.shape
+    total = total.reshape(WIDTH, rows_x * rows_y, depth)
+    for index in range(rows_x):
+        rows = total[:, index * rows_y : (index + 1) * rows_y, :]
+        ref[:, index, :, :] = rows.astype(jnp.bfloat16)
+
+
 def output_kernel(top_ref, wo_ref, both_ref, field_ref, out_ref):
     query = expand(both_ref[...].astype(jnp.float32)[:WIDTH])
     left = spread(wo_ref[...], top_ref[0])
-    out_ref[...] = (mul(left, query) + field_ref[...].astype(jnp.float32)).astype(jnp.bfloat16)
-
-
-def gram_kernel(cells, span_y, lengths, factor_z, place_ref, recv_ref, feat_ref, same_ref, qk_ref, out_ref,
-                found_ref):
-    places = recv_ref.shape[0] * cells
-    wide = recv_ref.shape[2]
+    put_cells(out_ref, mul(left, query) + field_ref[...].astype(jnp.float32))
+
+
+def gram_kernel(cells, lengths, factor_z, *refs):
+    lows, (feat_ref, full_ref, same_ref, qk_ref, out_ref) = refs[:-5], refs[-5:]
+    low_f, low_c = join_low(lows, cells)
+    places, wide = low_f.shape
     squares = HEAD_DIM * HEAD_DIM
-    both = recv_ref[...].astype(jnp.float32)
-    low_f = both[:, :cells].reshape(places, wide).astype(jnp.bfloat16)
-    low_c = both[:, cells:].reshape(places, wide).astype(jnp.bfloat16)
-    me = place_ref[0] * span_y + place_ref[1]
-    here = pl.ds(pl.multiple_of(me * cells, cells), cells)
     lane = number((places, LANES), 1)
     products = []
     for pair in range(wide // LANES):
@@ -409,34 +428,24 @@
             mine = (lane >> 6) == half
             products.append(mul(jnp.where(mine, part_c, jnp.zeros_like(part_c)), part_f, NT))
     product = jnp.concatenate(products, axis=0)
-    heads = number((HEADS * places, WIDTH), 0) // places == number((HEADS * places, WIDTH), 1) >> 3
-
-    def stack(part):
-        part = jnp.broadcast_to(part[None], (HEADS, places, WIDTH)).reshape(-1, WIDTH)
-        return jnp.where(heads, part, 0.0)
-
     factors = [1.0 / math.sqrt(HEAD_DIM * lengths[axis][0]) for axis in range(2)]
-    queries = [stack(feat_ref[4 * axis + 1]) for axis in range(2)]
-    keysets = [stack(feat_ref[4 * axis + 2]) for axis in range(2)]
-    kernels = []
-    for axis in range(2):
-        scores = mul_near(queries[axis], feat_ref[4 * axis + 2], NT) * factors[axis]
-        kernels.append(scores.astype(jnp.bfloat16).astype(jnp.float32))
+    queries = [by_head(feat_ref[4 * axis + 1]).astype(jnp.bfloat16) for axis in range(2)]
+    keysets = [by_head(feat_ref[4 * axis + 2]).astype(jnp.bfloat16) for axis in range(2)]
     total = jnp.zeros((cells, WIDTH), jnp.float32)
     for axis in range(2):
-        gram = (product * kernels[1 - axis]).astype(jnp.bfloat16)
+        gram = (product * full_ref[1 - axis]).astype(jnp.bfloat16)
         across = jnp.concatenate(
             [gram[h * places : (h + 1) * places] for h in range(HEADS)], axis=1
         )
         scale = factors[axis] * factor_z
-        grad_query = mul(across, keysets[axis].astype(jnp.bfloat16)) * scale
-        grad_keyset = mul(gram, queries[axis].astype(jnp.bfloat16), TN) * scale
+        grad_query = mul(across, keysets[axis]) * scale
+        grad_keyset = mul(gram, queries[axis], TN) * scale
         found = mul_near(grad_query, qk_ref[axis, 0], NT) + mul_near(grad_keyset, qk_ref[axis, 1], NT)
         high, low = split(found)
-        found_ref[...] = mul(same_ref[axis], high) + mul(same_ref[axis], low)
-        found = found_ref[here, :]
-        normed = feat_ref[4 * axis, here, :]
-        inverse = feat_ref[4 * axis + 3, here, :]
+        own = same_ref[axis, 0 : 2 * cells, :]
+        found = (mul(own, high) + mul(own, low))[:cells]
+        normed = feat_ref[4 * axis, 0:cells, :]
+        inverse = feat_ref[4 * axis + 3, 0:cells, :]
         found = found - normed * jnp.mean(found * normed, axis=1, keepdims=True)
         total = total + inverse * found * (1.0 / lengths[axis][1])
     out_ref[...] = total
@@ -461,7 +470,7 @@
     cells = rows // WIDTH
     found = join_quarters(place_ref, part_ref, quarters)
     total = base_ref[...].reshape(WIDTH, cells, depth) + found[:, None, :]
-    out_ref[...] = total.reshape(rows, depth).astype(jnp.bfloat16)
+    put_cells(out_ref, total)
 
 
 def run(kernel, outs, operands, scalars=0, flops=0, scratch=()):
@@ -518,7 +527,7 @@
         )
 
     sums = run(
-        sums_kernel, [like((WIDTH + cells, LANES), f32)] * span_x, (place, cols),
+        sums_kernel, [like((WIDTH + cells, LANES), f32)] * span_x, (place, field),
         scalars=1, flops=cube // 4, scratch=[parts],
     )
     wv, wo, wq, wk, wz = run(
@@ -537,42 +546,40 @@
         [like((2 * WIDTH, LANES), bf16), like((WIDTH + HEAD_DIM, LANES), f32)],
         totals + (wz,),
     )
-    mix, feat = run(
+    mix, feat, full = run(
         functools.partial(plane_kernel, cells, lengths),
-        [like((2, HEADS * cells, places), f32), like((8, places, WIDTH), f32)],
-        (place,) + totals + (same, qk_weight),
-        scalars=1,
+        [like((2, HEADS * cells, places), f32), like((8, places, WIDTH), f32),
+         like((2, HEADS * places, places), f32)],
+        totals + (same, qk_weight),
         flops=cube // 2,
-        scratch=[pltpu.VMEM((count, cells, LANES), f32)],
     )
     send, both = run(
         coef_kernel,
-        [like((count, 2 * cells, wide), bf16), like((2 * WIDTH, depth), bf16)],
+        [like((2 * cells, wide), bf16), like((2 * WIDTH, depth), bf16)],
         (place,) + swaps(mine, "gx", span_x) + (cols, cots, wv, wo),
         scalars=1,
         flops=2 * cube,
         scratch=[pltpu.VMEM((span_x, 2 * WIDTH, LANES), f32)],
     )
-    low = exchange(send)
+    low = jnp.concatenate(swaps(send, "gy", span_y), axis=0)
+    lows = swaps(low, "gx", span_x)
     top, *pulls = run(
-        functools.partial(mix_kernel, factor_z),
+        functools.partial(mix_kernel, factor_z, span_x),
         [like((2, cells, wide), f32)] + [block] * span_x,
-        (place, low, mix, wv, wo, wq, wk, cols, cots),
+        (place,) + lows + (mix, wv, wo, wq, wk, cols, cots),
         scalars=1,
         flops=cube,
         scratch=[parts],
     )
     total = sum(swaps(pulls, "gx", span_x))
     layer_output = run(
-        output_kernel, [like((rows, depth), bf16)], (top, wo, both, cols), flops=cube
+        output_kernel, [like(field.shape, bf16)], (top, wo, both, cols), flops=cube
     )
     plane = run(
-        functools.partial(gram_kernel, cells, span_y, lengths, factor_z),
+        functools.partial(gram_kernel, cells, lengths, factor_z),
         [like((cells, WIDTH), f32)],
-        (place, low, feat, same, qk_weight),
-        scalars=1,
+        lows + (feat, full, same, qk_weight),
         flops=2 * cube,
-        scratch=[pltpu.VMEM((places, WIDTH), f32)],
     )
     mine = run(
         functools.partial(pull_kernel, grid_x * grid_y),
@@ -582,12 +589,12 @@
     base = run(base_kernel, [like((rows, depth), f32)], (top, wv, both, cots, plane), flops=cube)
     field_grad = run(
         final_kernel,
-        [like((rows, depth), bf16)],
+        [like(field.shape, bf16)],
         (place,) + swaps(mine, "gx", span_x) + (base,),
         scalars=1,
         scratch=[parts],
     )
-    return (layer_output.reshape(field.shape), field_grad.reshape(field.shape))
+    return (layer_output, field_grad)
 
 
 def solution(mesh):

time: 58.4 us -> 60.3 us (1.033)
  starting transfers between devices: 21.8 us -> 24.1 us
    ppermute x18 -> x24, waiting for transfers between devices: 12.9 us -> 21.4 us  [swap(): return lax.ppermute(part, axis, [(i, i ^ step) for i in range(size)])]
    all_to_all x1 -> x0, waiting for transfers between devices: 8.29 us -> none  [exchange(): return lax.all_to_all(parts, AXES, split_axis=0, concat_axis=0, tiled=True)]
    ppermute x18 -> x24, starting transfers between devices: 17.8 us -> 24.1 us  [swap(): return lax.ppermute(part, axis, [(i, i ^ step) for i in range(size)])]
    all_to_all x1 -> x0, starting transfers between devices: 3.91 us -> none  [exchange(): return lax.all_to_all(parts, AXES, split_axis=0, concat_axis=0, tiled=True)]
    unnamed x10 -> x17, local copies, waits for them, and re-layouts: 0.02 us -> 2.51 us
    reshape x2 -> x0, local copies, waits for them, and re-layouts: 1.84 us -> none  [per_device_kernels(): return (layer_output.reshape(field.shape), field_grad.reshape(field.shape))]
    reshape x1, local copies, waits for them, and re-layouts: 1.22 us -> 0.12 us  [per_device_kernels(): cols = field.reshape(rows, depth)]
  transfers between devices with their start and end apart: 19 -> 24, of which waited for: 10 -> 15; matrix products, arithmetic and copies ran while one was open for 2% -> 0% of each run, Pallas kernels for 9% -> 8%
where the time goes in v5:
time: 60.3 us; the launch traced here: 60 us
  starting transfers between devices  24.1 us (40%)
  waiting for transfers between devices  21.4 us (35%)
  Pallas kernels  10.7 us (18%)
  local copies, waits for them, and re-layouts  2.76 us (5%)
  between operations  0.84 us (1%)
    ppermute x24, starting transfers between devices, swap(): return lax.ppermute(part, axis, [(i, i ^ step) for i in range(size)])  24.1 us
    ppermute x24, waiting for transfers between devices, swap(): return lax.ppermute(part, axis, [(i, i ^ step) for i in range(size)])  21.4 us
    pallas_call x12, Pallas kernels, run(): pl.pallas_call(kernel, out_shape=tuple(outs), in_specs=[smem] * scalars +...  10.7 us
    unnamed x17, local copies, waits for them, and re-layouts  2.51 us
  transfers between devices with their start and end apart: 24, of which 15 were waited for; matrix products, arithmetic and copies ran while one was open for 0% of the time, Pallas kernels for 8%

profile of v5, /device:TPU:0, one launch (start us, length us, event | category | flops | bytes accessed | tf_op | source)
XLA Modules:
  0.0 60.0 jit_solution(5774432133356674165)
XLA Ops:
  0.7 1.0 %copy-done = bf16[64,2,4,512]{3,2,1,0:T(4,128)(2,1)S(1)} copy-done((bf16[64,2,4,512]{3,2,1,0:T(4,128)(2,1)S(1)}, bf16[64,2,4,512]{3,2,1,0:T(4,128)(2,1)}, u32[]{:S(2)}) %copy-start) | copy-done | bytes 524312
  1.8 1.2 %shard_map.77 = (f32[72,128]{1,0:T(8,128)S(1)}, f32[72,128]{1,0:T(8,128)S(1)}, f32[72,128]{1,0:T(8,128)S(1)}, f32[72,128]{1,0:T(8,128)S(1)}) custom-call(s32[2]{0:T(128)S(1)} %pad_add_fusion.place_ref, bf16[64,2,4,512]{3,2,1,0:T(4,128)(2,1)S(1)} %copy-done), custom_call_target="tpu_custom_call" | custom-call | flops 67108864 | bytes 671752 | tf_op jit(solution)/shard_map/pallas_call | solution.py:480
  3.5 2.6 %collective-permute-start.1 = (f32[72,128]{1,0:T(8,128)S(1)}, f32[72,128]{1,0:T(8,128)S(1)}, u32[]{:S(2)}, u32[]{:S(2)}) collective-permute-start(f32[72,128]{1,0:T(8,128)S(1)} %get-tuple-element.25), channel_id=1, source_target_pairs={{0,8},{4,12},{8,0},{12,4},{1,9},{5,13},{9,1},{13,5},{2,10},{6,14},... | collective-permute-start | bytes 110600 | tf_op jit(solution)/shard_map/ppermute | solution.py:27
  6.1 2.0 %collective-permute-done.1.refs_2_ = f32[72,128]{1,0:T(8,128)S(1)} collective-permute-done((f32[72,128]{1,0:T(8,128)S(1)}, f32[72,128]{1,0:T(8,128)S(1)}, u32[]{:S(2)}, u32[]{:S(2)}) %collective-permute-start.1) | collective-permute-done | bytes 36896 | tf_op jit(solution)/shard_map/ppermute | solution.py:27
  8.1 1.4 %collective-permute-done.2.refs_3_ = f32[72,128]{1,0:T(8,128)S(1)} collective-permute-done((f32[72,128]{1,0:T(8,128)S(1)}, f32[72,128]{1,0:T(8,128)S(1)}, u32[]{:S(2)}, u32[]{:S(2)}) %collective-permute-start.2) | collective-permute-done | bytes 36896 | tf_op jit(solution)/shard_map/ppermute | solution.py:27
  9.5 1.6 %collective-permute-start.3 = (f32[96,128]{1,0:T(8,128)S(1)}, f32[96,128]{1,0:T(8,128)S(1)}, u32[]{:S(2)}, u32[]{:S(2)}) collective-permute-start(f32[96,128]{1,0:T(8,128)S(1)} %shard_map.78.refs_0_), channel_id=1, source_target_pairs={{0,1},{1,0},{2,3},{3,2},{4,5},{5,4},{6,7},{7,6},{8,9},{9,8},{10,11... | collective-permute-start | bytes 147464 | tf_op jit(solution)/shard_map/ppermute | solution.py:27
  11.1 2.6 %collective-permute-start.4 = (f32[96,128]{1,0:T(8,128)S(1)}, f32[96,128]{1,0:T(8,128)S(1)}, u32[]{:S(2)}, u32[]{:S(2)}) collective-permute-start(f32[96,128]{1,0:T(8,128)S(1)} %shard_map.78.refs_0_), channel_id=1, source_target_pairs={{0,2},{1,3},{2,0},{3,1},{4,6},{5,7},{6,4},{7,5},{8,10},{9,11},{10,... | collective-permute-start | bytes 147464 | tf_op jit(solution)/shard_map/ppermute | solution.py:27
  14.0 0.7 %copy-done.4 = bf16[64,64]{1,0:T(8,128)(2,1)S(1)} copy-done((bf16[64,64]{1,0:T(8,128)(2,1)S(1)}, bf16[64,64]{1,0:T(8,128)(2,1)}, u32[]{:S(2)}) %copy-start.4) | copy-done | bytes 8216
  15.7 1.4 %collective-permute-done.4.refs_2_ = f32[96,128]{1,0:T(8,128)S(1)} collective-permute-done((f32[96,128]{1,0:T(8,128)S(1)}, f32[96,128]{1,0:T(8,128)S(1)}, u32[]{:S(2)}, u32[]{:S(2)}) %collective-permute-start.4) | collective-permute-done | bytes 49184 | tf_op jit(solution)/shard_map/ppermute | solution.py:27
  17.0 2.6 %collective-permute-done.5.refs_3_ = f32[96,128]{1,0:T(8,128)S(1)} collective-permute-done((f32[96,128]{1,0:T(8,128)S(1)}, f32[96,128]{1,0:T(8,128)S(1)}, u32[]{:S(2)}, u32[]{:S(2)}) %collective-permute-start.5) | collective-permute-done | bytes 49184 | tf_op jit(solution)/shard_map/ppermute | solution.py:27
  19.9 0.9 %collective-permute-start.7 = (bf16[128,128]{1,0:T(8,128)(2,1)S(1)}, bf16[128,128]{1,0:T(8,128)(2,1)S(1)}, u32[]{:S(2)}, u32[]{:S(2)}) collective-permute-start(bf16[128,128]{1,0:T(8,128)(2,1)S(1)} %get-tuple-element.28.refs_0_), channel_id=1, source_target_pairs={{0,8},{4,12},{8,0},{12,4},{1,9},{5,13},{9,1},{13,5},{2,10},{6,14},... | collective-permute-start | bytes 98312 | tf_op jit(solution)/shard_map/ppermute | solution.py:27
  20.8 0.9 %collective-permute-start.8 = (bf16[128,128]{1,0:T(8,128)(2,1)S(1)}, bf16[128,128]{1,0:T(8,128)(2,1)S(1)}, u32[]{:S(2)}, u32[]{:S(2)}) collective-permute-start(bf16[128,128]{1,0:T(8,128)(2,1)S(1)} %get-tuple-element.28.refs_0_), channel_id=1, source_target_pairs={{0,12},{4,8},{8,4},{12,0},{1,13},{5,9},{9,5},{13,1},{2,14},{6,10},... | collective-permute-start | bytes 98312 | tf_op jit(solution)/shard_map/ppermute | solution.py:27
  22.0 1.9 %collective-permute-done.7.refs_2_ = bf16[128,128]{1,0:T(8,128)(2,1)S(1)} collective-permute-done((bf16[128,128]{1,0:T(8,128)(2,1)S(1)}, bf16[128,128]{1,0:T(8,128)(2,1)S(1)}, u32[]{:S(2)}, u32[]{:S(2)}) %collective-permute-start.7) | collective-permute-done | bytes 32800 | tf_op jit(solution)/shard_map/ppermute | solution.py:27
  24.3 1.3 %shard_map.81 = (bf16[16,512]{1,0:T(8,128)(2,1)S(1)}, bf16[128,512]{1,0:T(8,128)(2,1)S(1)}) custom-call(s32[2]{0:T(128)S(1)} %pad_add_fusion.place_ref, bf16[128,128]{1,0:T(8,128)(2,1)S(1)} %get-tuple-element.28.refs_0_, bf16[128,128]{1,0:T(8,128)(2,1)S(1)} %collective-permute-done.6.refs_1_, bf16[128,128]{1,0:T(8,128)(2,1)S(1)} %collective-permute-done.7.refs_2_, ...), custom_call_target="tpu_custom_call" | custom-call | flops 536870912 | bytes 1589256 | tf_op jit(solution)/shard_map/pallas_call | solution.py:480
  25.7 1.6 %collective-permute-start.10 = (bf16[16,512]{1,0:T(8,128)(2,1)S(1)}, bf16[16,512]{1,0:T(8,128)(2,1)S(1)}, u32[]{:S(2)}, u32[]{:S(2)}) collective-permute-start(bf16[16,512]{1,0:T(8,128)(2,1)S(1)} %get-tuple-element.31), channel_id=1, source_target_pairs={{0,2},{1,3},{2,0},{3,1},{4,6},{5,7},{6,4},{7,5},{8,10},{9,11},{10,... | collective-permute-start | bytes 49160 | tf_op jit(solution)/shard_map/ppermute | solution.py:27
  27.3 2.8 %collective-permute-start.11 = (bf16[16,512]{1,0:T(8,128)(2,1)S(1)}, bf16[16,512]{1,0:T(8,128)(2,1)S(1)}, u32[]{:S(2)}, u32[]{:S(2)}) collective-permute-start(bf16[16,512]{1,0:T(8,128)(2,1)S(1)} %get-tuple-element.31), channel_id=1, source_target_pairs={{0,3},{1,2},{2,1},{3,0},{4,7},{5,6},{6,5},{7,4},{8,11},{9,10},{10,... | collective-permute-start | bytes 49160 | tf_op jit(solution)/shard_map/ppermute | solution.py:27
  30.4 2.4 %collective-permute-done.11 = bf16[16,512]{1,0:T(8,128)(2,1)S(1)} collective-permute-done((bf16[16,512]{1,0:T(8,128)(2,1)S(1)}, bf16[16,512]{1,0:T(8,128)(2,1)S(1)}, u32[]{:S(2)}, u32[]{:S(2)}) %collective-permute-start.11) | collective-permute-done | bytes 16416 | tf_op jit(solution)/shard_map/ppermute | solution.py:27
  32.8 1.1 %collective-permute-start.13 = (bf16[64,512]{1,0:T(8,128)(2,1)S(1)}, bf16[64,512]{1,0:T(8,128)(2,1)S(1)}, u32[]{:S(2)}, u32[]{:S(2)}) collective-permute-start(bf16[64,512]{1,0:T(8,128)(2,1)S(1)} %constant_dynamic-update-slice_fusion.refs_0_), channel_id=1, source_target_pairs={{0,8},{4,12},{8,0},{12,4},{1,9},{5,13},{9,1},{13,5},{2,10},{6,14},... | collective-permute-start | bytes 196616 | tf_op jit(solution)/shard_map/ppermute | solution.py:27
  33.9 0.8 %collective-permute-start.14 = (bf16[64,512]{1,0:T(8,128)(2,1)S(1)}, bf16[64,512]{1,0:T(8,128)(2,1)S(1)}, u32[]{:S(2)}, u32[]{:S(2)}) collective-permute-start(bf16[64,512]{1,0:T(8,128)(2,1)S(1)} %constant_dynamic-update-slice_fusion.refs_0_), channel_id=1, source_target_pairs={{0,12},{4,8},{8,4},{12,0},{1,13},{5,9},{9,5},{13,1},{2,14},{6,10},... | collective-permute-start | bytes 196616 | tf_op jit(solution)/shard_map/ppermute | solution.py:27
  34.7 1.4 %shard_map.82 = (f32[2,64,128]{2,1,0:T(8,128)S(1)}, f32[8,128,64]{2,1,0:T(8,128)S(1)}, f32[2,1024,128]{2,1,0:T(8,128)S(1)}) custom-call(f32[96,128]{1,0:T(8,128)S(1)} %shard_map.78.refs_0_, f32[96,128]{1,0:T(8,128)S(1)} %collective-permute-done.3.refs_1_, f32[96,128]{1,0:T(8,128)S(1)} %collective-permute-done.4.refs_2_, ...), custom_call_target="tpu_custom_call" | custom-call | flops 134217728 | bytes 1736704 | tf_op jit(solution)/shard_map/pallas_call | solution.py:480
  36.1 1.6 %collective-permute-done.13.refs_2_ = bf16[64,512]{1,0:T(8,128)(2,1)S(1)} collective-permute-done((bf16[64,512]{1,0:T(8,128)(2,1)S(1)}, bf16[64,512]{1,0:T(8,128)(2,1)S(1)}, u32[]{:S(2)}, u32[]{:S(2)}) %collective-permute-start.13) | collective-permute-done | bytes 65568 | tf_op jit(solution)/shard_map/ppermute | solution.py:27
  38.3 1.6 %shard_map.83 = (f32[2,8,512]{2,1,0:T(8,128)S(1)}, f32[64,128]{1,0:T(8,128)S(1)}, f32[64,128]{1,0:T(8,128)S(1)}, f32[64,128]{1,0:T(8,128)S(1)}, f32[64,128]{1,0:T(8,128)S(1)}) custom-call(s32[2]{0:T(128)S(1)} %pad_add_fusion.place_ref, bf16[64,512]{1,0:T(8,128)(2,1)S(1)} %constant_dynamic-update-slice_fusion.refs_0_, ...), custom_call_target="tpu_custom_call" | custom-call | flops 268435456 | bytes 2064392 | tf_op jit(solution)/shard_map/pallas_call | solution.py:480
  40.2 1.1 %collective-permute-start.16 = (f32[64,128]{1,0:T(8,128)S(1)}, f32[64,128]{1,0:T(8,128)S(1)}, u32[]{:S(2)}, u32[]{:S(2)}) collective-permute-start(f32[64,128]{1,0:T(8,128)S(1)} %get-tuple-element.39), channel_id=1, source_target_pairs={{0,8},{4,12},{8,0},{12,4},{1,9},{5,13},{9,1},{13,5},{2,10},{6,14},... | collective-permute-start | bytes 98312 | tf_op jit(solution)/shard_map/ppermute | solution.py:27
  41.9 2.3 %collective-permute-done.16 = f32[64,128]{1,0:T(8,128)S(1)} collective-permute-done((f32[64,128]{1,0:T(8,128)S(1)}, f32[64,128]{1,0:T(8,128)S(1)}, u32[]{:S(2)}, u32[]{:S(2)}) %collective-permute-start.16) | collective-permute-done | bytes 32800 | tf_op jit(solution)/shard_map/ppermute | solution.py:27
  44.9 3.3 %collective-permute-start.19 = (f32[64,128]{1,0:T(8,128)S(1)}, f32[64,128]{1,0:T(8,128)S(1)}, u32[]{:S(2)}, u32[]{:S(2)}) collective-permute-start(f32[64,128]{1,0:T(8,128)S(1)} %add_add_fusion.refs_0_), channel_id=1, source_target_pairs={{0,2},{1,3},{2,0},{3,1},{4,6},{5,7},{6,4},{7,5},{8,10},{9,11},{10,... | collective-permute-start | bytes 98312 | tf_op jit(solution)/shard_map/ppermute | solution.py:27
  48.2 1.1 %collective-permute-start.20 = (f32[64,128]{1,0:T(8,128)S(1)}, f32[64,128]{1,0:T(8,128)S(1)}, u32[]{:S(2)}, u32[]{:S(2)}) collective-permute-start(f32[64,128]{1,0:T(8,128)S(1)} %add_add_fusion.refs_0_), channel_id=1, source_target_pairs={{0,3},{1,2},{2,1},{3,0},{4,7},{5,6},{6,5},{7,4},{8,11},{9,10},{10,... | collective-permute-start | bytes 98312 | tf_op jit(solution)/shard_map/ppermute | solution.py:27
  49.3 1.4 %shard_map.86.plane_ref = f32[8,64]{1,0:T(8,128)S(1)} custom-call(bf16[64,512]{1,0:T(8,128)(2,1)S(1)} %constant_dynamic-update-slice_fusion.refs_0_, bf16[64,512]{1,0:T(8,128)(2,1)S(1)} %collective-permute-done.12.refs_1_, bf16[64,512]{1,0:T(8,128)(2,1)S(1)} %collective-permute-done.13.refs_2_, bf16[64,512]{1,0:T(8,128)(2,1)S(1)} %collective-permute-done.14.refs_3_, ...), custom_call_target="tpu_custom_call" | custom-call | flops 536870912 | bytes 1738752 | tf_op jit(solution)/shard_map/pallas_call | solution.py:480
  50.7 3.2 %collective-permute-done.20.refs_3_ = f32[64,128]{1,0:T(8,128)S(1)} collective-permute-done((f32[64,128]{1,0:T(8,128)S(1)}, f32[64,128]{1,0:T(8,128)S(1)}, u32[]{:S(2)}, u32[]{:S(2)}) %collective-permute-start.20) | collective-permute-done | bytes 32800 | tf_op jit(solution)/shard_map/ppermute | solution.py:27
  54.0 1.0 %collective-permute-start.22 = (f32[64,128]{1,0:T(8,128)S(1)}, f32[64,128]{1,0:T(8,128)S(1)}, u32[]{:S(2)}, u32[]{:S(2)}) collective-permute-start(f32[64,128]{1,0:T(8,128)S(1)} %shard_map.85.refs_0_), channel_id=1, source_target_pairs={{0,8},{4,12},{8,0},{12,4},{1,9},{5,13},{9,1},{13,5},{2,10},{6,14},... | collective-permute-start | bytes 98312 | tf_op jit(solution)/shard_map/ppermute | solution.py:27
  55.0 0.8 %collective-permute-start.23 = (f32[64,128]{1,0:T(8,128)S(1)}, f32[64,128]{1,0:T(8,128)S(1)}, u32[]{:S(2)}, u32[]{:S(2)}) collective-permute-start(f32[64,128]{1,0:T(8,128)S(1)} %shard_map.85.refs_0_), channel_id=1, source_target_pairs={{0,12},{4,8},{8,4},{12,0},{1,13},{5,9},{9,5},{13,1},{2,14},{6,10},... | collective-permute-start | bytes 98312 | tf_op jit(solution)/shard_map/ppermute | solution.py:27
  55.9 1.2 %shard_map.84 = bf16[64,2,4,512]{3,2,1,0:T(4,128)(2,1)} custom-call(f32[2,8,512]{2,1,0:T(8,128)S(1)} %get-tuple-element.35.top_ref, f32[64,512]{1,0:T(8,128)S(1)} %get-tuple-element.30.refs_7_.refs_6_.wo_ref, bf16[128,512]{1,0:T(8,128)(2,1)S(1)} %get-tuple-element.36.both_ref, bf16[512,512]{1,0:T(8,128)(2,1)S(1)} %reshape.10.refs_4_.refs_9_.field_ref), custom_call_target="tpu_custom_call" | custom-call | flops 268435456 | bytes 1343488 | tf_op jit(solution)/shard_map/pallas_call | solution.py:480
  58.4 1.6 %shard_map.88 = bf16[64,2,4,512]{3,2,1,0:T(4,128)(2,1)} custom-call(s32[2]{0:T(128)S(1)} %pad_add_fusion.place_ref, f32[64,128]{1,0:T(8,128)S(1)} %shard_map.85.refs_0_, f32[64,128]{1,0:T(8,128)S(1)} %collective-permute-done.21.refs_1_, f32[64,128]{1,0:T(8,128)S(1)} %collective-permute-done.22.refs_2_, f32[64,128]{1,0:T(8,128)S(1)} %collective-permute-done.23.refs_3_, ...), custom_call_target="tpu_custom_call" | custom-call | bytes 1703944 | tf_op jit(solution)/shard_map/pallas_call | solution.py:480
  (50 shorter events, 6.7 us)
Async XLA Ops:
  0.7 1.0 %copy-start = (bf16[64,2,4,512]{3,2,1,0:T(4,128)(2,1)S(1)}, bf16[64,2,4,512]{3,2,1,0:T(4,128)(2,1)}, u32[]{:S(2)}) copy-start(bf16[64,2,4,512]{3,2,1,0:T(4,128)(2,1)} %field_ref.1) | copy-start | bytes 1572868
  1.8 20.0 %copy-start.1 = (bf16[64,2,4,512]{3,2,1,0:T(4,128)(2,1)S(1)}, bf16[64,2,4,512]{3,2,1,0:T(4,128)(2,1)}, u32[]{:S(2)}) copy-start(bf16[64,2,4,512]{3,2,1,0:T(4,128)(2,1)} %field_ref.1) | copy-start | bytes 1572868
  3.0 11.0 %copy-start.2 = (f32[3,2,64,64]{3,2,1,0:T(8,128)S(1)}, f32[3,2,64,64]{3,2,1,0:T(8,128)}, u32[]{:S(2)}) copy-start(f32[3,2,64,64]{3,2,1,0:T(8,128)} %refs_7_.1) | copy-start | bytes 294916
  3.0 3.2 %collective-permute-start = (f32[72,128]{1,0:T(8,128)S(1)}, f32[72,128]{1,0:T(8,128)S(1)}, u32[]{:S(2)}, u32[]{:S(2)}) collective-permute-start(f32[72,128]{1,0:T(8,128)S(1)} %get-tuple-element.24), channel_id=1, source_target_pairs={{0,4},{4,0},{8,12},{12,8},{1,5},{5,1},{9,13},{13,9},{2,6},{6,2},{1... | collective-permute-start | bytes 110600 | tf_op jit(solution)/shard_map/ppermute | solution.py:27
  3.5 4.6 %collective-permute-start.1 = (f32[72,128]{1,0:T(8,128)S(1)}, f32[72,128]{1,0:T(8,128)S(1)}, u32[]{:S(2)}, u32[]{:S(2)}) collective-permute-start(f32[72,128]{1,0:T(8,128)S(1)} %get-tuple-element.25), channel_id=1, source_target_pairs={{0,8},{4,12},{8,0},{12,4},{1,9},{5,13},{9,1},{13,5},{2,10},{6,14},... | collective-permute-start | bytes 110600 | tf_op jit(solution)/shard_map/ppermute | solution.py:27
  6.0 3.4 %collective-permute-start.2 = (f32[72,128]{1,0:T(8,128)S(1)}, f32[72,128]{1,0:T(8,128)S(1)}, u32[]{:S(2)}, u32[]{:S(2)}) collective-permute-start(f32[72,128]{1,0:T(8,128)S(1)} %get-tuple-element.26), channel_id=1, source_target_pairs={{0,12},{4,8},{8,4},{12,0},{1,13},{5,9},{9,5},{13,1},{2,14},{6,10},... | collective-permute-start | bytes 110600 | tf_op jit(solution)/shard_map/ppermute | solution.py:27
  9.5 6.2 %collective-permute-start.3 = (f32[96,128]{1,0:T(8,128)S(1)}, f32[96,128]{1,0:T(8,128)S(1)}, u32[]{:S(2)}, u32[]{:S(2)}) collective-permute-start(f32[96,128]{1,0:T(8,128)S(1)} %shard_map.78.refs_0_), channel_id=1, source_target_pairs={{0,1},{1,0},{2,3},{3,2},{4,5},{5,4},{6,7},{7,6},{8,9},{9,8},{10,11... | collective-permute-start | bytes 147464 | tf_op jit(solution)/shard_map/ppermute | solution.py:27
  11.1 5.9 %collective-permute-start.4 = (f32[96,128]{1,0:T(8,128)S(1)}, f32[96,128]{1,0:T(8,128)S(1)}, u32[]{:S(2)}, u32[]{:S(2)}) collective-permute-start(f32[96,128]{1,0:T(8,128)S(1)} %shard_map.78.refs_0_), channel_id=1, source_target_pairs={{0,2},{1,3},{2,0},{3,1},{4,6},{5,7},{6,4},{7,5},{8,10},{9,11},{10,... | collective-permute-start | bytes 147464 | tf_op jit(solution)/shard_map/ppermute | solution.py:27
  13.7 5.9 %collective-permute-start.5 = (f32[96,128]{1,0:T(8,128)S(1)}, f32[96,128]{1,0:T(8,128)S(1)}, u32[]{:S(2)}, u32[]{:S(2)}) collective-permute-start(f32[96,128]{1,0:T(8,128)S(1)} %shard_map.78.refs_0_), channel_id=1, source_target_pairs={{0,3},{1,2},{2,1},{3,0},{4,7},{5,6},{6,5},{7,4},{8,11},{9,10},{10,... | collective-permute-start | bytes 147464 | tf_op jit(solution)/shard_map/ppermute | solution.py:27
  13.9 0.7 %copy-start.4 = (bf16[64,64]{1,0:T(8,128)(2,1)S(1)}, bf16[64,64]{1,0:T(8,128)(2,1)}, u32[]{:S(2)}) copy-start(bf16[64,64]{1,0:T(8,128)(2,1)} %wv_ref.1) | copy-start | bytes 24580
  14.7 0.7 %copy-start.5 = (bf16[64,64]{1,0:T(8,128)(2,1)S(1)}, bf16[64,64]{1,0:T(8,128)(2,1)}, u32[]{:S(2)}) copy-start(bf16[64,64]{1,0:T(8,128)(2,1)} %wo_ref.1) | copy-start | bytes 24580
  19.8 2.1 %copy-start.6 = (bf16[64,2,4,512]{3,2,1,0:T(4,128)(2,1)S(1)}, bf16[64,2,4,512]{3,2,1,0:T(4,128)(2,1)}, u32[]{:S(2)}) copy-start(bf16[64,2,4,512]{3,2,1,0:T(4,128)(2,1)} %param.7) | copy-start | bytes 1572868
  19.8 2.2 %collective-permute-start.6 = (bf16[128,128]{1,0:T(8,128)(2,1)S(1)}, bf16[128,128]{1,0:T(8,128)(2,1)S(1)}, u32[]{:S(2)}, u32[]{:S(2)}) collective-permute-start(bf16[128,128]{1,0:T(8,128)(2,1)S(1)} %get-tuple-element.28.refs_0_), channel_id=1, source_target_pairs={{0,4},{4,0},{8,12},{12,8},{1,5},{5,1},{9,13},{13,9},{2,6},{6,2},{1... | collective-permute-start | bytes 98312 | tf_op jit(solution)/shard_map/ppermute | solution.py:27
  19.9 4.0 %collective-permute-start.7 = (bf16[128,128]{1,0:T(8,128)(2,1)S(1)}, bf16[128,128]{1,0:T(8,128)(2,1)S(1)}, u32[]{:S(2)}, u32[]{:S(2)}) collective-permute-start(bf16[128,128]{1,0:T(8,128)(2,1)S(1)} %get-tuple-element.28.refs_0_), channel_id=1, source_target_pairs={{0,8},{4,12},{8,0},{12,4},{1,9},{5,13},{9,1},{13,5},{2,10},{6,14},... | collective-permute-start | bytes 98312 | tf_op jit(solution)/shard_map/ppermute | solution.py:27
  20.8 3.4 %collective-permute-start.8 = (bf16[128,128]{1,0:T(8,128)(2,1)S(1)}, bf16[128,128]{1,0:T(8,128)(2,1)S(1)}, u32[]{:S(2)}, u32[]{:S(2)}) collective-permute-start(bf16[128,128]{1,0:T(8,128)(2,1)S(1)} %get-tuple-element.28.refs_0_), channel_id=1, source_target_pairs={{0,12},{4,8},{8,4},{12,0},{1,13},{5,9},{9,5},{13,1},{2,14},{6,10},... | collective-permute-start | bytes 98312 | tf_op jit(solution)/shard_map/ppermute | solution.py:27
  25.6 9.1 %copy-start.3 = (bf16[2,128,128]{2,1,0:T(8,128)(2,1)S(1)}, bf16[2,128,128]{2,1,0:T(8,128)(2,1)}, u32[]{:S(2)}) copy-start(bf16[2,128,128]{2,1,0:T(8,128)(2,1)} %constant.9.clone.refs_4_.refs_6_) | copy-start | bytes 196612
  25.6 4.5 %collective-permute-start.9 = (bf16[16,512]{1,0:T(8,128)(2,1)S(1)}, bf16[16,512]{1,0:T(8,128)(2,1)S(1)}, u32[]{:S(2)}, u32[]{:S(2)}) collective-permute-start(bf16[16,512]{1,0:T(8,128)(2,1)S(1)} %get-tuple-element.31), channel_id=1, source_target_pairs={{0,1},{1,0},{2,3},{3,2},{4,5},{5,4},{6,7},{7,6},{8,9},{9,8},{10,11... | collective-permute-start | bytes 49160 | tf_op jit(solution)/shard_map/ppermute | solution.py:27
  25.7 4.7 %collective-permute-start.10 = (bf16[16,512]{1,0:T(8,128)(2,1)S(1)}, bf16[16,512]{1,0:T(8,128)(2,1)S(1)}, u32[]{:S(2)}, u32[]{:S(2)}) collective-permute-start(bf16[16,512]{1,0:T(8,128)(2,1)S(1)} %get-tuple-element.31), channel_id=1, source_target_pairs={{0,2},{1,3},{2,0},{3,1},{4,6},{5,7},{6,4},{7,5},{8,10},{9,11},{10,... | collective-permute-start | bytes 49160 | tf_op jit(solution)/shard_map/ppermute | solution.py:27
  27.3 5.5 %collective-permute-start.11 = (bf16[16,512]{1,0:T(8,128)(2,1)S(1)}, bf16[16,512]{1,0:T(8,128)(2,1)S(1)}, u32[]{:S(2)}, u32[]{:S(2)}) collective-permute-start(bf16[16,512]{1,0:T(8,128)(2,1)S(1)} %get-tuple-element.31), channel_id=1, source_target_pairs={{0,3},{1,2},{2,1},{3,0},{4,7},{5,6},{6,5},{7,4},{8,11},{9,10},{10,... | collective-permute-start | bytes 49160 | tf_op jit(solution)/shard_map/ppermute | solution.py:27
  32.8 3.3 %collective-permute-start.12 = (bf16[64,512]{1,0:T(8,128)(2,1)S(1)}, bf16[64,512]{1,0:T(8,128)(2,1)S(1)}, u32[]{:S(2)}, u32[]{:S(2)}) collective-permute-start(bf16[64,512]{1,0:T(8,128)(2,1)S(1)} %constant_dynamic-update-slice_fusion.refs_0_), channel_id=1, source_target_pairs={{0,4},{4,0},{8,12},{12,8},{1,5},{5,1},{9,13},{13,9},{2,6},{6,2},{1... | collective-permute-start | bytes 196616 | tf_op jit(solution)/shard_map/ppermute | solution.py:27
  32.8 4.9 %collective-permute-start.13 = (bf16[64,512]{1,0:T(8,128)(2,1)S(1)}, bf16[64,512]{1,0:T(8,128)(2,1)S(1)}, u32[]{:S(2)}, u32[]{:S(2)}) collective-permute-start(bf16[64,512]{1,0:T(8,128)(2,1)S(1)} %constant_dynamic-update-slice_fusion.refs_0_), channel_id=1, source_target_pairs={{0,8},{4,12},{8,0},{12,4},{1,9},{5,13},{9,1},{13,5},{2,10},{6,14},... | collective-permute-start | bytes 196616 | tf_op jit(solution)/shard_map/ppermute | solution.py:27
  33.9 4.4 %collective-permute-start.14 = (bf16[64,512]{1,0:T(8,128)(2,1)S(1)}, bf16[64,512]{1,0:T(8,128)(2,1)S(1)}, u32[]{:S(2)}, u32[]{:S(2)}) collective-permute-start(bf16[64,512]{1,0:T(8,128)(2,1)S(1)} %constant_dynamic-update-slice_fusion.refs_0_), channel_id=1, source_target_pairs={{0,12},{4,8},{8,4},{12,0},{1,13},{5,9},{9,5},{13,1},{2,14},{6,10},... | collective-permute-start | bytes 196616 | tf_op jit(solution)/shard_map/ppermute | solution.py:27
  39.9 1.9 %collective-permute-start.15 = (f32[64,128]{1,0:T(8,128)S(1)}, f32[64,128]{1,0:T(8,128)S(1)}, u32[]{:S(2)}, u32[]{:S(2)}) collective-permute-start(f32[64,128]{1,0:T(8,128)S(1)} %get-tuple-element.38), channel_id=1, source_target_pairs={{0,4},{4,0},{8,12},{12,8},{1,5},{5,1},{9,13},{13,9},{2,6},{6,2},{1... | collective-permute-start | bytes 98312 | tf_op jit(solution)/shard_map/ppermute | solution.py:27
  40.2 3.9 %collective-permute-start.16 = (f32[64,128]{1,0:T(8,128)S(1)}, f32[64,128]{1,0:T(8,128)S(1)}, u32[]{:S(2)}, u32[]{:S(2)}) collective-permute-start(f32[64,128]{1,0:T(8,128)S(1)} %get-tuple-element.39), channel_id=1, source_target_pairs={{0,8},{4,12},{8,0},{12,4},{1,9},{5,13},{9,1},{13,5},{2,10},{6,14},... | collective-permute-start | bytes 98312 | tf_op jit(solution)/shard_map/ppermute | solution.py:27
  41.3 3.5 %collective-permute-start.17 = (f32[64,128]{1,0:T(8,128)S(1)}, f32[64,128]{1,0:T(8,128)S(1)}, u32[]{:S(2)}, u32[]{:S(2)}) collective-permute-start(f32[64,128]{1,0:T(8,128)S(1)} %get-tuple-element.40), channel_id=1, source_target_pairs={{0,12},{4,8},{8,4},{12,0},{1,13},{5,9},{9,5},{13,1},{2,14},{6,10},... | collective-permute-start | bytes 98312 | tf_op jit(solution)/shard_map/ppermute | solution.py:27
  44.8 5.9 %collective-permute-start.18 = (f32[64,128]{1,0:T(8,128)S(1)}, f32[64,128]{1,0:T(8,128)S(1)}, u32[]{:S(2)}, u32[]{:S(2)}) collective-permute-start(f32[64,128]{1,0:T(8,128)S(1)} %add_add_fusion.refs_0_), channel_id=1, source_target_pairs={{0,1},{1,0},{2,3},{3,2},{4,5},{5,4},{6,7},{7,6},{8,9},{9,8},{10,11... | collective-permute-start | bytes 98312 | tf_op jit(solution)/shard_map/ppermute | solution.py:27
  44.9 5.8 %collective-permute-start.19 = (f32[64,128]{1,0:T(8,128)S(1)}, f32[64,128]{1,0:T(8,128)S(1)}, u32[]{:S(2)}, u32[]{:S(2)}) collective-permute-start(f32[64,128]{1,0:T(8,128)S(1)} %add_add_fusion.refs_0_), channel_id=1, source_target_pairs={{0,2},{1,3},{2,0},{3,1},{4,6},{5,7},{6,4},{7,5},{8,10},{9,11},{10,... | collective-permute-start | bytes 98312 | tf_op jit(solution)/shard_map/ppermute | solution.py:27
  48.2 5.7 %collective-permute-start.20 = (f32[64,128]{1,0:T(8,128)S(1)}, f32[64,128]{1,0:T(8,128)S(1)}, u32[]{:S(2)}, u32[]{:S(2)}) collective-permute-start(f32[64,128]{1,0:T(8,128)S(1)} %add_add_fusion.refs_0_), channel_id=1, source_target_pairs={{0,3},{1,2},{2,1},{3,0},{4,7},{5,6},{6,5},{7,4},{8,11},{9,10},{10,... | collective-permute-start | bytes 98312 | tf_op jit(solution)/shard_map/ppermute | solution.py:27
  53.9 3.7 %collective-permute-start.21 = (f32[64,128]{1,0:T(8,128)S(1)}, f32[64,128]{1,0:T(8,128)S(1)}, u32[]{:S(2)}, u32[]{:S(2)}) collective-permute-start(f32[64,128]{1,0:T(8,128)S(1)} %shard_map.85.refs_0_), channel_id=1, source_target_pairs={{0,4},{4,0},{8,12},{12,8},{1,5},{5,1},{9,13},{13,9},{2,6},{6,2},{1... | collective-permute-start | bytes 98312 | tf_op jit(solution)/shard_map/ppermute | solution.py:27
  54.0 4.0 %collective-permute-start.22 = (f32[64,128]{1,0:T(8,128)S(1)}, f32[64,128]{1,0:T(8,128)S(1)}, u32[]{:S(2)}, u32[]{:S(2)}) collective-permute-start(f32[64,128]{1,0:T(8,128)S(1)} %shard_map.85.refs_0_), channel_id=1, source_target_pairs={{0,8},{4,12},{8,0},{12,4},{1,9},{5,13},{9,1},{13,5},{2,10},{6,14},... | collective-permute-start | bytes 98312 | tf_op jit(solution)/shard_map/ppermute | solution.py:27
  55.0 3.3 %collective-permute-start.23 = (f32[64,128]{1,0:T(8,128)S(1)}, f32[64,128]{1,0:T(8,128)S(1)}, u32[]{:S(2)}, u32[]{:S(2)}) collective-permute-start(f32[64,128]{1,0:T(8,128)S(1)} %shard_map.85.refs_0_), channel_id=1, source_target_pairs={{0,12},{4,8},{8,4},{12,0},{1,13},{5,9},{9,5},{13,1},{2,14},{6,10},... | collective-permute-start | bytes 98312 | tf_op jit(solution)/shard_map/ppermute | solution.py:27

commit v6 on v5

--- a/solution.py
+++ b/solution.py
@@ -202,16 +202,16 @@
     return lax.broadcasted_iota(jnp.int32, shape, dim)
 
 
-def put_quarters(place_ref, part_ref, total, outs):
+def put_quarters(part_ref, total, outs):
     for index in range(part_ref.shape[0]):
         part_ref[index] = total[:, index * LANES : (index + 1) * LANES]
     for step, out in enumerate(outs):
-        out[0:WIDTH, :] = part_ref[place_ref[0] ^ step]
-
-
-def join_quarters(place_ref, part_ref, quarters):
+        out[0:WIDTH, :] = part_ref[lax.axis_index("gx") ^ step]
+
+
+def join_quarters(part_ref, quarters):
     for step, quarter in enumerate(quarters):
-        part_ref[place_ref[0] ^ step] = quarter[...]
+        part_ref[lax.axis_index("gx") ^ step] = quarter[...]
     return jnp.concatenate([part_ref[index] for index in range(part_ref.shape[0])], axis=1)
 
 
@@ -242,19 +242,38 @@
         wz_out[index * WIDTH : (index + 1) * WIDTH, :] = qk_ref[2, index].T
 
 
-def sums_kernel(place_ref, field_ref, *refs):
-    outs, part_ref = refs[:-1], refs[-1]
-    data = field_ref[...].astype(jnp.float32)
-    _, rows_x, rows_y, depth = data.shape
-    part = jnp.sum(jnp.sum(data, axis=1), axis=1)
-    lanes = data[..., :LANES]
-    for start in range(LANES, depth, LANES):
-        lanes = lanes + data[..., start : start + LANES]
-    row_sums = jnp.sum(lanes, axis=3, keepdims=True)
-    shape = lanes.shape
-    own = jnp.sum(jnp.where(number(shape, 0) == number(shape, 3), row_sums, 0.0), axis=0)
-    put_quarters(place_ref, part_ref, part, outs)
-    for out in outs:
+def sums_kernel(field_ref, *refs):
+    outs, (part_ref, data_ref, semaphores) = refs[:-3], refs[-3:]
+    _, rows_x, rows_y, depth = data_ref.shape
+    chunks = semaphores.shape[0]
+    size = WIDTH // chunks
+    copies = [
+        pltpu.make_async_copy(
+            field_ref.at[pl.ds(index * size, size)],
+            data_ref.at[pl.ds(index * size, size)],
+            semaphores.at[index],
+        )
+        for index in range(chunks)
+    ]
+    for copy in copies:
+        copy.start()
+    own = jnp.zeros((rows_x, rows_y, LANES), jnp.float32)
+    for index, copy in enumerate(copies):
+        copy.wait()
+        rows = slice(index * size, (index + 1) * size)
+        data = data_ref[rows].astype(jnp.float32)
+        part = jnp.sum(jnp.sum(data, axis=1), axis=1)
+        for quarter in range(part_ref.shape[0]):
+            part_ref[quarter, rows, :] = part[:, quarter * LANES : (quarter + 1) * LANES]
+        lanes = data[..., :LANES]
+        for start in range(LANES, depth, LANES):
+            lanes = lanes + data[..., start : start + LANES]
+        row_sums = jnp.sum(lanes, axis=3, keepdims=True)
+        shape = lanes.shape
+        mine = number(shape, 0) + index * size == number(shape, 3)
+        own = own + jnp.sum(jnp.where(mine, row_sums, 0.0), axis=0)
+    for step, out in enumerate(outs):
+        out[0:WIDTH, :] = part_ref[lax.axis_index("gx") ^ step]
         for index in range(rows_x):
             start = WIDTH + index * rows_y
             out[start : start + rows_y, :] = own[index]
@@ -302,13 +321,14 @@
     return jnp.where(mine, part[None], 0.0).reshape(-1, WIDTH)
 
 
-def plane_kernel(cells, lengths, *refs):
+def plane_kernel(cells, span_x, lengths, *refs):
     parts, (same_ref, qk_ref, mix_ref, feat_ref, full_ref) = refs[:-5], refs[-5:]
     totals = jnp.concatenate(
         [
             part[WIDTH + step * cells : WIDTH + (step + 1) * cells, :]
-            for step in range((parts[0].shape[0] - WIDTH) // cells)
+            for first in range(span_x)
             for part in parts
+            for step in range(first, (parts[0].shape[0] - WIDTH) // cells, span_x)
         ],
         axis=0,
     )[:, :WIDTH]
@@ -342,14 +362,14 @@
     mix_ref[1] = backward
 
 
-def coef_kernel(place_ref, *refs):
+def coef_kernel(*refs):
     quarters, rest = refs[:-8], refs[-8:]
     field_ref, cot_ref, wv_ref, wo_ref, send_ref, both_ref, part_ref = rest[1:]
     quarters = quarters + rest[:1]
     rows, depth = field_ref.shape
     cells = rows // WIDTH
     wide = HEADS * HEAD_DIM * HEAD_DIM
-    both = join_quarters(place_ref, part_ref, [q[...].astype(jnp.float32) for q in quarters])
+    both = join_quarters(part_ref, [q[...].astype(jnp.float32) for q in quarters])
     both_ref[...] = both.astype(jnp.bfloat16)
     query = expand(both[:WIDTH])
     keyset = expand(both[WIDTH:])
@@ -371,7 +391,7 @@
     ]
 
 
-def mix_kernel(factor, spans, place_ref, *refs):
+def mix_kernel(factor, spans, *refs):
     lows, refs = refs[:spans], refs[spans:]
     mix_ref, wv_ref, wo_ref, wq_ref, wk_ref, field_ref, cot_ref, top_ref = refs[:8]
     outs, part_ref = refs[8:-1], refs[-1]
@@ -397,7 +417,7 @@
         return mul_left(found[:WIDTH] + found[WIDTH:], right)
 
     found = pull(wq_ref[...], left_f, cot_ref[...]) + pull(wk_ref[...], left_c, field_ref[...])
-    put_quarters(place_ref, part_ref, found, outs)
+    put_quarters(part_ref, found, outs)
 
 
 def put_cells(ref, total):
@@ -464,23 +484,22 @@
     out_ref[...] = found + jnp.concatenate([plane] * columns, axis=1)
 
 
-def final_kernel(place_ref, *refs):
+def final_kernel(*refs):
     quarters, (base_ref, out_ref, part_ref) = refs[:-3], refs[-3:]
     rows, depth = base_ref.shape
     cells = rows // WIDTH
-    found = join_quarters(place_ref, part_ref, quarters)
+    found = join_quarters(part_ref, quarters)
     total = base_ref[...].reshape(WIDTH, cells, depth) + found[:, None, :]
     put_cells(out_ref, total)
 
 
-def run(kernel, outs, operands, scalars=0, flops=0, scratch=()):
+def run(kernel, outs, operands, places=pltpu.VMEM, flops=0, scratch=()):
     vmem = pl.BlockSpec(memory_space=pltpu.VMEM)
-    smem = pl.BlockSpec(memory_space=pltpu.SMEM)
     moved = sum(x.size * x.dtype.itemsize for x in tuple(operands) + tuple(outs))
     found = pl.pallas_call(
         kernel,
         out_shape=tuple(outs),
-        in_specs=[smem] * scalars + [vmem] * (len(operands) - scalars),
+        in_specs=[pl.BlockSpec(memory_space=places)] * len(operands),
         out_specs=tuple(vmem for _ in outs),
         scratch_shapes=list(scratch),
         compiler_params=pltpu.CompilerParams(vmem_limit_bytes=16 * 1024 * 1024),
@@ -503,7 +522,6 @@
     f32, bf16 = jnp.float32, jnp.bfloat16
     like = jax.ShapeDtypeStruct
     lengths = ((grid_x, grid_y * depth), (grid_y, grid_x * depth))
-    place = jnp.stack([lax.axis_index("gx"), lax.axis_index("gy")]).astype(jnp.int32)
 
     cell = np.arange(places)
     at_x = cell // cells // span_y * rows_x + cell % cells // rows_y
@@ -527,8 +545,9 @@
         )
 
     sums = run(
-        sums_kernel, [like((WIDTH + cells, LANES), f32)] * span_x, (place, field),
-        scalars=1, flops=cube // 4, scratch=[parts],
+        sums_kernel, [like((WIDTH + cells, LANES), f32)] * span_x, (field,), places=pl.ANY,
+        flops=cube // 4,
+        scratch=[parts, pltpu.VMEM(field.shape, bf16), pltpu.SemaphoreType.DMA((4,))],
     )
     wv, wo, wq, wk, wz = run(
         prepare_kernel,
@@ -537,17 +556,24 @@
         (w_value, w_out, qk_weight),
         flops=cube // 8,
     )
-    total = run(
-        add_kernel, [like((WIDTH + span_x * cells, LANES), f32)], swaps(sums, "gx", span_x)
-    )
-    totals = swaps(total, "gy", span_y)
+    def add(sent, size):
+        return run(add_kernel, [like((WIDTH + size * cells, LANES), f32)], sent)
+
+    def pair(part, step):
+        return part, swap(part, "gy", span_y, step)
+
+    total = add(swaps(sums, "gx", span_x), span_x)
+    steps = [1 << level for level in range(span_y.bit_length() - 1)]
+    for step in steps[:-1]:
+        total = add(pair(total, step), 2 * step * span_x)
+    totals = pair(total, steps[-1])
     mine, feat_z = run(
         functools.partial(factor_kernel, grid_x * grid_y),
         [like((2 * WIDTH, LANES), bf16), like((WIDTH + HEAD_DIM, LANES), f32)],
         totals + (wz,),
     )
     mix, feat, full = run(
-        functools.partial(plane_kernel, cells, lengths),
+        functools.partial(plane_kernel, cells, span_x, lengths),
         [like((2, HEADS * cells, places), f32), like((8, places, WIDTH), f32),
          like((2, HEADS * places, places), f32)],
         totals + (same, qk_weight),
@@ -556,22 +582,24 @@
     send, both = run(
         coef_kernel,
         [like((2 * cells, wide), bf16), like((2 * WIDTH, depth), bf16)],
-        (place,) + swaps(mine, "gx", span_x) + (cols, cots, wv, wo),
-        scalars=1,
+        swaps(mine, "gx", span_x) + (cols, cots, wv, wo),
         flops=2 * cube,
         scratch=[pltpu.VMEM((span_x, 2 * WIDTH, LANES), f32)],
     )
-    low = jnp.concatenate(swaps(send, "gy", span_y), axis=0)
+    low = send
+    for step in steps:
+        low = jnp.concatenate(pair(low, step), axis=0)
     lows = swaps(low, "gx", span_x)
     top, *pulls = run(
         functools.partial(mix_kernel, factor_z, span_x),
         [like((2, cells, wide), f32)] + [block] * span_x,
-        (place,) + lows + (mix, wv, wo, wq, wk, cols, cots),
-        scalars=1,
+        lows + (mix, wv, wo, wq, wk, cols, cots),
         flops=cube,
         scratch=[parts],
     )
     total = sum(swaps(pulls, "gx", span_x))
+    for step in steps[:-1]:
+        total = sum(pair(total, step))
     layer_output = run(
         output_kernel, [like(field.shape, bf16)], (top, wo, both, cols), flops=cube
     )
@@ -584,14 +612,13 @@
     mine = run(
         functools.partial(pull_kernel, grid_x * grid_y),
         [block],
-        swaps(total, "gy", span_y) + (feat_z,),
+        pair(total, steps[-1]) + (feat_z,),
     )
     base = run(base_kernel, [like((rows, depth), f32)], (top, wv, both, cots, plane), flops=cube)
     field_grad = run(
         final_kernel,
         [like(field.shape, bf16)],
-        (place,) + swaps(mine, "gx", span_x) + (base,),
-        scalars=1,
+        swaps(mine, "gx", span_x) + (base,),
         scratch=[parts],
     )
     return (layer_output, field_grad)
@@ -606,6 +633,7 @@
         places = grid_x // mesh.shape["groups"] * grid_y
         small = places == LANES and places == 8 * count
         small = small and depth == LANES * mesh.shape["gx"] and count & (count - 1) == 0
+        small = small and mesh.shape["gy"] > 1
         return jax.shard_map(
             per_device_kernels if small else per_device,
             mesh=mesh,

time: 60.3 us -> 59.2 us (0.982)
  waiting for transfers between devices: 21.4 us -> 23.5 us
  local copies, waits for them, and re-layouts: 2.76 us -> 1.32 us
  Pallas kernels: 10.7 us -> 9.46 us
    ppermute x24 -> x21, waiting for transfers between devices: 21.4 us -> 23.5 us  [swap(): return lax.ppermute(part, axis, [(i, i ^ step) for i in range(size)])]
    unnamed x17 -> x16, local copies, waits for them, and re-layouts: 2.51 us -> 1.07 us
    pallas_call x12 -> x13, Pallas kernels: 10.7 us -> 9.46 us  [run(): pl.pallas_call(kernel, out_shape=tuple(outs), in_specs=[pl.BlockSpec(memo...]
    ppermute x24 -> x21, starting transfers between devices: 24.1 us -> 23.9 us  [swap(): return lax.ppermute(part, axis, [(i, i ^ step) for i in range(size)])]
  transfers between devices with their start and end apart: 24 -> 21, of which waited for: 15 -> 16; matrix products, arithmetic and copies ran while one was open for 0% -> 0% of each run, Pallas kernels for 8% -> 8%
where the time goes in v6:
time: 59.2 us; the launch traced here: 59.1 us
  starting transfers between devices  23.9 us (40%)
  waiting for transfers between devices  23.5 us (40%)
  Pallas kernels  9.46 us (16%)
  local copies, waits for them, and re-layouts  1.32 us (2%)
  between operations  0.8 us (1%)
    ppermute x21, starting transfers between devices, swap(): return lax.ppermute(part, axis, [(i, i ^ step) for i in range(size)])  23.9 us
    ppermute x21, waiting for transfers between devices, swap(): return lax.ppermute(part, axis, [(i, i ^ step) for i in range(size)])  23.5 us
    pallas_call x13, Pallas kernels, run(): pl.pallas_call(kernel, out_shape=tuple(outs), in_specs=[pl.BlockSpec(memo...  9.46 us
  transfers between devices with their start and end apart: 21, of which 16 were waited for; matrix products, arithmetic and copies ran while one was open for 0% of the time, Pallas kernels for 8%

profile of v6, /device:TPU:0, one launch (start us, length us, event | category | flops | bytes accessed | tf_op | source)
XLA Modules:
  0.0 59.1 jit_solution(12642096160359458895)
XLA Ops:
  0.6 1.0 %copy-done = bf16[64,2,4,512]{3,2,1,0:T(4,128)(2,1)S(1)} copy-done((bf16[64,2,4,512]{3,2,1,0:T(4,128)(2,1)S(1)}, bf16[64,2,4,512]{3,2,1,0:T(4,128)(2,1)}, u32[]{:S(2)}) %copy-start) | copy-done | bytes 524312
  1.7 1.5 %shard_map.77 = (f32[72,128]{1,0:T(8,128)S(1)}, f32[72,128]{1,0:T(8,128)S(1)}, f32[72,128]{1,0:T(8,128)S(1)}, f32[72,128]{1,0:T(8,128)S(1)}) custom-call(bf16[64,2,4,512]{3,2,1,0:T(4,128)(2,1)S(1)} %copy-done), custom_call_target="tpu_custom_call" | custom-call | flops 67108864 | bytes 671744 | tf_op jit(solution)/shard_map/pallas_call | solution.py:499
  3.8 2.6 %collective-permute-start.1 = (f32[72,128]{1,0:T(8,128)S(1)}, f32[72,128]{1,0:T(8,128)S(1)}, u32[]{:S(2)}, u32[]{:S(2)}) collective-permute-start(f32[72,128]{1,0:T(8,128)S(1)} %get-tuple-element.25), channel_id=1, source_target_pairs={{0,8},{4,12},{8,0},{12,4},{1,9},{5,13},{9,1},{13,5},{2,10},{6,14},... | collective-permute-start | bytes 110600 | tf_op jit(solution)/shard_map/ppermute | solution.py:27
  6.4 2.0 %collective-permute-done.1.refs_2_ = f32[72,128]{1,0:T(8,128)S(1)} collective-permute-done((f32[72,128]{1,0:T(8,128)S(1)}, f32[72,128]{1,0:T(8,128)S(1)}, u32[]{:S(2)}, u32[]{:S(2)}) %collective-permute-start.1) | collective-permute-done | bytes 36896 | tf_op jit(solution)/shard_map/ppermute | solution.py:27
  8.4 1.4 %collective-permute-done.2.refs_3_ = f32[72,128]{1,0:T(8,128)S(1)} collective-permute-done((f32[72,128]{1,0:T(8,128)S(1)}, f32[72,128]{1,0:T(8,128)S(1)}, u32[]{:S(2)}, u32[]{:S(2)}) %collective-permute-start.2) | collective-permute-done | bytes 36896 | tf_op jit(solution)/shard_map/ppermute | solution.py:27
  9.8 1.6 %collective-permute-start.3 = (f32[96,128]{1,0:T(8,128)S(1)}, f32[96,128]{1,0:T(8,128)S(1)}, u32[]{:S(2)}, u32[]{:S(2)}) collective-permute-start(f32[96,128]{1,0:T(8,128)S(1)} %shard_map.78.refs_0_), channel_id=1, source_target_pairs={{0,1},{1,0},{2,3},{3,2},{4,5},{5,4},{6,7},{7,6},{8,9},{9,8},{10,11... | collective-permute-start | bytes 147464 | tf_op jit(solution)/shard_map/ppermute | solution.py:27
  11.4 2.5 %collective-permute-done.3.refs_1_ = f32[96,128]{1,0:T(8,128)S(1)} collective-permute-done((f32[96,128]{1,0:T(8,128)S(1)}, f32[96,128]{1,0:T(8,128)S(1)}, u32[]{:S(2)}, u32[]{:S(2)}) %collective-permute-start.3) | collective-permute-done | bytes 49184 | tf_op jit(solution)/shard_map/ppermute | solution.py:27
  13.9 2.7 %collective-permute-start.4 = (f32[128,128]{1,0:T(8,128)S(1)}, f32[128,128]{1,0:T(8,128)S(1)}, u32[]{:S(2)}, u32[]{:S(2)}) collective-permute-start(f32[128,128]{1,0:T(8,128)S(1)} %shard_map.79.refs_0_), channel_id=1, source_target_pairs={{0,2},{1,3},{2,0},{3,1},{4,6},{5,7},{6,4},{7,5},{8,10},{9,11},{10,... | collective-permute-start | bytes 196616 | tf_op jit(solution)/shard_map/ppermute | solution.py:27
  16.9 2.3 %collective-permute-done.4.refs_1_ = f32[128,128]{1,0:T(8,128)S(1)} collective-permute-done((f32[128,128]{1,0:T(8,128)S(1)}, f32[128,128]{1,0:T(8,128)S(1)}, u32[]{:S(2)}, u32[]{:S(2)}) %collective-permute-start.4) | collective-permute-done | bytes 65568 | tf_op jit(solution)/shard_map/ppermute | solution.py:27
  19.4 0.9 %collective-permute-start.6 = (bf16[128,128]{1,0:T(8,128)(2,1)S(1)}, bf16[128,128]{1,0:T(8,128)(2,1)S(1)}, u32[]{:S(2)}, u32[]{:S(2)}) collective-permute-start(bf16[128,128]{1,0:T(8,128)(2,1)S(1)} %get-tuple-element.28.refs_0_), channel_id=1, source_target_pairs={{0,8},{4,12},{8,0},{12,4},{1,9},{5,13},{9,1},{13,5},{2,10},{6,14},... | collective-permute-start | bytes 98312 | tf_op jit(solution)/shard_map/ppermute | solution.py:27
  20.3 1.0 %collective-permute-start.7 = (bf16[128,128]{1,0:T(8,128)(2,1)S(1)}, bf16[128,128]{1,0:T(8,128)(2,1)S(1)}, u32[]{:S(2)}, u32[]{:S(2)}) collective-permute-start(bf16[128,128]{1,0:T(8,128)(2,1)S(1)} %get-tuple-element.28.refs_0_), channel_id=1, source_target_pairs={{0,12},{4,8},{8,4},{12,0},{1,13},{5,9},{9,5},{13,1},{2,14},{6,10},... | collective-permute-start | bytes 98312 | tf_op jit(solution)/shard_map/ppermute | solution.py:27
  21.6 2.0 %collective-permute-done.6.refs_2_ = bf16[128,128]{1,0:T(8,128)(2,1)S(1)} collective-permute-done((bf16[128,128]{1,0:T(8,128)(2,1)S(1)}, bf16[128,128]{1,0:T(8,128)(2,1)S(1)}, u32[]{:S(2)}, u32[]{:S(2)}) %collective-permute-start.6) | collective-permute-done | bytes 32800 | tf_op jit(solution)/shard_map/ppermute | solution.py:27
  23.9 0.8 %shard_map.82 = (bf16[16,512]{1,0:T(8,128)(2,1)S(1)}, bf16[128,512]{1,0:T(8,128)(2,1)S(1)}) custom-call(bf16[128,128]{1,0:T(8,128)(2,1)S(1)} %get-tuple-element.28.refs_0_, bf16[128,128]{1,0:T(8,128)(2,1)S(1)} %collective-permute-done.5.refs_1_, bf16[128,128]{1,0:T(8,128)(2,1)S(1)} %collective-permute-done.6.refs_2_, ...), custom_call_target="tpu_custom_call" | custom-call | flops 536870912 | bytes 1589248 | tf_op jit(solution)/shard_map/pallas_call | solution.py:499
  24.7 1.6 %collective-permute-start.8 = (bf16[16,512]{1,0:T(8,128)(2,1)S(1)}, bf16[16,512]{1,0:T(8,128)(2,1)S(1)}, u32[]{:S(2)}, u32[]{:S(2)}) collective-permute-start(bf16[16,512]{1,0:T(8,128)(2,1)S(1)} %get-tuple-element.31), channel_id=1, source_target_pairs={{0,1},{1,0},{2,3},{3,2},{4,5},{5,4},{6,7},{7,6},{8,9},{9,8},{10,11... | collective-permute-start | bytes 49160 | tf_op jit(solution)/shard_map/ppermute | solution.py:27
  26.2 2.3 %collective-permute-done.8 = bf16[16,512]{1,0:T(8,128)(2,1)S(1)} collective-permute-done((bf16[16,512]{1,0:T(8,128)(2,1)S(1)}, bf16[16,512]{1,0:T(8,128)(2,1)S(1)}, u32[]{:S(2)}, u32[]{:S(2)}) %collective-permute-start.8) | collective-permute-done | bytes 16416 | tf_op jit(solution)/shard_map/ppermute | solution.py:27
  28.5 2.6 %collective-permute-start.9 = (bf16[32,512]{1,0:T(8,128)(2,1)S(1)}, bf16[32,512]{1,0:T(8,128)(2,1)S(1)}, u32[]{:S(2)}, u32[]{:S(2)}) collective-permute-start(bf16[32,512]{1,0:T(8,128)(2,1)S(1)} %pad_maximum_fusion), channel_id=1, source_target_pairs={{0,2},{1,3},{2,0},{3,1},{4,6},{5,7},{6,4},{7,5},{8,10},{9,11},{10,... | collective-permute-start | bytes 98312 | tf_op jit(solution)/shard_map/ppermute | solution.py:27
  31.1 2.2 %collective-permute-done.9 = bf16[32,512]{1,0:T(8,128)(2,1)S(1)} collective-permute-done((bf16[32,512]{1,0:T(8,128)(2,1)S(1)}, bf16[32,512]{1,0:T(8,128)(2,1)S(1)}, u32[]{:S(2)}, u32[]{:S(2)}) %collective-permute-start.9) | collective-permute-done | bytes 32800 | tf_op jit(solution)/shard_map/ppermute | solution.py:27
  33.3 1.0 %collective-permute-start.11 = (bf16[64,512]{1,0:T(8,128)(2,1)S(1)}, bf16[64,512]{1,0:T(8,128)(2,1)S(1)}, u32[]{:S(2)}, u32[]{:S(2)}) collective-permute-start(bf16[64,512]{1,0:T(8,128)(2,1)S(1)} %constant_dynamic-update-slice_fusion.refs_0_), channel_id=1, source_target_pairs={{0,8},{4,12},{8,0},{12,4},{1,9},{5,13},{9,1},{13,5},{2,10},{6,14},... | collective-permute-start | bytes 196616 | tf_op jit(solution)/shard_map/ppermute | solution.py:27
  34.3 0.9 %collective-permute-start.12 = (bf16[64,512]{1,0:T(8,128)(2,1)S(1)}, bf16[64,512]{1,0:T(8,128)(2,1)S(1)}, u32[]{:S(2)}, u32[]{:S(2)}) collective-permute-start(bf16[64,512]{1,0:T(8,128)(2,1)S(1)} %constant_dynamic-update-slice_fusion.refs_0_), channel_id=1, source_target_pairs={{0,12},{4,8},{8,4},{12,0},{1,13},{5,9},{9,5},{13,1},{2,14},{6,10},... | collective-permute-start | bytes 196616 | tf_op jit(solution)/shard_map/ppermute | solution.py:27
  35.2 1.4 %shard_map.83 = (f32[2,64,128]{2,1,0:T(8,128)S(1)}, f32[8,128,64]{2,1,0:T(8,128)S(1)}, f32[2,1024,128]{2,1,0:T(8,128)S(1)}) custom-call(f32[128,128]{1,0:T(8,128)S(1)} %shard_map.79.refs_0_, f32[128,128]{1,0:T(8,128)S(1)} %collective-permute-done.4.refs_1_, bf16[2,128,128]{2,1,0:T(8,128)(2,1)S(1)} %copy-done.3, f32[3,2,64,64]{3,2,1,0:T(8,128)S(1)} %copy-done.2), custom_call_target="tpu_custom_call" | custom-call | flops 134217728 | bytes 1671168 | tf_op jit(solution)/shard_map/pallas_call | solution.py:499
  36.6 1.6 %collective-permute-done.11.refs_2_ = bf16[64,512]{1,0:T(8,128)(2,1)S(1)} collective-permute-done((bf16[64,512]{1,0:T(8,128)(2,1)S(1)}, bf16[64,512]{1,0:T(8,128)(2,1)S(1)}, u32[]{:S(2)}, u32[]{:S(2)}) %collective-permute-start.11) | collective-permute-done | bytes 65568 | tf_op jit(solution)/shard_map/ppermute | solution.py:27
  38.8 1.1 %shard_map.84 = (f32[2,8,512]{2,1,0:T(8,128)S(1)}, f32[64,128]{1,0:T(8,128)S(1)}, f32[64,128]{1,0:T(8,128)S(1)}, f32[64,128]{1,0:T(8,128)S(1)}, f32[64,128]{1,0:T(8,128)S(1)}) custom-call(bf16[64,512]{1,0:T(8,128)(2,1)S(1)} %constant_dynamic-update-slice_fusion.refs_0_, bf16[64,512]{1,0:T(8,128)(2,1)S(1)} %collective-permute-done.10.refs_1_, ...), custom_call_target="tpu_custom_call" | custom-call | flops 268435456 | bytes 2064384 | tf_op jit(solution)/shard_map/pallas_call | solution.py:499
  40.2 1.0 %collective-permute-start.14 = (f32[64,128]{1,0:T(8,128)S(1)}, f32[64,128]{1,0:T(8,128)S(1)}, u32[]{:S(2)}, u32[]{:S(2)}) collective-permute-start(f32[64,128]{1,0:T(8,128)S(1)} %get-tuple-element.39), channel_id=1, source_target_pairs={{0,8},{4,12},{8,0},{12,4},{1,9},{5,13},{9,1},{13,5},{2,10},{6,14},... | collective-permute-start | bytes 98312 | tf_op jit(solution)/shard_map/ppermute | solution.py:27
  41.8 2.3 %collective-permute-done.14 = f32[64,128]{1,0:T(8,128)S(1)} collective-permute-done((f32[64,128]{1,0:T(8,128)S(1)}, f32[64,128]{1,0:T(8,128)S(1)}, u32[]{:S(2)}, u32[]{:S(2)}) %collective-permute-start.14) | collective-permute-done | bytes 32800 | tf_op jit(solution)/shard_map/ppermute | solution.py:27
  44.7 1.9 %collective-permute-start.16 = (f32[64,128]{1,0:T(8,128)S(1)}, f32[64,128]{1,0:T(8,128)S(1)}, u32[]{:S(2)}, u32[]{:S(2)}) collective-permute-start(f32[64,128]{1,0:T(8,128)S(1)} %add_add_fusion), channel_id=1, source_target_pairs={{0,1},{1,0},{2,3},{3,2},{4,5},{5,4},{6,7},{7,6},{8,9},{9,8},{10,11... | collective-permute-start | bytes 98312 | tf_op jit(solution)/shard_map/ppermute | solution.py:27
  46.6 2.1 %collective-permute-done.16 = f32[64,128]{1,0:T(8,128)S(1)} collective-permute-done((f32[64,128]{1,0:T(8,128)S(1)}, f32[64,128]{1,0:T(8,128)S(1)}, u32[]{:S(2)}, u32[]{:S(2)}) %collective-permute-start.16) | collective-permute-done | bytes 32800 | tf_op jit(solution)/shard_map/ppermute | solution.py:27
  48.7 2.7 %collective-permute-start.17 = (f32[64,128]{1,0:T(8,128)S(1)}, f32[64,128]{1,0:T(8,128)S(1)}, u32[]{:S(2)}, u32[]{:S(2)}) collective-permute-start(f32[64,128]{1,0:T(8,128)S(1)} %add.15.refs_0_), channel_id=1, source_target_pairs={{0,2},{1,3},{2,0},{3,1},{4,6},{5,7},{6,4},{7,5},{8,10},{9,11},{10,... | collective-permute-start | bytes 98312 | tf_op jit(solution)/shard_map/ppermute | solution.py:27
  51.4 1.4 %shard_map.87.plane_ref = f32[8,64]{1,0:T(8,128)S(1)} custom-call(bf16[64,512]{1,0:T(8,128)(2,1)S(1)} %constant_dynamic-update-slice_fusion.refs_0_, bf16[64,512]{1,0:T(8,128)(2,1)S(1)} %collective-permute-done.10.refs_1_, bf16[64,512]{1,0:T(8,128)(2,1)S(1)} %collective-permute-done.11.refs_2_, bf16[64,512]{1,0:T(8,128)(2,1)S(1)} %collective-permute-done.12.refs_3_, ...), custom_call_target="tpu_custom_call" | custom-call | flops 536870912 | bytes 1738752 | tf_op jit(solution)/shard_map/pallas_call | solution.py:499
  53.6 1.1 %collective-permute-start.19 = (f32[64,128]{1,0:T(8,128)S(1)}, f32[64,128]{1,0:T(8,128)S(1)}, u32[]{:S(2)}, u32[]{:S(2)}) collective-permute-start(f32[64,128]{1,0:T(8,128)S(1)} %shard_map.86.refs_0_), channel_id=1, source_target_pairs={{0,8},{4,12},{8,0},{12,4},{1,9},{5,13},{9,1},{13,5},{2,10},{6,14},... | collective-permute-start | bytes 98312 | tf_op jit(solution)/shard_map/ppermute | solution.py:27
  54.7 0.7 %collective-permute-start.20 = (f32[64,128]{1,0:T(8,128)S(1)}, f32[64,128]{1,0:T(8,128)S(1)}, u32[]{:S(2)}, u32[]{:S(2)}) collective-permute-start(f32[64,128]{1,0:T(8,128)S(1)} %shard_map.86.refs_0_), channel_id=1, source_target_pairs={{0,12},{4,8},{8,4},{12,0},{1,13},{5,9},{9,5},{13,1},{2,14},{6,10},... | collective-permute-start | bytes 98312 | tf_op jit(solution)/shard_map/ppermute | solution.py:27
  55.4 1.2 %shard_map.85 = bf16[64,2,4,512]{3,2,1,0:T(4,128)(2,1)} custom-call(f32[2,8,512]{2,1,0:T(8,128)S(1)} %get-tuple-element.35.top_ref, f32[64,512]{1,0:T(8,128)S(1)} %get-tuple-element.30.refs_7_.refs_6_.wo_ref, bf16[128,512]{1,0:T(8,128)(2,1)S(1)} %get-tuple-element.36.both_ref, bf16[512,512]{1,0:T(8,128)(2,1)S(1)} %reshape.10.refs_4_.refs_9_.field_ref), custom_call_target="tpu_custom_call" | custom-call | flops 268435456 | bytes 1343488 | tf_op jit(solution)/shard_map/pallas_call | solution.py:499
  58.0 1.0 %shard_map.89 = bf16[64,2,4,512]{3,2,1,0:T(4,128)(2,1)} custom-call(f32[64,128]{1,0:T(8,128)S(1)} %shard_map.86.refs_0_, f32[64,128]{1,0:T(8,128)S(1)} %collective-permute-done.18.refs_1_, f32[64,128]{1,0:T(8,128)S(1)} %collective-permute-done.19.refs_2_, f32[64,128]{1,0:T(8,128)S(1)} %collective-permute-done.20.refs_3_, f32[512,512]{1,0:T(8,128)S(1)} %shard_map.88.refs_4_), custom_call_target="tpu_custom_call" | custom-call | bytes 1703936 | tf_op jit(solution)/shard_map/pallas_call | solution.py:499
  (45 shorter events, 6.0 us)
Async XLA Ops:
  0.6 1.0 %copy-start = (bf16[64,2,4,512]{3,2,1,0:T(4,128)(2,1)S(1)}, bf16[64,2,4,512]{3,2,1,0:T(4,128)(2,1)}, u32[]{:S(2)}) copy-start(bf16[64,2,4,512]{3,2,1,0:T(4,128)(2,1)} %field_ref.1) | copy-start | bytes 1572868
  1.7 14.9 %copy-start.2 = (f32[3,2,64,64]{3,2,1,0:T(8,128)S(1)}, f32[3,2,64,64]{3,2,1,0:T(8,128)}, u32[]{:S(2)}) copy-start(f32[3,2,64,64]{3,2,1,0:T(8,128)} %refs_7_.1) | copy-start | bytes 294916
  1.7 14.9 %copy-start.4 = (bf16[64,64]{1,0:T(8,128)(2,1)S(1)}, bf16[64,64]{1,0:T(8,128)(2,1)}, u32[]{:S(2)}) copy-start(bf16[64,64]{1,0:T(8,128)(2,1)} %wv_ref.1) | copy-start | bytes 24580
  1.7 14.9 %copy-start.5 = (bf16[64,64]{1,0:T(8,128)(2,1)S(1)}, bf16[64,64]{1,0:T(8,128)(2,1)}, u32[]{:S(2)}) copy-start(bf16[64,64]{1,0:T(8,128)(2,1)} %wo_ref.1) | copy-start | bytes 24580
  3.2 18.1 %copy-start.1 = (bf16[64,2,4,512]{3,2,1,0:T(4,128)(2,1)S(1)}, bf16[64,2,4,512]{3,2,1,0:T(4,128)(2,1)}, u32[]{:S(2)}) copy-start(bf16[64,2,4,512]{3,2,1,0:T(4,128)(2,1)} %field_ref.1) | copy-start | bytes 1572868
  3.2 3.2 %collective-permute-start = (f32[72,128]{1,0:T(8,128)S(1)}, f32[72,128]{1,0:T(8,128)S(1)}, u32[]{:S(2)}, u32[]{:S(2)}) collective-permute-start(f32[72,128]{1,0:T(8,128)S(1)} %get-tuple-element.24), channel_id=1, source_target_pairs={{0,4},{4,0},{8,12},{12,8},{1,5},{5,1},{9,13},{13,9},{2,6},{6,2},{1... | collective-permute-start | bytes 110600 | tf_op jit(solution)/shard_map/ppermute | solution.py:27
  3.8 4.6 %collective-permute-start.1 = (f32[72,128]{1,0:T(8,128)S(1)}, f32[72,128]{1,0:T(8,128)S(1)}, u32[]{:S(2)}, u32[]{:S(2)}) collective-permute-start(f32[72,128]{1,0:T(8,128)S(1)} %get-tuple-element.25), channel_id=1, source_target_pairs={{0,8},{4,12},{8,0},{12,4},{1,9},{5,13},{9,1},{13,5},{2,10},{6,14},... | collective-permute-start | bytes 110600 | tf_op jit(solution)/shard_map/ppermute | solution.py:27
  6.3 3.4 %collective-permute-start.2 = (f32[72,128]{1,0:T(8,128)S(1)}, f32[72,128]{1,0:T(8,128)S(1)}, u32[]{:S(2)}, u32[]{:S(2)}) collective-permute-start(f32[72,128]{1,0:T(8,128)S(1)} %get-tuple-element.26), channel_id=1, source_target_pairs={{0,12},{4,8},{8,4},{12,0},{1,13},{5,9},{9,5},{13,1},{2,14},{6,10},... | collective-permute-start | bytes 110600 | tf_op jit(solution)/shard_map/ppermute | solution.py:27
  9.8 4.2 %collective-permute-start.3 = (f32[96,128]{1,0:T(8,128)S(1)}, f32[96,128]{1,0:T(8,128)S(1)}, u32[]{:S(2)}, u32[]{:S(2)}) collective-permute-start(f32[96,128]{1,0:T(8,128)S(1)} %shard_map.78.refs_0_), channel_id=1, source_target_pairs={{0,1},{1,0},{2,3},{3,2},{4,5},{5,4},{6,7},{7,6},{8,9},{9,8},{10,11... | collective-permute-start | bytes 147464 | tf_op jit(solution)/shard_map/ppermute | solution.py:27
  13.9 5.2 %collective-permute-start.4 = (f32[128,128]{1,0:T(8,128)S(1)}, f32[128,128]{1,0:T(8,128)S(1)}, u32[]{:S(2)}, u32[]{:S(2)}) collective-permute-start(f32[128,128]{1,0:T(8,128)S(1)} %shard_map.79.refs_0_), channel_id=1, source_target_pairs={{0,2},{1,3},{2,0},{3,1},{4,6},{5,7},{6,4},{7,5},{8,10},{9,11},{10,... | collective-permute-start | bytes 196616 | tf_op jit(solution)/shard_map/ppermute | solution.py:27
  19.4 2.1 %copy-start.6 = (bf16[64,2,4,512]{3,2,1,0:T(4,128)(2,1)S(1)}, bf16[64,2,4,512]{3,2,1,0:T(4,128)(2,1)}, u32[]{:S(2)}) copy-start(bf16[64,2,4,512]{3,2,1,0:T(4,128)(2,1)} %param.7) | copy-start | bytes 1572868
  19.4 2.2 %collective-permute-start.5 = (bf16[128,128]{1,0:T(8,128)(2,1)S(1)}, bf16[128,128]{1,0:T(8,128)(2,1)S(1)}, u32[]{:S(2)}, u32[]{:S(2)}) collective-permute-start(bf16[128,128]{1,0:T(8,128)(2,1)S(1)} %get-tuple-element.28.refs_0_), channel_id=1, source_target_pairs={{0,4},{4,0},{8,12},{12,8},{1,5},{5,1},{9,13},{13,9},{2,6},{6,2},{1... | collective-permute-start | bytes 98312 | tf_op jit(solution)/shard_map/ppermute | solution.py:27
  19.4 4.1 %collective-permute-start.6 = (bf16[128,128]{1,0:T(8,128)(2,1)S(1)}, bf16[128,128]{1,0:T(8,128)(2,1)S(1)}, u32[]{:S(2)}, u32[]{:S(2)}) collective-permute-start(bf16[128,128]{1,0:T(8,128)(2,1)S(1)} %get-tuple-element.28.refs_0_), channel_id=1, source_target_pairs={{0,8},{4,12},{8,0},{12,4},{1,9},{5,13},{9,1},{13,5},{2,10},{6,14},... | collective-permute-start | bytes 98312 | tf_op jit(solution)/shard_map/ppermute | solution.py:27
  20.3 3.6 %collective-permute-start.7 = (bf16[128,128]{1,0:T(8,128)(2,1)S(1)}, bf16[128,128]{1,0:T(8,128)(2,1)S(1)}, u32[]{:S(2)}, u32[]{:S(2)}) collective-permute-start(bf16[128,128]{1,0:T(8,128)(2,1)S(1)} %get-tuple-element.28.refs_0_), channel_id=1, source_target_pairs={{0,12},{4,8},{8,4},{12,0},{1,13},{5,9},{9,5},{13,1},{2,14},{6,10},... | collective-permute-start | bytes 98312 | tf_op jit(solution)/shard_map/ppermute | solution.py:27
  24.7 3.8 %collective-permute-start.8 = (bf16[16,512]{1,0:T(8,128)(2,1)S(1)}, bf16[16,512]{1,0:T(8,128)(2,1)S(1)}, u32[]{:S(2)}, u32[]{:S(2)}) collective-permute-start(bf16[16,512]{1,0:T(8,128)(2,1)S(1)} %get-tuple-element.31), channel_id=1, source_target_pairs={{0,1},{1,0},{2,3},{3,2},{4,5},{5,4},{6,7},{7,6},{8,9},{9,8},{10,11... | collective-permute-start | bytes 49160 | tf_op jit(solution)/shard_map/ppermute | solution.py:27
  28.5 6.7 %copy-start.3 = (bf16[2,128,128]{2,1,0:T(8,128)(2,1)S(1)}, bf16[2,128,128]{2,1,0:T(8,128)(2,1)}, u32[]{:S(2)}) copy-start(bf16[2,128,128]{2,1,0:T(8,128)(2,1)} %constant.2.clone.refs_2_.refs_6_) | copy-start | bytes 196612
  28.5 4.8 %collective-permute-start.9 = (bf16[32,512]{1,0:T(8,128)(2,1)S(1)}, bf16[32,512]{1,0:T(8,128)(2,1)S(1)}, u32[]{:S(2)}, u32[]{:S(2)}) collective-permute-start(bf16[32,512]{1,0:T(8,128)(2,1)S(1)} %pad_maximum_fusion), channel_id=1, source_target_pairs={{0,2},{1,3},{2,0},{3,1},{4,6},{5,7},{6,4},{7,5},{8,10},{9,11},{10,... | collective-permute-start | bytes 98312 | tf_op jit(solution)/shard_map/ppermute | solution.py:27
  33.3 3.3 %collective-permute-start.10 = (bf16[64,512]{1,0:T(8,128)(2,1)S(1)}, bf16[64,512]{1,0:T(8,128)(2,1)S(1)}, u32[]{:S(2)}, u32[]{:S(2)}) collective-permute-start(bf16[64,512]{1,0:T(8,128)(2,1)S(1)} %constant_dynamic-update-slice_fusion.refs_0_), channel_id=1, source_target_pairs={{0,4},{4,0},{8,12},{12,8},{1,5},{5,1},{9,13},{13,9},{2,6},{6,2},{1... | collective-permute-start | bytes 196616 | tf_op jit(solution)/shard_map/ppermute | solution.py:27
  33.3 4.9 %collective-permute-start.11 = (bf16[64,512]{1,0:T(8,128)(2,1)S(1)}, bf16[64,512]{1,0:T(8,128)(2,1)S(1)}, u32[]{:S(2)}, u32[]{:S(2)}) collective-permute-start(bf16[64,512]{1,0:T(8,128)(2,1)S(1)} %constant_dynamic-update-slice_fusion.refs_0_), channel_id=1, source_target_pairs={{0,8},{4,12},{8,0},{12,4},{1,9},{5,13},{9,1},{13,5},{2,10},{6,14},... | collective-permute-start | bytes 196616 | tf_op jit(solution)/shard_map/ppermute | solution.py:27
  34.3 4.5 %collective-permute-start.12 = (bf16[64,512]{1,0:T(8,128)(2,1)S(1)}, bf16[64,512]{1,0:T(8,128)(2,1)S(1)}, u32[]{:S(2)}, u32[]{:S(2)}) collective-permute-start(bf16[64,512]{1,0:T(8,128)(2,1)S(1)} %constant_dynamic-update-slice_fusion.refs_0_), channel_id=1, source_target_pairs={{0,12},{4,8},{8,4},{12,0},{1,13},{5,9},{9,5},{13,1},{2,14},{6,10},... | collective-permute-start | bytes 196616 | tf_op jit(solution)/shard_map/ppermute | solution.py:27
  39.9 1.9 %collective-permute-start.13 = (f32[64,128]{1,0:T(8,128)S(1)}, f32[64,128]{1,0:T(8,128)S(1)}, u32[]{:S(2)}, u32[]{:S(2)}) collective-permute-start(f32[64,128]{1,0:T(8,128)S(1)} %get-tuple-element.38), channel_id=1, source_target_pairs={{0,4},{4,0},{8,12},{12,8},{1,5},{5,1},{9,13},{13,9},{2,6},{6,2},{1... | collective-permute-start | bytes 98312 | tf_op jit(solution)/shard_map/ppermute | solution.py:27
  40.2 3.9 %collective-permute-start.14 = (f32[64,128]{1,0:T(8,128)S(1)}, f32[64,128]{1,0:T(8,128)S(1)}, u32[]{:S(2)}, u32[]{:S(2)}) collective-permute-start(f32[64,128]{1,0:T(8,128)S(1)} %get-tuple-element.39), channel_id=1, source_target_pairs={{0,8},{4,12},{8,0},{12,4},{1,9},{5,13},{9,1},{13,5},{2,10},{6,14},... | collective-permute-start | bytes 98312 | tf_op jit(solution)/shard_map/ppermute | solution.py:27
  41.2 3.5 %collective-permute-start.15 = (f32[64,128]{1,0:T(8,128)S(1)}, f32[64,128]{1,0:T(8,128)S(1)}, u32[]{:S(2)}, u32[]{:S(2)}) collective-permute-start(f32[64,128]{1,0:T(8,128)S(1)} %get-tuple-element.40), channel_id=1, source_target_pairs={{0,12},{4,8},{8,4},{12,0},{1,13},{5,9},{9,5},{13,1},{2,14},{6,10},... | collective-permute-start | bytes 98312 | tf_op jit(solution)/shard_map/ppermute | solution.py:27
  44.7 4.0 %collective-permute-start.16 = (f32[64,128]{1,0:T(8,128)S(1)}, f32[64,128]{1,0:T(8,128)S(1)}, u32[]{:S(2)}, u32[]{:S(2)}) collective-permute-start(f32[64,128]{1,0:T(8,128)S(1)} %add_add_fusion), channel_id=1, source_target_pairs={{0,1},{1,0},{2,3},{3,2},{4,5},{5,4},{6,7},{7,6},{8,9},{9,8},{10,11... | collective-permute-start | bytes 98312 | tf_op jit(solution)/shard_map/ppermute | solution.py:27
  48.7 4.8 %collective-permute-start.17 = (f32[64,128]{1,0:T(8,128)S(1)}, f32[64,128]{1,0:T(8,128)S(1)}, u32[]{:S(2)}, u32[]{:S(2)}) collective-permute-start(f32[64,128]{1,0:T(8,128)S(1)} %add.15.refs_0_), channel_id=1, source_target_pairs={{0,2},{1,3},{2,0},{3,1},{4,6},{5,7},{6,4},{7,5},{8,10},{9,11},{10,... | collective-permute-start | bytes 98312 | tf_op jit(solution)/shard_map/ppermute | solution.py:27
  53.5 3.7 %collective-permute-start.18 = (f32[64,128]{1,0:T(8,128)S(1)}, f32[64,128]{1,0:T(8,128)S(1)}, u32[]{:S(2)}, u32[]{:S(2)}) collective-permute-start(f32[64,128]{1,0:T(8,128)S(1)} %shard_map.86.refs_0_), channel_id=1, source_target_pairs={{0,4},{4,0},{8,12},{12,8},{1,5},{5,1},{9,13},{13,9},{2,6},{6,2},{1... | collective-permute-start | bytes 98312 | tf_op jit(solution)/shard_map/ppermute | solution.py:27
  53.6 4.0 %collective-permute-start.19 = (f32[64,128]{1,0:T(8,128)S(1)}, f32[64,128]{1,0:T(8,128)S(1)}, u32[]{:S(2)}, u32[]{:S(2)}) collective-permute-start(f32[64,128]{1,0:T(8,128)S(1)} %shard_map.86.refs_0_), channel_id=1, source_target_pairs={{0,8},{4,12},{8,0},{12,4},{1,9},{5,13},{9,1},{13,5},{2,10},{6,14},... | collective-permute-start | bytes 98312 | tf_op jit(solution)/shard_map/ppermute | solution.py:27
  54.7 3.3 %collective-permute-start.20 = (f32[64,128]{1,0:T(8,128)S(1)}, f32[64,128]{1,0:T(8,128)S(1)}, u32[]{:S(2)}, u32[]{:S(2)}) collective-permute-start(f32[64,128]{1,0:T(8,128)S(1)} %shard_map.86.refs_0_), channel_id=1, source_target_pairs={{0,12},{4,8},{8,4},{12,0},{1,13},{5,9},{9,5},{13,1},{2,14},{6,10},... | collective-permute-start | bytes 98312 | tf_op jit(solution)/shard_map/ppermute | solution.py:27

commit v7 on v6

--- a/solution.py
+++ b/solution.py
@@ -200,13 +200,6 @@
 
 def number(shape, dim):
     return lax.broadcasted_iota(jnp.int32, shape, dim)
-
-
-def put_quarters(part_ref, total, outs):
-    for index in range(part_ref.shape[0]):
-        part_ref[index] = total[:, index * LANES : (index + 1) * LANES]
-    for step, out in enumerate(outs):
-        out[0:WIDTH, :] = part_ref[lax.axis_index("gx") ^ step]
 
 
 def join_quarters(part_ref, quarters):
@@ -292,7 +285,7 @@
 
 
 def factor_kernel(places, *refs):
-    parts, (wz_ref, both_ref, feat_ref) = refs[:-3], refs[-3:]
+    parts, feat_ref = refs[:-1], refs[-1]
     total = parts[0][0:WIDTH, :]
     for part in parts[1:]:
         total = total + part[0:WIDTH, :]
@@ -301,18 +294,13 @@
     normed = pooled * inverse
     feat_ref[0:WIDTH, :] = normed
     feat_ref[WIDTH:, :] = jnp.broadcast_to(inverse, (HEAD_DIM, LANES))
-    both_ref[...] = mul_near(wz_ref[...], normed).astype(jnp.bfloat16)
-
-
-def pull_kernel(places, *refs):
-    parts, (feat_ref, out_ref) = refs[:-2], refs[-2:]
-    found = parts[0][...]
-    for part in parts[1:]:
-        found = found + part[...]
-    normed = feat_ref[0:WIDTH, :]
-    inverse = feat_ref[WIDTH : WIDTH + 1, :]
-    found = inverse * (found - normed * jnp.mean(found * normed, axis=0, keepdims=True))
-    out_ref[...] = found * (1.0 / places)
+
+
+def add_pull_kernel(*refs):
+    total = refs[0][...].astype(jnp.float32)
+    for part in refs[1:-1]:
+        total = total + part[...].astype(jnp.float32)
+    refs[-1][...] = total.astype(jnp.bfloat16)
 
 
 def by_head(part):
@@ -362,14 +350,16 @@
     mix_ref[1] = backward
 
 
-def coef_kernel(*refs):
-    quarters, rest = refs[:-8], refs[-8:]
-    field_ref, cot_ref, wv_ref, wo_ref, send_ref, both_ref, part_ref = rest[1:]
-    quarters = quarters + rest[:1]
+def coef_kernel(spans, *refs):
+    quarters, refs = refs[:spans], refs[spans:]
+    wz_ref, field_ref, cot_ref, wv_ref, wo_ref, send_ref, both_ref, feat_ref, part_ref = refs
     rows, depth = field_ref.shape
     cells = rows // WIDTH
     wide = HEADS * HEAD_DIM * HEAD_DIM
-    both = join_quarters(part_ref, [q[...].astype(jnp.float32) for q in quarters])
+    feat = join_quarters(part_ref, quarters)
+    feat_ref[...] = feat
+    high, low = split(feat[:WIDTH])
+    both = mul_left(wz_ref[...], high) + mul(wz_ref[...].astype(jnp.bfloat16), low)
     both_ref[...] = both.astype(jnp.bfloat16)
     query = expand(both[:WIDTH])
     keyset = expand(both[WIDTH:])
@@ -393,8 +383,7 @@
 
 def mix_kernel(factor, spans, *refs):
     lows, refs = refs[:spans], refs[spans:]
-    mix_ref, wv_ref, wo_ref, wq_ref, wk_ref, field_ref, cot_ref, top_ref = refs[:8]
-    outs, part_ref = refs[8:-1], refs[-1]
+    mix_ref, wv_ref, wo_ref, wq_ref, wk_ref, field_ref, cot_ref, top_ref, out_ref = refs
     cells = field_ref.shape[0] // WIDTH
     low_f, low_c = join_low(lows, cells)
     wide = low_f.shape[1]
@@ -417,7 +406,7 @@
         return mul_left(found[:WIDTH] + found[WIDTH:], right)
 
     found = pull(wq_ref[...], left_f, cot_ref[...]) + pull(wk_ref[...], left_c, field_ref[...])
-    put_quarters(part_ref, found, outs)
+    out_ref[...] = found.astype(jnp.bfloat16)
 
 
 def put_cells(ref, total):
@@ -484,23 +473,46 @@
     out_ref[...] = found + jnp.concatenate([plane] * columns, axis=1)
 
 
-def final_kernel(*refs):
-    quarters, (base_ref, out_ref, part_ref) = refs[:-3], refs[-3:]
-    rows, depth = base_ref.shape
-    cells = rows // WIDTH
-    found = join_quarters(part_ref, quarters)
-    total = base_ref[...].reshape(WIDTH, cells, depth) + found[:, None, :]
-    put_cells(out_ref, total)
-
-
-def run(kernel, outs, operands, places=pltpu.VMEM, flops=0, scratch=()):
-    vmem = pl.BlockSpec(memory_space=pltpu.VMEM)
+def final_kernel(places, *refs):
+    parts, (feat_ref, base_ref, out_ref, data_ref, semaphores) = refs[:-5], refs[-5:]
+    depth = base_ref.shape[1]
+    _, rows_x, rows_y, _ = data_ref.shape
+    found = parts[0][...].astype(jnp.float32)
+    for part in parts[1:]:
+        found = found + part[...].astype(jnp.float32)
+    normed = feat_ref[0:WIDTH, :]
+    inverse = feat_ref[WIDTH : WIDTH + 1, :]
+    found = inverse * (found - normed * jnp.mean(found * normed, axis=0, keepdims=True))
+    found = found * (1.0 / places)
+    cells = rows_x * rows_y
+    chunks = semaphores.shape[0]
+    size = WIDTH // chunks
+    copies = []
+    for index in range(chunks):
+        rows = slice(index * size, (index + 1) * size)
+        base = base_ref[index * size * cells : (index + 1) * size * cells, :]
+        total = base.reshape(size, cells, depth) + found[rows][:, None, :]
+        for at_x in range(rows_x):
+            part = total[:, at_x * rows_y : (at_x + 1) * rows_y, :]
+            data_ref[rows, at_x, :, :] = part.astype(jnp.bfloat16)
+        copy = pltpu.make_async_copy(
+            data_ref.at[pl.ds(index * size, size)],
+            out_ref.at[pl.ds(index * size, size)],
+            semaphores.at[index],
+        )
+        copy.start()
+        copies.append(copy)
+    for copy in copies:
+        copy.wait()
+
+
+def run(kernel, outs, operands, places=pltpu.VMEM, target=pltpu.VMEM, flops=0, scratch=()):
     moved = sum(x.size * x.dtype.itemsize for x in tuple(operands) + tuple(outs))
     found = pl.pallas_call(
         kernel,
         out_shape=tuple(outs),
         in_specs=[pl.BlockSpec(memory_space=places)] * len(operands),
-        out_specs=tuple(vmem for _ in outs),
+        out_specs=tuple(pl.BlockSpec(memory_space=target) for _ in outs),
         scratch_shapes=list(scratch),
         compiler_params=pltpu.CompilerParams(vmem_limit_bytes=16 * 1024 * 1024),
         cost_estimate=pl.CostEstimate(flops=flops, bytes_accessed=moved, transcendentals=0),
@@ -532,8 +544,8 @@
 
     cols = field.reshape(rows, depth)
     cots = cotangent.reshape(rows, depth)
-    block = like((WIDTH, LANES), f32)
     parts = pltpu.VMEM((span_x, WIDTH, LANES), f32)
+    chunked = [pltpu.VMEM(field.shape, bf16), pltpu.SemaphoreType.DMA((4,))]
     factor_z = 1.0 / math.sqrt(HEAD_DIM * depth)
     cube = rows * wide * depth * 2
 
@@ -545,9 +557,9 @@
         )
 
     sums = run(
-        sums_kernel, [like((WIDTH + cells, LANES), f32)] * span_x, (field,), places=pl.ANY,
+        sums_kernel, [like((WIDTH + cells, LANES), f32)] * span_x, (field,), places=pltpu.HBM,
         flops=cube // 4,
-        scratch=[parts, pltpu.VMEM(field.shape, bf16), pltpu.SemaphoreType.DMA((4,))],
+        scratch=[parts] + chunked,
     )
     wv, wo, wq, wk, wz = run(
         prepare_kernel,
@@ -559,18 +571,11 @@
     def add(sent, size):
         return run(add_kernel, [like((WIDTH + size * cells, LANES), f32)], sent)
 
-    def pair(part, step):
-        return part, swap(part, "gy", span_y, step)
-
-    total = add(swaps(sums, "gx", span_x), span_x)
-    steps = [1 << level for level in range(span_y.bit_length() - 1)]
-    for step in steps[:-1]:
-        total = add(pair(total, step), 2 * step * span_x)
-    totals = pair(total, steps[-1])
-    mine, feat_z = run(
+    totals = swaps(add(swaps(sums, "gx", span_x), span_x), "gy", span_y)
+    mine = run(
         functools.partial(factor_kernel, grid_x * grid_y),
-        [like((2 * WIDTH, LANES), bf16), like((WIDTH + HEAD_DIM, LANES), f32)],
-        totals + (wz,),
+        [like((WIDTH + HEAD_DIM, LANES), f32)],
+        totals,
     )
     mix, feat, full = run(
         functools.partial(plane_kernel, cells, span_x, lengths),
@@ -579,27 +584,24 @@
         totals + (same, qk_weight),
         flops=cube // 2,
     )
-    send, both = run(
-        coef_kernel,
-        [like((2 * cells, wide), bf16), like((2 * WIDTH, depth), bf16)],
-        swaps(mine, "gx", span_x) + (cols, cots, wv, wo),
+    send, both, feat_z = run(
+        functools.partial(coef_kernel, span_x),
+        [like((2 * cells, wide), bf16), like((2 * WIDTH, depth), bf16),
+         like((WIDTH + HEAD_DIM, depth), f32)],
+        swaps(mine, "gx", span_x) + (wz, cols, cots, wv, wo),
         flops=2 * cube,
-        scratch=[pltpu.VMEM((span_x, 2 * WIDTH, LANES), f32)],
-    )
-    low = send
-    for step in steps:
-        low = jnp.concatenate(pair(low, step), axis=0)
+        scratch=[pltpu.VMEM((span_x, WIDTH + HEAD_DIM, LANES), f32)],
+    )
+    low = jnp.concatenate(swaps(send, "gy", span_y), axis=0)
     lows = swaps(low, "gx", span_x)
-    top, *pulls = run(
+    pulled = like((WIDTH, depth), bf16)
+    top, total = run(
         functools.partial(mix_kernel, factor_z, span_x),
-        [like((2, cells, wide), f32)] + [block] * span_x,
+        [like((2, cells, wide), f32), pulled],
         lows + (mix, wv, wo, wq, wk, cols, cots),
         flops=cube,
-        scratch=[parts],
-    )
-    total = sum(swaps(pulls, "gx", span_x))
-    for step in steps[:-1]:
-        total = sum(pair(total, step))
+    )
+    total = run(add_pull_kernel, [pulled], swaps(total, "gx", span_x))
     layer_output = run(
         output_kernel, [like(field.shape, bf16)], (top, wo, both, cols), flops=cube
     )
@@ -609,17 +611,13 @@
         lows + (feat, full, same, qk_weight),
         flops=2 * cube,
     )
-    mine = run(
-        functools.partial(pull_kernel, grid_x * grid_y),
-        [block],
-        pair(total, steps[-1]) + (feat_z,),
-    )
     base = run(base_kernel, [like((rows, depth), f32)], (top, wv, both, cots, plane), flops=cube)
     field_grad = run(
-        final_kernel,
+        functools.partial(final_kernel, grid_x * grid_y),
         [like(field.shape, bf16)],
-        swaps(mine, "gx", span_x) + (base,),
-        scratch=[parts],
+        swaps(total, "gy", span_y) + (feat_z, base),
+        target=pltpu.HBM,
+        scratch=chunked,
     )
     return (layer_output, field_grad)
 
@@ -633,7 +631,6 @@
         places = grid_x // mesh.shape["groups"] * grid_y
         small = places == LANES and places == 8 * count
         small = small and depth == LANES * mesh.shape["gx"] and count & (count - 1) == 0
-        small = small and mesh.shape["gy"] > 1
         return jax.shard_map(
             per_device_kernels if small else per_device,
             mesh=mesh,

time: 59.2 us -> 53.2 us (0.90)
  waiting for transfers between devices: 23.5 us -> 18.4 us
  starting transfers between devices: 23.9 us -> 22.3 us
  local copies, waits for them, and re-layouts: 1.32 us -> 2.09 us
    ppermute x21, waiting for transfers between devices: 23.5 us -> 18.4 us  [swap(): return lax.ppermute(part, axis, [(i, i ^ step) for i in range(size)])]
    ppermute x21, starting transfers between devices: 23.9 us -> 22.3 us  [swap(): return lax.ppermute(part, axis, [(i, i ^ step) for i in range(size)])]
    unnamed x16 -> x17, local copies, waits for them, and re-layouts: 1.07 us -> 1.84 us
    pallas_call x13 -> x12, Pallas kernels: 9.46 us -> 9.42 us  [run(): pl.pallas_call(kernel, out_shape=tuple(outs), in_specs=[pl.BlockSpec(memo...]
  transfers between devices with their start and end apart: 21 -> 21, of which waited for: 16 -> 14; matrix products, arithmetic and copies ran while one was open for 0% -> 0% of each run, Pallas kernels for 8% -> 9%
where the time goes in v7:
time: 53.2 us; the launch traced here: 53 us
  starting transfers between devices  22.3 us (42%)
  waiting for transfers between devices  18.4 us (35%)
  Pallas kernels  9.42 us (18%)
  local copies, waits for them, and re-layouts  2.09 us (4%)
  between operations  0.79 us (1%)
    ppermute x21, starting transfers between devices, swap(): return lax.ppermute(part, axis, [(i, i ^ step) for i in range(size)])  22.3 us
    ppermute x21, waiting for transfers between devices, swap(): return lax.ppermute(part, axis, [(i, i ^ step) for i in range(size)])  18.4 us
    pallas_call x12, Pallas kernels, run(): pl.pallas_call(kernel, out_shape=tuple(outs), in_specs=[pl.BlockSpec(memo...  9.42 us
    unnamed x17, local copies, waits for them, and re-layouts  1.84 us
  transfers between devices with their start and end apart: 21, of which 14 were waited for; matrix products, arithmetic and copies ran while one was open for 0% of the time, Pallas kernels for 9%

profile of v7, /device:TPU:0, one launch (start us, length us, event | category | flops | bytes accessed | tf_op | source)
XLA Modules:
  0.0 53.0 jit_solution(751559840508478598)
XLA Ops:
  0.6 1.0 %copy-done = bf16[64,2,4,512]{3,2,1,0:T(4,128)(2,1)S(1)} copy-done((bf16[64,2,4,512]{3,2,1,0:T(4,128)(2,1)S(1)}, bf16[64,2,4,512]{3,2,1,0:T(4,128)(2,1)}, u32[]{:S(2)}) %copy-start) | copy-done | bytes 524312
  1.7 1.5 %shard_map.77 = (f32[72,128]{1,0:T(8,128)S(1)}, f32[72,128]{1,0:T(8,128)S(1)}, f32[72,128]{1,0:T(8,128)S(1)}, f32[72,128]{1,0:T(8,128)S(1)}) custom-call(bf16[64,2,4,512]{3,2,1,0:T(4,128)(2,1)S(1)} %copy-done), custom_call_target="tpu_custom_call" | custom-call | flops 67108864 | bytes 671744 | tf_op jit(solution)/shard_map/pallas_call | solution.py:511
  3.7 2.6 %collective-permute-start.1 = (f32[72,128]{1,0:T(8,128)S(1)}, f32[72,128]{1,0:T(8,128)S(1)}, u32[]{:S(2)}, u32[]{:S(2)}) collective-permute-start(f32[72,128]{1,0:T(8,128)S(1)} %get-tuple-element.21), channel_id=1, source_target_pairs={{0,8},{4,12},{8,0},{12,4},{1,9},{5,13},{9,1},{13,5},{2,10},{6,14},... | collective-permute-start | bytes 110600 | tf_op jit(solution)/shard_map/ppermute | solution.py:27
  6.4 2.0 %collective-permute-done.1.refs_2_ = f32[72,128]{1,0:T(8,128)S(1)} collective-permute-done((f32[72,128]{1,0:T(8,128)S(1)}, f32[72,128]{1,0:T(8,128)S(1)}, u32[]{:S(2)}, u32[]{:S(2)}) %collective-permute-start.1) | collective-permute-done | bytes 36896 | tf_op jit(solution)/shard_map/ppermute | solution.py:27
  8.4 1.4 %collective-permute-done.2.refs_3_ = f32[72,128]{1,0:T(8,128)S(1)} collective-permute-done((f32[72,128]{1,0:T(8,128)S(1)}, f32[72,128]{1,0:T(8,128)S(1)}, u32[]{:S(2)}, u32[]{:S(2)}) %collective-permute-start.2) | collective-permute-done | bytes 36896 | tf_op jit(solution)/shard_map/ppermute | solution.py:27
  9.7 3.7 %collective-permute-start.5 = (f32[96,128]{1,0:T(8,128)S(1)}, f32[96,128]{1,0:T(8,128)S(1)}, u32[]{:S(2)}, u32[]{:S(2)}) collective-permute-start(f32[96,128]{1,0:T(8,128)S(1)} %shard_map.78.refs_0_), channel_id=1, source_target_pairs={{0,3},{1,2},{2,1},{3,0},{4,7},{5,6},{6,5},{7,4},{8,11},{9,10},{10,... | collective-permute-start | bytes 147464 | tf_op jit(solution)/shard_map/ppermute | solution.py:27
  13.4 0.8 %collective-permute-start.3 = (f32[96,128]{1,0:T(8,128)S(1)}, f32[96,128]{1,0:T(8,128)S(1)}, u32[]{:S(2)}, u32[]{:S(2)}) collective-permute-start(f32[96,128]{1,0:T(8,128)S(1)} %shard_map.78.refs_0_), channel_id=1, source_target_pairs={{0,1},{1,0},{2,3},{3,2},{4,5},{5,4},{6,7},{7,6},{8,9},{9,8},{10,11... | collective-permute-start | bytes 147464 | tf_op jit(solution)/shard_map/ppermute | solution.py:27
  14.2 1.6 %collective-permute-done.5.refs_3_ = f32[96,128]{1,0:T(8,128)S(1)} collective-permute-done((f32[96,128]{1,0:T(8,128)S(1)}, f32[96,128]{1,0:T(8,128)S(1)}, u32[]{:S(2)}, u32[]{:S(2)}) %collective-permute-start.5) | collective-permute-done | bytes 49184 | tf_op jit(solution)/shard_map/ppermute | solution.py:27
  15.8 2.6 %collective-permute-done.4.refs_2_ = f32[96,128]{1,0:T(8,128)S(1)} collective-permute-done((f32[96,128]{1,0:T(8,128)S(1)}, f32[96,128]{1,0:T(8,128)S(1)}, u32[]{:S(2)}, u32[]{:S(2)}) %collective-permute-start.4) | collective-permute-done | bytes 49184 | tf_op jit(solution)/shard_map/ppermute | solution.py:27
  18.6 0.9 %collective-permute-start.7 = (f32[72,128]{1,0:T(8,128)S(1)}, f32[72,128]{1,0:T(8,128)S(1)}, u32[]{:S(2)}, u32[]{:S(2)}) collective-permute-start(f32[72,128]{1,0:T(8,128)S(1)} %shard_map.79.refs_0_), channel_id=1, source_target_pairs={{0,8},{4,12},{8,0},{12,4},{1,9},{5,13},{9,1},{13,5},{2,10},{6,14},... | collective-permute-start | bytes 110600 | tf_op jit(solution)/shard_map/ppermute | solution.py:27
  19.5 0.9 %collective-permute-start.6 = (f32[72,128]{1,0:T(8,128)S(1)}, f32[72,128]{1,0:T(8,128)S(1)}, u32[]{:S(2)}, u32[]{:S(2)}) collective-permute-start(f32[72,128]{1,0:T(8,128)S(1)} %shard_map.79.refs_0_), channel_id=1, source_target_pairs={{0,4},{4,0},{8,12},{12,8},{1,5},{5,1},{9,13},{13,9},{2,6},{6,2},{1... | collective-permute-start | bytes 110600 | tf_op jit(solution)/shard_map/ppermute | solution.py:27
  21.9 1.0 %collective-permute-done.7.refs_2_ = f32[72,128]{1,0:T(8,128)S(1)} collective-permute-done((f32[72,128]{1,0:T(8,128)S(1)}, f32[72,128]{1,0:T(8,128)S(1)}, u32[]{:S(2)}, u32[]{:S(2)}) %collective-permute-start.7) | collective-permute-done | bytes 36896 | tf_op jit(solution)/shard_map/ppermute | solution.py:27
  22.9 1.0 %shard_map.81 = (bf16[16,512]{1,0:T(8,128)(2,1)S(1)}, bf16[128,512]{1,0:T(8,128)(2,1)S(1)}, f32[72,512]{1,0:T(8,128)S(1)}) custom-call(f32[72,128]{1,0:T(8,128)S(1)} %shard_map.79.refs_0_, f32[72,128]{1,0:T(8,128)S(1)} %collective-permute-done.6.refs_1_, f32[72,128]{1,0:T(8,128)S(1)} %collective-permute-done.7.refs_2_, ...), custom_call_target="tpu_custom_call" | custom-call | flops 536870912 | bytes 1785856 | tf_op jit(solution)/shard_map/pallas_call | solution.py:511
  23.9 2.3 %collective-permute-start.11 = (bf16[16,512]{1,0:T(8,128)(2,1)S(1)}, bf16[16,512]{1,0:T(8,128)(2,1)S(1)}, u32[]{:S(2)}, u32[]{:S(2)}) collective-permute-start(bf16[16,512]{1,0:T(8,128)(2,1)S(1)} %get-tuple-element.26), channel_id=1, source_target_pairs={{0,3},{1,2},{2,1},{3,0},{4,7},{5,6},{6,5},{7,4},{8,11},{9,10},{10,... | collective-permute-start | bytes 49160 | tf_op jit(solution)/shard_map/ppermute | solution.py:27
  26.4 2.0 %collective-permute-start.9 = (bf16[16,512]{1,0:T(8,128)(2,1)S(1)}, bf16[16,512]{1,0:T(8,128)(2,1)S(1)}, u32[]{:S(2)}, u32[]{:S(2)}) collective-permute-start(bf16[16,512]{1,0:T(8,128)(2,1)S(1)} %get-tuple-element.26), channel_id=1, source_target_pairs={{0,1},{1,0},{2,3},{3,2},{4,5},{5,4},{6,7},{7,6},{8,9},{9,8},{10,11... | collective-permute-start | bytes 49160 | tf_op jit(solution)/shard_map/ppermute | solution.py:27
  28.4 1.7 %collective-permute-done.9 = bf16[16,512]{1,0:T(8,128)(2,1)S(1)} collective-permute-done((bf16[16,512]{1,0:T(8,128)(2,1)S(1)}, bf16[16,512]{1,0:T(8,128)(2,1)S(1)}, u32[]{:S(2)}, u32[]{:S(2)}) %collective-permute-start.9) | collective-permute-done | bytes 16416 | tf_op jit(solution)/shard_map/ppermute | solution.py:27
  30.9 0.8 %collective-permute-start.13 = (bf16[64,512]{1,0:T(8,128)(2,1)S(1)}, bf16[64,512]{1,0:T(8,128)(2,1)S(1)}, u32[]{:S(2)}, u32[]{:S(2)}) collective-permute-start(bf16[64,512]{1,0:T(8,128)(2,1)S(1)} %constant_dynamic-update-slice_fusion.refs_0_), channel_id=1, source_target_pairs={{0,8},{4,12},{8,0},{12,4},{1,9},{5,13},{9,1},{13,5},{2,10},{6,14},... | collective-permute-start | bytes 196616 | tf_op jit(solution)/shard_map/ppermute | solution.py:27
  31.8 1.0 %collective-permute-start.12 = (bf16[64,512]{1,0:T(8,128)(2,1)S(1)}, bf16[64,512]{1,0:T(8,128)(2,1)S(1)}, u32[]{:S(2)}, u32[]{:S(2)}) collective-permute-start(bf16[64,512]{1,0:T(8,128)(2,1)S(1)} %constant_dynamic-update-slice_fusion.refs_0_), channel_id=1, source_target_pairs={{0,4},{4,0},{8,12},{12,8},{1,5},{5,1},{9,13},{13,9},{2,6},{6,2},{1... | collective-permute-start | bytes 196616 | tf_op jit(solution)/shard_map/ppermute | solution.py:27
  32.8 1.4 %shard_map.82 = (f32[2,64,128]{2,1,0:T(8,128)S(1)}, f32[8,128,64]{2,1,0:T(8,128)S(1)}, f32[2,1024,128]{2,1,0:T(8,128)S(1)}) custom-call(f32[96,128]{1,0:T(8,128)S(1)} %shard_map.78.refs_0_, f32[96,128]{1,0:T(8,128)S(1)} %collective-permute-done.3.refs_1_, f32[96,128]{1,0:T(8,128)S(1)} %collective-permute-done.4.refs_2_, ...), custom_call_target="tpu_custom_call" | custom-call | flops 134217728 | bytes 1736704 | tf_op jit(solution)/shard_map/pallas_call | solution.py:511
  34.7 1.2 %collective-permute-done.13.refs_2_ = bf16[64,512]{1,0:T(8,128)(2,1)S(1)} collective-permute-done((bf16[64,512]{1,0:T(8,128)(2,1)S(1)}, bf16[64,512]{1,0:T(8,128)(2,1)S(1)}, u32[]{:S(2)}, u32[]{:S(2)}) %collective-permute-start.13) | collective-permute-done | bytes 65568 | tf_op jit(solution)/shard_map/ppermute | solution.py:27
  35.9 1.0 %shard_map.83 = (f32[2,8,512]{2,1,0:T(8,128)S(1)}, bf16[64,512]{1,0:T(8,128)(2,1)S(1)}) custom-call(bf16[64,512]{1,0:T(8,128)(2,1)S(1)} %constant_dynamic-update-slice_fusion.refs_0_, bf16[64,512]{1,0:T(8,128)(2,1)S(1)} %collective-permute-done.12.refs_1_, bf16[64,512]{1,0:T(8,128)(2,1)S(1)} %collective-permute-done.13.refs_2_, ...), custom_call_target="tpu_custom_call" | custom-call | flops 268435456 | bytes 1998848 | tf_op jit(solution)/shard_map/pallas_call | solution.py:511
  37.0 1.0 %collective-permute-start.17 = (bf16[64,512]{1,0:T(8,128)(2,1)S(1)}, bf16[64,512]{1,0:T(8,128)(2,1)S(1)}, u32[]{:S(2)}, u32[]{:S(2)}) collective-permute-start(bf16[64,512]{1,0:T(8,128)(2,1)S(1)} %get-tuple-element.32.refs_0_), channel_id=1, source_target_pairs={{0,12},{4,8},{8,4},{12,0},{1,13},{5,9},{9,5},{13,1},{2,14},{6,10},... | collective-permute-start | bytes 196616 | tf_op jit(solution)/shard_map/ppermute | solution.py:27
  38.0 0.8 %collective-permute-start.16 = (bf16[64,512]{1,0:T(8,128)(2,1)S(1)}, bf16[64,512]{1,0:T(8,128)(2,1)S(1)}, u32[]{:S(2)}, u32[]{:S(2)}) collective-permute-start(bf16[64,512]{1,0:T(8,128)(2,1)S(1)} %get-tuple-element.32.refs_0_), channel_id=1, source_target_pairs={{0,8},{4,12},{8,0},{12,4},{1,9},{5,13},{9,1},{13,5},{2,10},{6,14},... | collective-permute-start | bytes 196616 | tf_op jit(solution)/shard_map/ppermute | solution.py:27
  38.9 1.2 %shard_map.84 = bf16[64,2,4,512]{3,2,1,0:T(4,128)(2,1)} custom-call(f32[2,8,512]{2,1,0:T(8,128)S(1)} %get-tuple-element.30.top_ref, f32[64,512]{1,0:T(8,128)S(1)} %get-tuple-element.25.refs_8_.refs_6_.wo_ref, bf16[128,512]{1,0:T(8,128)(2,1)S(1)} %get-tuple-element.31.both_ref, bf16[512,512]{1,0:T(8,128)(2,1)S(1)} %reshape.10.refs_5_.refs_9_.field_ref), custom_call_target="tpu_custom_call" | custom-call | flops 268435456 | bytes 1343488 | tf_op jit(solution)/shard_map/pallas_call | solution.py:511
  40.2 1.0 %collective-permute-done.17.refs_3_ = bf16[64,512]{1,0:T(8,128)(2,1)S(1)} collective-permute-done((bf16[64,512]{1,0:T(8,128)(2,1)S(1)}, bf16[64,512]{1,0:T(8,128)(2,1)S(1)}, u32[]{:S(2)}, u32[]{:S(2)}) %collective-permute-start.17) | collective-permute-done | bytes 65568 | tf_op jit(solution)/shard_map/ppermute | solution.py:27
  41.1 1.7 %collective-permute-done.16.refs_2_ = bf16[64,512]{1,0:T(8,128)(2,1)S(1)} collective-permute-done((bf16[64,512]{1,0:T(8,128)(2,1)S(1)}, bf16[64,512]{1,0:T(8,128)(2,1)S(1)}, u32[]{:S(2)}, u32[]{:S(2)}) %collective-permute-start.16) | collective-permute-done | bytes 65568 | tf_op jit(solution)/shard_map/ppermute | solution.py:27
  42.9 1.9 %collective-permute-start.20 = (bf16[64,512]{1,0:T(8,128)(2,1)S(1)}, bf16[64,512]{1,0:T(8,128)(2,1)S(1)}, u32[]{:S(2)}, u32[]{:S(2)}) collective-permute-start(bf16[64,512]{1,0:T(8,128)(2,1)S(1)} %shard_map.85.refs_0_), channel_id=1, source_target_pairs={{0,3},{1,2},{2,1},{3,0},{4,7},{5,6},{6,5},{7,4},{8,11},{9,10},{10,... | collective-permute-start | bytes 196616 | tf_op jit(solution)/shard_map/ppermute | solution.py:27
  44.8 0.9 %collective-permute-start.19 = (bf16[64,512]{1,0:T(8,128)(2,1)S(1)}, bf16[64,512]{1,0:T(8,128)(2,1)S(1)}, u32[]{:S(2)}, u32[]{:S(2)}) collective-permute-start(bf16[64,512]{1,0:T(8,128)(2,1)S(1)} %shard_map.85.refs_0_), channel_id=1, source_target_pairs={{0,2},{1,3},{2,0},{3,1},{4,6},{5,7},{6,4},{7,5},{8,10},{9,11},{10,... | collective-permute-start | bytes 196616 | tf_op jit(solution)/shard_map/ppermute | solution.py:27
  45.7 1.6 %collective-permute-start.18 = (bf16[64,512]{1,0:T(8,128)(2,1)S(1)}, bf16[64,512]{1,0:T(8,128)(2,1)S(1)}, u32[]{:S(2)}, u32[]{:S(2)}) collective-permute-start(bf16[64,512]{1,0:T(8,128)(2,1)S(1)} %shard_map.85.refs_0_), channel_id=1, source_target_pairs={{0,1},{1,0},{2,3},{3,2},{4,5},{5,4},{6,7},{7,6},{8,9},{9,8},{10,11... | collective-permute-start | bytes 196616 | tf_op jit(solution)/shard_map/ppermute | solution.py:27
  47.3 1.4 %shard_map.86.plane_ref = f32[8,64]{1,0:T(8,128)S(1)} custom-call(bf16[64,512]{1,0:T(8,128)(2,1)S(1)} %constant_dynamic-update-slice_fusion.refs_0_, bf16[64,512]{1,0:T(8,128)(2,1)S(1)} %collective-permute-done.12.refs_1_, bf16[64,512]{1,0:T(8,128)(2,1)S(1)} %collective-permute-done.13.refs_2_, bf16[64,512]{1,0:T(8,128)(2,1)S(1)} %collective-permute-done.14.refs_3_, ...), custom_call_target="tpu_custom_call" | custom-call | flops 536870912 | bytes 1738752 | tf_op jit(solution)/shard_map/pallas_call | solution.py:511
  49.7 2.4 %collective-permute-done.19.refs_2_ = bf16[64,512]{1,0:T(8,128)(2,1)S(1)} collective-permute-done((bf16[64,512]{1,0:T(8,128)(2,1)S(1)}, bf16[64,512]{1,0:T(8,128)(2,1)S(1)}, u32[]{:S(2)}, u32[]{:S(2)}) %collective-permute-start.19) | collective-permute-done | bytes 65568 | tf_op jit(solution)/shard_map/ppermute | solution.py:27
  52.1 0.9 %shard_map.88 = bf16[64,2,4,512]{3,2,1,0:T(4,128)(2,1)} custom-call(bf16[64,512]{1,0:T(8,128)(2,1)S(1)} %shard_map.85.refs_0_, bf16[64,512]{1,0:T(8,128)(2,1)S(1)} %collective-permute-done.18.refs_1_, bf16[64,512]{1,0:T(8,128)(2,1)S(1)} %collective-permute-done.19.refs_2_, bf16[64,512]{1,0:T(8,128)(2,1)S(1)} %collective-permute-done.20.refs_3_, ...), custom_call_target="tpu_custom_call" | custom-call | bytes 1982464 | tf_op jit(solution)/shard_map/pallas_call | solution.py:511
  (42 shorter events, 4.9 us)
Async XLA Ops:
  0.6 1.0 %copy-start = (bf16[64,2,4,512]{3,2,1,0:T(4,128)(2,1)S(1)}, bf16[64,2,4,512]{3,2,1,0:T(4,128)(2,1)}, u32[]{:S(2)}) copy-start(bf16[64,2,4,512]{3,2,1,0:T(4,128)(2,1)} %field_ref.1) | copy-start | bytes 1572868
  1.7 18.7 %copy-start.1 = (bf16[64,2,4,512]{3,2,1,0:T(4,128)(2,1)S(1)}, bf16[64,2,4,512]{3,2,1,0:T(4,128)(2,1)}, u32[]{:S(2)}) copy-start(bf16[64,2,4,512]{3,2,1,0:T(4,128)(2,1)} %field_ref.1) | copy-start | bytes 1572868
  3.2 3.2 %collective-permute-start = (f32[72,128]{1,0:T(8,128)S(1)}, f32[72,128]{1,0:T(8,128)S(1)}, u32[]{:S(2)}, u32[]{:S(2)}) collective-permute-start(f32[72,128]{1,0:T(8,128)S(1)} %get-tuple-element.20), channel_id=1, source_target_pairs={{0,4},{4,0},{8,12},{12,8},{1,5},{5,1},{9,13},{13,9},{2,6},{6,2},{1... | collective-permute-start | bytes 110600 | tf_op jit(solution)/shard_map/ppermute | solution.py:27
  3.7 4.6 %collective-permute-start.1 = (f32[72,128]{1,0:T(8,128)S(1)}, f32[72,128]{1,0:T(8,128)S(1)}, u32[]{:S(2)}, u32[]{:S(2)}) collective-permute-start(f32[72,128]{1,0:T(8,128)S(1)} %get-tuple-element.21), channel_id=1, source_target_pairs={{0,8},{4,12},{8,0},{12,4},{1,9},{5,13},{9,1},{13,5},{2,10},{6,14},... | collective-permute-start | bytes 110600 | tf_op jit(solution)/shard_map/ppermute | solution.py:27
  6.3 3.4 %collective-permute-start.2 = (f32[72,128]{1,0:T(8,128)S(1)}, f32[72,128]{1,0:T(8,128)S(1)}, u32[]{:S(2)}, u32[]{:S(2)}) collective-permute-start(f32[72,128]{1,0:T(8,128)S(1)} %get-tuple-element.22), channel_id=1, source_target_pairs={{0,12},{4,8},{8,4},{12,0},{1,13},{5,9},{9,5},{13,1},{2,14},{6,10},... | collective-permute-start | bytes 110600 | tf_op jit(solution)/shard_map/ppermute | solution.py:27
  9.7 6.0 %collective-permute-start.5 = (f32[96,128]{1,0:T(8,128)S(1)}, f32[96,128]{1,0:T(8,128)S(1)}, u32[]{:S(2)}, u32[]{:S(2)}) collective-permute-start(f32[96,128]{1,0:T(8,128)S(1)} %shard_map.78.refs_0_), channel_id=1, source_target_pairs={{0,3},{1,2},{2,1},{3,0},{4,7},{5,6},{6,5},{7,4},{8,11},{9,10},{10,... | collective-permute-start | bytes 147464 | tf_op jit(solution)/shard_map/ppermute | solution.py:27
  13.4 5.0 %collective-permute-start.4 = (f32[96,128]{1,0:T(8,128)S(1)}, f32[96,128]{1,0:T(8,128)S(1)}, u32[]{:S(2)}, u32[]{:S(2)}) collective-permute-start(f32[96,128]{1,0:T(8,128)S(1)} %shard_map.78.refs_0_), channel_id=1, source_target_pairs={{0,2},{1,3},{2,0},{3,1},{4,6},{5,7},{6,4},{7,5},{8,10},{9,11},{10,... | collective-permute-start | bytes 147464 | tf_op jit(solution)/shard_map/ppermute | solution.py:27
  13.4 5.0 %collective-permute-start.3 = (f32[96,128]{1,0:T(8,128)S(1)}, f32[96,128]{1,0:T(8,128)S(1)}, u32[]{:S(2)}, u32[]{:S(2)}) collective-permute-start(f32[96,128]{1,0:T(8,128)S(1)} %shard_map.78.refs_0_), channel_id=1, source_target_pairs={{0,1},{1,0},{2,3},{3,2},{4,5},{5,4},{6,7},{7,6},{8,9},{9,8},{10,11... | collective-permute-start | bytes 147464 | tf_op jit(solution)/shard_map/ppermute | solution.py:27
  18.4 2.1 %copy-start.6 = (bf16[64,2,4,512]{3,2,1,0:T(4,128)(2,1)S(1)}, bf16[64,2,4,512]{3,2,1,0:T(4,128)(2,1)}, u32[]{:S(2)}) copy-start(bf16[64,2,4,512]{3,2,1,0:T(4,128)(2,1)} %param.7) | copy-start | bytes 1572868
  18.4 3.4 %collective-permute-start.8 = (f32[72,128]{1,0:T(8,128)S(1)}, f32[72,128]{1,0:T(8,128)S(1)}, u32[]{:S(2)}, u32[]{:S(2)}) collective-permute-start(f32[72,128]{1,0:T(8,128)S(1)} %shard_map.79.refs_0_), channel_id=1, source_target_pairs={{0,12},{4,8},{8,4},{12,0},{1,13},{5,9},{9,5},{13,1},{2,14},{6,10},... | collective-permute-start | bytes 110600 | tf_op jit(solution)/shard_map/ppermute | solution.py:27
  18.6 4.3 %collective-permute-start.7 = (f32[72,128]{1,0:T(8,128)S(1)}, f32[72,128]{1,0:T(8,128)S(1)}, u32[]{:S(2)}, u32[]{:S(2)}) collective-permute-start(f32[72,128]{1,0:T(8,128)S(1)} %shard_map.79.refs_0_), channel_id=1, source_target_pairs={{0,8},{4,12},{8,0},{12,4},{1,9},{5,13},{9,1},{13,5},{2,10},{6,14},... | collective-permute-start | bytes 110600 | tf_op jit(solution)/shard_map/ppermute | solution.py:27
  19.5 3.4 %collective-permute-start.6 = (f32[72,128]{1,0:T(8,128)S(1)}, f32[72,128]{1,0:T(8,128)S(1)}, u32[]{:S(2)}, u32[]{:S(2)}) collective-permute-start(f32[72,128]{1,0:T(8,128)S(1)} %shard_map.79.refs_0_), channel_id=1, source_target_pairs={{0,4},{4,0},{8,12},{12,8},{1,5},{5,1},{9,13},{13,9},{2,6},{6,2},{1... | collective-permute-start | bytes 110600 | tf_op jit(solution)/shard_map/ppermute | solution.py:27
  20.5 0.9 %copy-start.2 = (f32[3,2,64,64]{3,2,1,0:T(8,128)S(1)}, f32[3,2,64,64]{3,2,1,0:T(8,128)}, u32[]{:S(2)}) copy-start(f32[3,2,64,64]{3,2,1,0:T(8,128)} %refs_7_.1) | copy-start | bytes 294916
  20.5 0.9 %copy-start.4 = (bf16[64,64]{1,0:T(8,128)(2,1)S(1)}, bf16[64,64]{1,0:T(8,128)(2,1)}, u32[]{:S(2)}) copy-start(bf16[64,64]{1,0:T(8,128)(2,1)} %wv_ref.1) | copy-start | bytes 24580
  20.5 0.9 %copy-start.5 = (bf16[64,64]{1,0:T(8,128)(2,1)S(1)}, bf16[64,64]{1,0:T(8,128)(2,1)}, u32[]{:S(2)}) copy-start(bf16[64,64]{1,0:T(8,128)(2,1)} %wo_ref.1) | copy-start | bytes 24580
  23.9 8.9 %copy-start.3 = (bf16[2,128,128]{2,1,0:T(8,128)(2,1)S(1)}, bf16[2,128,128]{2,1,0:T(8,128)(2,1)}, u32[]{:S(2)}) copy-start(bf16[2,128,128]{2,1,0:T(8,128)(2,1)} %constant.2.clone.refs_4_.refs_6_) | copy-start | bytes 196612
  23.9 6.9 %collective-permute-start.11 = (bf16[16,512]{1,0:T(8,128)(2,1)S(1)}, bf16[16,512]{1,0:T(8,128)(2,1)S(1)}, u32[]{:S(2)}, u32[]{:S(2)}) collective-permute-start(bf16[16,512]{1,0:T(8,128)(2,1)S(1)} %get-tuple-element.26), channel_id=1, source_target_pairs={{0,3},{1,2},{2,1},{3,0},{4,7},{5,6},{6,5},{7,4},{8,11},{9,10},{10,... | collective-permute-start | bytes 49160 | tf_op jit(solution)/shard_map/ppermute | solution.py:27
  26.2 4.6 %collective-permute-start.10 = (bf16[16,512]{1,0:T(8,128)(2,1)S(1)}, bf16[16,512]{1,0:T(8,128)(2,1)S(1)}, u32[]{:S(2)}, u32[]{:S(2)}) collective-permute-start(bf16[16,512]{1,0:T(8,128)(2,1)S(1)} %get-tuple-element.26), channel_id=1, source_target_pairs={{0,2},{1,3},{2,0},{3,1},{4,6},{5,7},{6,4},{7,5},{8,10},{9,11},{10,... | collective-permute-start | bytes 49160 | tf_op jit(solution)/shard_map/ppermute | solution.py:27
  26.4 3.7 %collective-permute-start.9 = (bf16[16,512]{1,0:T(8,128)(2,1)S(1)}, bf16[16,512]{1,0:T(8,128)(2,1)S(1)}, u32[]{:S(2)}, u32[]{:S(2)}) collective-permute-start(bf16[16,512]{1,0:T(8,128)(2,1)S(1)} %get-tuple-element.26), channel_id=1, source_target_pairs={{0,1},{1,0},{2,3},{3,2},{4,5},{5,4},{6,7},{7,6},{8,9},{9,8},{10,11... | collective-permute-start | bytes 49160 | tf_op jit(solution)/shard_map/ppermute | solution.py:27
  30.9 3.9 %collective-permute-start.14 = (bf16[64,512]{1,0:T(8,128)(2,1)S(1)}, bf16[64,512]{1,0:T(8,128)(2,1)S(1)}, u32[]{:S(2)}, u32[]{:S(2)}) collective-permute-start(bf16[64,512]{1,0:T(8,128)(2,1)S(1)} %constant_dynamic-update-slice_fusion.refs_0_), channel_id=1, source_target_pairs={{0,12},{4,8},{8,4},{12,0},{1,13},{5,9},{9,5},{13,1},{2,14},{6,10},... | collective-permute-start | bytes 196616 | tf_op jit(solution)/shard_map/ppermute | solution.py:27
  30.9 5.0 %collective-permute-start.13 = (bf16[64,512]{1,0:T(8,128)(2,1)S(1)}, bf16[64,512]{1,0:T(8,128)(2,1)S(1)}, u32[]{:S(2)}, u32[]{:S(2)}) collective-permute-start(bf16[64,512]{1,0:T(8,128)(2,1)S(1)} %constant_dynamic-update-slice_fusion.refs_0_), channel_id=1, source_target_pairs={{0,8},{4,12},{8,0},{12,4},{1,9},{5,13},{9,1},{13,5},{2,10},{6,14},... | collective-permute-start | bytes 196616 | tf_op jit(solution)/shard_map/ppermute | solution.py:27
  31.8 4.2 %collective-permute-start.12 = (bf16[64,512]{1,0:T(8,128)(2,1)S(1)}, bf16[64,512]{1,0:T(8,128)(2,1)S(1)}, u32[]{:S(2)}, u32[]{:S(2)}) collective-permute-start(bf16[64,512]{1,0:T(8,128)(2,1)S(1)} %constant_dynamic-update-slice_fusion.refs_0_), channel_id=1, source_target_pairs={{0,4},{4,0},{8,12},{12,8},{1,5},{5,1},{9,13},{13,9},{2,6},{6,2},{1... | collective-permute-start | bytes 196616 | tf_op jit(solution)/shard_map/ppermute | solution.py:27
  37.0 4.2 %collective-permute-start.17 = (bf16[64,512]{1,0:T(8,128)(2,1)S(1)}, bf16[64,512]{1,0:T(8,128)(2,1)S(1)}, u32[]{:S(2)}, u32[]{:S(2)}) collective-permute-start(bf16[64,512]{1,0:T(8,128)(2,1)S(1)} %get-tuple-element.32.refs_0_), channel_id=1, source_target_pairs={{0,12},{4,8},{8,4},{12,0},{1,13},{5,9},{9,5},{13,1},{2,14},{6,10},... | collective-permute-start | bytes 196616 | tf_op jit(solution)/shard_map/ppermute | solution.py:27
  38.0 4.9 %collective-permute-start.16 = (bf16[64,512]{1,0:T(8,128)(2,1)S(1)}, bf16[64,512]{1,0:T(8,128)(2,1)S(1)}, u32[]{:S(2)}, u32[]{:S(2)}) collective-permute-start(bf16[64,512]{1,0:T(8,128)(2,1)S(1)} %get-tuple-element.32.refs_0_), channel_id=1, source_target_pairs={{0,8},{4,12},{8,0},{12,4},{1,9},{5,13},{9,1},{13,5},{2,10},{6,14},... | collective-permute-start | bytes 196616 | tf_op jit(solution)/shard_map/ppermute | solution.py:27
  38.8 4.1 %collective-permute-start.15 = (bf16[64,512]{1,0:T(8,128)(2,1)S(1)}, bf16[64,512]{1,0:T(8,128)(2,1)S(1)}, u32[]{:S(2)}, u32[]{:S(2)}) collective-permute-start(bf16[64,512]{1,0:T(8,128)(2,1)S(1)} %get-tuple-element.32.refs_0_), channel_id=1, source_target_pairs={{0,4},{4,0},{8,12},{12,8},{1,5},{5,1},{9,13},{13,9},{2,6},{6,2},{1... | collective-permute-start | bytes 196616 | tf_op jit(solution)/shard_map/ppermute | solution.py:27
  42.9 6.8 %collective-permute-start.20 = (bf16[64,512]{1,0:T(8,128)(2,1)S(1)}, bf16[64,512]{1,0:T(8,128)(2,1)S(1)}, u32[]{:S(2)}, u32[]{:S(2)}) collective-permute-start(bf16[64,512]{1,0:T(8,128)(2,1)S(1)} %shard_map.85.refs_0_), channel_id=1, source_target_pairs={{0,3},{1,2},{2,1},{3,0},{4,7},{5,6},{6,5},{7,4},{8,11},{9,10},{10,... | collective-permute-start | bytes 196616 | tf_op jit(solution)/shard_map/ppermute | solution.py:27
  44.8 7.3 %collective-permute-start.19 = (bf16[64,512]{1,0:T(8,128)(2,1)S(1)}, bf16[64,512]{1,0:T(8,128)(2,1)S(1)}, u32[]{:S(2)}, u32[]{:S(2)}) collective-permute-start(bf16[64,512]{1,0:T(8,128)(2,1)S(1)} %shard_map.85.refs_0_), channel_id=1, source_target_pairs={{0,2},{1,3},{2,0},{3,1},{4,6},{5,7},{6,4},{7,5},{8,10},{9,11},{10,... | collective-permute-start | bytes 196616 | tf_op jit(solution)/shard_map/ppermute | solution.py:27
  45.7 6.4 %collective-permute-start.18 = (bf16[64,512]{1,0:T(8,128)(2,1)S(1)}, bf16[64,512]{1,0:T(8,128)(2,1)S(1)}, u32[]{:S(2)}, u32[]{:S(2)}) collective-permute-start(bf16[64,512]{1,0:T(8,128)(2,1)S(1)} %shard_map.85.refs_0_), channel_id=1, source_target_pairs={{0,1},{1,0},{2,3},{3,2},{4,5},{5,4},{6,7},{7,6},{8,9},{9,8},{10,11... | collective-permute-start | bytes 196616 | tf_op jit(solution)/shard_map/ppermute | solution.py:27

commit v8 on v7

--- a/solution.py
+++ b/solution.py
@@ -506,7 +506,8 @@
         copy.wait()
 
 
-def run(kernel, outs, operands, places=pltpu.VMEM, target=pltpu.VMEM, flops=0, scratch=()):
+def run(kernel, outs, operands, places=pltpu.VMEM, target=pltpu.VMEM, flops=0, scratch=(),
+        mebibytes=16):
     moved = sum(x.size * x.dtype.itemsize for x in tuple(operands) + tuple(outs))
     found = pl.pallas_call(
         kernel,
@@ -514,7 +515,7 @@
         in_specs=[pl.BlockSpec(memory_space=places)] * len(operands),
         out_specs=tuple(pl.BlockSpec(memory_space=target) for _ in outs),
         scratch_shapes=list(scratch),
-        compiler_params=pltpu.CompilerParams(vmem_limit_bytes=16 * 1024 * 1024),
+        compiler_params=pltpu.CompilerParams(vmem_limit_bytes=mebibytes * 1024 * 1024),
         cost_estimate=pl.CostEstimate(flops=flops, bytes_accessed=moved, transcendentals=0),
     )(*operands)
     return found[0] if len(outs) == 1 else found
@@ -557,7 +558,7 @@
         )
 
     sums = run(
-        sums_kernel, [like((WIDTH + cells, LANES), f32)] * span_x, (field,), places=pltpu.HBM,
+        sums_kernel, [like((WIDTH + cells, LANES), f32)] * span_x, (pltpu.with_memory_space_constraint(field, pltpu.HBM),), places=pltpu.HBM,
         flops=cube // 4,
         scratch=[parts] + chunked,
     )

time: 53.2 us -> 52.4 us (0.985)
  local copies, waits for them, and re-layouts: 2.09 us -> 1.05 us
    unnamed x17 -> x15, local copies, waits for them, and re-layouts: 1.84 us -> 0.8 us
where the time goes in v8:
time: 52.4 us; the launch traced here: 52.3 us
  starting transfers between devices  22.3 us (43%)
  waiting for transfers between devices  18.4 us (35%)
  Pallas kernels  9.74 us (19%)
  local copies, waits for them, and re-layouts  1.05 us (2%)
  between operations  0.79 us (2%)
    ppermute x21, starting transfers between devices, swap(): return lax.ppermute(part, axis, [(i, i ^ step) for i in range(size)])  22.3 us
    ppermute x21, waiting for transfers between devices, swap(): return lax.ppermute(part, axis, [(i, i ^ step) for i in range(size)])  18.4 us
    pallas_call x12, Pallas kernels, run(): pl.pallas_call(kernel, out_shape=tuple(outs), in_specs=[pl.BlockSpec(memo...  9.74 us
  transfers between devices with their start and end apart: 21, of which 14 were waited for; matrix products, arithmetic and copies ran while one was open for 0% of the time, Pallas kernels for 9%

profile of v8, /device:TPU:0, one launch (start us, length us, event | category | flops | bytes accessed | tf_op | source)
XLA Modules:
  0.0 52.3 jit_solution(7663697787950049094)
XLA Ops:
  0.6 1.8 %shard_map.77 = (f32[72,128]{1,0:T(8,128)S(1)}, f32[72,128]{1,0:T(8,128)S(1)}, f32[72,128]{1,0:T(8,128)S(1)}, f32[72,128]{1,0:T(8,128)S(1)}) custom-call(bf16[64,2,4,512]{3,2,1,0:T(4,128)(2,1)} %field_ref.1), custom_call_target="tpu_custom_call" | custom-call | flops 67108864 | bytes 671744 | tf_op jit(solution)/shard_map/pallas_call | solution.py:512
  3.0 2.6 %collective-permute-start.1 = (f32[72,128]{1,0:T(8,128)S(1)}, f32[72,128]{1,0:T(8,128)S(1)}, u32[]{:S(2)}, u32[]{:S(2)}) collective-permute-start(f32[72,128]{1,0:T(8,128)S(1)} %get-tuple-element.21), channel_id=1, source_target_pairs={{0,8},{4,12},{8,0},{12,4},{1,9},{5,13},{9,1},{13,5},{2,10},{6,14},... | collective-permute-start | bytes 110600 | tf_op jit(solution)/shard_map/ppermute | solution.py:27
  5.6 2.0 %collective-permute-done.1.refs_2_ = f32[72,128]{1,0:T(8,128)S(1)} collective-permute-done((f32[72,128]{1,0:T(8,128)S(1)}, f32[72,128]{1,0:T(8,128)S(1)}, u32[]{:S(2)}, u32[]{:S(2)}) %collective-permute-start.1) | collective-permute-done | bytes 36896 | tf_op jit(solution)/shard_map/ppermute | solution.py:27
  7.6 1.4 %collective-permute-done.2.refs_3_ = f32[72,128]{1,0:T(8,128)S(1)} collective-permute-done((f32[72,128]{1,0:T(8,128)S(1)}, f32[72,128]{1,0:T(8,128)S(1)}, u32[]{:S(2)}, u32[]{:S(2)}) %collective-permute-start.2) | collective-permute-done | bytes 36896 | tf_op jit(solution)/shard_map/ppermute | solution.py:27
  9.0 3.7 %collective-permute-start.5 = (f32[96,128]{1,0:T(8,128)S(1)}, f32[96,128]{1,0:T(8,128)S(1)}, u32[]{:S(2)}, u32[]{:S(2)}) collective-permute-start(f32[96,128]{1,0:T(8,128)S(1)} %shard_map.78.refs_0_), channel_id=1, source_target_pairs={{0,3},{1,2},{2,1},{3,0},{4,7},{5,6},{6,5},{7,4},{8,11},{9,10},{10,... | collective-permute-start | bytes 147464 | tf_op jit(solution)/shard_map/ppermute | solution.py:27
  12.7 0.8 %collective-permute-start.3 = (f32[96,128]{1,0:T(8,128)S(1)}, f32[96,128]{1,0:T(8,128)S(1)}, u32[]{:S(2)}, u32[]{:S(2)}) collective-permute-start(f32[96,128]{1,0:T(8,128)S(1)} %shard_map.78.refs_0_), channel_id=1, source_target_pairs={{0,1},{1,0},{2,3},{3,2},{4,5},{5,4},{6,7},{7,6},{8,9},{9,8},{10,11... | collective-permute-start | bytes 147464 | tf_op jit(solution)/shard_map/ppermute | solution.py:27
  13.5 1.6 %collective-permute-done.5.refs_3_ = f32[96,128]{1,0:T(8,128)S(1)} collective-permute-done((f32[96,128]{1,0:T(8,128)S(1)}, f32[96,128]{1,0:T(8,128)S(1)}, u32[]{:S(2)}, u32[]{:S(2)}) %collective-permute-start.5) | collective-permute-done | bytes 49184 | tf_op jit(solution)/shard_map/ppermute | solution.py:27
  15.0 2.6 %collective-permute-done.4.refs_2_ = f32[96,128]{1,0:T(8,128)S(1)} collective-permute-done((f32[96,128]{1,0:T(8,128)S(1)}, f32[96,128]{1,0:T(8,128)S(1)}, u32[]{:S(2)}, u32[]{:S(2)}) %collective-permute-start.4) | collective-permute-done | bytes 49184 | tf_op jit(solution)/shard_map/ppermute | solution.py:27
  17.9 0.9 %collective-permute-start.7 = (f32[72,128]{1,0:T(8,128)S(1)}, f32[72,128]{1,0:T(8,128)S(1)}, u32[]{:S(2)}, u32[]{:S(2)}) collective-permute-start(f32[72,128]{1,0:T(8,128)S(1)} %shard_map.79.refs_0_), channel_id=1, source_target_pairs={{0,8},{4,12},{8,0},{12,4},{1,9},{5,13},{9,1},{13,5},{2,10},{6,14},... | collective-permute-start | bytes 110600 | tf_op jit(solution)/shard_map/ppermute | solution.py:27
  18.8 0.9 %collective-permute-start.6 = (f32[72,128]{1,0:T(8,128)S(1)}, f32[72,128]{1,0:T(8,128)S(1)}, u32[]{:S(2)}, u32[]{:S(2)}) collective-permute-start(f32[72,128]{1,0:T(8,128)S(1)} %shard_map.79.refs_0_), channel_id=1, source_target_pairs={{0,4},{4,0},{8,12},{12,8},{1,5},{5,1},{9,13},{13,9},{2,6},{6,2},{1... | collective-permute-start | bytes 110600 | tf_op jit(solution)/shard_map/ppermute | solution.py:27
  20.0 0.8 %copy-done = f32[3,2,64,64]{3,2,1,0:T(8,128)S(1)} copy-done((f32[3,2,64,64]{3,2,1,0:T(8,128)S(1)}, f32[3,2,64,64]{3,2,1,0:T(8,128)}, u32[]{:S(2)}) %copy-start) | copy-done | bytes 98328
  21.2 1.0 %collective-permute-done.7.refs_2_ = f32[72,128]{1,0:T(8,128)S(1)} collective-permute-done((f32[72,128]{1,0:T(8,128)S(1)}, f32[72,128]{1,0:T(8,128)S(1)}, u32[]{:S(2)}, u32[]{:S(2)}) %collective-permute-start.7) | collective-permute-done | bytes 36896 | tf_op jit(solution)/shard_map/ppermute | solution.py:27
  22.2 1.0 %shard_map.81 = (bf16[16,512]{1,0:T(8,128)(2,1)S(1)}, bf16[128,512]{1,0:T(8,128)(2,1)S(1)}, f32[72,512]{1,0:T(8,128)S(1)}) custom-call(f32[72,128]{1,0:T(8,128)S(1)} %shard_map.79.refs_0_, f32[72,128]{1,0:T(8,128)S(1)} %collective-permute-done.6.refs_1_, f32[72,128]{1,0:T(8,128)S(1)} %collective-permute-done.7.refs_2_, ...), custom_call_target="tpu_custom_call" | custom-call | flops 536870912 | bytes 1785856 | tf_op jit(solution)/shard_map/pallas_call | solution.py:512
  23.2 2.3 %collective-permute-start.11 = (bf16[16,512]{1,0:T(8,128)(2,1)S(1)}, bf16[16,512]{1,0:T(8,128)(2,1)S(1)}, u32[]{:S(2)}, u32[]{:S(2)}) collective-permute-start(bf16[16,512]{1,0:T(8,128)(2,1)S(1)} %get-tuple-element.26), channel_id=1, source_target_pairs={{0,3},{1,2},{2,1},{3,0},{4,7},{5,6},{6,5},{7,4},{8,11},{9,10},{10,... | collective-permute-start | bytes 49160 | tf_op jit(solution)/shard_map/ppermute | solution.py:27
  25.7 2.0 %collective-permute-start.9 = (bf16[16,512]{1,0:T(8,128)(2,1)S(1)}, bf16[16,512]{1,0:T(8,128)(2,1)S(1)}, u32[]{:S(2)}, u32[]{:S(2)}) collective-permute-start(bf16[16,512]{1,0:T(8,128)(2,1)S(1)} %get-tuple-element.26), channel_id=1, source_target_pairs={{0,1},{1,0},{2,3},{3,2},{4,5},{5,4},{6,7},{7,6},{8,9},{9,8},{10,11... | collective-permute-start | bytes 49160 | tf_op jit(solution)/shard_map/ppermute | solution.py:27
  27.7 1.7 %collective-permute-done.9 = bf16[16,512]{1,0:T(8,128)(2,1)S(1)} collective-permute-done((bf16[16,512]{1,0:T(8,128)(2,1)S(1)}, bf16[16,512]{1,0:T(8,128)(2,1)S(1)}, u32[]{:S(2)}, u32[]{:S(2)}) %collective-permute-start.9) | collective-permute-done | bytes 16416 | tf_op jit(solution)/shard_map/ppermute | solution.py:27
  30.2 0.8 %collective-permute-start.13 = (bf16[64,512]{1,0:T(8,128)(2,1)S(1)}, bf16[64,512]{1,0:T(8,128)(2,1)S(1)}, u32[]{:S(2)}, u32[]{:S(2)}) collective-permute-start(bf16[64,512]{1,0:T(8,128)(2,1)S(1)} %constant_dynamic-update-slice_fusion.refs_0_), channel_id=1, source_target_pairs={{0,8},{4,12},{8,0},{12,4},{1,9},{5,13},{9,1},{13,5},{2,10},{6,14},... | collective-permute-start | bytes 196616 | tf_op jit(solution)/shard_map/ppermute | solution.py:27
  31.1 1.0 %collective-permute-start.12 = (bf16[64,512]{1,0:T(8,128)(2,1)S(1)}, bf16[64,512]{1,0:T(8,128)(2,1)S(1)}, u32[]{:S(2)}, u32[]{:S(2)}) collective-permute-start(bf16[64,512]{1,0:T(8,128)(2,1)S(1)} %constant_dynamic-update-slice_fusion.refs_0_), channel_id=1, source_target_pairs={{0,4},{4,0},{8,12},{12,8},{1,5},{5,1},{9,13},{13,9},{2,6},{6,2},{1... | collective-permute-start | bytes 196616 | tf_op jit(solution)/shard_map/ppermute | solution.py:27
  32.1 1.4 %shard_map.82 = (f32[2,64,128]{2,1,0:T(8,128)S(1)}, f32[8,128,64]{2,1,0:T(8,128)S(1)}, f32[2,1024,128]{2,1,0:T(8,128)S(1)}) custom-call(f32[96,128]{1,0:T(8,128)S(1)} %shard_map.78.refs_0_, f32[96,128]{1,0:T(8,128)S(1)} %collective-permute-done.3.refs_1_, f32[96,128]{1,0:T(8,128)S(1)} %collective-permute-done.4.refs_2_, ...), custom_call_target="tpu_custom_call" | custom-call | flops 134217728 | bytes 1736704 | tf_op jit(solution)/shard_map/pallas_call | solution.py:512
  34.0 1.2 %collective-permute-done.13.refs_2_ = bf16[64,512]{1,0:T(8,128)(2,1)S(1)} collective-permute-done((bf16[64,512]{1,0:T(8,128)(2,1)S(1)}, bf16[64,512]{1,0:T(8,128)(2,1)S(1)}, u32[]{:S(2)}, u32[]{:S(2)}) %collective-permute-start.13) | collective-permute-done | bytes 65568 | tf_op jit(solution)/shard_map/ppermute | solution.py:27
  35.2 1.0 %shard_map.83 = (f32[2,8,512]{2,1,0:T(8,128)S(1)}, bf16[64,512]{1,0:T(8,128)(2,1)S(1)}) custom-call(bf16[64,512]{1,0:T(8,128)(2,1)S(1)} %constant_dynamic-update-slice_fusion.refs_0_, bf16[64,512]{1,0:T(8,128)(2,1)S(1)} %collective-permute-done.12.refs_1_, bf16[64,512]{1,0:T(8,128)(2,1)S(1)} %collective-permute-done.13.refs_2_, ...), custom_call_target="tpu_custom_call" | custom-call | flops 268435456 | bytes 1998848 | tf_op jit(solution)/shard_map/pallas_call | solution.py:512
  36.3 1.0 %collective-permute-start.17 = (bf16[64,512]{1,0:T(8,128)(2,1)S(1)}, bf16[64,512]{1,0:T(8,128)(2,1)S(1)}, u32[]{:S(2)}, u32[]{:S(2)}) collective-permute-start(bf16[64,512]{1,0:T(8,128)(2,1)S(1)} %get-tuple-element.32.refs_0_), channel_id=1, source_target_pairs={{0,12},{4,8},{8,4},{12,0},{1,13},{5,9},{9,5},{13,1},{2,14},{6,10},... | collective-permute-start | bytes 196616 | tf_op jit(solution)/shard_map/ppermute | solution.py:27
  37.2 0.8 %collective-permute-start.16 = (bf16[64,512]{1,0:T(8,128)(2,1)S(1)}, bf16[64,512]{1,0:T(8,128)(2,1)S(1)}, u32[]{:S(2)}, u32[]{:S(2)}) collective-permute-start(bf16[64,512]{1,0:T(8,128)(2,1)S(1)} %get-tuple-element.32.refs_0_), channel_id=1, source_target_pairs={{0,8},{4,12},{8,0},{12,4},{1,9},{5,13},{9,1},{13,5},{2,10},{6,14},... | collective-permute-start | bytes 196616 | tf_op jit(solution)/shard_map/ppermute | solution.py:27
  38.2 1.2 %shard_map.84 = bf16[64,2,4,512]{3,2,1,0:T(4,128)(2,1)} custom-call(f32[2,8,512]{2,1,0:T(8,128)S(1)} %get-tuple-element.30.top_ref, f32[64,512]{1,0:T(8,128)S(1)} %get-tuple-element.25.refs_8_.refs_6_.wo_ref, bf16[128,512]{1,0:T(8,128)(2,1)S(1)} %get-tuple-element.31.both_ref, bf16[512,512]{1,0:T(8,128)(2,1)S(1)} %reshape.10.refs_5_.refs_9_.field_ref), custom_call_target="tpu_custom_call" | custom-call | flops 268435456 | bytes 1343488 | tf_op jit(solution)/shard_map/pallas_call | solution.py:512
  39.5 1.0 %collective-permute-done.17.refs_3_ = bf16[64,512]{1,0:T(8,128)(2,1)S(1)} collective-permute-done((bf16[64,512]{1,0:T(8,128)(2,1)S(1)}, bf16[64,512]{1,0:T(8,128)(2,1)S(1)}, u32[]{:S(2)}, u32[]{:S(2)}) %collective-permute-start.17) | collective-permute-done | bytes 65568 | tf_op jit(solution)/shard_map/ppermute | solution.py:27
  40.4 1.7 %collective-permute-done.16.refs_2_ = bf16[64,512]{1,0:T(8,128)(2,1)S(1)} collective-permute-done((bf16[64,512]{1,0:T(8,128)(2,1)S(1)}, bf16[64,512]{1,0:T(8,128)(2,1)S(1)}, u32[]{:S(2)}, u32[]{:S(2)}) %collective-permute-start.16) | collective-permute-done | bytes 65568 | tf_op jit(solution)/shard_map/ppermute | solution.py:27
  42.2 1.9 %collective-permute-start.20 = (bf16[64,512]{1,0:T(8,128)(2,1)S(1)}, bf16[64,512]{1,0:T(8,128)(2,1)S(1)}, u32[]{:S(2)}, u32[]{:S(2)}) collective-permute-start(bf16[64,512]{1,0:T(8,128)(2,1)S(1)} %shard_map.85.refs_0_), channel_id=1, source_target_pairs={{0,3},{1,2},{2,1},{3,0},{4,7},{5,6},{6,5},{7,4},{8,11},{9,10},{10,... | collective-permute-start | bytes 196616 | tf_op jit(solution)/shard_map/ppermute | solution.py:27
  44.1 0.9 %collective-permute-start.19 = (bf16[64,512]{1,0:T(8,128)(2,1)S(1)}, bf16[64,512]{1,0:T(8,128)(2,1)S(1)}, u32[]{:S(2)}, u32[]{:S(2)}) collective-permute-start(bf16[64,512]{1,0:T(8,128)(2,1)S(1)} %shard_map.85.refs_0_), channel_id=1, source_target_pairs={{0,2},{1,3},{2,0},{3,1},{4,6},{5,7},{6,4},{7,5},{8,10},{9,11},{10,... | collective-permute-start | bytes 196616 | tf_op jit(solution)/shard_map/ppermute | solution.py:27
  45.0 1.6 %collective-permute-start.18 = (bf16[64,512]{1,0:T(8,128)(2,1)S(1)}, bf16[64,512]{1,0:T(8,128)(2,1)S(1)}, u32[]{:S(2)}, u32[]{:S(2)}) collective-permute-start(bf16[64,512]{1,0:T(8,128)(2,1)S(1)} %shard_map.85.refs_0_), channel_id=1, source_target_pairs={{0,1},{1,0},{2,3},{3,2},{4,5},{5,4},{6,7},{7,6},{8,9},{9,8},{10,11... | collective-permute-start | bytes 196616 | tf_op jit(solution)/shard_map/ppermute | solution.py:27
  46.6 1.4 %shard_map.86.plane_ref = f32[8,64]{1,0:T(8,128)S(1)} custom-call(bf16[64,512]{1,0:T(8,128)(2,1)S(1)} %constant_dynamic-update-slice_fusion.refs_0_, bf16[64,512]{1,0:T(8,128)(2,1)S(1)} %collective-permute-done.12.refs_1_, bf16[64,512]{1,0:T(8,128)(2,1)S(1)} %collective-permute-done.13.refs_2_, bf16[64,512]{1,0:T(8,128)(2,1)S(1)} %collective-permute-done.14.refs_3_, ...), custom_call_target="tpu_custom_call" | custom-call | flops 536870912 | bytes 1738752 | tf_op jit(solution)/shard_map/pallas_call | solution.py:512
  49.0 2.4 %collective-permute-done.19.refs_2_ = bf16[64,512]{1,0:T(8,128)(2,1)S(1)} collective-permute-done((bf16[64,512]{1,0:T(8,128)(2,1)S(1)}, bf16[64,512]{1,0:T(8,128)(2,1)S(1)}, u32[]{:S(2)}, u32[]{:S(2)}) %collective-permute-start.19) | collective-permute-done | bytes 65568 | tf_op jit(solution)/shard_map/ppermute | solution.py:27
  51.4 0.9 %shard_map.88 = bf16[64,2,4,512]{3,2,1,0:T(4,128)(2,1)} custom-call(bf16[64,512]{1,0:T(8,128)(2,1)S(1)} %shard_map.85.refs_0_, bf16[64,512]{1,0:T(8,128)(2,1)S(1)} %collective-permute-done.18.refs_1_, bf16[64,512]{1,0:T(8,128)(2,1)S(1)} %collective-permute-done.19.refs_2_, bf16[64,512]{1,0:T(8,128)(2,1)S(1)} %collective-permute-done.20.refs_3_, ...), custom_call_target="tpu_custom_call" | custom-call | bytes 1982464 | tf_op jit(solution)/shard_map/pallas_call | solution.py:512
  (40 shorter events, 4.2 us)
Async XLA Ops:
  0.6 19.0 %copy-start.4 = (bf16[64,2,4,512]{3,2,1,0:T(4,128)(2,1)S(1)}, bf16[64,2,4,512]{3,2,1,0:T(4,128)(2,1)}, u32[]{:S(2)}) copy-start(bf16[64,2,4,512]{3,2,1,0:T(4,128)(2,1)} %field_ref.1) | copy-start | bytes 1572868
  2.5 3.2 %collective-permute-start = (f32[72,128]{1,0:T(8,128)S(1)}, f32[72,128]{1,0:T(8,128)S(1)}, u32[]{:S(2)}, u32[]{:S(2)}) collective-permute-start(f32[72,128]{1,0:T(8,128)S(1)} %get-tuple-element.20), channel_id=1, source_target_pairs={{0,4},{4,0},{8,12},{12,8},{1,5},{5,1},{9,13},{13,9},{2,6},{6,2},{1... | collective-permute-start | bytes 110600 | tf_op jit(solution)/shard_map/ppermute | solution.py:27
  3.0 4.6 %collective-permute-start.1 = (f32[72,128]{1,0:T(8,128)S(1)}, f32[72,128]{1,0:T(8,128)S(1)}, u32[]{:S(2)}, u32[]{:S(2)}) collective-permute-start(f32[72,128]{1,0:T(8,128)S(1)} %get-tuple-element.21), channel_id=1, source_target_pairs={{0,8},{4,12},{8,0},{12,4},{1,9},{5,13},{9,1},{13,5},{2,10},{6,14},... | collective-permute-start | bytes 110600 | tf_op jit(solution)/shard_map/ppermute | solution.py:27
  5.6 3.4 %collective-permute-start.2 = (f32[72,128]{1,0:T(8,128)S(1)}, f32[72,128]{1,0:T(8,128)S(1)}, u32[]{:S(2)}, u32[]{:S(2)}) collective-permute-start(f32[72,128]{1,0:T(8,128)S(1)} %get-tuple-element.22), channel_id=1, source_target_pairs={{0,12},{4,8},{8,4},{12,0},{1,13},{5,9},{9,5},{13,1},{2,14},{6,10},... | collective-permute-start | bytes 110600 | tf_op jit(solution)/shard_map/ppermute | solution.py:27
  9.0 6.0 %collective-permute-start.5 = (f32[96,128]{1,0:T(8,128)S(1)}, f32[96,128]{1,0:T(8,128)S(1)}, u32[]{:S(2)}, u32[]{:S(2)}) collective-permute-start(f32[96,128]{1,0:T(8,128)S(1)} %shard_map.78.refs_0_), channel_id=1, source_target_pairs={{0,3},{1,2},{2,1},{3,0},{4,7},{5,6},{6,5},{7,4},{8,11},{9,10},{10,... | collective-permute-start | bytes 147464 | tf_op jit(solution)/shard_map/ppermute | solution.py:27
  12.7 5.0 %collective-permute-start.4 = (f32[96,128]{1,0:T(8,128)S(1)}, f32[96,128]{1,0:T(8,128)S(1)}, u32[]{:S(2)}, u32[]{:S(2)}) collective-permute-start(f32[96,128]{1,0:T(8,128)S(1)} %shard_map.78.refs_0_), channel_id=1, source_target_pairs={{0,2},{1,3},{2,0},{3,1},{4,6},{5,7},{6,4},{7,5},{8,10},{9,11},{10,... | collective-permute-start | bytes 147464 | tf_op jit(solution)/shard_map/ppermute | solution.py:27
  12.7 5.0 %collective-permute-start.3 = (f32[96,128]{1,0:T(8,128)S(1)}, f32[96,128]{1,0:T(8,128)S(1)}, u32[]{:S(2)}, u32[]{:S(2)}) collective-permute-start(f32[96,128]{1,0:T(8,128)S(1)} %shard_map.78.refs_0_), channel_id=1, source_target_pairs={{0,1},{1,0},{2,3},{3,2},{4,5},{5,4},{6,7},{7,6},{8,9},{9,8},{10,11... | collective-permute-start | bytes 147464 | tf_op jit(solution)/shard_map/ppermute | solution.py:27
  17.7 2.1 %copy-start.5 = (bf16[64,2,4,512]{3,2,1,0:T(4,128)(2,1)S(1)}, bf16[64,2,4,512]{3,2,1,0:T(4,128)(2,1)}, u32[]{:S(2)}) copy-start(bf16[64,2,4,512]{3,2,1,0:T(4,128)(2,1)} %param.7) | copy-start | bytes 1572868
  17.7 3.4 %collective-permute-start.8 = (f32[72,128]{1,0:T(8,128)S(1)}, f32[72,128]{1,0:T(8,128)S(1)}, u32[]{:S(2)}, u32[]{:S(2)}) collective-permute-start(f32[72,128]{1,0:T(8,128)S(1)} %shard_map.79.refs_0_), channel_id=1, source_target_pairs={{0,12},{4,8},{8,4},{12,0},{1,13},{5,9},{9,5},{13,1},{2,14},{6,10},... | collective-permute-start | bytes 110600 | tf_op jit(solution)/shard_map/ppermute | solution.py:27
  17.9 4.3 %collective-permute-start.7 = (f32[72,128]{1,0:T(8,128)S(1)}, f32[72,128]{1,0:T(8,128)S(1)}, u32[]{:S(2)}, u32[]{:S(2)}) collective-permute-start(f32[72,128]{1,0:T(8,128)S(1)} %shard_map.79.refs_0_), channel_id=1, source_target_pairs={{0,8},{4,12},{8,0},{12,4},{1,9},{5,13},{9,1},{13,5},{2,10},{6,14},... | collective-permute-start | bytes 110600 | tf_op jit(solution)/shard_map/ppermute | solution.py:27
  18.8 3.4 %collective-permute-start.6 = (f32[72,128]{1,0:T(8,128)S(1)}, f32[72,128]{1,0:T(8,128)S(1)}, u32[]{:S(2)}, u32[]{:S(2)}) collective-permute-start(f32[72,128]{1,0:T(8,128)S(1)} %shard_map.79.refs_0_), channel_id=1, source_target_pairs={{0,4},{4,0},{8,12},{12,8},{1,5},{5,1},{9,13},{13,9},{2,6},{6,2},{1... | collective-permute-start | bytes 110600 | tf_op jit(solution)/shard_map/ppermute | solution.py:27
  19.8 0.9 %copy-start = (f32[3,2,64,64]{3,2,1,0:T(8,128)S(1)}, f32[3,2,64,64]{3,2,1,0:T(8,128)}, u32[]{:S(2)}) copy-start(f32[3,2,64,64]{3,2,1,0:T(8,128)} %refs_7_.1) | copy-start | bytes 294916
  19.8 0.9 %copy-start.2 = (bf16[64,64]{1,0:T(8,128)(2,1)S(1)}, bf16[64,64]{1,0:T(8,128)(2,1)}, u32[]{:S(2)}) copy-start(bf16[64,64]{1,0:T(8,128)(2,1)} %wv_ref.1) | copy-start | bytes 24580
  19.8 0.9 %copy-start.3 = (bf16[64,64]{1,0:T(8,128)(2,1)S(1)}, bf16[64,64]{1,0:T(8,128)(2,1)}, u32[]{:S(2)}) copy-start(bf16[64,64]{1,0:T(8,128)(2,1)} %wo_ref.1) | copy-start | bytes 24580
  23.2 8.9 %copy-start.1 = (bf16[2,128,128]{2,1,0:T(8,128)(2,1)S(1)}, bf16[2,128,128]{2,1,0:T(8,128)(2,1)}, u32[]{:S(2)}) copy-start(bf16[2,128,128]{2,1,0:T(8,128)(2,1)} %constant.2.clone.refs_4_.refs_6_) | copy-start | bytes 196612
  23.2 6.9 %collective-permute-start.11 = (bf16[16,512]{1,0:T(8,128)(2,1)S(1)}, bf16[16,512]{1,0:T(8,128)(2,1)S(1)}, u32[]{:S(2)}, u32[]{:S(2)}) collective-permute-start(bf16[16,512]{1,0:T(8,128)(2,1)S(1)} %get-tuple-element.26), channel_id=1, source_target_pairs={{0,3},{1,2},{2,1},{3,0},{4,7},{5,6},{6,5},{7,4},{8,11},{9,10},{10,... | collective-permute-start | bytes 49160 | tf_op jit(solution)/shard_map/ppermute | solution.py:27
  25.5 4.6 %collective-permute-start.10 = (bf16[16,512]{1,0:T(8,128)(2,1)S(1)}, bf16[16,512]{1,0:T(8,128)(2,1)S(1)}, u32[]{:S(2)}, u32[]{:S(2)}) collective-permute-start(bf16[16,512]{1,0:T(8,128)(2,1)S(1)} %get-tuple-element.26), channel_id=1, source_target_pairs={{0,2},{1,3},{2,0},{3,1},{4,6},{5,7},{6,4},{7,5},{8,10},{9,11},{10,... | collective-permute-start | bytes 49160 | tf_op jit(solution)/shard_map/ppermute | solution.py:27
  25.7 3.7 %collective-permute-start.9 = (bf16[16,512]{1,0:T(8,128)(2,1)S(1)}, bf16[16,512]{1,0:T(8,128)(2,1)S(1)}, u32[]{:S(2)}, u32[]{:S(2)}) collective-permute-start(bf16[16,512]{1,0:T(8,128)(2,1)S(1)} %get-tuple-element.26), channel_id=1, source_target_pairs={{0,1},{1,0},{2,3},{3,2},{4,5},{5,4},{6,7},{7,6},{8,9},{9,8},{10,11... | collective-permute-start | bytes 49160 | tf_op jit(solution)/shard_map/ppermute | solution.py:27
  30.1 3.9 %collective-permute-start.14 = (bf16[64,512]{1,0:T(8,128)(2,1)S(1)}, bf16[64,512]{1,0:T(8,128)(2,1)S(1)}, u32[]{:S(2)}, u32[]{:S(2)}) collective-permute-start(bf16[64,512]{1,0:T(8,128)(2,1)S(1)} %constant_dynamic-update-slice_fusion.refs_0_), channel_id=1, source_target_pairs={{0,12},{4,8},{8,4},{12,0},{1,13},{5,9},{9,5},{13,1},{2,14},{6,10},... | collective-permute-start | bytes 196616 | tf_op jit(solution)/shard_map/ppermute | solution.py:27
  30.2 5.0 %collective-permute-start.13 = (bf16[64,512]{1,0:T(8,128)(2,1)S(1)}, bf16[64,512]{1,0:T(8,128)(2,1)S(1)}, u32[]{:S(2)}, u32[]{:S(2)}) collective-permute-start(bf16[64,512]{1,0:T(8,128)(2,1)S(1)} %constant_dynamic-update-slice_fusion.refs_0_), channel_id=1, source_target_pairs={{0,8},{4,12},{8,0},{12,4},{1,9},{5,13},{9,1},{13,5},{2,10},{6,14},... | collective-permute-start | bytes 196616 | tf_op jit(solution)/shard_map/ppermute | solution.py:27
  31.1 4.2 %collective-permute-start.12 = (bf16[64,512]{1,0:T(8,128)(2,1)S(1)}, bf16[64,512]{1,0:T(8,128)(2,1)S(1)}, u32[]{:S(2)}, u32[]{:S(2)}) collective-permute-start(bf16[64,512]{1,0:T(8,128)(2,1)S(1)} %constant_dynamic-update-slice_fusion.refs_0_), channel_id=1, source_target_pairs={{0,4},{4,0},{8,12},{12,8},{1,5},{5,1},{9,13},{13,9},{2,6},{6,2},{1... | collective-permute-start | bytes 196616 | tf_op jit(solution)/shard_map/ppermute | solution.py:27
  36.3 4.2 %collective-permute-start.17 = (bf16[64,512]{1,0:T(8,128)(2,1)S(1)}, bf16[64,512]{1,0:T(8,128)(2,1)S(1)}, u32[]{:S(2)}, u32[]{:S(2)}) collective-permute-start(bf16[64,512]{1,0:T(8,128)(2,1)S(1)} %get-tuple-element.32.refs_0_), channel_id=1, source_target_pairs={{0,12},{4,8},{8,4},{12,0},{1,13},{5,9},{9,5},{13,1},{2,14},{6,10},... | collective-permute-start | bytes 196616 | tf_op jit(solution)/shard_map/ppermute | solution.py:27
  37.2 4.9 %collective-permute-start.16 = (bf16[64,512]{1,0:T(8,128)(2,1)S(1)}, bf16[64,512]{1,0:T(8,128)(2,1)S(1)}, u32[]{:S(2)}, u32[]{:S(2)}) collective-permute-start(bf16[64,512]{1,0:T(8,128)(2,1)S(1)} %get-tuple-element.32.refs_0_), channel_id=1, source_target_pairs={{0,8},{4,12},{8,0},{12,4},{1,9},{5,13},{9,1},{13,5},{2,10},{6,14},... | collective-permute-start | bytes 196616 | tf_op jit(solution)/shard_map/ppermute | solution.py:27
  38.1 4.1 %collective-permute-start.15 = (bf16[64,512]{1,0:T(8,128)(2,1)S(1)}, bf16[64,512]{1,0:T(8,128)(2,1)S(1)}, u32[]{:S(2)}, u32[]{:S(2)}) collective-permute-start(bf16[64,512]{1,0:T(8,128)(2,1)S(1)} %get-tuple-element.32.refs_0_), channel_id=1, source_target_pairs={{0,4},{4,0},{8,12},{12,8},{1,5},{5,1},{9,13},{13,9},{2,6},{6,2},{1... | collective-permute-start | bytes 196616 | tf_op jit(solution)/shard_map/ppermute | solution.py:27
  42.2 6.8 %collective-permute-start.20 = (bf16[64,512]{1,0:T(8,128)(2,1)S(1)}, bf16[64,512]{1,0:T(8,128)(2,1)S(1)}, u32[]{:S(2)}, u32[]{:S(2)}) collective-permute-start(bf16[64,512]{1,0:T(8,128)(2,1)S(1)} %shard_map.85.refs_0_), channel_id=1, source_target_pairs={{0,3},{1,2},{2,1},{3,0},{4,7},{5,6},{6,5},{7,4},{8,11},{9,10},{10,... | collective-permute-start | bytes 196616 | tf_op jit(solution)/shard_map/ppermute | solution.py:27
  44.1 7.3 %collective-permute-start.19 = (bf16[64,512]{1,0:T(8,128)(2,1)S(1)}, bf16[64,512]{1,0:T(8,128)(2,1)S(1)}, u32[]{:S(2)}, u32[]{:S(2)}) collective-permute-start(bf16[64,512]{1,0:T(8,128)(2,1)S(1)} %shard_map.85.refs_0_), channel_id=1, source_target_pairs={{0,2},{1,3},{2,0},{3,1},{4,6},{5,7},{6,4},{7,5},{8,10},{9,11},{10,... | collective-permute-start | bytes 196616 | tf_op jit(solution)/shard_map/ppermute | solution.py:27
  45.0 6.4 %collective-permute-start.18 = (bf16[64,512]{1,0:T(8,128)(2,1)S(1)}, bf16[64,512]{1,0:T(8,128)(2,1)S(1)}, u32[]{:S(2)}, u32[]{:S(2)}) collective-permute-start(bf16[64,512]{1,0:T(8,128)(2,1)S(1)} %shard_map.85.refs_0_), channel_id=1, source_target_pairs={{0,1},{1,0},{2,3},{3,2},{4,5},{5,4},{6,7},{7,6},{8,9},{9,8},{10,11... | collective-permute-start | bytes 196616 | tf_op jit(solution)/shard_map/ppermute | solution.py:27

commit v9 on v8

--- a/solution.py
+++ b/solution.py
@@ -236,7 +236,7 @@
 
 
 def sums_kernel(field_ref, *refs):
-    outs, (part_ref, data_ref, semaphores) = refs[:-3], refs[-3:]
+    outs, (data_ref, part_ref, semaphores) = refs[:-3], refs[-3:]
     _, rows_x, rows_y, depth = data_ref.shape
     chunks = semaphores.shape[0]
     size = WIDTH // chunks
@@ -543,7 +543,6 @@
         np.stack([at_x[:, None] == at_x[None], at_y[:, None] == at_y[None]]), dtype=bf16
     )
 
-    cols = field.reshape(rows, depth)
     cots = cotangent.reshape(rows, depth)
     parts = pltpu.VMEM((span_x, WIDTH, LANES), f32)
     chunked = [pltpu.VMEM(field.shape, bf16), pltpu.SemaphoreType.DMA((4,))]
@@ -557,11 +556,15 @@
             swap(sent[step], axis, size, step) for step in range(1, size)
         )
 
-    sums = run(
-        sums_kernel, [like((WIDTH + cells, LANES), f32)] * span_x, (pltpu.with_memory_space_constraint(field, pltpu.HBM),), places=pltpu.HBM,
+    *sums, held = run(
+        sums_kernel,
+        [like((WIDTH + cells, LANES), f32)] * span_x + [like(field.shape, bf16)],
+        (pltpu.with_memory_space_constraint(field, pltpu.HBM),),
+        places=pltpu.HBM,
         flops=cube // 4,
-        scratch=[parts] + chunked,
-    )
+        scratch=[parts, pltpu.SemaphoreType.DMA((4,))],
+    )
+    cols = held.reshape(rows, depth)
     wv, wo, wq, wk, wz = run(
         prepare_kernel,
         [like((WIDTH, wide), f32)] * 2 + [like((2 * WIDTH, wide), bf16)] * 2
@@ -602,7 +605,8 @@
         lows + (mix, wv, wo, wq, wk, cols, cots),
         flops=cube,
     )
-    total = run(add_pull_kernel, [pulled], swaps(total, "gx", span_x))
+    for level in range(span_x.bit_length() - 1):
+        total = run(add_pull_kernel, [pulled], (total, swap(total, "gx", span_x, 1 << level)))
     layer_output = run(
         output_kernel, [like(field.shape, bf16)], (top, wo, both, cols), flops=cube
     )

time: 52.4 us -> 54.8 us (1.046)
  waiting for transfers between devices: 18.4 us -> 20.5 us
  local copies, waits for them, and re-layouts: 1.05 us -> 1.98 us
  starting transfers between devices: 22.3 us -> 21.6 us
    ppermute x21 -> x20, waiting for transfers between devices: 18.4 us -> 20.5 us  [swap(): return lax.ppermute(part, axis, [(i, i ^ step) for i in range(size)])]
    unnamed x15 -> x13, local copies, waits for them, and re-layouts: 0.8 us -> 1.73 us
    ppermute x21 -> x20, starting transfers between devices: 22.3 us -> 21.6 us  [swap(): return lax.ppermute(part, axis, [(i, i ^ step) for i in range(size)])]
    pallas_call x12 -> x13, Pallas kernels: 9.74 us -> 9.69 us  [run(): pl.pallas_call(kernel, out_shape=tuple(outs), in_specs=[pl.BlockSpec(memo...]
  transfers between devices with their start and end apart: 21 -> 20, of which waited for: 14 -> 12; matrix products, arithmetic and copies ran while one was open for 0% -> 0% of each run, Pallas kernels for 9% -> 9%
where the time goes in v9:
time: 54.8 us; the launch traced here: 54.6 us
  starting transfers between devices  21.6 us (39%)
  waiting for transfers between devices  20.5 us (37%)
  Pallas kernels  9.69 us (18%)
  local copies, waits for them, and re-layouts  1.98 us (4%)
  between operations  0.8 us (1%)
    ppermute x20, starting transfers between devices, swap(): return lax.ppermute(part, axis, [(i, i ^ step) for i in range(size)])  21.6 us
    ppermute x20, waiting for transfers between devices, swap(): return lax.ppermute(part, axis, [(i, i ^ step) for i in range(size)])  20.5 us
    pallas_call x13, Pallas kernels, run(): pl.pallas_call(kernel, out_shape=tuple(outs), in_specs=[pl.BlockSpec(memo...  9.69 us
    unnamed x13, local copies, waits for them, and re-layouts  1.73 us
  transfers between devices with their start and end apart: 20, of which 12 were waited for; matrix products, arithmetic and copies ran while one was open for 0% of the time, Pallas kernels for 9%

profile of v9, /device:TPU:0, one launch (start us, length us, event | category | flops | bytes accessed | tf_op | source)
XLA Modules:
  0.0 54.6 jit_solution(16376601831103305392)
XLA Ops:
  0.6 1.8 %shard_map.77 = (f32[72,128]{1,0:T(8,128)S(1)}, f32[72,128]{1,0:T(8,128)S(1)}, f32[72,128]{1,0:T(8,128)S(1)}, f32[72,128]{1,0:T(8,128)S(1)}, bf16[64,2,4,512]{3,2,1,0:T(4,128)(2,1)S(1)}) custom-call(bf16[64,2,4,512]{3,2,1,0:T(4,128)(2,1)} %field_ref.1), custom_call_target="tpu_custom_call" | custom-call | flops 67108864 | bytes 1196032 | tf_op jit(solution)/shard_map/pallas_call | solution.py:512
  2.4 0.5 collective-permute-start
  2.9 2.6 %collective-permute-start.1 = (f32[72,128]{1,0:T(8,128)S(1)}, f32[72,128]{1,0:T(8,128)S(1)}, u32[]{:S(2)}, u32[]{:S(2)}) collective-permute-start(f32[72,128]{1,0:T(8,128)S(1)} %get-tuple-element.22), channel_id=1, source_target_pairs={{0,8},{4,12},{8,0},{12,4},{1,9},{5,13},{9,1},{13,5},{2,10},{6,14},... | collective-permute-start | bytes 110600 | tf_op jit(solution)/shard_map/ppermute | solution.py:27
  5.6 2.0 %collective-permute-done.1.refs_2_ = f32[72,128]{1,0:T(8,128)S(1)} collective-permute-done((f32[72,128]{1,0:T(8,128)S(1)}, f32[72,128]{1,0:T(8,128)S(1)}, u32[]{:S(2)}, u32[]{:S(2)}) %collective-permute-start.1) | collective-permute-done | bytes 36896 | tf_op jit(solution)/shard_map/ppermute | solution.py:27
  7.6 1.4 %collective-permute-done.2.refs_3_ = f32[72,128]{1,0:T(8,128)S(1)} collective-permute-done((f32[72,128]{1,0:T(8,128)S(1)}, f32[72,128]{1,0:T(8,128)S(1)}, u32[]{:S(2)}, u32[]{:S(2)}) %collective-permute-start.2) | collective-permute-done | bytes 36896 | tf_op jit(solution)/shard_map/ppermute | solution.py:27
  9.0 1.6 %collective-permute-start.3 = (f32[96,128]{1,0:T(8,128)S(1)}, f32[96,128]{1,0:T(8,128)S(1)}, u32[]{:S(2)}, u32[]{:S(2)}) collective-permute-start(f32[96,128]{1,0:T(8,128)S(1)} %shard_map.78.refs_0_), channel_id=1, source_target_pairs={{0,1},{1,0},{2,3},{3,2},{4,5},{5,4},{6,7},{7,6},{8,9},{9,8},{10,11... | collective-permute-start | bytes 147464 | tf_op jit(solution)/shard_map/ppermute | solution.py:27
  10.6 2.6 %collective-permute-start.4 = (f32[96,128]{1,0:T(8,128)S(1)}, f32[96,128]{1,0:T(8,128)S(1)}, u32[]{:S(2)}, u32[]{:S(2)}) collective-permute-start(f32[96,128]{1,0:T(8,128)S(1)} %shard_map.78.refs_0_), channel_id=1, source_target_pairs={{0,2},{1,3},{2,0},{3,1},{4,6},{5,7},{6,4},{7,5},{8,10},{9,11},{10,... | collective-permute-start | bytes 147464 | tf_op jit(solution)/shard_map/ppermute | solution.py:27
  13.4 3.1 %collective-permute-done.4.refs_2_ = f32[96,128]{1,0:T(8,128)S(1)} collective-permute-done((f32[96,128]{1,0:T(8,128)S(1)}, f32[96,128]{1,0:T(8,128)S(1)}, u32[]{:S(2)}, u32[]{:S(2)}) %collective-permute-start.4) | collective-permute-done | bytes 49184 | tf_op jit(solution)/shard_map/ppermute | solution.py:27
  16.5 2.6 %collective-permute-done.5.refs_3_ = f32[96,128]{1,0:T(8,128)S(1)} collective-permute-done((f32[96,128]{1,0:T(8,128)S(1)}, f32[96,128]{1,0:T(8,128)S(1)}, u32[]{:S(2)}, u32[]{:S(2)}) %collective-permute-start.5) | collective-permute-done | bytes 49184 | tf_op jit(solution)/shard_map/ppermute | solution.py:27
  19.2 0.9 %collective-permute-start.7 = (f32[72,128]{1,0:T(8,128)S(1)}, f32[72,128]{1,0:T(8,128)S(1)}, u32[]{:S(2)}, u32[]{:S(2)}) collective-permute-start(f32[72,128]{1,0:T(8,128)S(1)} %shard_map.79.refs_0_), channel_id=1, source_target_pairs={{0,8},{4,12},{8,0},{12,4},{1,9},{5,13},{9,1},{13,5},{2,10},{6,14},... | collective-permute-start | bytes 110600 | tf_op jit(solution)/shard_map/ppermute | solution.py:27
  20.1 0.9 %collective-permute-start.8 = (f32[72,128]{1,0:T(8,128)S(1)}, f32[72,128]{1,0:T(8,128)S(1)}, u32[]{:S(2)}, u32[]{:S(2)}) collective-permute-start(f32[72,128]{1,0:T(8,128)S(1)} %shard_map.79.refs_0_), channel_id=1, source_target_pairs={{0,12},{4,8},{8,4},{12,0},{1,13},{5,9},{9,5},{13,1},{2,14},{6,10},... | collective-permute-start | bytes 110600 | tf_op jit(solution)/shard_map/ppermute | solution.py:27
  21.2 0.9 %copy-done.4 = bf16[64,2,4,512]{3,2,1,0:T(4,128)(2,1)S(1)} copy-done((bf16[64,2,4,512]{3,2,1,0:T(4,128)(2,1)S(1)}, bf16[64,2,4,512]{3,2,1,0:T(4,128)(2,1)}, u32[]{:S(2)}) %copy-start.4) | copy-done | bytes 524312
  22.2 0.8 %copy-done = f32[3,2,64,64]{3,2,1,0:T(8,128)S(1)} copy-done((f32[3,2,64,64]{3,2,1,0:T(8,128)S(1)}, f32[3,2,64,64]{3,2,1,0:T(8,128)}, u32[]{:S(2)}) %copy-start) | copy-done | bytes 98328
  23.7 1.0 %shard_map.81 = (bf16[16,512]{1,0:T(8,128)(2,1)S(1)}, bf16[128,512]{1,0:T(8,128)(2,1)S(1)}, f32[72,512]{1,0:T(8,128)S(1)}) custom-call(f32[72,128]{1,0:T(8,128)S(1)} %shard_map.79.refs_0_, f32[72,128]{1,0:T(8,128)S(1)} %collective-permute-done.6.refs_1_, f32[72,128]{1,0:T(8,128)S(1)} %collective-permute-done.7.refs_2_, ...), custom_call_target="tpu_custom_call" | custom-call | flops 536870912 | bytes 1785856 | tf_op jit(solution)/shard_map/pallas_call | solution.py:512
  24.8 1.6 %collective-permute-start.10 = (bf16[16,512]{1,0:T(8,128)(2,1)S(1)}, bf16[16,512]{1,0:T(8,128)(2,1)S(1)}, u32[]{:S(2)}, u32[]{:S(2)}) collective-permute-start(bf16[16,512]{1,0:T(8,128)(2,1)S(1)} %get-tuple-element.28), channel_id=1, source_target_pairs={{0,2},{1,3},{2,0},{3,1},{4,6},{5,7},{6,4},{7,5},{8,10},{9,11},{10,... | collective-permute-start | bytes 49160 | tf_op jit(solution)/shard_map/ppermute | solution.py:27
  26.4 2.8 %collective-permute-start.11 = (bf16[16,512]{1,0:T(8,128)(2,1)S(1)}, bf16[16,512]{1,0:T(8,128)(2,1)S(1)}, u32[]{:S(2)}, u32[]{:S(2)}) collective-permute-start(bf16[16,512]{1,0:T(8,128)(2,1)S(1)} %get-tuple-element.28), channel_id=1, source_target_pairs={{0,3},{1,2},{2,1},{3,0},{4,7},{5,6},{6,5},{7,4},{8,11},{9,10},{10,... | collective-permute-start | bytes 49160 | tf_op jit(solution)/shard_map/ppermute | solution.py:27
  29.5 2.4 %collective-permute-done.11 = bf16[16,512]{1,0:T(8,128)(2,1)S(1)} collective-permute-done((bf16[16,512]{1,0:T(8,128)(2,1)S(1)}, bf16[16,512]{1,0:T(8,128)(2,1)S(1)}, u32[]{:S(2)}, u32[]{:S(2)}) %collective-permute-start.11) | collective-permute-done | bytes 16416 | tf_op jit(solution)/shard_map/ppermute | solution.py:27
  31.9 1.0 %collective-permute-start.13 = (bf16[64,512]{1,0:T(8,128)(2,1)S(1)}, bf16[64,512]{1,0:T(8,128)(2,1)S(1)}, u32[]{:S(2)}, u32[]{:S(2)}) collective-permute-start(bf16[64,512]{1,0:T(8,128)(2,1)S(1)} %constant_dynamic-update-slice_fusion.refs_0_), channel_id=1, source_target_pairs={{0,8},{4,12},{8,0},{12,4},{1,9},{5,13},{9,1},{13,5},{2,10},{6,14},... | collective-permute-start | bytes 196616 | tf_op jit(solution)/shard_map/ppermute | solution.py:27
  33.0 0.8 %collective-permute-start.14 = (bf16[64,512]{1,0:T(8,128)(2,1)S(1)}, bf16[64,512]{1,0:T(8,128)(2,1)S(1)}, u32[]{:S(2)}, u32[]{:S(2)}) collective-permute-start(bf16[64,512]{1,0:T(8,128)(2,1)S(1)} %constant_dynamic-update-slice_fusion.refs_0_), channel_id=1, source_target_pairs={{0,12},{4,8},{8,4},{12,0},{1,13},{5,9},{9,5},{13,1},{2,14},{6,10},... | collective-permute-start | bytes 196616 | tf_op jit(solution)/shard_map/ppermute | solution.py:27
  33.8 1.4 %shard_map.82 = (f32[2,64,128]{2,1,0:T(8,128)S(1)}, f32[8,128,64]{2,1,0:T(8,128)S(1)}, f32[2,1024,128]{2,1,0:T(8,128)S(1)}) custom-call(f32[96,128]{1,0:T(8,128)S(1)} %shard_map.78.refs_0_, f32[96,128]{1,0:T(8,128)S(1)} %collective-permute-done.3.refs_1_, f32[96,128]{1,0:T(8,128)S(1)} %collective-permute-done.4.refs_2_, ...), custom_call_target="tpu_custom_call" | custom-call | flops 134217728 | bytes 1736704 | tf_op jit(solution)/shard_map/pallas_call | solution.py:512
  35.3 1.6 %collective-permute-done.13.refs_2_ = bf16[64,512]{1,0:T(8,128)(2,1)S(1)} collective-permute-done((bf16[64,512]{1,0:T(8,128)(2,1)S(1)}, bf16[64,512]{1,0:T(8,128)(2,1)S(1)}, u32[]{:S(2)}, u32[]{:S(2)}) %collective-permute-start.13) | collective-permute-done | bytes 65568 | tf_op jit(solution)/shard_map/ppermute | solution.py:27
  36.8 0.6 %collective-permute-done.14.refs_3_ = bf16[64,512]{1,0:T(8,128)(2,1)S(1)} collective-permute-done((bf16[64,512]{1,0:T(8,128)(2,1)S(1)}, bf16[64,512]{1,0:T(8,128)(2,1)S(1)}, u32[]{:S(2)}, u32[]{:S(2)}) %collective-permute-start.14) | collective-permute-done | bytes 65568 | tf_op jit(solution)/shard_map/ppermute | solution.py:27
  37.5 1.0 %shard_map.83 = (f32[2,8,512]{2,1,0:T(8,128)S(1)}, bf16[64,512]{1,0:T(8,128)(2,1)S(1)}) custom-call(bf16[64,512]{1,0:T(8,128)(2,1)S(1)} %constant_dynamic-update-slice_fusion.refs_0_, bf16[64,512]{1,0:T(8,128)(2,1)S(1)} %collective-permute-done.12.refs_1_, bf16[64,512]{1,0:T(8,128)(2,1)S(1)} %collective-permute-done.13.refs_2_, ...), custom_call_target="tpu_custom_call" | custom-call | flops 268435456 | bytes 1998848 | tf_op jit(solution)/shard_map/pallas_call | solution.py:512
  38.8 1.0 %collective-permute-done.15.refs_1_ = bf16[64,512]{1,0:T(8,128)(2,1)S(1)} collective-permute-done((bf16[64,512]{1,0:T(8,128)(2,1)S(1)}, bf16[64,512]{1,0:T(8,128)(2,1)S(1)}, u32[]{:S(2)}, u32[]{:S(2)}) %collective-permute-start.15) | collective-permute-done | bytes 65568 | tf_op jit(solution)/shard_map/ppermute | solution.py:27
  39.9 1.1 %collective-permute-start.16 = (bf16[64,512]{1,0:T(8,128)(2,1)S(1)}, bf16[64,512]{1,0:T(8,128)(2,1)S(1)}, u32[]{:S(2)}, u32[]{:S(2)}) collective-permute-start(bf16[64,512]{1,0:T(8,128)(2,1)S(1)} %shard_map.85.refs_0_), channel_id=1, source_target_pairs={{0,8},{4,12},{8,0},{12,4},{1,9},{5,13},{9,1},{13,5},{2,10},{6,14},... | collective-permute-start | bytes 196616 | tf_op jit(solution)/shard_map/ppermute | solution.py:27
  40.9 1.3 %shard_map.84 = bf16[64,2,4,512]{3,2,1,0:T(4,128)(2,1)} custom-call(f32[2,8,512]{2,1,0:T(8,128)S(1)} %get-tuple-element.32.top_ref, f32[64,512]{1,0:T(8,128)S(1)} %get-tuple-element.27.refs_8_.refs_6_.wo_ref, bf16[128,512]{1,0:T(8,128)(2,1)S(1)} %get-tuple-element.33.both_ref, bf16[512,512]{1,0:T(8,128)(2,1)S(1)} %reshape.10.refs_5_.refs_9_.field_ref), custom_call_target="tpu_custom_call" | custom-call | flops 268435456 | bytes 1343488 | tf_op jit(solution)/shard_map/pallas_call | solution.py:512
  42.2 2.0 %collective-permute-done.16.refs_1_ = bf16[64,512]{1,0:T(8,128)(2,1)S(1)} collective-permute-done((bf16[64,512]{1,0:T(8,128)(2,1)S(1)}, bf16[64,512]{1,0:T(8,128)(2,1)S(1)}, u32[]{:S(2)}, u32[]{:S(2)}) %collective-permute-start.16) | collective-permute-done | bytes 65568 | tf_op jit(solution)/shard_map/ppermute | solution.py:27
  44.3 3.3 %collective-permute-start.18 = (bf16[64,512]{1,0:T(8,128)(2,1)S(1)}, bf16[64,512]{1,0:T(8,128)(2,1)S(1)}, u32[]{:S(2)}, u32[]{:S(2)}) collective-permute-start(bf16[64,512]{1,0:T(8,128)(2,1)S(1)} %shard_map.86.refs_0_), channel_id=1, source_target_pairs={{0,2},{1,3},{2,0},{3,1},{4,6},{5,7},{6,4},{7,5},{8,10},{9,11},{10,... | collective-permute-start | bytes 196616 | tf_op jit(solution)/shard_map/ppermute | solution.py:27
  47.6 1.0 %collective-permute-start.19 = (bf16[64,512]{1,0:T(8,128)(2,1)S(1)}, bf16[64,512]{1,0:T(8,128)(2,1)S(1)}, u32[]{:S(2)}, u32[]{:S(2)}) collective-permute-start(bf16[64,512]{1,0:T(8,128)(2,1)S(1)} %shard_map.86.refs_0_), channel_id=1, source_target_pairs={{0,3},{1,2},{2,1},{3,0},{4,7},{5,6},{6,5},{7,4},{8,11},{9,10},{10,... | collective-permute-start | bytes 196616 | tf_op jit(solution)/shard_map/ppermute | solution.py:27
  48.7 1.4 %shard_map.87.plane_ref = f32[8,64]{1,0:T(8,128)S(1)} custom-call(bf16[64,512]{1,0:T(8,128)(2,1)S(1)} %constant_dynamic-update-slice_fusion.refs_0_, bf16[64,512]{1,0:T(8,128)(2,1)S(1)} %collective-permute-done.12.refs_1_, bf16[64,512]{1,0:T(8,128)(2,1)S(1)} %collective-permute-done.13.refs_2_, bf16[64,512]{1,0:T(8,128)(2,1)S(1)} %collective-permute-done.14.refs_3_, ...), custom_call_target="tpu_custom_call" | custom-call | flops 536870912 | bytes 1738752 | tf_op jit(solution)/shard_map/pallas_call | solution.py:512
  50.6 3.1 %collective-permute-done.19.refs_3_ = bf16[64,512]{1,0:T(8,128)(2,1)S(1)} collective-permute-done((bf16[64,512]{1,0:T(8,128)(2,1)S(1)}, bf16[64,512]{1,0:T(8,128)(2,1)S(1)}, u32[]{:S(2)}, u32[]{:S(2)}) %collective-permute-start.19) | collective-permute-done | bytes 65568 | tf_op jit(solution)/shard_map/ppermute | solution.py:27
  53.7 0.9 %shard_map.89 = bf16[64,2,4,512]{3,2,1,0:T(4,128)(2,1)} custom-call(bf16[64,512]{1,0:T(8,128)(2,1)S(1)} %shard_map.86.refs_0_, bf16[64,512]{1,0:T(8,128)(2,1)S(1)} %collective-permute-done.17.refs_1_, bf16[64,512]{1,0:T(8,128)(2,1)S(1)} %collective-permute-done.18.refs_2_, bf16[64,512]{1,0:T(8,128)(2,1)S(1)} %collective-permute-done.19.refs_3_, ...), custom_call_target="tpu_custom_call" | custom-call | bytes 1982464 | tf_op jit(solution)/shard_map/pallas_call | solution.py:512
  (37 shorter events, 2.7 us)
Async XLA Ops:
  2.4 3.2 %collective-permute-start = (f32[72,128]{1,0:T(8,128)S(1)}, f32[72,128]{1,0:T(8,128)S(1)}, u32[]{:S(2)}, u32[]{:S(2)}) collective-permute-start(f32[72,128]{1,0:T(8,128)S(1)} %get-tuple-element.21), channel_id=1, source_target_pairs={{0,4},{4,0},{8,12},{12,8},{1,5},{5,1},{9,13},{13,9},{2,6},{6,2},{1... | collective-permute-start | bytes 110600 | tf_op jit(solution)/shard_map/ppermute | solution.py:27
  2.9 4.6 %collective-permute-start.1 = (f32[72,128]{1,0:T(8,128)S(1)}, f32[72,128]{1,0:T(8,128)S(1)}, u32[]{:S(2)}, u32[]{:S(2)}) collective-permute-start(f32[72,128]{1,0:T(8,128)S(1)} %get-tuple-element.22), channel_id=1, source_target_pairs={{0,8},{4,12},{8,0},{12,4},{1,9},{5,13},{9,1},{13,5},{2,10},{6,14},... | collective-permute-start | bytes 110600 | tf_op jit(solution)/shard_map/ppermute | solution.py:27
  5.5 3.4 %collective-permute-start.2 = (f32[72,128]{1,0:T(8,128)S(1)}, f32[72,128]{1,0:T(8,128)S(1)}, u32[]{:S(2)}, u32[]{:S(2)}) collective-permute-start(f32[72,128]{1,0:T(8,128)S(1)} %get-tuple-element.23), channel_id=1, source_target_pairs={{0,12},{4,8},{8,4},{12,0},{1,13},{5,9},{9,5},{13,1},{2,14},{6,10},... | collective-permute-start | bytes 110600 | tf_op jit(solution)/shard_map/ppermute | solution.py:27
  9.0 4.5 %collective-permute-start.3 = (f32[96,128]{1,0:T(8,128)S(1)}, f32[96,128]{1,0:T(8,128)S(1)}, u32[]{:S(2)}, u32[]{:S(2)}) collective-permute-start(f32[96,128]{1,0:T(8,128)S(1)} %shard_map.78.refs_0_), channel_id=1, source_target_pairs={{0,1},{1,0},{2,3},{3,2},{4,5},{5,4},{6,7},{7,6},{8,9},{9,8},{10,11... | collective-permute-start | bytes 147464 | tf_op jit(solution)/shard_map/ppermute | solution.py:27
  10.6 5.9 %collective-permute-start.4 = (f32[96,128]{1,0:T(8,128)S(1)}, f32[96,128]{1,0:T(8,128)S(1)}, u32[]{:S(2)}, u32[]{:S(2)}) collective-permute-start(f32[96,128]{1,0:T(8,128)S(1)} %shard_map.78.refs_0_), channel_id=1, source_target_pairs={{0,2},{1,3},{2,0},{3,1},{4,6},{5,7},{6,4},{7,5},{8,10},{9,11},{10,... | collective-permute-start | bytes 147464 | tf_op jit(solution)/shard_map/ppermute | solution.py:27
  13.2 5.9 %collective-permute-start.5 = (f32[96,128]{1,0:T(8,128)S(1)}, f32[96,128]{1,0:T(8,128)S(1)}, u32[]{:S(2)}, u32[]{:S(2)}) collective-permute-start(f32[96,128]{1,0:T(8,128)S(1)} %shard_map.78.refs_0_), channel_id=1, source_target_pairs={{0,3},{1,2},{2,1},{3,0},{4,7},{5,6},{6,5},{7,4},{8,11},{9,10},{10,... | collective-permute-start | bytes 147464 | tf_op jit(solution)/shard_map/ppermute | solution.py:27
  19.1 4.2 %collective-permute-start.6 = (f32[72,128]{1,0:T(8,128)S(1)}, f32[72,128]{1,0:T(8,128)S(1)}, u32[]{:S(2)}, u32[]{:S(2)}) collective-permute-start(f32[72,128]{1,0:T(8,128)S(1)} %shard_map.79.refs_0_), channel_id=1, source_target_pairs={{0,4},{4,0},{8,12},{12,8},{1,5},{5,1},{9,13},{13,9},{2,6},{6,2},{1... | collective-permute-start | bytes 110600 | tf_op jit(solution)/shard_map/ppermute | solution.py:27
  19.2 4.1 %collective-permute-start.7 = (f32[72,128]{1,0:T(8,128)S(1)}, f32[72,128]{1,0:T(8,128)S(1)}, u32[]{:S(2)}, u32[]{:S(2)}) collective-permute-start(f32[72,128]{1,0:T(8,128)S(1)} %shard_map.79.refs_0_), channel_id=1, source_target_pairs={{0,8},{4,12},{8,0},{12,4},{1,9},{5,13},{9,1},{13,5},{2,10},{6,14},... | collective-permute-start | bytes 110600 | tf_op jit(solution)/shard_map/ppermute | solution.py:27
  20.1 3.6 %collective-permute-start.8 = (f32[72,128]{1,0:T(8,128)S(1)}, f32[72,128]{1,0:T(8,128)S(1)}, u32[]{:S(2)}, u32[]{:S(2)}) collective-permute-start(f32[72,128]{1,0:T(8,128)S(1)} %shard_map.79.refs_0_), channel_id=1, source_target_pairs={{0,12},{4,8},{8,4},{12,0},{1,13},{5,9},{9,5},{13,1},{2,14},{6,10},... | collective-permute-start | bytes 110600 | tf_op jit(solution)/shard_map/ppermute | solution.py:27
  21.0 1.0 %copy-start.4 = (bf16[64,2,4,512]{3,2,1,0:T(4,128)(2,1)S(1)}, bf16[64,2,4,512]{3,2,1,0:T(4,128)(2,1)}, u32[]{:S(2)}) copy-start(bf16[64,2,4,512]{3,2,1,0:T(4,128)(2,1)} %param.7) | copy-start | bytes 1572868
  22.1 0.9 %copy-start = (f32[3,2,64,64]{3,2,1,0:T(8,128)S(1)}, f32[3,2,64,64]{3,2,1,0:T(8,128)}, u32[]{:S(2)}) copy-start(f32[3,2,64,64]{3,2,1,0:T(8,128)} %refs_7_.1) | copy-start | bytes 294916
  22.1 0.9 %copy-start.2 = (bf16[64,64]{1,0:T(8,128)(2,1)S(1)}, bf16[64,64]{1,0:T(8,128)(2,1)}, u32[]{:S(2)}) copy-start(bf16[64,64]{1,0:T(8,128)(2,1)} %wv_ref.1) | copy-start | bytes 24580
  22.1 0.9 %copy-start.3 = (bf16[64,64]{1,0:T(8,128)(2,1)S(1)}, bf16[64,64]{1,0:T(8,128)(2,1)}, u32[]{:S(2)}) copy-start(bf16[64,64]{1,0:T(8,128)(2,1)} %wo_ref.1) | copy-start | bytes 24580
  24.7 9.1 %copy-start.1 = (bf16[2,128,128]{2,1,0:T(8,128)(2,1)S(1)}, bf16[2,128,128]{2,1,0:T(8,128)(2,1)}, u32[]{:S(2)}) copy-start(bf16[2,128,128]{2,1,0:T(8,128)(2,1)} %constant.2.clone.refs_4_.refs_6_) | copy-start | bytes 196612
  24.7 4.5 %collective-permute-start.9 = (bf16[16,512]{1,0:T(8,128)(2,1)S(1)}, bf16[16,512]{1,0:T(8,128)(2,1)S(1)}, u32[]{:S(2)}, u32[]{:S(2)}) collective-permute-start(bf16[16,512]{1,0:T(8,128)(2,1)S(1)} %get-tuple-element.28), channel_id=1, source_target_pairs={{0,1},{1,0},{2,3},{3,2},{4,5},{5,4},{6,7},{7,6},{8,9},{9,8},{10,11... | collective-permute-start | bytes 49160 | tf_op jit(solution)/shard_map/ppermute | solution.py:27
  24.8 4.7 %collective-permute-start.10 = (bf16[16,512]{1,0:T(8,128)(2,1)S(1)}, bf16[16,512]{1,0:T(8,128)(2,1)S(1)}, u32[]{:S(2)}, u32[]{:S(2)}) collective-permute-start(bf16[16,512]{1,0:T(8,128)(2,1)S(1)} %get-tuple-element.28), channel_id=1, source_target_pairs={{0,2},{1,3},{2,0},{3,1},{4,6},{5,7},{6,4},{7,5},{8,10},{9,11},{10,... | collective-permute-start | bytes 49160 | tf_op jit(solution)/shard_map/ppermute | solution.py:27
  26.4 5.5 %collective-permute-start.11 = (bf16[16,512]{1,0:T(8,128)(2,1)S(1)}, bf16[16,512]{1,0:T(8,128)(2,1)S(1)}, u32[]{:S(2)}, u32[]{:S(2)}) collective-permute-start(bf16[16,512]{1,0:T(8,128)(2,1)S(1)} %get-tuple-element.28), channel_id=1, source_target_pairs={{0,3},{1,2},{2,1},{3,0},{4,7},{5,6},{6,5},{7,4},{8,11},{9,10},{10,... | collective-permute-start | bytes 49160 | tf_op jit(solution)/shard_map/ppermute | solution.py:27
  31.9 3.3 %collective-permute-start.12 = (bf16[64,512]{1,0:T(8,128)(2,1)S(1)}, bf16[64,512]{1,0:T(8,128)(2,1)S(1)}, u32[]{:S(2)}, u32[]{:S(2)}) collective-permute-start(bf16[64,512]{1,0:T(8,128)(2,1)S(1)} %constant_dynamic-update-slice_fusion.refs_0_), channel_id=1, source_target_pairs={{0,4},{4,0},{8,12},{12,8},{1,5},{5,1},{9,13},{13,9},{2,6},{6,2},{1... | collective-permute-start | bytes 196616 | tf_op jit(solution)/shard_map/ppermute | solution.py:27
  31.9 4.9 %collective-permute-start.13 = (bf16[64,512]{1,0:T(8,128)(2,1)S(1)}, bf16[64,512]{1,0:T(8,128)(2,1)S(1)}, u32[]{:S(2)}, u32[]{:S(2)}) collective-permute-start(bf16[64,512]{1,0:T(8,128)(2,1)S(1)} %constant_dynamic-update-slice_fusion.refs_0_), channel_id=1, source_target_pairs={{0,8},{4,12},{8,0},{12,4},{1,9},{5,13},{9,1},{13,5},{2,10},{6,14},... | collective-permute-start | bytes 196616 | tf_op jit(solution)/shard_map/ppermute | solution.py:27
  33.0 4.5 %collective-permute-start.14 = (bf16[64,512]{1,0:T(8,128)(2,1)S(1)}, bf16[64,512]{1,0:T(8,128)(2,1)S(1)}, u32[]{:S(2)}, u32[]{:S(2)}) collective-permute-start(bf16[64,512]{1,0:T(8,128)(2,1)S(1)} %constant_dynamic-update-slice_fusion.refs_0_), channel_id=1, source_target_pairs={{0,12},{4,8},{8,4},{12,0},{1,13},{5,9},{9,5},{13,1},{2,14},{6,10},... | collective-permute-start | bytes 196616 | tf_op jit(solution)/shard_map/ppermute | solution.py:27
  38.5 1.3 %collective-permute-start.15 = (bf16[64,512]{1,0:T(8,128)(2,1)S(1)}, bf16[64,512]{1,0:T(8,128)(2,1)S(1)}, u32[]{:S(2)}, u32[]{:S(2)}) collective-permute-start(bf16[64,512]{1,0:T(8,128)(2,1)S(1)} %get-tuple-element.34.refs_0_), channel_id=1, source_target_pairs={{0,4},{4,0},{8,12},{12,8},{1,5},{5,1},{9,13},{13,9},{2,6},{6,2},{1... | collective-permute-start | bytes 196616 | tf_op jit(solution)/shard_map/ppermute | solution.py:27
  39.9 4.3 %collective-permute-start.16 = (bf16[64,512]{1,0:T(8,128)(2,1)S(1)}, bf16[64,512]{1,0:T(8,128)(2,1)S(1)}, u32[]{:S(2)}, u32[]{:S(2)}) collective-permute-start(bf16[64,512]{1,0:T(8,128)(2,1)S(1)} %shard_map.85.refs_0_), channel_id=1, source_target_pairs={{0,8},{4,12},{8,0},{12,4},{1,9},{5,13},{9,1},{13,5},{2,10},{6,14},... | collective-permute-start | bytes 196616 | tf_op jit(solution)/shard_map/ppermute | solution.py:27
  44.2 6.4 %collective-permute-start.17 = (bf16[64,512]{1,0:T(8,128)(2,1)S(1)}, bf16[64,512]{1,0:T(8,128)(2,1)S(1)}, u32[]{:S(2)}, u32[]{:S(2)}) collective-permute-start(bf16[64,512]{1,0:T(8,128)(2,1)S(1)} %shard_map.86.refs_0_), channel_id=1, source_target_pairs={{0,1},{1,0},{2,3},{3,2},{4,5},{5,4},{6,7},{7,6},{8,9},{9,8},{10,11... | collective-permute-start | bytes 196616 | tf_op jit(solution)/shard_map/ppermute | solution.py:27
  44.3 6.3 %collective-permute-start.18 = (bf16[64,512]{1,0:T(8,128)(2,1)S(1)}, bf16[64,512]{1,0:T(8,128)(2,1)S(1)}, u32[]{:S(2)}, u32[]{:S(2)}) collective-permute-start(bf16[64,512]{1,0:T(8,128)(2,1)S(1)} %shard_map.86.refs_0_), channel_id=1, source_target_pairs={{0,2},{1,3},{2,0},{3,1},{4,6},{5,7},{6,4},{7,5},{8,10},{9,11},{10,... | collective-permute-start | bytes 196616 | tf_op jit(solution)/shard_map/ppermute | solution.py:27
  47.6 6.1 %collective-permute-start.19 = (bf16[64,512]{1,0:T(8,128)(2,1)S(1)}, bf16[64,512]{1,0:T(8,128)(2,1)S(1)}, u32[]{:S(2)}, u32[]{:S(2)}) collective-permute-start(bf16[64,512]{1,0:T(8,128)(2,1)S(1)} %shard_map.86.refs_0_), channel_id=1, source_target_pairs={{0,3},{1,2},{2,1},{3,0},{4,7},{5,6},{6,5},{7,4},{8,11},{9,10},{10,... | collective-permute-start | bytes 196616 | tf_op jit(solution)/shard_map/ppermute | solution.py:27

commit v10 on v9

--- a/solution.py
+++ b/solution.py
@@ -203,7 +203,8 @@
 
 
 def join_quarters(part_ref, quarters):
-    for step, quarter in enumerate(quarters):
+    size = len(quarters)
+    for step, quarter in zip([0, *range(size - 1, 0, -1)], quarters):
         part_ref[lax.axis_index("gx") ^ step] = quarter[...]
     return jnp.concatenate([part_ref[index] for index in range(part_ref.shape[0])], axis=1)
 
@@ -236,8 +237,9 @@
 
 
 def sums_kernel(field_ref, *refs):
-    outs, (data_ref, part_ref, semaphores) = refs[:-3], refs[-3:]
+    outs, (cols_ref, data_ref, part_ref, semaphores) = refs[:-4], refs[-4:]
     _, rows_x, rows_y, depth = data_ref.shape
+    cells = rows_x * rows_y
     chunks = semaphores.shape[0]
     size = WIDTH // chunks
     copies = [
@@ -250,26 +252,27 @@
     ]
     for copy in copies:
         copy.start()
-    own = jnp.zeros((rows_x, rows_y, LANES), jnp.float32)
+    own = jnp.zeros((cells, LANES), jnp.float32)
+    pick = number((size, size * cells), 1) // cells == number((size, size * cells), 0)
+    pick = pick.astype(jnp.bfloat16)
+    ones = jnp.ones((depth, LANES), jnp.bfloat16)
     for index, copy in enumerate(copies):
         copy.wait()
         rows = slice(index * size, (index + 1) * size)
         data = data_ref[rows].astype(jnp.float32)
-        part = jnp.sum(jnp.sum(data, axis=1), axis=1)
+        data = jnp.concatenate([data[:, at_x] for at_x in range(rows_x)], axis=1)
+        data = data.reshape(size * cells, depth).astype(jnp.bfloat16)
+        cols_ref[index * size * cells : (index + 1) * size * cells, :] = data
+        part = mul(pick, data)
         for quarter in range(part_ref.shape[0]):
             part_ref[quarter, rows, :] = part[:, quarter * LANES : (quarter + 1) * LANES]
-        lanes = data[..., :LANES]
-        for start in range(LANES, depth, LANES):
-            lanes = lanes + data[..., start : start + LANES]
-        row_sums = jnp.sum(lanes, axis=3, keepdims=True)
-        shape = lanes.shape
-        mine = number(shape, 0) + index * size == number(shape, 3)
+        row_sums = mul(data, ones).reshape(size, cells, LANES)
+        shape = row_sums.shape
+        mine = number(shape, 0) + index * size == number(shape, 2)
         own = own + jnp.sum(jnp.where(mine, row_sums, 0.0), axis=0)
     for step, out in enumerate(outs):
         out[0:WIDTH, :] = part_ref[lax.axis_index("gx") ^ step]
-        for index in range(rows_x):
-            start = WIDTH + index * rows_y
-            out[start : start + rows_y, :] = own[index]
+        out[WIDTH:, :] = own
 
 
 def add_kernel(*refs):
@@ -278,10 +281,15 @@
     for part in parts[1:]:
         total = total + part[0:WIDTH, :]
     out_ref[0:WIDTH, :] = total
-    cells = parts[0].shape[0] - WIDTH
-    for step, part in enumerate(parts):
-        start = WIDTH + step * cells
-        out_ref[start : start + cells, :] = part[WIDTH:, :]
+    start = WIDTH
+    for part in parts:
+        more = part.shape[0] - WIDTH
+        out_ref[start : start + more, :] = part[WIDTH:, :]
+        start += more
+
+
+def stack_kernel(*refs):
+    refs[-1][...] = jnp.concatenate([ref[...] for ref in refs[:-1]], axis=0)
 
 
 def factor_kernel(places, *refs):
@@ -300,7 +308,7 @@
     total = refs[0][...].astype(jnp.float32)
     for part in refs[1:-1]:
         total = total + part[...].astype(jnp.float32)
-    refs[-1][...] = total.astype(jnp.bfloat16)
+    refs[-1][...] = total.astype(refs[-1].dtype)
 
 
 def by_head(part):
@@ -316,7 +324,7 @@
             part[WIDTH + step * cells : WIDTH + (step + 1) * cells, :]
             for first in range(span_x)
             for part in parts
-            for step in range(first, (parts[0].shape[0] - WIDTH) // cells, span_x)
+            for step in range(first, (part.shape[0] - WIDTH) // cells, span_x)
         ],
         axis=0,
     )[:, :WIDTH]
@@ -553,18 +561,25 @@
         if not isinstance(sent, (tuple, list)):
             sent = [sent] * size
         return tuple(sent[:1]) + tuple(
-            swap(sent[step], axis, size, step) for step in range(1, size)
+            swap(sent[step], axis, size, step) for step in range(size - 1, 0, -1)
         )
 
-    *sums, held = run(
+    def taken(kernel, sent, dtype=None, last=False):
+        found, *others = sent
+        for part in others if last else others[:-1]:
+            more = part.shape[0] if kernel is stack_kernel else part.shape[0] - WIDTH
+            shape = (found.shape[0] + more,) + part.shape[1:]
+            found = run(kernel, [like(shape, dtype or found.dtype)], (found, part))
+        return (found,) if last else (found, others[-1])
+
+    *sums, cols = run(
         sums_kernel,
-        [like((WIDTH + cells, LANES), f32)] * span_x + [like(field.shape, bf16)],
+        [like((WIDTH + cells, LANES), f32)] * span_x + [like((rows, depth), bf16)],
         (pltpu.with_memory_space_constraint(field, pltpu.HBM),),
         places=pltpu.HBM,
         flops=cube // 4,
-        scratch=[parts, pltpu.SemaphoreType.DMA((4,))],
-    )
-    cols = held.reshape(rows, depth)
+        scratch=[chunked[0], parts, chunked[1]],
+    )
     wv, wo, wq, wk, wz = run(
         prepare_kernel,
         [like((WIDTH, wide), f32)] * 2 + [like((2 * WIDTH, wide), bf16)] * 2
@@ -572,10 +587,10 @@
         (w_value, w_out, qk_weight),
         flops=cube // 8,
     )
-    def add(sent, size):
-        return run(add_kernel, [like((WIDTH + size * cells, LANES), f32)], sent)
-
-    totals = swaps(add(swaps(sums, "gx", span_x), span_x), "gy", span_y)
+    total = run(
+        add_kernel, [like((WIDTH + span_x * cells, LANES), f32)], swaps(sums, "gx", span_x)
+    )
+    totals = taken(add_kernel, swaps(total, "gy", span_y))
     mine = run(
         functools.partial(factor_kernel, grid_x * grid_y),
         [like((WIDTH + HEAD_DIM, LANES), f32)],
@@ -596,7 +611,7 @@
         flops=2 * cube,
         scratch=[pltpu.VMEM((span_x, WIDTH + HEAD_DIM, LANES), f32)],
     )
-    low = jnp.concatenate(swaps(send, "gy", span_y), axis=0)
+    (low,) = taken(stack_kernel, swaps(send, "gy", span_y), last=True)
     lows = swaps(low, "gx", span_x)
     pulled = like((WIDTH, depth), bf16)
     top, total = run(
@@ -620,7 +635,7 @@
     field_grad = run(
         functools.partial(final_kernel, grid_x * grid_y),
         [like(field.shape, bf16)],
-        swaps(total, "gy", span_y) + (feat_z, base),
+        taken(add_pull_kernel, swaps(total, "gy", span_y), f32) + (feat_z, base),
         target=pltpu.HBM,
         scratch=chunked,
     )

time: 54.8 us -> 52.5 us (0.958)
  local copies, waits for them, and re-layouts: 1.98 us -> 0.15 us
  waiting for transfers between devices: 20.5 us -> 19.8 us
    unnamed x13 -> x10, local copies, waits for them, and re-layouts: 1.73 us -> 0.03 us
    ppermute x20, waiting for transfers between devices: 20.5 us -> 19.8 us  [swap(): return lax.ppermute(part, axis, [(i, i ^ step) for i in range(size)])]
    pallas_call x13 -> x20, Pallas kernels: 9.69 us -> 9.78 us  [run(): pl.pallas_call(kernel, out_shape=tuple(outs), in_specs=[pl.BlockSpec(memo...]
  transfers between devices with their start and end apart: 20 -> 20, of which waited for: 12 -> 14; matrix products, arithmetic and copies ran while one was open for 0% -> 0% of each run, Pallas kernels for 9% -> 9%
where the time goes in v10:
time: 52.5 us; the launch traced here: 52.3 us
  starting transfers between devices  21.8 us (42%)
  waiting for transfers between devices  19.8 us (38%)
  Pallas kernels  9.78 us (19%)
  between operations  0.84 us (2%)
    ppermute x20, starting transfers between devices, swap(): return lax.ppermute(part, axis, [(i, i ^ step) for i in range(size)])  21.8 us
    ppermute x20, waiting for transfers between devices, swap(): return lax.ppermute(part, axis, [(i, i ^ step) for i in range(size)])  19.8 us
    pallas_call x20, Pallas kernels, run(): pl.pallas_call(kernel, out_shape=tuple(outs), in_specs=[pl.BlockSpec(memo...  9.78 us
  transfers between devices with their start and end apart: 20, of which 14 were waited for; matrix products, arithmetic and copies ran while one was open for 0% of the time, Pallas kernels for 9%

profile of v10, /device:TPU:0, one launch (start us, length us, event | category | flops | bytes accessed | tf_op | source)
XLA Modules:
  0.0 52.3 jit_solution(10460895818143842845)
XLA Ops:
  0.6 1.9 %shard_map.77 = (f32[72,128]{1,0:T(8,128)S(1)}, f32[72,128]{1,0:T(8,128)S(1)}, f32[72,128]{1,0:T(8,128)S(1)}, f32[72,128]{1,0:T(8,128)S(1)}, bf16[512,512]{1,0:T(8,128)(2,1)S(1)}) custom-call(bf16[64,2,4,512]{3,2,1,0:T(4,128)(2,1)} %field_ref.1), custom_call_target="tpu_custom_call" | custom-call | flops 67108864 | bytes 1196032 | tf_op jit(solution)/shard_map/pallas_call | solution.py:520
  2.5 2.4 %collective-permute-start = (f32[72,128]{1,0:T(8,128)S(1)}, f32[72,128]{1,0:T(8,128)S(1)}, u32[]{:S(2)}, u32[]{:S(2)}) collective-permute-start(f32[72,128]{1,0:T(8,128)S(1)} %get-tuple-element.21), channel_id=1, source_target_pairs={{0,12},{4,8},{8,4},{12,0},{1,13},{5,9},{9,5},{13,1},{2,14},{6,10},... | collective-permute-start | bytes 110600 | tf_op jit(solution)/shard_map/ppermute | solution.py:27
  4.9 0.6 %collective-permute-start.1 = (f32[72,128]{1,0:T(8,128)S(1)}, f32[72,128]{1,0:T(8,128)S(1)}, u32[]{:S(2)}, u32[]{:S(2)}) collective-permute-start(f32[72,128]{1,0:T(8,128)S(1)} %get-tuple-element.22), channel_id=1, source_target_pairs={{0,8},{4,12},{8,0},{12,4},{1,9},{5,13},{9,1},{13,5},{2,10},{6,14},... | collective-permute-start | bytes 110600 | tf_op jit(solution)/shard_map/ppermute | solution.py:27
  5.6 1.2 %collective-permute-done.refs_1_ = f32[72,128]{1,0:T(8,128)S(1)} collective-permute-done((f32[72,128]{1,0:T(8,128)S(1)}, f32[72,128]{1,0:T(8,128)S(1)}, u32[]{:S(2)}, u32[]{:S(2)}) %collective-permute-start) | collective-permute-done | bytes 36896 | tf_op jit(solution)/shard_map/ppermute | solution.py:27
  6.8 2.2 %collective-permute-done.1.refs_2_ = f32[72,128]{1,0:T(8,128)S(1)} collective-permute-done((f32[72,128]{1,0:T(8,128)S(1)}, f32[72,128]{1,0:T(8,128)S(1)}, u32[]{:S(2)}, u32[]{:S(2)}) %collective-permute-start.1) | collective-permute-done | bytes 36896 | tf_op jit(solution)/shard_map/ppermute | solution.py:27
  9.0 3.7 %collective-permute-start.3 = (f32[96,128]{1,0:T(8,128)S(1)}, f32[96,128]{1,0:T(8,128)S(1)}, u32[]{:S(2)}, u32[]{:S(2)}) collective-permute-start(f32[96,128]{1,0:T(8,128)S(1)} %shard_map.78.refs_0_), channel_id=1, source_target_pairs={{0,3},{1,2},{2,1},{3,0},{4,7},{5,6},{6,5},{7,4},{8,11},{9,10},{10,... | collective-permute-start | bytes 147464 | tf_op jit(solution)/shard_map/ppermute | solution.py:27
  12.7 0.8 %collective-permute-start.5 = (f32[96,128]{1,0:T(8,128)S(1)}, f32[96,128]{1,0:T(8,128)S(1)}, u32[]{:S(2)}, u32[]{:S(2)}) collective-permute-start(f32[96,128]{1,0:T(8,128)S(1)} %shard_map.78.refs_0_), channel_id=1, source_target_pairs={{0,1},{1,0},{2,3},{3,2},{4,5},{5,4},{6,7},{7,6},{8,9},{9,8},{10,11... | collective-permute-start | bytes 147464 | tf_op jit(solution)/shard_map/ppermute | solution.py:27
  13.5 1.8 %collective-permute-done.3.refs_1_ = f32[96,128]{1,0:T(8,128)S(1)} collective-permute-done((f32[96,128]{1,0:T(8,128)S(1)}, f32[96,128]{1,0:T(8,128)S(1)}, u32[]{:S(2)}, u32[]{:S(2)}) %collective-permute-start.3) | collective-permute-done | bytes 49184 | tf_op jit(solution)/shard_map/ppermute | solution.py:27
  15.2 2.4 %collective-permute-done.4.refs_1_ = f32[96,128]{1,0:T(8,128)S(1)} collective-permute-done((f32[96,128]{1,0:T(8,128)S(1)}, f32[96,128]{1,0:T(8,128)S(1)}, u32[]{:S(2)}, u32[]{:S(2)}) %collective-permute-start.4) | collective-permute-done | bytes 49184 | tf_op jit(solution)/shard_map/ppermute | solution.py:27
  17.8 1.1 %collective-permute-start.7 = (f32[72,128]{1,0:T(8,128)S(1)}, f32[72,128]{1,0:T(8,128)S(1)}, u32[]{:S(2)}, u32[]{:S(2)}) collective-permute-start(f32[72,128]{1,0:T(8,128)S(1)} %shard_map.81.refs_0_), channel_id=1, source_target_pairs={{0,8},{4,12},{8,0},{12,4},{1,9},{5,13},{9,1},{13,5},{2,10},{6,14},... | collective-permute-start | bytes 110600 | tf_op jit(solution)/shard_map/ppermute | solution.py:27
  19.0 0.7 %collective-permute-start.6 = (f32[72,128]{1,0:T(8,128)S(1)}, f32[72,128]{1,0:T(8,128)S(1)}, u32[]{:S(2)}, u32[]{:S(2)}) collective-permute-start(f32[72,128]{1,0:T(8,128)S(1)} %shard_map.81.refs_0_), channel_id=1, source_target_pairs={{0,12},{4,8},{8,4},{12,0},{1,13},{5,9},{9,5},{13,1},{2,14},{6,10},... | collective-permute-start | bytes 110600 | tf_op jit(solution)/shard_map/ppermute | solution.py:27
  20.1 1.7 %collective-permute-done.7.refs_2_ = f32[72,128]{1,0:T(8,128)S(1)} collective-permute-done((f32[72,128]{1,0:T(8,128)S(1)}, f32[72,128]{1,0:T(8,128)S(1)}, u32[]{:S(2)}, u32[]{:S(2)}) %collective-permute-start.7) | collective-permute-done | bytes 36896 | tf_op jit(solution)/shard_map/ppermute | solution.py:27
  22.4 1.0 %shard_map.83 = (bf16[16,512]{1,0:T(8,128)(2,1)S(1)}, bf16[128,512]{1,0:T(8,128)(2,1)S(1)}, f32[72,512]{1,0:T(8,128)S(1)}) custom-call(f32[72,128]{1,0:T(8,128)S(1)} %shard_map.81.refs_0_, f32[72,128]{1,0:T(8,128)S(1)} %collective-permute-done.6.refs_1_, f32[72,128]{1,0:T(8,128)S(1)} %collective-permute-done.7.refs_2_, ...), custom_call_target="tpu_custom_call" | custom-call | flops 536870912 | bytes 1785856 | tf_op jit(solution)/shard_map/pallas_call | solution.py:520
  23.4 2.2 %collective-permute-start.9 = (bf16[16,512]{1,0:T(8,128)(2,1)S(1)}, bf16[16,512]{1,0:T(8,128)(2,1)S(1)}, u32[]{:S(2)}, u32[]{:S(2)}) collective-permute-start(bf16[16,512]{1,0:T(8,128)(2,1)S(1)} %get-tuple-element.28.refs_0_), channel_id=1, source_target_pairs={{0,3},{1,2},{2,1},{3,0},{4,7},{5,6},{6,5},{7,4},{8,11},{9,10},{10,... | collective-permute-start | bytes 49160 | tf_op jit(solution)/shard_map/ppermute | solution.py:27
  25.8 2.1 %collective-permute-start.11 = (bf16[16,512]{1,0:T(8,128)(2,1)S(1)}, bf16[16,512]{1,0:T(8,128)(2,1)S(1)}, u32[]{:S(2)}, u32[]{:S(2)}) collective-permute-start(bf16[16,512]{1,0:T(8,128)(2,1)S(1)} %get-tuple-element.28.refs_0_), channel_id=1, source_target_pairs={{0,1},{1,0},{2,3},{3,2},{4,5},{5,4},{6,7},{7,6},{8,9},{9,8},{10,11... | collective-permute-start | bytes 49160 | tf_op jit(solution)/shard_map/ppermute | solution.py:27
  27.9 1.3 %collective-permute-done.9.refs_1_ = bf16[16,512]{1,0:T(8,128)(2,1)S(1)} collective-permute-done((bf16[16,512]{1,0:T(8,128)(2,1)S(1)}, bf16[16,512]{1,0:T(8,128)(2,1)S(1)}, u32[]{:S(2)}, u32[]{:S(2)}) %collective-permute-start.9) | collective-permute-done | bytes 16416 | tf_op jit(solution)/shard_map/ppermute | solution.py:27
  29.2 1.1 %collective-permute-done.10.refs_1_ = bf16[16,512]{1,0:T(8,128)(2,1)S(1)} collective-permute-done((bf16[16,512]{1,0:T(8,128)(2,1)S(1)}, bf16[16,512]{1,0:T(8,128)(2,1)S(1)}, u32[]{:S(2)}, u32[]{:S(2)}) %collective-permute-start.10) | collective-permute-done | bytes 16416 | tf_op jit(solution)/shard_map/ppermute | solution.py:27
  30.4 1.1 %collective-permute-start.13 = (bf16[64,512]{1,0:T(8,128)(2,1)S(1)}, bf16[64,512]{1,0:T(8,128)(2,1)S(1)}, u32[]{:S(2)}, u32[]{:S(2)}) collective-permute-start(bf16[64,512]{1,0:T(8,128)(2,1)S(1)} %shard_map.86.refs_0_), channel_id=1, source_target_pairs={{0,8},{4,12},{8,0},{12,4},{1,9},{5,13},{9,1},{13,5},{2,10},{6,14},... | collective-permute-start | bytes 196616 | tf_op jit(solution)/shard_map/ppermute | solution.py:27
  31.5 0.8 %collective-permute-start.12 = (bf16[64,512]{1,0:T(8,128)(2,1)S(1)}, bf16[64,512]{1,0:T(8,128)(2,1)S(1)}, u32[]{:S(2)}, u32[]{:S(2)}) collective-permute-start(bf16[64,512]{1,0:T(8,128)(2,1)S(1)} %shard_map.86.refs_0_), channel_id=1, source_target_pairs={{0,12},{4,8},{8,4},{12,0},{1,13},{5,9},{9,5},{13,1},{2,14},{6,10},... | collective-permute-start | bytes 196616 | tf_op jit(solution)/shard_map/ppermute | solution.py:27
  32.3 1.4 %shard_map.87 = (f32[2,64,128]{2,1,0:T(8,128)S(1)}, f32[8,128,64]{2,1,0:T(8,128)S(1)}, f32[2,1024,128]{2,1,0:T(8,128)S(1)}) custom-call(f32[160,128]{1,0:T(8,128)S(1)} %shard_map.80.refs_0_, f32[96,128]{1,0:T(8,128)S(1)} %collective-permute-done.5.refs_1_, bf16[2,128,128]{2,1,0:T(8,128)(2,1)S(1)} %copy-done.1, f32[3,2,64,64]{3,2,1,0:T(8,128)S(1)} %copy-done), custom_call_target="tpu_custom_call" | custom-call | flops 134217728 | bytes 1671168 | tf_op jit(solution)/shard_map/pallas_call | solution.py:520
  33.7 1.6 %collective-permute-done.13.refs_2_ = bf16[64,512]{1,0:T(8,128)(2,1)S(1)} collective-permute-done((bf16[64,512]{1,0:T(8,128)(2,1)S(1)}, bf16[64,512]{1,0:T(8,128)(2,1)S(1)}, u32[]{:S(2)}, u32[]{:S(2)}) %collective-permute-start.13) | collective-permute-done | bytes 65568 | tf_op jit(solution)/shard_map/ppermute | solution.py:27
  35.9 1.0 %shard_map.88 = (f32[2,8,512]{2,1,0:T(8,128)S(1)}, bf16[64,512]{1,0:T(8,128)(2,1)S(1)}) custom-call(bf16[64,512]{1,0:T(8,128)(2,1)S(1)} %shard_map.86.refs_0_, bf16[64,512]{1,0:T(8,128)(2,1)S(1)} %collective-permute-done.12.refs_1_, bf16[64,512]{1,0:T(8,128)(2,1)S(1)} %collective-permute-done.13.refs_2_, ...), custom_call_target="tpu_custom_call" | custom-call | flops 268435456 | bytes 1998848 | tf_op jit(solution)/shard_map/pallas_call | solution.py:520
  37.3 1.0 %collective-permute-done.15.refs_1_ = bf16[64,512]{1,0:T(8,128)(2,1)S(1)} collective-permute-done((bf16[64,512]{1,0:T(8,128)(2,1)S(1)}, bf16[64,512]{1,0:T(8,128)(2,1)S(1)}, u32[]{:S(2)}, u32[]{:S(2)}) %collective-permute-start.15) | collective-permute-done | bytes 65568 | tf_op jit(solution)/shard_map/ppermute | solution.py:27
  38.3 1.1 %collective-permute-start.16 = (bf16[64,512]{1,0:T(8,128)(2,1)S(1)}, bf16[64,512]{1,0:T(8,128)(2,1)S(1)}, u32[]{:S(2)}, u32[]{:S(2)}) collective-permute-start(bf16[64,512]{1,0:T(8,128)(2,1)S(1)} %shard_map.90.refs_0_), channel_id=1, source_target_pairs={{0,8},{4,12},{8,0},{12,4},{1,9},{5,13},{9,1},{13,5},{2,10},{6,14},... | collective-permute-start | bytes 196616 | tf_op jit(solution)/shard_map/ppermute | solution.py:27
  39.3 1.3 %shard_map.89 = bf16[64,2,4,512]{3,2,1,0:T(4,128)(2,1)} custom-call(f32[2,8,512]{2,1,0:T(8,128)S(1)} %get-tuple-element.32.top_ref, f32[64,512]{1,0:T(8,128)S(1)} %get-tuple-element.27.refs_8_.refs_6_.wo_ref, bf16[128,512]{1,0:T(8,128)(2,1)S(1)} %get-tuple-element.33.both_ref, bf16[512,512]{1,0:T(8,128)(2,1)S(1)} %get-tuple-element.25.refs_5_.refs_9_.field_ref), custom_call_target="tpu_custom_call" | custom-call | flops 268435456 | bytes 1343488 | tf_op jit(solution)/shard_map/pallas_call | solution.py:520
  40.6 2.0 %collective-permute-done.16.refs_1_ = bf16[64,512]{1,0:T(8,128)(2,1)S(1)} collective-permute-done((bf16[64,512]{1,0:T(8,128)(2,1)S(1)}, bf16[64,512]{1,0:T(8,128)(2,1)S(1)}, u32[]{:S(2)}, u32[]{:S(2)}) %collective-permute-start.16) | collective-permute-done | bytes 65568 | tf_op jit(solution)/shard_map/ppermute | solution.py:27
  42.6 1.3 %collective-permute-start.19 = (bf16[64,512]{1,0:T(8,128)(2,1)S(1)}, bf16[64,512]{1,0:T(8,128)(2,1)S(1)}, u32[]{:S(2)}, u32[]{:S(2)}) collective-permute-start(bf16[64,512]{1,0:T(8,128)(2,1)S(1)} %shard_map.91.refs_0_), channel_id=1, source_target_pairs={{0,1},{1,0},{2,3},{3,2},{4,5},{5,4},{6,7},{7,6},{8,9},{9,8},{10,11... | collective-permute-start | bytes 196616 | tf_op jit(solution)/shard_map/ppermute | solution.py:27
  43.9 1.1 %collective-permute-start.18 = (bf16[64,512]{1,0:T(8,128)(2,1)S(1)}, bf16[64,512]{1,0:T(8,128)(2,1)S(1)}, u32[]{:S(2)}, u32[]{:S(2)}) collective-permute-start(bf16[64,512]{1,0:T(8,128)(2,1)S(1)} %shard_map.91.refs_0_), channel_id=1, source_target_pairs={{0,2},{1,3},{2,0},{3,1},{4,6},{5,7},{6,4},{7,5},{8,10},{9,11},{10,... | collective-permute-start | bytes 196616 | tf_op jit(solution)/shard_map/ppermute | solution.py:27
  45.0 2.1 %collective-permute-start.17 = (bf16[64,512]{1,0:T(8,128)(2,1)S(1)}, bf16[64,512]{1,0:T(8,128)(2,1)S(1)}, u32[]{:S(2)}, u32[]{:S(2)}) collective-permute-start(bf16[64,512]{1,0:T(8,128)(2,1)S(1)} %shard_map.91.refs_0_), channel_id=1, source_target_pairs={{0,3},{1,2},{2,1},{3,0},{4,7},{5,6},{6,5},{7,4},{8,11},{9,10},{10,... | collective-permute-start | bytes 196616 | tf_op jit(solution)/shard_map/ppermute | solution.py:27
  47.1 1.4 %shard_map.94.plane_ref = f32[8,64]{1,0:T(8,128)S(1)} custom-call(bf16[64,512]{1,0:T(8,128)(2,1)S(1)} %shard_map.86.refs_0_, bf16[64,512]{1,0:T(8,128)(2,1)S(1)} %collective-permute-done.12.refs_1_, bf16[64,512]{1,0:T(8,128)(2,1)S(1)} %collective-permute-done.13.refs_2_, bf16[64,512]{1,0:T(8,128)(2,1)S(1)} %collective-permute-done.14.refs_3_, ...), custom_call_target="tpu_custom_call" | custom-call | flops 536870912 | bytes 1738752 | tf_op jit(solution)/shard_map/pallas_call | solution.py:520
  49.0 2.2 %collective-permute-done.17.refs_1_ = bf16[64,512]{1,0:T(8,128)(2,1)S(1)} collective-permute-done((bf16[64,512]{1,0:T(8,128)(2,1)S(1)}, bf16[64,512]{1,0:T(8,128)(2,1)S(1)}, u32[]{:S(2)}, u32[]{:S(2)}) %collective-permute-start.17) | collective-permute-done | bytes 65568 | tf_op jit(solution)/shard_map/ppermute | solution.py:27
  51.4 0.9 %shard_map.96 = bf16[64,2,4,512]{3,2,1,0:T(4,128)(2,1)} custom-call(f32[64,512]{1,0:T(8,128)S(1)} %shard_map.93.refs_0_, bf16[64,512]{1,0:T(8,128)(2,1)S(1)} %collective-permute-done.19.refs_1_, f32[72,512]{1,0:T(8,128)S(1)} %get-tuple-element.35.refs_2_, f32[512,512]{1,0:T(8,128)S(1)} %shard_map.95.refs_3_), custom_call_target="tpu_custom_call" | custom-call | bytes 1916928 | tf_op jit(solution)/shard_map/pallas_call | solution.py:520
  (39 shorter events, 3.0 us)
Async XLA Ops:
  0.6 19.1 %copy-start.4 = (bf16[64,2,4,512]{3,2,1,0:T(4,128)(2,1)S(1)}, bf16[64,2,4,512]{3,2,1,0:T(4,128)(2,1)}, u32[]{:S(2)}) copy-start(bf16[64,2,4,512]{3,2,1,0:T(4,128)(2,1)} %param.7) | copy-start | bytes 1572868
  2.5 4.3 %collective-permute-start = (f32[72,128]{1,0:T(8,128)S(1)}, f32[72,128]{1,0:T(8,128)S(1)}, u32[]{:S(2)}, u32[]{:S(2)}) collective-permute-start(f32[72,128]{1,0:T(8,128)S(1)} %get-tuple-element.21), channel_id=1, source_target_pairs={{0,12},{4,8},{8,4},{12,0},{1,13},{5,9},{9,5},{13,1},{2,14},{6,10},... | collective-permute-start | bytes 110600 | tf_op jit(solution)/shard_map/ppermute | solution.py:27
  4.9 4.1 %collective-permute-start.1 = (f32[72,128]{1,0:T(8,128)S(1)}, f32[72,128]{1,0:T(8,128)S(1)}, u32[]{:S(2)}, u32[]{:S(2)}) collective-permute-start(f32[72,128]{1,0:T(8,128)S(1)} %get-tuple-element.22), channel_id=1, source_target_pairs={{0,8},{4,12},{8,0},{12,4},{1,9},{5,13},{9,1},{13,5},{2,10},{6,14},... | collective-permute-start | bytes 110600 | tf_op jit(solution)/shard_map/ppermute | solution.py:27
  5.6 3.4 %collective-permute-start.2 = (f32[72,128]{1,0:T(8,128)S(1)}, f32[72,128]{1,0:T(8,128)S(1)}, u32[]{:S(2)}, u32[]{:S(2)}) collective-permute-start(f32[72,128]{1,0:T(8,128)S(1)} %get-tuple-element.23), channel_id=1, source_target_pairs={{0,4},{4,0},{8,12},{12,8},{1,5},{5,1},{9,13},{13,9},{2,6},{6,2},{1... | collective-permute-start | bytes 110600 | tf_op jit(solution)/shard_map/ppermute | solution.py:27
  9.0 6.2 %collective-permute-start.3 = (f32[96,128]{1,0:T(8,128)S(1)}, f32[96,128]{1,0:T(8,128)S(1)}, u32[]{:S(2)}, u32[]{:S(2)}) collective-permute-start(f32[96,128]{1,0:T(8,128)S(1)} %shard_map.78.refs_0_), channel_id=1, source_target_pairs={{0,3},{1,2},{2,1},{3,0},{4,7},{5,6},{6,5},{7,4},{8,11},{9,10},{10,... | collective-permute-start | bytes 147464 | tf_op jit(solution)/shard_map/ppermute | solution.py:27
  12.7 5.0 %collective-permute-start.4 = (f32[96,128]{1,0:T(8,128)S(1)}, f32[96,128]{1,0:T(8,128)S(1)}, u32[]{:S(2)}, u32[]{:S(2)}) collective-permute-start(f32[96,128]{1,0:T(8,128)S(1)} %shard_map.78.refs_0_), channel_id=1, source_target_pairs={{0,2},{1,3},{2,0},{3,1},{4,6},{5,7},{6,4},{7,5},{8,10},{9,11},{10,... | collective-permute-start | bytes 147464 | tf_op jit(solution)/shard_map/ppermute | solution.py:27
  12.7 5.0 %collective-permute-start.5 = (f32[96,128]{1,0:T(8,128)S(1)}, f32[96,128]{1,0:T(8,128)S(1)}, u32[]{:S(2)}, u32[]{:S(2)}) collective-permute-start(f32[96,128]{1,0:T(8,128)S(1)} %shard_map.78.refs_0_), channel_id=1, source_target_pairs={{0,1},{1,0},{2,3},{3,2},{4,5},{5,4},{6,7},{7,6},{8,9},{9,8},{10,11... | collective-permute-start | bytes 147464 | tf_op jit(solution)/shard_map/ppermute | solution.py:27
  17.7 2.1 %copy-start = (f32[3,2,64,64]{3,2,1,0:T(8,128)S(1)}, f32[3,2,64,64]{3,2,1,0:T(8,128)}, u32[]{:S(2)}) copy-start(f32[3,2,64,64]{3,2,1,0:T(8,128)} %refs_7_.1) | copy-start | bytes 294916
  17.7 2.1 %copy-start.2 = (bf16[64,64]{1,0:T(8,128)(2,1)S(1)}, bf16[64,64]{1,0:T(8,128)(2,1)}, u32[]{:S(2)}) copy-start(bf16[64,64]{1,0:T(8,128)(2,1)} %wv_ref.1) | copy-start | bytes 24580
  17.7 2.1 %copy-start.3 = (bf16[64,64]{1,0:T(8,128)(2,1)S(1)}, bf16[64,64]{1,0:T(8,128)(2,1)}, u32[]{:S(2)}) copy-start(bf16[64,64]{1,0:T(8,128)(2,1)} %wo_ref.1) | copy-start | bytes 24580
  17.8 2.4 %collective-permute-start.8 = (f32[72,128]{1,0:T(8,128)S(1)}, f32[72,128]{1,0:T(8,128)S(1)}, u32[]{:S(2)}, u32[]{:S(2)}) collective-permute-start(f32[72,128]{1,0:T(8,128)S(1)} %shard_map.81.refs_0_), channel_id=1, source_target_pairs={{0,4},{4,0},{8,12},{12,8},{1,5},{5,1},{9,13},{13,9},{2,6},{6,2},{1... | collective-permute-start | bytes 110600 | tf_op jit(solution)/shard_map/ppermute | solution.py:27
  17.8 4.0 %collective-permute-start.7 = (f32[72,128]{1,0:T(8,128)S(1)}, f32[72,128]{1,0:T(8,128)S(1)}, u32[]{:S(2)}, u32[]{:S(2)}) collective-permute-start(f32[72,128]{1,0:T(8,128)S(1)} %shard_map.81.refs_0_), channel_id=1, source_target_pairs={{0,8},{4,12},{8,0},{12,4},{1,9},{5,13},{9,1},{13,5},{2,10},{6,14},... | collective-permute-start | bytes 110600 | tf_op jit(solution)/shard_map/ppermute | solution.py:27
  19.0 3.4 %collective-permute-start.6 = (f32[72,128]{1,0:T(8,128)S(1)}, f32[72,128]{1,0:T(8,128)S(1)}, u32[]{:S(2)}, u32[]{:S(2)}) collective-permute-start(f32[72,128]{1,0:T(8,128)S(1)} %shard_map.81.refs_0_), channel_id=1, source_target_pairs={{0,12},{4,8},{8,4},{12,0},{1,13},{5,9},{9,5},{13,1},{2,14},{6,10},... | collective-permute-start | bytes 110600 | tf_op jit(solution)/shard_map/ppermute | solution.py:27
  23.4 5.8 %collective-permute-start.9 = (bf16[16,512]{1,0:T(8,128)(2,1)S(1)}, bf16[16,512]{1,0:T(8,128)(2,1)S(1)}, u32[]{:S(2)}, u32[]{:S(2)}) collective-permute-start(bf16[16,512]{1,0:T(8,128)(2,1)S(1)} %get-tuple-element.28.refs_0_), channel_id=1, source_target_pairs={{0,3},{1,2},{2,1},{3,0},{4,7},{5,6},{6,5},{7,4},{8,11},{9,10},{10,... | collective-permute-start | bytes 49160 | tf_op jit(solution)/shard_map/ppermute | solution.py:27
  25.6 4.7 %collective-permute-start.10 = (bf16[16,512]{1,0:T(8,128)(2,1)S(1)}, bf16[16,512]{1,0:T(8,128)(2,1)S(1)}, u32[]{:S(2)}, u32[]{:S(2)}) collective-permute-start(bf16[16,512]{1,0:T(8,128)(2,1)S(1)} %get-tuple-element.28.refs_0_), channel_id=1, source_target_pairs={{0,2},{1,3},{2,0},{3,1},{4,6},{5,7},{6,4},{7,5},{8,10},{9,11},{10,... | collective-permute-start | bytes 49160 | tf_op jit(solution)/shard_map/ppermute | solution.py:27
  25.8 4.5 %collective-permute-start.11 = (bf16[16,512]{1,0:T(8,128)(2,1)S(1)}, bf16[16,512]{1,0:T(8,128)(2,1)S(1)}, u32[]{:S(2)}, u32[]{:S(2)}) collective-permute-start(bf16[16,512]{1,0:T(8,128)(2,1)S(1)} %get-tuple-element.28.refs_0_), channel_id=1, source_target_pairs={{0,1},{1,0},{2,3},{3,2},{4,5},{5,4},{6,7},{7,6},{8,9},{9,8},{10,11... | collective-permute-start | bytes 49160 | tf_op jit(solution)/shard_map/ppermute | solution.py:27
  30.3 2.0 %copy-start.1 = (bf16[2,128,128]{2,1,0:T(8,128)(2,1)S(1)}, bf16[2,128,128]{2,1,0:T(8,128)(2,1)}, u32[]{:S(2)}) copy-start(bf16[2,128,128]{2,1,0:T(8,128)(2,1)} %constant.2.clone.refs_2_.refs_6_) | copy-start | bytes 196612
  30.3 3.4 %collective-permute-start.14 = (bf16[64,512]{1,0:T(8,128)(2,1)S(1)}, bf16[64,512]{1,0:T(8,128)(2,1)S(1)}, u32[]{:S(2)}, u32[]{:S(2)}) collective-permute-start(bf16[64,512]{1,0:T(8,128)(2,1)S(1)} %shard_map.86.refs_0_), channel_id=1, source_target_pairs={{0,4},{4,0},{8,12},{12,8},{1,5},{5,1},{9,13},{13,9},{2,6},{6,2},{1... | collective-permute-start | bytes 196616 | tf_op jit(solution)/shard_map/ppermute | solution.py:27
  30.4 4.9 %collective-permute-start.13 = (bf16[64,512]{1,0:T(8,128)(2,1)S(1)}, bf16[64,512]{1,0:T(8,128)(2,1)S(1)}, u32[]{:S(2)}, u32[]{:S(2)}) collective-permute-start(bf16[64,512]{1,0:T(8,128)(2,1)S(1)} %shard_map.86.refs_0_), channel_id=1, source_target_pairs={{0,8},{4,12},{8,0},{12,4},{1,9},{5,13},{9,1},{13,5},{2,10},{6,14},... | collective-permute-start | bytes 196616 | tf_op jit(solution)/shard_map/ppermute | solution.py:27
  31.5 4.4 %collective-permute-start.12 = (bf16[64,512]{1,0:T(8,128)(2,1)S(1)}, bf16[64,512]{1,0:T(8,128)(2,1)S(1)}, u32[]{:S(2)}, u32[]{:S(2)}) collective-permute-start(bf16[64,512]{1,0:T(8,128)(2,1)S(1)} %shard_map.86.refs_0_), channel_id=1, source_target_pairs={{0,12},{4,8},{8,4},{12,0},{1,13},{5,9},{9,5},{13,1},{2,14},{6,10},... | collective-permute-start | bytes 196616 | tf_op jit(solution)/shard_map/ppermute | solution.py:27
  36.9 1.3 %collective-permute-start.15 = (bf16[64,512]{1,0:T(8,128)(2,1)S(1)}, bf16[64,512]{1,0:T(8,128)(2,1)S(1)}, u32[]{:S(2)}, u32[]{:S(2)}) collective-permute-start(bf16[64,512]{1,0:T(8,128)(2,1)S(1)} %get-tuple-element.34.refs_0_), channel_id=1, source_target_pairs={{0,4},{4,0},{8,12},{12,8},{1,5},{5,1},{9,13},{13,9},{2,6},{6,2},{1... | collective-permute-start | bytes 196616 | tf_op jit(solution)/shard_map/ppermute | solution.py:27
  38.3 4.3 %collective-permute-start.16 = (bf16[64,512]{1,0:T(8,128)(2,1)S(1)}, bf16[64,512]{1,0:T(8,128)(2,1)S(1)}, u32[]{:S(2)}, u32[]{:S(2)}) collective-permute-start(bf16[64,512]{1,0:T(8,128)(2,1)S(1)} %shard_map.90.refs_0_), channel_id=1, source_target_pairs={{0,8},{4,12},{8,0},{12,4},{1,9},{5,13},{9,1},{13,5},{2,10},{6,14},... | collective-permute-start | bytes 196616 | tf_op jit(solution)/shard_map/ppermute | solution.py:27
  42.6 8.8 %collective-permute-start.19 = (bf16[64,512]{1,0:T(8,128)(2,1)S(1)}, bf16[64,512]{1,0:T(8,128)(2,1)S(1)}, u32[]{:S(2)}, u32[]{:S(2)}) collective-permute-start(bf16[64,512]{1,0:T(8,128)(2,1)S(1)} %shard_map.91.refs_0_), channel_id=1, source_target_pairs={{0,1},{1,0},{2,3},{3,2},{4,5},{5,4},{6,7},{7,6},{8,9},{9,8},{10,11... | collective-permute-start | bytes 196616 | tf_op jit(solution)/shard_map/ppermute | solution.py:27
  43.9 7.5 %collective-permute-start.18 = (bf16[64,512]{1,0:T(8,128)(2,1)S(1)}, bf16[64,512]{1,0:T(8,128)(2,1)S(1)}, u32[]{:S(2)}, u32[]{:S(2)}) collective-permute-start(bf16[64,512]{1,0:T(8,128)(2,1)S(1)} %shard_map.91.refs_0_), channel_id=1, source_target_pairs={{0,2},{1,3},{2,0},{3,1},{4,6},{5,7},{6,4},{7,5},{8,10},{9,11},{10,... | collective-permute-start | bytes 196616 | tf_op jit(solution)/shard_map/ppermute | solution.py:27
  45.0 6.2 %collective-permute-start.17 = (bf16[64,512]{1,0:T(8,128)(2,1)S(1)}, bf16[64,512]{1,0:T(8,128)(2,1)S(1)}, u32[]{:S(2)}, u32[]{:S(2)}) collective-permute-start(bf16[64,512]{1,0:T(8,128)(2,1)S(1)} %shard_map.91.refs_0_), channel_id=1, source_target_pairs={{0,3},{1,2},{2,1},{3,0},{4,7},{5,6},{6,5},{7,4},{8,11},{9,10},{10,... | collective-permute-start | bytes 196616 | tf_op jit(solution)/shard_map/ppermute | solution.py:27

commit v11 on v10

--- a/solution.py
+++ b/solution.py
@@ -391,7 +391,8 @@
 
 def mix_kernel(factor, spans, *refs):
     lows, refs = refs[:spans], refs[spans:]
-    mix_ref, wv_ref, wo_ref, wq_ref, wk_ref, field_ref, cot_ref, top_ref, out_ref = refs
+    mix_ref, wv_ref, wo_ref, wq_ref, wk_ref, field_ref, cot_ref, top_ref = refs[:8]
+    mine_ref, other_ref, half_ref = refs[8:]
     cells = field_ref.shape[0] // WIDTH
     low_f, low_c = join_low(lows, cells)
     wide = low_f.shape[1]
@@ -414,7 +415,12 @@
         return mul_left(found[:WIDTH] + found[WIDTH:], right)
 
     found = pull(wq_ref[...], left_f, cot_ref[...]) + pull(wk_ref[...], left_c, field_ref[...])
-    out_ref[...] = found.astype(jnp.bfloat16)
+    half = found.shape[1] // 2
+    half_ref[0] = found[:, :half]
+    half_ref[1] = found[:, half:]
+    core = lax.axis_index("gx") & 1
+    mine_ref[...] = half_ref[core].astype(jnp.bfloat16)
+    other_ref[...] = half_ref[core ^ 1].astype(jnp.bfloat16)
 
 
 def put_cells(ref, total):
@@ -481,13 +487,13 @@
     out_ref[...] = found + jnp.concatenate([plane] * columns, axis=1)
 
 
-def final_kernel(places, *refs):
-    parts, (feat_ref, base_ref, out_ref, data_ref, semaphores) = refs[:-5], refs[-5:]
+def final_kernel(places, mine_ref, other_ref, feat_ref, base_ref, out_ref, data_ref, half_ref, semaphores):
     depth = base_ref.shape[1]
     _, rows_x, rows_y, _ = data_ref.shape
-    found = parts[0][...].astype(jnp.float32)
-    for part in parts[1:]:
-        found = found + part[...].astype(jnp.float32)
+    core = lax.axis_index("gx") & 1
+    half_ref[core] = mine_ref[...]
+    half_ref[core ^ 1] = other_ref[...]
+    found = jnp.concatenate([half_ref[0], half_ref[1]], axis=1)
     normed = feat_ref[0:WIDTH, :]
     inverse = feat_ref[WIDTH : WIDTH + 1, :]
     found = inverse * (found - normed * jnp.mean(found * normed, axis=0, keepdims=True))
@@ -514,6 +520,29 @@
         copy.wait()
 
 
+def rows_kernel(cot_ref, rows_ref, data_ref, semaphores):
+    _, rows_x, rows_y, depth = data_ref.shape
+    cells = rows_x * rows_y
+    chunks = semaphores.shape[0]
+    size = WIDTH // chunks
+    copies = [
+        pltpu.make_async_copy(
+            cot_ref.at[pl.ds(index * size, size)],
+            data_ref.at[pl.ds(index * size, size)],
+            semaphores.at[index],
+        )
+        for index in range(chunks)
+    ]
+    for copy in copies:
+        copy.start()
+    for index, copy in enumerate(copies):
+        copy.wait()
+        data = data_ref[index * size : (index + 1) * size].astype(jnp.float32)
+        data = jnp.concatenate([data[:, at_x] for at_x in range(rows_x)], axis=1)
+        data = data.reshape(size * cells, depth).astype(jnp.bfloat16)
+        rows_ref[index * size * cells : (index + 1) * size * cells, :] = data
+
+
 def run(kernel, outs, operands, places=pltpu.VMEM, target=pltpu.VMEM, flops=0, scratch=(),
         mebibytes=16):
     moved = sum(x.size * x.dtype.itemsize for x in tuple(operands) + tuple(outs))
@@ -551,18 +580,28 @@
         np.stack([at_x[:, None] == at_x[None], at_y[:, None] == at_y[None]]), dtype=bf16
     )
 
-    cots = cotangent.reshape(rows, depth)
     parts = pltpu.VMEM((span_x, WIDTH, LANES), f32)
     chunked = [pltpu.VMEM(field.shape, bf16), pltpu.SemaphoreType.DMA((4,))]
     factor_z = 1.0 / math.sqrt(HEAD_DIM * depth)
     cube = rows * wide * depth * 2
 
-    def swaps(sent, axis, size):
+    cots = run(
+        rows_kernel,
+        [like((rows, depth), bf16)],
+        (pltpu.with_memory_space_constraint(cotangent, pltpu.HBM),),
+        places=pltpu.HBM,
+        flops=cube,
+        scratch=chunked,
+    )
+
+    def swaps(sent, axis, size, farthest=True):
         if not isinstance(sent, (tuple, list)):
             sent = [sent] * size
-        return tuple(sent[:1]) + tuple(
-            swap(sent[step], axis, size, step) for step in range(size - 1, 0, -1)
-        )
+        steps = range(size - 1, 0, -1)
+        found = {}
+        for step in steps if farthest else reversed(steps):
+            found[step] = swap(sent[step], axis, size, step)
+        return tuple(sent[:1]) + tuple(found[step] for step in steps)
 
     def taken(kernel, sent, dtype=None, last=False):
         found, *others = sent
@@ -607,23 +646,30 @@
         functools.partial(coef_kernel, span_x),
         [like((2 * cells, wide), bf16), like((2 * WIDTH, depth), bf16),
          like((WIDTH + HEAD_DIM, depth), f32)],
-        swaps(mine, "gx", span_x) + (wz, cols, cots, wv, wo),
+        swaps(mine, "gx", span_x, False) + (wz, cols, cots, wv, wo),
         flops=2 * cube,
         scratch=[pltpu.VMEM((span_x, WIDTH + HEAD_DIM, LANES), f32)],
     )
     (low,) = taken(stack_kernel, swaps(send, "gy", span_y), last=True)
-    lows = swaps(low, "gx", span_x)
-    pulled = like((WIDTH, depth), bf16)
-    top, total = run(
+    lows = swaps(low, "gx", span_x, False)
+    pulled = like((WIDTH, depth // 2), bf16)
+    halves = pltpu.VMEM((2, WIDTH, depth // 2), f32)
+    top, mine, other = run(
         functools.partial(mix_kernel, factor_z, span_x),
-        [like((2, cells, wide), f32), pulled],
+        [like((2, cells, wide), f32), pulled, pulled],
         lows + (mix, wv, wo, wq, wk, cols, cots),
         flops=cube,
-    )
-    for level in range(span_x.bit_length() - 1):
+        scratch=[halves],
+    )
+    total = run(add_pull_kernel, [pulled], (mine, swap(other, "gx", span_x, 1)))
+    for level in range(1, span_x.bit_length() - 1):
         total = run(add_pull_kernel, [pulled], (total, swap(total, "gx", span_x, 1 << level)))
     layer_output = run(
         output_kernel, [like(field.shape, bf16)], (top, wo, both, cols), flops=cube
+    )
+    total, layer_output = lax.optimization_barrier((total, layer_output))
+    total = run(
+        add_pull_kernel, [like(pulled.shape, f32)], swaps(total, "gy", span_y, False)
     )
     plane = run(
         functools.partial(gram_kernel, cells, lengths, factor_z),
@@ -632,12 +678,14 @@
         flops=2 * cube,
     )
     base = run(base_kernel, [like((rows, depth), f32)], (top, wv, both, cots, plane), flops=cube)
+    total, base = lax.optimization_barrier((total, base))
+    other = swap(total, "gx", span_x, 1)
     field_grad = run(
         functools.partial(final_kernel, grid_x * grid_y),
         [like(field.shape, bf16)],
-        taken(add_pull_kernel, swaps(total, "gy", span_y), f32) + (feat_z, base),
+        (total, other, feat_z, base),
         target=pltpu.HBM,
-        scratch=chunked,
+        scratch=[chunked[0], halves, chunked[1]],
     )
     return (layer_output, field_grad)
 
@@ -651,6 +699,7 @@
         places = grid_x // mesh.shape["groups"] * grid_y
         small = places == LANES and places == 8 * count
         small = small and depth == LANES * mesh.shape["gx"] and count & (count - 1) == 0
+        small = small and mesh.shape["gx"] > 1
         return jax.shard_map(
             per_device_kernels if small else per_device,
             mesh=mesh,

time: 52.5 us -> 52.6 us (level)
  Pallas kernels: 9.78 us -> 10.9 us
  waiting for transfers between devices: 19.8 us -> 18.9 us
    pallas_call x20, Pallas kernels: 9.78 us -> 10.9 us  [run(): pl.pallas_call(kernel, out_shape=tuple(outs), in_specs=[pl.BlockSpec(memo...]
    ppermute x20 -> x21, waiting for transfers between devices: 19.8 us -> 18.9 us  [swap(): return lax.ppermute(part, axis, [(i, i ^ step) for i in range(size)])]
    ppermute x20 -> x21, starting transfers between devices: 21.8 us -> 21.8 us  [swap(): return lax.ppermute(part, axis, [(i, i ^ step) for i in range(size)])]
  transfers between devices with their start and end apart: 20 -> 21, of which waited for: 14 -> 14; matrix products, arithmetic and copies ran while one was open for 0% -> 0% of each run, Pallas kernels for 9% -> 12%
where the time goes in v11:
time: 52.6 us; the launch traced here: 52.4 us
  starting transfers between devices  21.8 us (41%)
  waiting for transfers between devices  18.9 us (36%)
  Pallas kernels  10.9 us (21%)
  between operations  0.82 us (2%)
    ppermute x21, starting transfers between devices, swap(): return lax.ppermute(part, axis, [(i, i ^ step) for i in range(size)])  21.8 us
    ppermute x21, waiting for transfers between devices, swap(): return lax.ppermute(part, axis, [(i, i ^ step) for i in range(size)])  18.9 us
    pallas_call x20, Pallas kernels, run(): pl.pallas_call(kernel, out_shape=tuple(outs), in_specs=[pl.BlockSpec(memo...  10.9 us
  transfers between devices with their start and end apart: 21, of which 14 were waited for; matrix products, arithmetic and copies ran while one was open for 0% of the time, Pallas kernels for 12%

profile of v11, /device:TPU:0, one launch (start us, length us, event | category | flops | bytes accessed | tf_op | source)
XLA Modules:
  0.0 52.4 jit_solution(11951797440449111739)
XLA Ops:
  0.6 1.8 %shard_map.77 = (f32[72,128]{1,0:T(8,128)S(1)}, f32[72,128]{1,0:T(8,128)S(1)}, f32[72,128]{1,0:T(8,128)S(1)}, f32[72,128]{1,0:T(8,128)S(1)}, bf16[512,512]{1,0:T(8,128)(2,1)S(1)}) custom-call(bf16[64,2,4,512]{3,2,1,0:T(4,128)(2,1)} %field_ref.1), custom_call_target="tpu_custom_call" | custom-call | flops 67108864 | bytes 1196032 | tf_op jit(solution)/shard_map/pallas_call | solution.py:549
  2.4 2.4 %collective-permute-start = (f32[72,128]{1,0:T(8,128)S(1)}, f32[72,128]{1,0:T(8,128)S(1)}, u32[]{:S(2)}, u32[]{:S(2)}) collective-permute-start(f32[72,128]{1,0:T(8,128)S(1)} %get-tuple-element.26), channel_id=1, source_target_pairs={{0,12},{4,8},{8,4},{12,0},{1,13},{5,9},{9,5},{13,1},{2,14},{6,10},... | collective-permute-start | bytes 110600 | tf_op jit(solution)/shard_map/ppermute | solution.py:27
  5.6 1.2 %collective-permute-done.refs_1_ = f32[72,128]{1,0:T(8,128)S(1)} collective-permute-done((f32[72,128]{1,0:T(8,128)S(1)}, f32[72,128]{1,0:T(8,128)S(1)}, u32[]{:S(2)}, u32[]{:S(2)}) %collective-permute-start) | collective-permute-done | bytes 36896 | tf_op jit(solution)/shard_map/ppermute | solution.py:27
  6.7 2.2 %collective-permute-done.1.refs_2_ = f32[72,128]{1,0:T(8,128)S(1)} collective-permute-done((f32[72,128]{1,0:T(8,128)S(1)}, f32[72,128]{1,0:T(8,128)S(1)}, u32[]{:S(2)}, u32[]{:S(2)}) %collective-permute-start.1) | collective-permute-done | bytes 36896 | tf_op jit(solution)/shard_map/ppermute | solution.py:27
  9.0 3.7 %collective-permute-start.3 = (f32[96,128]{1,0:T(8,128)S(1)}, f32[96,128]{1,0:T(8,128)S(1)}, u32[]{:S(2)}, u32[]{:S(2)}) collective-permute-start(f32[96,128]{1,0:T(8,128)S(1)} %shard_map.78.refs_0_), channel_id=1, source_target_pairs={{0,3},{1,2},{2,1},{3,0},{4,7},{5,6},{6,5},{7,4},{8,11},{9,10},{10,... | collective-permute-start | bytes 147464 | tf_op jit(solution)/shard_map/ppermute | solution.py:27
  12.6 0.8 %collective-permute-start.5 = (f32[96,128]{1,0:T(8,128)S(1)}, f32[96,128]{1,0:T(8,128)S(1)}, u32[]{:S(2)}, u32[]{:S(2)}) collective-permute-start(f32[96,128]{1,0:T(8,128)S(1)} %shard_map.78.refs_0_), channel_id=1, source_target_pairs={{0,1},{1,0},{2,3},{3,2},{4,5},{5,4},{6,7},{7,6},{8,9},{9,8},{10,11... | collective-permute-start | bytes 147464 | tf_op jit(solution)/shard_map/ppermute | solution.py:27
  13.4 1.8 %collective-permute-done.3.refs_1_ = f32[96,128]{1,0:T(8,128)S(1)} collective-permute-done((f32[96,128]{1,0:T(8,128)S(1)}, f32[96,128]{1,0:T(8,128)S(1)}, u32[]{:S(2)}, u32[]{:S(2)}) %collective-permute-start.3) | collective-permute-done | bytes 49184 | tf_op jit(solution)/shard_map/ppermute | solution.py:27
  15.2 2.4 %collective-permute-done.4.refs_1_ = f32[96,128]{1,0:T(8,128)S(1)} collective-permute-done((f32[96,128]{1,0:T(8,128)S(1)}, f32[96,128]{1,0:T(8,128)S(1)}, u32[]{:S(2)}, u32[]{:S(2)}) %collective-permute-start.4) | collective-permute-done | bytes 49184 | tf_op jit(solution)/shard_map/ppermute | solution.py:27
  17.8 1.1 %collective-permute-start.7 = (f32[72,128]{1,0:T(8,128)S(1)}, f32[72,128]{1,0:T(8,128)S(1)}, u32[]{:S(2)}, u32[]{:S(2)}) collective-permute-start(f32[72,128]{1,0:T(8,128)S(1)} %shard_map.81.refs_0_), channel_id=1, source_target_pairs={{0,8},{4,12},{8,0},{12,4},{1,9},{5,13},{9,1},{13,5},{2,10},{6,14},... | collective-permute-start | bytes 110600 | tf_op jit(solution)/shard_map/ppermute | solution.py:27
  18.9 0.7 %collective-permute-start.6 = (f32[72,128]{1,0:T(8,128)S(1)}, f32[72,128]{1,0:T(8,128)S(1)}, u32[]{:S(2)}, u32[]{:S(2)}) collective-permute-start(f32[72,128]{1,0:T(8,128)S(1)} %shard_map.81.refs_0_), channel_id=1, source_target_pairs={{0,12},{4,8},{8,4},{12,0},{1,13},{5,9},{9,5},{13,1},{2,14},{6,10},... | collective-permute-start | bytes 110600 | tf_op jit(solution)/shard_map/ppermute | solution.py:27
  19.9 1.2 %shard_map.83.refs_6_.refs_10_.cot_ref = bf16[512,512]{1,0:T(8,128)(2,1)S(1)} custom-call(bf16[64,2,4,512]{3,2,1,0:T(4,128)(2,1)} %cot_ref.1), custom_call_target="tpu_custom_call" | custom-call | flops 268435456 | bytes 1048576 | tf_op jit(solution)/shard_map/pallas_call | solution.py:549
  22.3 1.0 %shard_map.84 = (bf16[16,512]{1,0:T(8,128)(2,1)S(1)}, bf16[128,512]{1,0:T(8,128)(2,1)S(1)}, f32[72,512]{1,0:T(8,128)S(1)}) custom-call(f32[72,128]{1,0:T(8,128)S(1)} %shard_map.81.refs_0_, f32[72,128]{1,0:T(8,128)S(1)} %collective-permute-done.6.refs_1_, f32[72,128]{1,0:T(8,128)S(1)} %collective-permute-done.7.refs_2_, ...), custom_call_target="tpu_custom_call" | custom-call | flops 536870912 | bytes 1785856 | tf_op jit(solution)/shard_map/pallas_call | solution.py:549
  23.3 2.2 %collective-permute-start.9 = (bf16[16,512]{1,0:T(8,128)(2,1)S(1)}, bf16[16,512]{1,0:T(8,128)(2,1)S(1)}, u32[]{:S(2)}, u32[]{:S(2)}) collective-permute-start(bf16[16,512]{1,0:T(8,128)(2,1)S(1)} %get-tuple-element.33.refs_0_), channel_id=1, source_target_pairs={{0,3},{1,2},{2,1},{3,0},{4,7},{5,6},{6,5},{7,4},{8,11},{9,10},{10,... | collective-permute-start | bytes 49160 | tf_op jit(solution)/shard_map/ppermute | solution.py:27
  25.7 2.1 %collective-permute-start.11 = (bf16[16,512]{1,0:T(8,128)(2,1)S(1)}, bf16[16,512]{1,0:T(8,128)(2,1)S(1)}, u32[]{:S(2)}, u32[]{:S(2)}) collective-permute-start(bf16[16,512]{1,0:T(8,128)(2,1)S(1)} %get-tuple-element.33.refs_0_), channel_id=1, source_target_pairs={{0,1},{1,0},{2,3},{3,2},{4,5},{5,4},{6,7},{7,6},{8,9},{9,8},{10,11... | collective-permute-start | bytes 49160 | tf_op jit(solution)/shard_map/ppermute | solution.py:27
  27.8 1.3 %collective-permute-done.9.refs_1_ = bf16[16,512]{1,0:T(8,128)(2,1)S(1)} collective-permute-done((bf16[16,512]{1,0:T(8,128)(2,1)S(1)}, bf16[16,512]{1,0:T(8,128)(2,1)S(1)}, u32[]{:S(2)}, u32[]{:S(2)}) %collective-permute-start.9) | collective-permute-done | bytes 16416 | tf_op jit(solution)/shard_map/ppermute | solution.py:27
  29.1 1.1 %collective-permute-done.10.refs_1_ = bf16[16,512]{1,0:T(8,128)(2,1)S(1)} collective-permute-done((bf16[16,512]{1,0:T(8,128)(2,1)S(1)}, bf16[16,512]{1,0:T(8,128)(2,1)S(1)}, u32[]{:S(2)}, u32[]{:S(2)}) %collective-permute-start.10) | collective-permute-done | bytes 16416 | tf_op jit(solution)/shard_map/ppermute | solution.py:27
  30.3 1.1 %collective-permute-start.13 = (bf16[64,512]{1,0:T(8,128)(2,1)S(1)}, bf16[64,512]{1,0:T(8,128)(2,1)S(1)}, u32[]{:S(2)}, u32[]{:S(2)}) collective-permute-start(bf16[64,512]{1,0:T(8,128)(2,1)S(1)} %shard_map.87.refs_0_), channel_id=1, source_target_pairs={{0,8},{4,12},{8,0},{12,4},{1,9},{5,13},{9,1},{13,5},{2,10},{6,14},... | collective-permute-start | bytes 196616 | tf_op jit(solution)/shard_map/ppermute | solution.py:27
  31.4 0.8 %collective-permute-start.12 = (bf16[64,512]{1,0:T(8,128)(2,1)S(1)}, bf16[64,512]{1,0:T(8,128)(2,1)S(1)}, u32[]{:S(2)}, u32[]{:S(2)}) collective-permute-start(bf16[64,512]{1,0:T(8,128)(2,1)S(1)} %shard_map.87.refs_0_), channel_id=1, source_target_pairs={{0,12},{4,8},{8,4},{12,0},{1,13},{5,9},{9,5},{13,1},{2,14},{6,10},... | collective-permute-start | bytes 196616 | tf_op jit(solution)/shard_map/ppermute | solution.py:27
  32.2 1.4 %shard_map.88 = (f32[2,64,128]{2,1,0:T(8,128)S(1)}, f32[8,128,64]{2,1,0:T(8,128)S(1)}, f32[2,1024,128]{2,1,0:T(8,128)S(1)}) custom-call(f32[160,128]{1,0:T(8,128)S(1)} %shard_map.80.refs_0_, f32[96,128]{1,0:T(8,128)S(1)} %collective-permute-done.5.refs_1_, bf16[2,128,128]{2,1,0:T(8,128)(2,1)S(1)} %copy-done.1, f32[3,2,64,64]{3,2,1,0:T(8,128)S(1)} %copy-done), custom_call_target="tpu_custom_call" | custom-call | flops 134217728 | bytes 1671168 | tf_op jit(solution)/shard_map/pallas_call | solution.py:549
  33.6 1.6 %collective-permute-done.13.refs_2_ = bf16[64,512]{1,0:T(8,128)(2,1)S(1)} collective-permute-done((bf16[64,512]{1,0:T(8,128)(2,1)S(1)}, bf16[64,512]{1,0:T(8,128)(2,1)S(1)}, u32[]{:S(2)}, u32[]{:S(2)}) %collective-permute-start.13) | collective-permute-done | bytes 65568 | tf_op jit(solution)/shard_map/ppermute | solution.py:27
  35.8 1.1 %shard_map.89 = (f32[2,8,512]{2,1,0:T(8,128)S(1)}, bf16[64,256]{1,0:T(8,128)(2,1)S(1)}, bf16[64,256]{1,0:T(8,128)(2,1)S(1)}) custom-call(bf16[64,512]{1,0:T(8,128)(2,1)S(1)} %shard_map.87.refs_0_, bf16[64,512]{1,0:T(8,128)(2,1)S(1)} %collective-permute-done.12.refs_1_, bf16[64,512]{1,0:T(8,128)(2,1)S(1)} %collective-permute-done.13.refs_2_, ...), custom_call_target="tpu_custom_call" | custom-call | flops 268435456 | bytes 1998848 | tf_op jit(solution)/shard_map/pallas_call | solution.py:549
  37.2 1.0 %collective-permute-done.15.refs_1_ = bf16[64,256]{1,0:T(8,128)(2,1)S(1)} collective-permute-done((bf16[64,256]{1,0:T(8,128)(2,1)S(1)}, bf16[64,256]{1,0:T(8,128)(2,1)S(1)}, u32[]{:S(2)}, u32[]{:S(2)}) %collective-permute-start.15) | collective-permute-done | bytes 32800 | tf_op jit(solution)/shard_map/ppermute | solution.py:27
  38.2 1.1 %collective-permute-start.16 = (bf16[64,256]{1,0:T(8,128)(2,1)S(1)}, bf16[64,256]{1,0:T(8,128)(2,1)S(1)}, u32[]{:S(2)}, u32[]{:S(2)}) collective-permute-start(bf16[64,256]{1,0:T(8,128)(2,1)S(1)} %shard_map.90.refs_0_), channel_id=1, source_target_pairs={{0,8},{4,12},{8,0},{12,4},{1,9},{5,13},{9,1},{13,5},{2,10},{6,14},... | collective-permute-start | bytes 98312 | tf_op jit(solution)/shard_map/ppermute | solution.py:27
  39.2 1.2 %shard_map.92 = bf16[64,2,4,512]{3,2,1,0:T(4,128)(2,1)} custom-call(f32[2,8,512]{2,1,0:T(8,128)S(1)} %get-tuple-element.39.top_ref, f32[64,512]{1,0:T(8,128)S(1)} %get-tuple-element.32.refs_8_.refs_6_.wo_ref, bf16[128,512]{1,0:T(8,128)(2,1)S(1)} %get-tuple-element.40.both_ref, bf16[512,512]{1,0:T(8,128)(2,1)S(1)} %get-tuple-element.30.refs_5_.refs_9_.field_ref), custom_call_target="tpu_custom_call" | custom-call | flops 268435456 | bytes 1343488 | tf_op jit(solution)/shard_map/pallas_call | solution.py:549
  40.5 1.7 %collective-permute-done.16.refs_1_ = bf16[64,256]{1,0:T(8,128)(2,1)S(1)} collective-permute-done((bf16[64,256]{1,0:T(8,128)(2,1)S(1)}, bf16[64,256]{1,0:T(8,128)(2,1)S(1)}, u32[]{:S(2)}, u32[]{:S(2)}) %collective-permute-start.16) | collective-permute-done | bytes 32800 | tf_op jit(solution)/shard_map/ppermute | solution.py:27
  42.1 1.3 %collective-permute-start.19 = (bf16[64,256]{1,0:T(8,128)(2,1)S(1)}, bf16[64,256]{1,0:T(8,128)(2,1)S(1)}, u32[]{:S(2)}, u32[]{:S(2)}) collective-permute-start(bf16[64,256]{1,0:T(8,128)(2,1)S(1)} %shard_map.91.refs_0_), channel_id=1, source_target_pairs={{0,1},{1,0},{2,3},{3,2},{4,5},{5,4},{6,7},{7,6},{8,9},{9,8},{10,11... | collective-permute-start | bytes 98312 | tf_op jit(solution)/shard_map/ppermute | solution.py:27
  43.4 1.1 %collective-permute-start.18 = (bf16[64,256]{1,0:T(8,128)(2,1)S(1)}, bf16[64,256]{1,0:T(8,128)(2,1)S(1)}, u32[]{:S(2)}, u32[]{:S(2)}) collective-permute-start(bf16[64,256]{1,0:T(8,128)(2,1)S(1)} %shard_map.91.refs_0_), channel_id=1, source_target_pairs={{0,2},{1,3},{2,0},{3,1},{4,6},{5,7},{6,4},{7,5},{8,10},{9,11},{10,... | collective-permute-start | bytes 98312 | tf_op jit(solution)/shard_map/ppermute | solution.py:27
  44.5 2.1 %collective-permute-start.17 = (bf16[64,256]{1,0:T(8,128)(2,1)S(1)}, bf16[64,256]{1,0:T(8,128)(2,1)S(1)}, u32[]{:S(2)}, u32[]{:S(2)}) collective-permute-start(bf16[64,256]{1,0:T(8,128)(2,1)S(1)} %shard_map.91.refs_0_), channel_id=1, source_target_pairs={{0,3},{1,2},{2,1},{3,0},{4,7},{5,6},{6,5},{7,4},{8,11},{9,10},{10,... | collective-permute-start | bytes 98312 | tf_op jit(solution)/shard_map/ppermute | solution.py:27
  46.6 1.4 %shard_map.94.plane_ref = f32[8,64]{1,0:T(8,128)S(1)} custom-call(bf16[64,512]{1,0:T(8,128)(2,1)S(1)} %shard_map.87.refs_0_, bf16[64,512]{1,0:T(8,128)(2,1)S(1)} %collective-permute-done.12.refs_1_, bf16[64,512]{1,0:T(8,128)(2,1)S(1)} %collective-permute-done.13.refs_2_, bf16[64,512]{1,0:T(8,128)(2,1)S(1)} %collective-permute-done.14.refs_3_, ...), custom_call_target="tpu_custom_call" | custom-call | flops 536870912 | bytes 1738752 | tf_op jit(solution)/shard_map/pallas_call | solution.py:549
  48.5 1.6 %collective-permute-done.17.refs_1_ = bf16[64,256]{1,0:T(8,128)(2,1)S(1)} collective-permute-done((bf16[64,256]{1,0:T(8,128)(2,1)S(1)}, bf16[64,256]{1,0:T(8,128)(2,1)S(1)}, u32[]{:S(2)}, u32[]{:S(2)}) %collective-permute-start.17) | collective-permute-done | bytes 32800 | tf_op jit(solution)/shard_map/ppermute | solution.py:27
  50.3 1.2 %collective-permute-done.20.other_ref = f32[64,256]{1,0:T(8,128)S(1)} collective-permute-done((f32[64,256]{1,0:T(8,128)S(1)}, f32[64,256]{1,0:T(8,128)S(1)}, u32[]{:S(2)}, u32[]{:S(2)}) %collective-permute-start.20) | collective-permute-done | bytes 65568 | tf_op jit(solution)/shard_map/ppermute | solution.py:27
  51.5 0.9 %shard_map.96 = bf16[64,2,4,512]{3,2,1,0:T(4,128)(2,1)} custom-call(f32[64,256]{1,0:T(8,128)S(1)} %shard_map.93.mine_ref, f32[64,256]{1,0:T(8,128)S(1)} %collective-permute-done.20.other_ref, f32[72,512]{1,0:T(8,128)S(1)} %get-tuple-element.46.feat_ref, f32[512,512]{1,0:T(8,128)S(1)} %shard_map.95.base_ref), custom_call_target="tpu_custom_call" | custom-call | bytes 1851392 | tf_op jit(solution)/shard_map/pallas_call | solution.py:549
  (38 shorter events, 4.1 us)
Async XLA Ops:
  2.4 4.3 %collective-permute-start = (f32[72,128]{1,0:T(8,128)S(1)}, f32[72,128]{1,0:T(8,128)S(1)}, u32[]{:S(2)}, u32[]{:S(2)}) collective-permute-start(f32[72,128]{1,0:T(8,128)S(1)} %get-tuple-element.26), channel_id=1, source_target_pairs={{0,12},{4,8},{8,4},{12,0},{1,13},{5,9},{9,5},{13,1},{2,14},{6,10},... | collective-permute-start | bytes 110600 | tf_op jit(solution)/shard_map/ppermute | solution.py:27
  4.9 4.1 %collective-permute-start.1 = (f32[72,128]{1,0:T(8,128)S(1)}, f32[72,128]{1,0:T(8,128)S(1)}, u32[]{:S(2)}, u32[]{:S(2)}) collective-permute-start(f32[72,128]{1,0:T(8,128)S(1)} %get-tuple-element.27), channel_id=1, source_target_pairs={{0,8},{4,12},{8,0},{12,4},{1,9},{5,13},{9,1},{13,5},{2,10},{6,14},... | collective-permute-start | bytes 110600 | tf_op jit(solution)/shard_map/ppermute | solution.py:27
  5.5 3.4 %collective-permute-start.2 = (f32[72,128]{1,0:T(8,128)S(1)}, f32[72,128]{1,0:T(8,128)S(1)}, u32[]{:S(2)}, u32[]{:S(2)}) collective-permute-start(f32[72,128]{1,0:T(8,128)S(1)} %get-tuple-element.28), channel_id=1, source_target_pairs={{0,4},{4,0},{8,12},{12,8},{1,5},{5,1},{9,13},{13,9},{2,6},{6,2},{1... | collective-permute-start | bytes 110600 | tf_op jit(solution)/shard_map/ppermute | solution.py:27
  9.0 6.2 %collective-permute-start.3 = (f32[96,128]{1,0:T(8,128)S(1)}, f32[96,128]{1,0:T(8,128)S(1)}, u32[]{:S(2)}, u32[]{:S(2)}) collective-permute-start(f32[96,128]{1,0:T(8,128)S(1)} %shard_map.78.refs_0_), channel_id=1, source_target_pairs={{0,3},{1,2},{2,1},{3,0},{4,7},{5,6},{6,5},{7,4},{8,11},{9,10},{10,... | collective-permute-start | bytes 147464 | tf_op jit(solution)/shard_map/ppermute | solution.py:27
  12.6 5.0 %collective-permute-start.4 = (f32[96,128]{1,0:T(8,128)S(1)}, f32[96,128]{1,0:T(8,128)S(1)}, u32[]{:S(2)}, u32[]{:S(2)}) collective-permute-start(f32[96,128]{1,0:T(8,128)S(1)} %shard_map.78.refs_0_), channel_id=1, source_target_pairs={{0,2},{1,3},{2,0},{3,1},{4,6},{5,7},{6,4},{7,5},{8,10},{9,11},{10,... | collective-permute-start | bytes 147464 | tf_op jit(solution)/shard_map/ppermute | solution.py:27
  12.6 5.0 %collective-permute-start.5 = (f32[96,128]{1,0:T(8,128)S(1)}, f32[96,128]{1,0:T(8,128)S(1)}, u32[]{:S(2)}, u32[]{:S(2)}) collective-permute-start(f32[96,128]{1,0:T(8,128)S(1)} %shard_map.78.refs_0_), channel_id=1, source_target_pairs={{0,1},{1,0},{2,3},{3,2},{4,5},{5,4},{6,7},{7,6},{8,9},{9,8},{10,11... | collective-permute-start | bytes 147464 | tf_op jit(solution)/shard_map/ppermute | solution.py:27
  15.2 4.4 %copy-start = (f32[3,2,64,64]{3,2,1,0:T(8,128)S(1)}, f32[3,2,64,64]{3,2,1,0:T(8,128)}, u32[]{:S(2)}) copy-start(f32[3,2,64,64]{3,2,1,0:T(8,128)} %refs_7_.1) | copy-start | bytes 294916
  17.6 2.0 %copy-start.2 = (bf16[64,64]{1,0:T(8,128)(2,1)S(1)}, bf16[64,64]{1,0:T(8,128)(2,1)}, u32[]{:S(2)}) copy-start(bf16[64,64]{1,0:T(8,128)(2,1)} %wv_ref.1) | copy-start | bytes 24580
  17.6 2.0 %copy-start.3 = (bf16[64,64]{1,0:T(8,128)(2,1)S(1)}, bf16[64,64]{1,0:T(8,128)(2,1)}, u32[]{:S(2)}) copy-start(bf16[64,64]{1,0:T(8,128)(2,1)} %wo_ref.1) | copy-start | bytes 24580
  17.7 3.4 %collective-permute-start.8 = (f32[72,128]{1,0:T(8,128)S(1)}, f32[72,128]{1,0:T(8,128)S(1)}, u32[]{:S(2)}, u32[]{:S(2)}) collective-permute-start(f32[72,128]{1,0:T(8,128)S(1)} %shard_map.81.refs_0_), channel_id=1, source_target_pairs={{0,4},{4,0},{8,12},{12,8},{1,5},{5,1},{9,13},{13,9},{2,6},{6,2},{1... | collective-permute-start | bytes 110600 | tf_op jit(solution)/shard_map/ppermute | solution.py:27
  17.8 4.0 %collective-permute-start.7 = (f32[72,128]{1,0:T(8,128)S(1)}, f32[72,128]{1,0:T(8,128)S(1)}, u32[]{:S(2)}, u32[]{:S(2)}) collective-permute-start(f32[72,128]{1,0:T(8,128)S(1)} %shard_map.81.refs_0_), channel_id=1, source_target_pairs={{0,8},{4,12},{8,0},{12,4},{1,9},{5,13},{9,1},{13,5},{2,10},{6,14},... | collective-permute-start | bytes 110600 | tf_op jit(solution)/shard_map/ppermute | solution.py:27
  18.9 3.4 %collective-permute-start.6 = (f32[72,128]{1,0:T(8,128)S(1)}, f32[72,128]{1,0:T(8,128)S(1)}, u32[]{:S(2)}, u32[]{:S(2)}) collective-permute-start(f32[72,128]{1,0:T(8,128)S(1)} %shard_map.81.refs_0_), channel_id=1, source_target_pairs={{0,12},{4,8},{8,4},{12,0},{1,13},{5,9},{9,5},{13,1},{2,14},{6,10},... | collective-permute-start | bytes 110600 | tf_op jit(solution)/shard_map/ppermute | solution.py:27
  23.3 5.8 %collective-permute-start.9 = (bf16[16,512]{1,0:T(8,128)(2,1)S(1)}, bf16[16,512]{1,0:T(8,128)(2,1)S(1)}, u32[]{:S(2)}, u32[]{:S(2)}) collective-permute-start(bf16[16,512]{1,0:T(8,128)(2,1)S(1)} %get-tuple-element.33.refs_0_), channel_id=1, source_target_pairs={{0,3},{1,2},{2,1},{3,0},{4,7},{5,6},{6,5},{7,4},{8,11},{9,10},{10,... | collective-permute-start | bytes 49160 | tf_op jit(solution)/shard_map/ppermute | solution.py:27
  25.5 4.6 %collective-permute-start.10 = (bf16[16,512]{1,0:T(8,128)(2,1)S(1)}, bf16[16,512]{1,0:T(8,128)(2,1)S(1)}, u32[]{:S(2)}, u32[]{:S(2)}) collective-permute-start(bf16[16,512]{1,0:T(8,128)(2,1)S(1)} %get-tuple-element.33.refs_0_), channel_id=1, source_target_pairs={{0,2},{1,3},{2,0},{3,1},{4,6},{5,7},{6,4},{7,5},{8,10},{9,11},{10,... | collective-permute-start | bytes 49160 | tf_op jit(solution)/shard_map/ppermute | solution.py:27
  25.7 4.5 %collective-permute-start.11 = (bf16[16,512]{1,0:T(8,128)(2,1)S(1)}, bf16[16,512]{1,0:T(8,128)(2,1)S(1)}, u32[]{:S(2)}, u32[]{:S(2)}) collective-permute-start(bf16[16,512]{1,0:T(8,128)(2,1)S(1)} %get-tuple-element.33.refs_0_), channel_id=1, source_target_pairs={{0,1},{1,0},{2,3},{3,2},{4,5},{5,4},{6,7},{7,6},{8,9},{9,8},{10,11... | collective-permute-start | bytes 49160 | tf_op jit(solution)/shard_map/ppermute | solution.py:27
  30.2 2.0 %copy-start.1 = (bf16[2,128,128]{2,1,0:T(8,128)(2,1)S(1)}, bf16[2,128,128]{2,1,0:T(8,128)(2,1)}, u32[]{:S(2)}) copy-start(bf16[2,128,128]{2,1,0:T(8,128)(2,1)} %constant.2.clone.refs_2_.refs_6_) | copy-start | bytes 196612
  30.2 3.4 %collective-permute-start.14 = (bf16[64,512]{1,0:T(8,128)(2,1)S(1)}, bf16[64,512]{1,0:T(8,128)(2,1)S(1)}, u32[]{:S(2)}, u32[]{:S(2)}) collective-permute-start(bf16[64,512]{1,0:T(8,128)(2,1)S(1)} %shard_map.87.refs_0_), channel_id=1, source_target_pairs={{0,4},{4,0},{8,12},{12,8},{1,5},{5,1},{9,13},{13,9},{2,6},{6,2},{1... | collective-permute-start | bytes 196616 | tf_op jit(solution)/shard_map/ppermute | solution.py:27
  30.3 4.9 %collective-permute-start.13 = (bf16[64,512]{1,0:T(8,128)(2,1)S(1)}, bf16[64,512]{1,0:T(8,128)(2,1)S(1)}, u32[]{:S(2)}, u32[]{:S(2)}) collective-permute-start(bf16[64,512]{1,0:T(8,128)(2,1)S(1)} %shard_map.87.refs_0_), channel_id=1, source_target_pairs={{0,8},{4,12},{8,0},{12,4},{1,9},{5,13},{9,1},{13,5},{2,10},{6,14},... | collective-permute-start | bytes 196616 | tf_op jit(solution)/shard_map/ppermute | solution.py:27
  31.4 4.4 %collective-permute-start.12 = (bf16[64,512]{1,0:T(8,128)(2,1)S(1)}, bf16[64,512]{1,0:T(8,128)(2,1)S(1)}, u32[]{:S(2)}, u32[]{:S(2)}) collective-permute-start(bf16[64,512]{1,0:T(8,128)(2,1)S(1)} %shard_map.87.refs_0_), channel_id=1, source_target_pairs={{0,12},{4,8},{8,4},{12,0},{1,13},{5,9},{9,5},{13,1},{2,14},{6,10},... | collective-permute-start | bytes 196616 | tf_op jit(solution)/shard_map/ppermute | solution.py:27
  36.9 1.3 %collective-permute-start.15 = (bf16[64,256]{1,0:T(8,128)(2,1)S(1)}, bf16[64,256]{1,0:T(8,128)(2,1)S(1)}, u32[]{:S(2)}, u32[]{:S(2)}) collective-permute-start(bf16[64,256]{1,0:T(8,128)(2,1)S(1)} %get-tuple-element.38), channel_id=1, source_target_pairs={{0,4},{4,0},{8,12},{12,8},{1,5},{5,1},{9,13},{13,9},{2,6},{6,2},{1... | collective-permute-start | bytes 98312 | tf_op jit(solution)/shard_map/ppermute | solution.py:27
  38.2 4.0 %collective-permute-start.16 = (bf16[64,256]{1,0:T(8,128)(2,1)S(1)}, bf16[64,256]{1,0:T(8,128)(2,1)S(1)}, u32[]{:S(2)}, u32[]{:S(2)}) collective-permute-start(bf16[64,256]{1,0:T(8,128)(2,1)S(1)} %shard_map.90.refs_0_), channel_id=1, source_target_pairs={{0,8},{4,12},{8,0},{12,4},{1,9},{5,13},{9,1},{13,5},{2,10},{6,14},... | collective-permute-start | bytes 98312 | tf_op jit(solution)/shard_map/ppermute | solution.py:27
  42.1 6.4 %collective-permute-start.19 = (bf16[64,256]{1,0:T(8,128)(2,1)S(1)}, bf16[64,256]{1,0:T(8,128)(2,1)S(1)}, u32[]{:S(2)}, u32[]{:S(2)}) collective-permute-start(bf16[64,256]{1,0:T(8,128)(2,1)S(1)} %shard_map.91.refs_0_), channel_id=1, source_target_pairs={{0,1},{1,0},{2,3},{3,2},{4,5},{5,4},{6,7},{7,6},{8,9},{9,8},{10,11... | collective-permute-start | bytes 98312 | tf_op jit(solution)/shard_map/ppermute | solution.py:27
  43.4 5.1 %collective-permute-start.18 = (bf16[64,256]{1,0:T(8,128)(2,1)S(1)}, bf16[64,256]{1,0:T(8,128)(2,1)S(1)}, u32[]{:S(2)}, u32[]{:S(2)}) collective-permute-start(bf16[64,256]{1,0:T(8,128)(2,1)S(1)} %shard_map.91.refs_0_), channel_id=1, source_target_pairs={{0,2},{1,3},{2,0},{3,1},{4,6},{5,7},{6,4},{7,5},{8,10},{9,11},{10,... | collective-permute-start | bytes 98312 | tf_op jit(solution)/shard_map/ppermute | solution.py:27
  44.5 5.7 %collective-permute-start.17 = (bf16[64,256]{1,0:T(8,128)(2,1)S(1)}, bf16[64,256]{1,0:T(8,128)(2,1)S(1)}, u32[]{:S(2)}, u32[]{:S(2)}) collective-permute-start(bf16[64,256]{1,0:T(8,128)(2,1)S(1)} %shard_map.91.refs_0_), channel_id=1, source_target_pairs={{0,3},{1,2},{2,1},{3,0},{4,7},{5,6},{6,5},{7,4},{8,11},{9,10},{10,... | collective-permute-start | bytes 98312 | tf_op jit(solution)/shard_map/ppermute | solution.py:27
  50.2 1.3 %collective-permute-start.20 = (f32[64,256]{1,0:T(8,128)S(1)}, f32[64,256]{1,0:T(8,128)S(1)}, u32[]{:S(2)}, u32[]{:S(2)}) collective-permute-start(f32[64,256]{1,0:T(8,128)S(1)} %shard_map.93.mine_ref), channel_id=1, source_target_pairs={{0,4},{4,0},{8,12},{12,8},{1,5},{5,1},{9,13},{13,9},{2,6},{6,2},{1... | collective-permute-start | bytes 196616 | tf_op jit(solution)/shard_map/ppermute | solution.py:27

commit v12 on v11

--- a/solution.py
+++ b/solution.py
@@ -202,11 +202,11 @@
     return lax.broadcasted_iota(jnp.int32, shape, dim)
 
 
-def join_quarters(part_ref, quarters):
-    size = len(quarters)
-    for step, quarter in zip([0, *range(size - 1, 0, -1)], quarters):
-        part_ref[lax.axis_index("gx") ^ step] = quarter[...]
-    return jnp.concatenate([part_ref[index] for index in range(part_ref.shape[0])], axis=1)
+def join_halves(half_ref, mine_ref, other_ref):
+    core = lax.axis_index("gx") & 1
+    half_ref[core] = mine_ref[...]
+    half_ref[core ^ 1] = other_ref[...]
+    return jnp.concatenate([half_ref[0], half_ref[1]], axis=1)
 
 
 def expand(part):
@@ -237,7 +237,7 @@
 
 
 def sums_kernel(field_ref, *refs):
-    outs, (cols_ref, data_ref, part_ref, semaphores) = refs[:-4], refs[-4:]
+    outs, (cols_ref, data_ref, half_ref, semaphores) = refs[:-4], refs[-4:]
     _, rows_x, rows_y, depth = data_ref.shape
     cells = rows_x * rows_y
     chunks = semaphores.shape[0]
@@ -264,15 +264,15 @@
         data = data.reshape(size * cells, depth).astype(jnp.bfloat16)
         cols_ref[index * size * cells : (index + 1) * size * cells, :] = data
         part = mul(pick, data)
-        for quarter in range(part_ref.shape[0]):
-            part_ref[quarter, rows, :] = part[:, quarter * LANES : (quarter + 1) * LANES]
+        half_ref[0, rows, :] = part[:, : depth // 2]
+        half_ref[1, rows, :] = part[:, depth // 2 :]
         row_sums = mul(data, ones).reshape(size, cells, LANES)
         shape = row_sums.shape
         mine = number(shape, 0) + index * size == number(shape, 2)
         own = own + jnp.sum(jnp.where(mine, row_sums, 0.0), axis=0)
     for step, out in enumerate(outs):
-        out[0:WIDTH, :] = part_ref[lax.axis_index("gx") ^ step]
-        out[WIDTH:, :] = own
+        out[0:WIDTH, :] = half_ref[(lax.axis_index("gx") & 1) ^ step]
+        out[WIDTH:, :] = jnp.concatenate([own] * (depth // 2 // LANES), axis=1)
 
 
 def add_kernel(*refs):
@@ -288,6 +288,12 @@
         start += more
 
 
+def add_core_kernel(mine_ref, other_ref, out_ref):
+    out_ref[0:WIDTH, :] = mine_ref[0:WIDTH, :] + other_ref[0:WIDTH, :]
+    out_ref[WIDTH:, 0:LANES] = mine_ref[WIDTH:, 0:LANES]
+    out_ref[WIDTH:, LANES : 2 * LANES] = other_ref[WIDTH:, 0:LANES]
+
+
 def stack_kernel(*refs):
     refs[-1][...] = jnp.concatenate([ref[...] for ref in refs[:-1]], axis=0)
 
@@ -301,7 +307,7 @@
     inverse = lax.rsqrt(jnp.mean(pooled * pooled, axis=0, keepdims=True) + EPSILON)
     normed = pooled * inverse
     feat_ref[0:WIDTH, :] = normed
-    feat_ref[WIDTH:, :] = jnp.broadcast_to(inverse, (HEAD_DIM, LANES))
+    feat_ref[WIDTH:, :] = jnp.broadcast_to(inverse, (HEAD_DIM, inverse.shape[1]))
 
 
 def add_pull_kernel(*refs):
@@ -319,15 +325,17 @@
 
 def plane_kernel(cells, span_x, lengths, *refs):
     parts, (same_ref, qk_ref, mix_ref, feat_ref, full_ref) = refs[:-5], refs[-5:]
+    chips = span_x // 2
     totals = jnp.concatenate(
         [
-            part[WIDTH + step * cells : WIDTH + (step + 1) * cells, :]
-            for first in range(span_x)
+            part[WIDTH + step * cells : WIDTH + (step + 1) * cells, core * LANES : core * LANES + WIDTH]
+            for chip in range(chips)
+            for core in range(2)
             for part in parts
-            for step in range(first, (part.shape[0] - WIDTH) // cells, span_x)
+            for step in range(chip, (part.shape[0] - WIDTH) // cells, chips)
         ],
         axis=0,
-    )[:, :WIDTH]
+    )
     places = totals.shape[0]
     high, low = split(totals)
     forward = backward = None
@@ -358,13 +366,12 @@
     mix_ref[1] = backward
 
 
-def coef_kernel(spans, *refs):
-    quarters, refs = refs[:spans], refs[spans:]
-    wz_ref, field_ref, cot_ref, wv_ref, wo_ref, send_ref, both_ref, feat_ref, part_ref = refs
+def coef_kernel(mine_ref, other_ref, wz_ref, field_ref, cot_ref, wv_ref, wo_ref,
+                send_ref, both_ref, feat_ref, half_ref):
     rows, depth = field_ref.shape
     cells = rows // WIDTH
     wide = HEADS * HEAD_DIM * HEAD_DIM
-    feat = join_quarters(part_ref, quarters)
+    feat = join_halves(half_ref, mine_ref, other_ref)
     feat_ref[...] = feat
     high, low = split(feat[:WIDTH])
     both = mul_left(wz_ref[...], high) + mul(wz_ref[...].astype(jnp.bfloat16), low)
@@ -471,29 +478,22 @@
         inverse = feat_ref[4 * axis + 3, 0:cells, :]
         found = found - normed * jnp.mean(found * normed, axis=1, keepdims=True)
         total = total + inverse * found * (1.0 / lengths[axis][1])
-    out_ref[...] = total
-
-
-def base_kernel(top_ref, wv_ref, both_ref, cot_ref, plane_ref, out_ref):
-    rows = cot_ref.shape[0]
-    cells = rows // WIDTH
     shape = (WIDTH, cells, WIDTH)
-    own = jnp.where(number(shape, 0) == number(shape, 2), plane_ref[...][None], 0.0)
-    plane = mul_left(own.reshape(rows, WIDTH), jnp.ones((WIDTH, LANES), jnp.bfloat16))
+    own = jnp.where(number(shape, 0) == number(shape, 2), total[None], 0.0)
+    out_ref[...] = mul_left(own.reshape(-1, WIDTH), jnp.ones((WIDTH, LANES), jnp.bfloat16))
+
+
+def base_kernel(top_ref, wv_ref, both_ref, cot_ref, out_ref):
     keyset = expand(both_ref[...].astype(jnp.float32)[WIDTH:])
     left = spread(wv_ref[...], top_ref[1])
-    found = mul(left, keyset) + cot_ref[...].astype(jnp.float32)
-    columns = found.shape[1] // LANES
-    out_ref[...] = found + jnp.concatenate([plane] * columns, axis=1)
-
-
-def final_kernel(places, mine_ref, other_ref, feat_ref, base_ref, out_ref, data_ref, half_ref, semaphores):
+    out_ref[...] = mul(left, keyset) + cot_ref[...].astype(jnp.float32)
+
+
+def final_kernel(places, mine_ref, other_ref, feat_ref, base_ref, plane_ref, out_ref, data_ref,
+                 half_ref, semaphores):
     depth = base_ref.shape[1]
     _, rows_x, rows_y, _ = data_ref.shape
-    core = lax.axis_index("gx") & 1
-    half_ref[core] = mine_ref[...]
-    half_ref[core ^ 1] = other_ref[...]
-    found = jnp.concatenate([half_ref[0], half_ref[1]], axis=1)
+    found = join_halves(half_ref, mine_ref, other_ref)
     normed = feat_ref[0:WIDTH, :]
     inverse = feat_ref[WIDTH : WIDTH + 1, :]
     found = inverse * (found - normed * jnp.mean(found * normed, axis=0, keepdims=True))
@@ -505,6 +505,8 @@
     for index in range(chunks):
         rows = slice(index * size, (index + 1) * size)
         base = base_ref[index * size * cells : (index + 1) * size * cells, :]
+        plane = plane_ref[index * size * cells : (index + 1) * size * cells, :]
+        base = base + jnp.concatenate([plane] * (depth // LANES), axis=1)
         total = base.reshape(size, cells, depth) + found[rows][:, None, :]
         for at_x in range(rows_x):
             part = total[:, at_x * rows_y : (at_x + 1) * rows_y, :]
@@ -580,7 +582,8 @@
         np.stack([at_x[:, None] == at_x[None], at_y[:, None] == at_y[None]]), dtype=bf16
     )
 
-    parts = pltpu.VMEM((span_x, WIDTH, LANES), f32)
+    half = depth // 2
+    halves = pltpu.VMEM((2, WIDTH, half), f32)
     chunked = [pltpu.VMEM(field.shape, bf16), pltpu.SemaphoreType.DMA((4,))]
     factor_z = 1.0 / math.sqrt(HEAD_DIM * depth)
     cube = rows * wide * depth * 2
@@ -613,11 +616,11 @@
 
     *sums, cols = run(
         sums_kernel,
-        [like((WIDTH + cells, LANES), f32)] * span_x + [like((rows, depth), bf16)],
+        [like((WIDTH + cells, half), f32)] * 2 + [like((rows, depth), bf16)],
         (pltpu.with_memory_space_constraint(field, pltpu.HBM),),
         places=pltpu.HBM,
         flops=cube // 4,
-        scratch=[chunked[0], parts, chunked[1]],
+        scratch=[chunked[0], halves, chunked[1]],
     )
     wv, wo, wq, wk, wz = run(
         prepare_kernel,
@@ -627,12 +630,17 @@
         flops=cube // 8,
     )
     total = run(
-        add_kernel, [like((WIDTH + span_x * cells, LANES), f32)], swaps(sums, "gx", span_x)
-    )
+        add_core_kernel,
+        [like((WIDTH + cells, half), f32)],
+        (sums[0], swap(sums[1], "gx", span_x, 1)),
+    )
+    for level in range(1, span_x.bit_length() - 1):
+        (total,) = taken(add_kernel, (total, swap(total, "gx", span_x, 1 << level)), last=True)
     totals = taken(add_kernel, swaps(total, "gy", span_y))
+    totals, cots, wz = lax.optimization_barrier((totals, cots, wz))
     mine = run(
         functools.partial(factor_kernel, grid_x * grid_y),
-        [like((WIDTH + HEAD_DIM, LANES), f32)],
+        [like((WIDTH + HEAD_DIM, half), f32)],
         totals,
     )
     mix, feat, full = run(
@@ -643,17 +651,17 @@
         flops=cube // 2,
     )
     send, both, feat_z = run(
-        functools.partial(coef_kernel, span_x),
+        coef_kernel,
         [like((2 * cells, wide), bf16), like((2 * WIDTH, depth), bf16),
          like((WIDTH + HEAD_DIM, depth), f32)],
-        swaps(mine, "gx", span_x, False) + (wz, cols, cots, wv, wo),
+        (mine, swap(mine, "gx", span_x, 1), wz, cols, cots, wv, wo),
         flops=2 * cube,
-        scratch=[pltpu.VMEM((span_x, WIDTH + HEAD_DIM, LANES), f32)],
+        scratch=[pltpu.VMEM((2, WIDTH + HEAD_DIM, half), f32)],
     )
     (low,) = taken(stack_kernel, swaps(send, "gy", span_y), last=True)
-    lows = swaps(low, "gx", span_x, False)
-    pulled = like((WIDTH, depth // 2), bf16)
-    halves = pltpu.VMEM((2, WIDTH, depth // 2), f32)
+    first, *others = swaps(low, "gx", span_x, False)
+    lows = (first,) + tuple(reversed(others))
+    pulled = like((WIDTH, half), bf16)
     top, mine, other = run(
         functools.partial(mix_kernel, factor_z, span_x),
         [like((2, cells, wide), f32), pulled, pulled],
@@ -662,28 +670,27 @@
         scratch=[halves],
     )
     total = run(add_pull_kernel, [pulled], (mine, swap(other, "gx", span_x, 1)))
+    base = run(base_kernel, [like((rows, depth), f32)], (top, wv, both, cots), flops=cube)
+    total, base = lax.optimization_barrier((total, base))
     for level in range(1, span_x.bit_length() - 1):
         total = run(add_pull_kernel, [pulled], (total, swap(total, "gx", span_x, 1 << level)))
     layer_output = run(
         output_kernel, [like(field.shape, bf16)], (top, wo, both, cols), flops=cube
     )
-    total, layer_output = lax.optimization_barrier((total, layer_output))
+    plane = run(
+        functools.partial(gram_kernel, cells, lengths, factor_z),
+        [like((rows, LANES), f32)],
+        lows + (feat, full, same, qk_weight),
+        flops=2 * cube,
+    )
+    total, layer_output, plane = lax.optimization_barrier((total, layer_output, plane))
     total = run(
         add_pull_kernel, [like(pulled.shape, f32)], swaps(total, "gy", span_y, False)
     )
-    plane = run(
-        functools.partial(gram_kernel, cells, lengths, factor_z),
-        [like((cells, WIDTH), f32)],
-        lows + (feat, full, same, qk_weight),
-        flops=2 * cube,
-    )
-    base = run(base_kernel, [like((rows, depth), f32)], (top, wv, both, cots, plane), flops=cube)
-    total, base = lax.optimization_barrier((total, base))
-    other = swap(total, "gx", span_x, 1)
     field_grad = run(
         functools.partial(final_kernel, grid_x * grid_y),
         [like(field.shape, bf16)],
-        (total, other, feat_z, base),
+        (total, swap(total, "gx", span_x, 1), feat_z, base, plane),
         target=pltpu.HBM,
         scratch=[chunked[0], halves, chunked[1]],
     )
@@ -699,7 +706,7 @@
         places = grid_x // mesh.shape["groups"] * grid_y
         small = places == LANES and places == 8 * count
         small = small and depth == LANES * mesh.shape["gx"] and count & (count - 1) == 0
-        small = small and mesh.shape["gx"] > 1
+        small = small and mesh.shape["gx"] > 3
         return jax.shard_map(
             per_device_kernels if small else per_device,
             mesh=mesh,

time: 52.6 us -> 51.6 us (0.981)
  starting transfers between devices: 21.8 us -> 20 us
    ppermute x21 -> x18, starting transfers between devices: 21.8 us -> 20 us  [swap(): return lax.ppermute(part, axis, [(i, i ^ step) for i in range(size)])]
    ppermute x21 -> x18, waiting for transfers between devices: 18.9 us -> 19.4 us  [swap(): return lax.ppermute(part, axis, [(i, i ^ step) for i in range(size)])]
    pallas_call x20 -> x21, Pallas kernels: 10.9 us -> 11.1 us  [run(): pl.pallas_call(kernel, out_shape=tuple(outs), in_specs=[pl.BlockSpec(memo...]
  transfers between devices with their start and end apart: 21 -> 18, of which waited for: 14 -> 14; matrix products, arithmetic and copies ran while one was open for 0% -> 0% of each run, Pallas kernels for 12% -> 12%
where the time goes in v12:
time: 51.6 us; the launch traced here: 51.4 us
  starting transfers between devices  20 us (39%)
  waiting for transfers between devices  19.4 us (38%)
  Pallas kernels  11.1 us (22%)
  between operations  0.79 us (2%)
    ppermute x18, starting transfers between devices, swap(): return lax.ppermute(part, axis, [(i, i ^ step) for i in range(size)])  20 us
    ppermute x18, waiting for transfers between devices, swap(): return lax.ppermute(part, axis, [(i, i ^ step) for i in range(size)])  19.4 us
    pallas_call x21, Pallas kernels, run(): pl.pallas_call(kernel, out_shape=tuple(outs), in_specs=[pl.BlockSpec(memo...  11.1 us
  transfers between devices with their start and end apart: 18, of which 14 were waited for; matrix products, arithmetic and copies ran while one was open for 0% of the time, Pallas kernels for 12%

profile of v12, /device:TPU:0, one launch (start us, length us, event | category | flops | bytes accessed | tf_op | source)
XLA Modules:
  0.0 51.4 jit_solution(4110780004756298764)
XLA Ops:
  0.6 1.8 %shard_map.77 = (f32[72,256]{1,0:T(8,128)S(1)}, f32[72,256]{1,0:T(8,128)S(1)}, bf16[512,512]{1,0:T(8,128)(2,1)S(1)}) custom-call(bf16[64,2,4,512]{3,2,1,0:T(4,128)(2,1)} %field_ref.1), custom_call_target="tpu_custom_call" | custom-call | flops 67108864 | bytes 1196032 | tf_op jit(solution)/shard_map/pallas_call | solution.py:551
  2.9 0.9 %collective-permute-done.other_ref = f32[72,256]{1,0:T(8,128)S(1)} collective-permute-done((f32[72,256]{1,0:T(8,128)S(1)}, f32[72,256]{1,0:T(8,128)S(1)}, u32[]{:S(2)}, u32[]{:S(2)}) %collective-permute-start) | collective-permute-done | bytes 73760 | tf_op jit(solution)/shard_map/ppermute | solution.py:27
  3.9 2.9 %collective-permute-start.1 = (f32[72,256]{1,0:T(8,128)S(1)}, f32[72,256]{1,0:T(8,128)S(1)}, u32[]{:S(2)}, u32[]{:S(2)}) collective-permute-start(f32[72,256]{1,0:T(8,128)S(1)} %shard_map.78.refs_0_), channel_id=1, source_target_pairs={{0,8},{4,12},{8,0},{12,4},{1,9},{5,13},{9,1},{13,5},{2,10},{6,14},... | collective-permute-start | bytes 221192 | tf_op jit(solution)/shard_map/ppermute | solution.py:27
  6.8 2.6 %collective-permute-done.1.refs_1_ = f32[72,256]{1,0:T(8,128)S(1)} collective-permute-done((f32[72,256]{1,0:T(8,128)S(1)}, f32[72,256]{1,0:T(8,128)S(1)}, u32[]{:S(2)}, u32[]{:S(2)}) %collective-permute-start.1) | collective-permute-done | bytes 73760 | tf_op jit(solution)/shard_map/ppermute | solution.py:27
  9.4 3.9 %collective-permute-start.2 = (f32[80,256]{1,0:T(8,128)S(1)}, f32[80,256]{1,0:T(8,128)S(1)}, u32[]{:S(2)}, u32[]{:S(2)}) collective-permute-start(f32[80,256]{1,0:T(8,128)S(1)} %shard_map.79.refs_0_), channel_id=1, source_target_pairs={{0,3},{1,2},{2,1},{3,0},{4,7},{5,6},{6,5},{7,4},{8,11},{9,10},{10,... | collective-permute-start | bytes 245768 | tf_op jit(solution)/shard_map/ppermute | solution.py:27
  13.4 0.6 %collective-permute-start.4 = (f32[80,256]{1,0:T(8,128)S(1)}, f32[80,256]{1,0:T(8,128)S(1)}, u32[]{:S(2)}, u32[]{:S(2)}) collective-permute-start(f32[80,256]{1,0:T(8,128)S(1)} %shard_map.79.refs_0_), channel_id=1, source_target_pairs={{0,1},{1,0},{2,3},{3,2},{4,5},{5,4},{6,7},{7,6},{8,9},{9,8},{10,11... | collective-permute-start | bytes 245768 | tf_op jit(solution)/shard_map/ppermute | solution.py:27
  14.3 1.2 %shard_map.82.cot_ref.refs_10_ = bf16[512,512]{1,0:T(8,128)(2,1)S(1)} custom-call(bf16[64,2,4,512]{3,2,1,0:T(4,128)(2,1)} %cot_ref.1), custom_call_target="tpu_custom_call" | custom-call | flops 268435456 | bytes 1048576 | tf_op jit(solution)/shard_map/pallas_call | solution.py:551
  15.4 1.0 %collective-permute-done.2.refs_1_ = f32[80,256]{1,0:T(8,128)S(1)} collective-permute-done((f32[80,256]{1,0:T(8,128)S(1)}, f32[80,256]{1,0:T(8,128)S(1)}, u32[]{:S(2)}, u32[]{:S(2)}) %collective-permute-start.2) | collective-permute-done | bytes 81952 | tf_op jit(solution)/shard_map/ppermute | solution.py:27
  16.4 3.2 %collective-permute-done.3.refs_1_ = f32[80,256]{1,0:T(8,128)S(1)} collective-permute-done((f32[80,256]{1,0:T(8,128)S(1)}, f32[80,256]{1,0:T(8,128)S(1)}, u32[]{:S(2)}, u32[]{:S(2)}) %collective-permute-start.3) | collective-permute-done | bytes 81952 | tf_op jit(solution)/shard_map/ppermute | solution.py:27
  19.8 1.3 %collective-permute-done.5.other_ref = f32[72,256]{1,0:T(8,128)S(1)} collective-permute-done((f32[72,256]{1,0:T(8,128)S(1)}, f32[72,256]{1,0:T(8,128)S(1)}, u32[]{:S(2)}, u32[]{:S(2)}) %collective-permute-start.5) | collective-permute-done | bytes 73760 | tf_op jit(solution)/shard_map/ppermute | solution.py:27
  21.1 1.0 %shard_map.85 = (bf16[16,512]{1,0:T(8,128)(2,1)S(1)}, bf16[128,512]{1,0:T(8,128)(2,1)S(1)}, f32[72,512]{1,0:T(8,128)S(1)}) custom-call(f32[72,256]{1,0:T(8,128)S(1)} %shard_map.84.mine_ref, f32[72,256]{1,0:T(8,128)S(1)} %collective-permute-done.5.other_ref, f32[128,64]{1,0:T(8,128)S(1)} %get-tuple-element.33.wz_ref, ...), custom_call_target="tpu_custom_call" | custom-call | flops 536870912 | bytes 1785856 | tf_op jit(solution)/shard_map/pallas_call | solution.py:551
  22.1 2.7 %collective-permute-start.6 = (bf16[16,512]{1,0:T(8,128)(2,1)S(1)}, bf16[16,512]{1,0:T(8,128)(2,1)S(1)}, u32[]{:S(2)}, u32[]{:S(2)}) collective-permute-start(bf16[16,512]{1,0:T(8,128)(2,1)S(1)} %get-tuple-element.38.refs_0_), channel_id=1, source_target_pairs={{0,3},{1,2},{2,1},{3,0},{4,7},{5,6},{6,5},{7,4},{8,11},{9,10},{10,... | collective-permute-start | bytes 49160 | tf_op jit(solution)/shard_map/ppermute | solution.py:27
  24.8 1.7 %collective-permute-start.8 = (bf16[16,512]{1,0:T(8,128)(2,1)S(1)}, bf16[16,512]{1,0:T(8,128)(2,1)S(1)}, u32[]{:S(2)}, u32[]{:S(2)}) collective-permute-start(bf16[16,512]{1,0:T(8,128)(2,1)S(1)} %get-tuple-element.38.refs_0_), channel_id=1, source_target_pairs={{0,1},{1,0},{2,3},{3,2},{4,5},{5,4},{6,7},{7,6},{8,9},{9,8},{10,11... | collective-permute-start | bytes 49160 | tf_op jit(solution)/shard_map/ppermute | solution.py:27
  26.5 1.1 %collective-permute-done.6.refs_1_ = bf16[16,512]{1,0:T(8,128)(2,1)S(1)} collective-permute-done((bf16[16,512]{1,0:T(8,128)(2,1)S(1)}, bf16[16,512]{1,0:T(8,128)(2,1)S(1)}, u32[]{:S(2)}, u32[]{:S(2)}) %collective-permute-start.6) | collective-permute-done | bytes 16416 | tf_op jit(solution)/shard_map/ppermute | solution.py:27
  27.7 1.7 %collective-permute-done.7.refs_1_ = bf16[16,512]{1,0:T(8,128)(2,1)S(1)} collective-permute-done((bf16[16,512]{1,0:T(8,128)(2,1)S(1)}, bf16[16,512]{1,0:T(8,128)(2,1)S(1)}, u32[]{:S(2)}, u32[]{:S(2)}) %collective-permute-start.7) | collective-permute-done | bytes 16416 | tf_op jit(solution)/shard_map/ppermute | solution.py:27
  29.5 1.3 %collective-permute-start.10 = (bf16[64,512]{1,0:T(8,128)(2,1)S(1)}, bf16[64,512]{1,0:T(8,128)(2,1)S(1)}, u32[]{:S(2)}, u32[]{:S(2)}) collective-permute-start(bf16[64,512]{1,0:T(8,128)(2,1)S(1)} %shard_map.88.refs_0_), channel_id=1, source_target_pairs={{0,8},{4,12},{8,0},{12,4},{1,9},{5,13},{9,1},{13,5},{2,10},{6,14},... | collective-permute-start | bytes 196616 | tf_op jit(solution)/shard_map/ppermute | solution.py:27
  30.8 0.5 %collective-permute-start.9 = (bf16[64,512]{1,0:T(8,128)(2,1)S(1)}, bf16[64,512]{1,0:T(8,128)(2,1)S(1)}, u32[]{:S(2)}, u32[]{:S(2)}) collective-permute-start(bf16[64,512]{1,0:T(8,128)(2,1)S(1)} %shard_map.88.refs_0_), channel_id=1, source_target_pairs={{0,4},{4,0},{8,12},{12,8},{1,5},{5,1},{9,13},{13,9},{2,6},{6,2},{1... | collective-permute-start | bytes 196616 | tf_op jit(solution)/shard_map/ppermute | solution.py:27
  31.4 1.4 %shard_map.89 = (f32[2,64,128]{2,1,0:T(8,128)S(1)}, f32[8,128,64]{2,1,0:T(8,128)S(1)}, f32[2,1024,128]{2,1,0:T(8,128)S(1)}) custom-call(f32[112,256]{1,0:T(8,128)S(1)} %shard_map.81.refs_0_, f32[80,256]{1,0:T(8,128)S(1)} %collective-permute-done.4.refs_1_, bf16[2,128,128]{2,1,0:T(8,128)(2,1)S(1)} %copy-done.1, f32[3,2,64,64]{3,2,1,0:T(8,128)S(1)} %copy-done), custom_call_target="tpu_custom_call" | custom-call | flops 134217728 | bytes 1736704 | tf_op jit(solution)/shard_map/pallas_call | solution.py:551
  32.8 1.1 %collective-permute-done.11.refs_3_ = bf16[64,512]{1,0:T(8,128)(2,1)S(1)} collective-permute-done((bf16[64,512]{1,0:T(8,128)(2,1)S(1)}, bf16[64,512]{1,0:T(8,128)(2,1)S(1)}, u32[]{:S(2)}, u32[]{:S(2)}) %collective-permute-start.11) | collective-permute-done | bytes 65568 | tf_op jit(solution)/shard_map/ppermute | solution.py:27
  33.9 1.0 %collective-permute-done.10.refs_2_ = bf16[64,512]{1,0:T(8,128)(2,1)S(1)} collective-permute-done((bf16[64,512]{1,0:T(8,128)(2,1)S(1)}, bf16[64,512]{1,0:T(8,128)(2,1)S(1)}, u32[]{:S(2)}, u32[]{:S(2)}) %collective-permute-start.10) | collective-permute-done | bytes 65568 | tf_op jit(solution)/shard_map/ppermute | solution.py:27
  34.9 1.1 %shard_map.90 = (f32[2,8,512]{2,1,0:T(8,128)S(1)}, bf16[64,256]{1,0:T(8,128)(2,1)S(1)}, bf16[64,256]{1,0:T(8,128)(2,1)S(1)}) custom-call(bf16[64,512]{1,0:T(8,128)(2,1)S(1)} %shard_map.88.refs_0_, bf16[64,512]{1,0:T(8,128)(2,1)S(1)} %collective-permute-done.9.refs_1_, bf16[64,512]{1,0:T(8,128)(2,1)S(1)} %collective-permute-done.10.refs_2_, ...), custom_call_target="tpu_custom_call" | custom-call | flops 268435456 | bytes 1998848 | tf_op jit(solution)/shard_map/pallas_call | solution.py:551
  36.7 0.6 %collective-permute-done.12.refs_1_ = bf16[64,256]{1,0:T(8,128)(2,1)S(1)} collective-permute-done((bf16[64,256]{1,0:T(8,128)(2,1)S(1)}, bf16[64,256]{1,0:T(8,128)(2,1)S(1)}, u32[]{:S(2)}, u32[]{:S(2)}) %collective-permute-start.12) | collective-permute-done | bytes 32800 | tf_op jit(solution)/shard_map/ppermute | solution.py:27
  37.3 0.9 %collective-permute-start.13 = (bf16[64,256]{1,0:T(8,128)(2,1)S(1)}, bf16[64,256]{1,0:T(8,128)(2,1)S(1)}, u32[]{:S(2)}, u32[]{:S(2)}) collective-permute-start(bf16[64,256]{1,0:T(8,128)(2,1)S(1)} %shard_map.91.refs_0_), channel_id=1, source_target_pairs={{0,8},{4,12},{8,0},{12,4},{1,9},{5,13},{9,1},{13,5},{2,10},{6,14},... | collective-permute-start | bytes 98312 | tf_op jit(solution)/shard_map/ppermute | solution.py:27
  38.2 1.6 %shard_map.95.plane_ref = f32[512,128]{1,0:T(8,128)S(1)} custom-call(bf16[64,512]{1,0:T(8,128)(2,1)S(1)} %shard_map.88.refs_0_, bf16[64,512]{1,0:T(8,128)(2,1)S(1)} %collective-permute-done.9.refs_1_, bf16[64,512]{1,0:T(8,128)(2,1)S(1)} %collective-permute-done.10.refs_2_, bf16[64,512]{1,0:T(8,128)(2,1)S(1)} %collective-permute-done.11.refs_3_, ...), custom_call_target="tpu_custom_call" | custom-call | flops 536870912 | bytes 1998848 | tf_op jit(solution)/shard_map/pallas_call | solution.py:551
  39.8 1.3 %shard_map.94 = bf16[64,2,4,512]{3,2,1,0:T(4,128)(2,1)} custom-call(f32[2,8,512]{2,1,0:T(8,128)S(1)} %get-tuple-element.44.top_ref, f32[64,512]{1,0:T(8,128)S(1)} %get-tuple-element.37.wo_ref.refs_6_, bf16[128,512]{1,0:T(8,128)(2,1)S(1)} %get-tuple-element.45.both_ref, bf16[512,512]{1,0:T(8,128)(2,1)S(1)} %get-tuple-element.34.field_ref.refs_9_), custom_call_target="tpu_custom_call" | custom-call | flops 268435456 | bytes 1343488 | tf_op jit(solution)/shard_map/pallas_call | solution.py:551
  41.3 1.1 %collective-permute-start.16 = (bf16[64,256]{1,0:T(8,128)(2,1)S(1)}, bf16[64,256]{1,0:T(8,128)(2,1)S(1)}, u32[]{:S(2)}, u32[]{:S(2)}) collective-permute-start(bf16[64,256]{1,0:T(8,128)(2,1)S(1)} %shard_map.93.refs_0_), channel_id=1, source_target_pairs={{0,1},{1,0},{2,3},{3,2},{4,5},{5,4},{6,7},{7,6},{8,9},{9,8},{10,11... | collective-permute-start | bytes 98312 | tf_op jit(solution)/shard_map/ppermute | solution.py:27
  42.4 1.0 %collective-permute-start.15 = (bf16[64,256]{1,0:T(8,128)(2,1)S(1)}, bf16[64,256]{1,0:T(8,128)(2,1)S(1)}, u32[]{:S(2)}, u32[]{:S(2)}) collective-permute-start(bf16[64,256]{1,0:T(8,128)(2,1)S(1)} %shard_map.93.refs_0_), channel_id=1, source_target_pairs={{0,2},{1,3},{2,0},{3,1},{4,6},{5,7},{6,4},{7,5},{8,10},{9,11},{10,... | collective-permute-start | bytes 98312 | tf_op jit(solution)/shard_map/ppermute | solution.py:27
  43.4 2.3 %collective-permute-start.14 = (bf16[64,256]{1,0:T(8,128)(2,1)S(1)}, bf16[64,256]{1,0:T(8,128)(2,1)S(1)}, u32[]{:S(2)}, u32[]{:S(2)}) collective-permute-start(bf16[64,256]{1,0:T(8,128)(2,1)S(1)} %shard_map.93.refs_0_), channel_id=1, source_target_pairs={{0,3},{1,2},{2,1},{3,0},{4,7},{5,6},{6,5},{7,4},{8,11},{9,10},{10,... | collective-permute-start | bytes 98312 | tf_op jit(solution)/shard_map/ppermute | solution.py:27
  45.7 1.5 %collective-permute-done.15.refs_2_ = bf16[64,256]{1,0:T(8,128)(2,1)S(1)} collective-permute-done((bf16[64,256]{1,0:T(8,128)(2,1)S(1)}, bf16[64,256]{1,0:T(8,128)(2,1)S(1)}, u32[]{:S(2)}, u32[]{:S(2)}) %collective-permute-start.15) | collective-permute-done | bytes 32800 | tf_op jit(solution)/shard_map/ppermute | solution.py:27
  47.3 1.8 %collective-permute-done.14.refs_1_ = bf16[64,256]{1,0:T(8,128)(2,1)S(1)} collective-permute-done((bf16[64,256]{1,0:T(8,128)(2,1)S(1)}, bf16[64,256]{1,0:T(8,128)(2,1)S(1)}, u32[]{:S(2)}, u32[]{:S(2)}) %collective-permute-start.14) | collective-permute-done | bytes 32800 | tf_op jit(solution)/shard_map/ppermute | solution.py:27
  49.2 1.2 %collective-permute-done.17.other_ref = f32[64,256]{1,0:T(8,128)S(1)} collective-permute-done((f32[64,256]{1,0:T(8,128)S(1)}, f32[64,256]{1,0:T(8,128)S(1)}, u32[]{:S(2)}, u32[]{:S(2)}) %collective-permute-start.17) | collective-permute-done | bytes 65568 | tf_op jit(solution)/shard_map/ppermute | solution.py:27
  50.4 1.0 %shard_map.97 = bf16[64,2,4,512]{3,2,1,0:T(4,128)(2,1)} custom-call(f32[64,256]{1,0:T(8,128)S(1)} %shard_map.96.mine_ref, f32[64,256]{1,0:T(8,128)S(1)} %collective-permute-done.17.other_ref, f32[72,512]{1,0:T(8,128)S(1)} %get-tuple-element.51.feat_ref, f32[512,512]{1,0:T(8,128)S(1)} %shard_map.92.base_ref, f32[512,128]{1,0:T(8,128)S(1)} %shard_map.95.plane_ref), custom_call_target="tpu_custom_call" | custom-call | bytes 2113536 | tf_op jit(solution)/shard_map/pallas_call | solution.py:551
  (33 shorter events, 2.0 us)
Async XLA Ops:
  2.4 1.4 %collective-permute-start = (f32[72,256]{1,0:T(8,128)S(1)}, f32[72,256]{1,0:T(8,128)S(1)}, u32[]{:S(2)}, u32[]{:S(2)}) collective-permute-start(f32[72,256]{1,0:T(8,128)S(1)} %get-tuple-element.29), channel_id=1, source_target_pairs={{0,4},{4,0},{8,12},{12,8},{1,5},{5,1},{9,13},{13,9},{2,6},{6,2},{1... | collective-permute-start | bytes 221192 | tf_op jit(solution)/shard_map/ppermute | solution.py:27
  3.9 10.1 %copy-start = (f32[3,2,64,64]{3,2,1,0:T(8,128)S(1)}, f32[3,2,64,64]{3,2,1,0:T(8,128)}, u32[]{:S(2)}) copy-start(f32[3,2,64,64]{3,2,1,0:T(8,128)} %refs_7_.1) | copy-start | bytes 294916
  3.9 10.1 %copy-start.2 = (bf16[64,64]{1,0:T(8,128)(2,1)S(1)}, bf16[64,64]{1,0:T(8,128)(2,1)}, u32[]{:S(2)}) copy-start(bf16[64,64]{1,0:T(8,128)(2,1)} %wv_ref.1) | copy-start | bytes 24580
  3.9 10.1 %copy-start.3 = (bf16[64,64]{1,0:T(8,128)(2,1)S(1)}, bf16[64,64]{1,0:T(8,128)(2,1)}, u32[]{:S(2)}) copy-start(bf16[64,64]{1,0:T(8,128)(2,1)} %wo_ref.1) | copy-start | bytes 24580
  3.9 5.5 %collective-permute-start.1 = (f32[72,256]{1,0:T(8,128)S(1)}, f32[72,256]{1,0:T(8,128)S(1)}, u32[]{:S(2)}, u32[]{:S(2)}) collective-permute-start(f32[72,256]{1,0:T(8,128)S(1)} %shard_map.78.refs_0_), channel_id=1, source_target_pairs={{0,8},{4,12},{8,0},{12,4},{1,9},{5,13},{9,1},{13,5},{2,10},{6,14},... | collective-permute-start | bytes 221192 | tf_op jit(solution)/shard_map/ppermute | solution.py:27
  9.4 7.0 %collective-permute-start.2 = (f32[80,256]{1,0:T(8,128)S(1)}, f32[80,256]{1,0:T(8,128)S(1)}, u32[]{:S(2)}, u32[]{:S(2)}) collective-permute-start(f32[80,256]{1,0:T(8,128)S(1)} %shard_map.79.refs_0_), channel_id=1, source_target_pairs={{0,3},{1,2},{2,1},{3,0},{4,7},{5,6},{6,5},{7,4},{8,11},{9,10},{10,... | collective-permute-start | bytes 245768 | tf_op jit(solution)/shard_map/ppermute | solution.py:27
  13.3 6.3 %collective-permute-start.3 = (f32[80,256]{1,0:T(8,128)S(1)}, f32[80,256]{1,0:T(8,128)S(1)}, u32[]{:S(2)}, u32[]{:S(2)}) collective-permute-start(f32[80,256]{1,0:T(8,128)S(1)} %shard_map.79.refs_0_), channel_id=1, source_target_pairs={{0,2},{1,3},{2,0},{3,1},{4,6},{5,7},{6,4},{7,5},{8,10},{9,11},{10,... | collective-permute-start | bytes 245768 | tf_op jit(solution)/shard_map/ppermute | solution.py:27
  13.4 6.3 %collective-permute-start.4 = (f32[80,256]{1,0:T(8,128)S(1)}, f32[80,256]{1,0:T(8,128)S(1)}, u32[]{:S(2)}, u32[]{:S(2)}) collective-permute-start(f32[80,256]{1,0:T(8,128)S(1)} %shard_map.79.refs_0_), channel_id=1, source_target_pairs={{0,1},{1,0},{2,3},{3,2},{4,5},{5,4},{6,7},{7,6},{8,9},{9,8},{10,11... | collective-permute-start | bytes 245768 | tf_op jit(solution)/shard_map/ppermute | solution.py:27
  19.7 1.3 %collective-permute-start.5 = (f32[72,256]{1,0:T(8,128)S(1)}, f32[72,256]{1,0:T(8,128)S(1)}, u32[]{:S(2)}, u32[]{:S(2)}) collective-permute-start(f32[72,256]{1,0:T(8,128)S(1)} %shard_map.84.mine_ref), channel_id=1, source_target_pairs={{0,4},{4,0},{8,12},{12,8},{1,5},{5,1},{9,13},{13,9},{2,6},{6,2},{1... | collective-permute-start | bytes 221192 | tf_op jit(solution)/shard_map/ppermute | solution.py:27
  22.1 5.6 %collective-permute-start.6 = (bf16[16,512]{1,0:T(8,128)(2,1)S(1)}, bf16[16,512]{1,0:T(8,128)(2,1)S(1)}, u32[]{:S(2)}, u32[]{:S(2)}) collective-permute-start(bf16[16,512]{1,0:T(8,128)(2,1)S(1)} %get-tuple-element.38.refs_0_), channel_id=1, source_target_pairs={{0,3},{1,2},{2,1},{3,0},{4,7},{5,6},{6,5},{7,4},{8,11},{9,10},{10,... | collective-permute-start | bytes 49160 | tf_op jit(solution)/shard_map/ppermute | solution.py:27
  24.8 4.6 %collective-permute-start.7 = (bf16[16,512]{1,0:T(8,128)(2,1)S(1)}, bf16[16,512]{1,0:T(8,128)(2,1)S(1)}, u32[]{:S(2)}, u32[]{:S(2)}) collective-permute-start(bf16[16,512]{1,0:T(8,128)(2,1)S(1)} %get-tuple-element.38.refs_0_), channel_id=1, source_target_pairs={{0,2},{1,3},{2,0},{3,1},{4,6},{5,7},{6,4},{7,5},{8,10},{9,11},{10,... | collective-permute-start | bytes 49160 | tf_op jit(solution)/shard_map/ppermute | solution.py:27
  24.8 4.6 %collective-permute-start.8 = (bf16[16,512]{1,0:T(8,128)(2,1)S(1)}, bf16[16,512]{1,0:T(8,128)(2,1)S(1)}, u32[]{:S(2)}, u32[]{:S(2)}) collective-permute-start(bf16[16,512]{1,0:T(8,128)(2,1)S(1)} %get-tuple-element.38.refs_0_), channel_id=1, source_target_pairs={{0,1},{1,0},{2,3},{3,2},{4,5},{5,4},{6,7},{7,6},{8,9},{9,8},{10,11... | collective-permute-start | bytes 49160 | tf_op jit(solution)/shard_map/ppermute | solution.py:27
  29.4 2.0 %copy-start.1 = (bf16[2,128,128]{2,1,0:T(8,128)(2,1)S(1)}, bf16[2,128,128]{2,1,0:T(8,128)(2,1)}, u32[]{:S(2)}) copy-start(bf16[2,128,128]{2,1,0:T(8,128)(2,1)} %constant.2.clone.refs_2_.refs_6_) | copy-start | bytes 196612
  29.4 4.5 %collective-permute-start.11 = (bf16[64,512]{1,0:T(8,128)(2,1)S(1)}, bf16[64,512]{1,0:T(8,128)(2,1)S(1)}, u32[]{:S(2)}, u32[]{:S(2)}) collective-permute-start(bf16[64,512]{1,0:T(8,128)(2,1)S(1)} %shard_map.88.refs_0_), channel_id=1, source_target_pairs={{0,12},{4,8},{8,4},{12,0},{1,13},{5,9},{9,5},{13,1},{2,14},{6,10},... | collective-permute-start | bytes 196616 | tf_op jit(solution)/shard_map/ppermute | solution.py:27
  29.5 5.4 %collective-permute-start.10 = (bf16[64,512]{1,0:T(8,128)(2,1)S(1)}, bf16[64,512]{1,0:T(8,128)(2,1)S(1)}, u32[]{:S(2)}, u32[]{:S(2)}) collective-permute-start(bf16[64,512]{1,0:T(8,128)(2,1)S(1)} %shard_map.88.refs_0_), channel_id=1, source_target_pairs={{0,8},{4,12},{8,0},{12,4},{1,9},{5,13},{9,1},{13,5},{2,10},{6,14},... | collective-permute-start | bytes 196616 | tf_op jit(solution)/shard_map/ppermute | solution.py:27
  30.8 4.1 %collective-permute-start.9 = (bf16[64,512]{1,0:T(8,128)(2,1)S(1)}, bf16[64,512]{1,0:T(8,128)(2,1)S(1)}, u32[]{:S(2)}, u32[]{:S(2)}) collective-permute-start(bf16[64,512]{1,0:T(8,128)(2,1)S(1)} %shard_map.88.refs_0_), channel_id=1, source_target_pairs={{0,4},{4,0},{8,12},{12,8},{1,5},{5,1},{9,13},{13,9},{2,6},{6,2},{1... | collective-permute-start | bytes 196616 | tf_op jit(solution)/shard_map/ppermute | solution.py:27
  36.0 1.3 %collective-permute-start.12 = (bf16[64,256]{1,0:T(8,128)(2,1)S(1)}, bf16[64,256]{1,0:T(8,128)(2,1)S(1)}, u32[]{:S(2)}, u32[]{:S(2)}) collective-permute-start(bf16[64,256]{1,0:T(8,128)(2,1)S(1)} %get-tuple-element.43), channel_id=1, source_target_pairs={{0,4},{4,0},{8,12},{12,8},{1,5},{5,1},{9,13},{13,9},{2,6},{6,2},{1... | collective-permute-start | bytes 98312 | tf_op jit(solution)/shard_map/ppermute | solution.py:27
  37.3 4.0 %collective-permute-start.13 = (bf16[64,256]{1,0:T(8,128)(2,1)S(1)}, bf16[64,256]{1,0:T(8,128)(2,1)S(1)}, u32[]{:S(2)}, u32[]{:S(2)}) collective-permute-start(bf16[64,256]{1,0:T(8,128)(2,1)S(1)} %shard_map.91.refs_0_), channel_id=1, source_target_pairs={{0,8},{4,12},{8,0},{12,4},{1,9},{5,13},{9,1},{13,5},{2,10},{6,14},... | collective-permute-start | bytes 98312 | tf_op jit(solution)/shard_map/ppermute | solution.py:27
  41.3 4.5 %collective-permute-start.16 = (bf16[64,256]{1,0:T(8,128)(2,1)S(1)}, bf16[64,256]{1,0:T(8,128)(2,1)S(1)}, u32[]{:S(2)}, u32[]{:S(2)}) collective-permute-start(bf16[64,256]{1,0:T(8,128)(2,1)S(1)} %shard_map.93.refs_0_), channel_id=1, source_target_pairs={{0,1},{1,0},{2,3},{3,2},{4,5},{5,4},{6,7},{7,6},{8,9},{9,8},{10,11... | collective-permute-start | bytes 98312 | tf_op jit(solution)/shard_map/ppermute | solution.py:27
  42.4 4.8 %collective-permute-start.15 = (bf16[64,256]{1,0:T(8,128)(2,1)S(1)}, bf16[64,256]{1,0:T(8,128)(2,1)S(1)}, u32[]{:S(2)}, u32[]{:S(2)}) collective-permute-start(bf16[64,256]{1,0:T(8,128)(2,1)S(1)} %shard_map.93.refs_0_), channel_id=1, source_target_pairs={{0,2},{1,3},{2,0},{3,1},{4,6},{5,7},{6,4},{7,5},{8,10},{9,11},{10,... | collective-permute-start | bytes 98312 | tf_op jit(solution)/shard_map/ppermute | solution.py:27
  43.4 5.7 %collective-permute-start.14 = (bf16[64,256]{1,0:T(8,128)(2,1)S(1)}, bf16[64,256]{1,0:T(8,128)(2,1)S(1)}, u32[]{:S(2)}, u32[]{:S(2)}) collective-permute-start(bf16[64,256]{1,0:T(8,128)(2,1)S(1)} %shard_map.93.refs_0_), channel_id=1, source_target_pairs={{0,3},{1,2},{2,1},{3,0},{4,7},{5,6},{6,5},{7,4},{8,11},{9,10},{10,... | collective-permute-start | bytes 98312 | tf_op jit(solution)/shard_map/ppermute | solution.py:27
  49.1 1.3 %collective-permute-start.17 = (f32[64,256]{1,0:T(8,128)S(1)}, f32[64,256]{1,0:T(8,128)S(1)}, u32[]{:S(2)}, u32[]{:S(2)}) collective-permute-start(f32[64,256]{1,0:T(8,128)S(1)} %shard_map.96.mine_ref), channel_id=1, source_target_pairs={{0,4},{4,0},{8,12},{12,8},{1,5},{5,1},{9,13},{13,9},{2,6},{6,2},{1... | collective-permute-start | bytes 196616 | tf_op jit(solution)/shard_map/ppermute | solution.py:27

commit v13 on v12

--- a/solution.py
+++ b/solution.py
@@ -288,10 +288,14 @@
         start += more
 
 
-def add_core_kernel(mine_ref, other_ref, out_ref):
+def add_beside_kernel(known, mine_ref, other_ref, out_ref):
     out_ref[0:WIDTH, :] = mine_ref[0:WIDTH, :] + other_ref[0:WIDTH, :]
-    out_ref[WIDTH:, 0:LANES] = mine_ref[WIDTH:, 0:LANES]
-    out_ref[WIDTH:, LANES : 2 * LANES] = other_ref[WIDTH:, 0:LANES]
+    lanes = known * WIDTH
+    rest = out_ref.shape[1] - 2 * lanes
+    rows = [mine_ref[WIDTH:, 0:lanes], other_ref[WIDTH:, 0:lanes]]
+    if rest > 0:
+        rows.append(jnp.zeros((rows[0].shape[0], rest), jnp.float32))
+    out_ref[WIDTH:, :] = jnp.concatenate(rows, axis=1)
 
 
 def stack_kernel(*refs):
@@ -325,14 +329,12 @@
 
 def plane_kernel(cells, span_x, lengths, *refs):
     parts, (same_ref, qk_ref, mix_ref, feat_ref, full_ref) = refs[:-5], refs[-5:]
-    chips = span_x // 2
     totals = jnp.concatenate(
         [
-            part[WIDTH + step * cells : WIDTH + (step + 1) * cells, core * LANES : core * LANES + WIDTH]
-            for chip in range(chips)
-            for core in range(2)
+            part[start : start + cells, step * WIDTH : (step + 1) * WIDTH]
+            for step in range(span_x)
             for part in parts
-            for step in range(chip, (part.shape[0] - WIDTH) // cells, chips)
+            for start in range(WIDTH, part.shape[0], cells)
         ],
         axis=0,
     )
@@ -398,8 +400,7 @@
 
 def mix_kernel(factor, spans, *refs):
     lows, refs = refs[:spans], refs[spans:]
-    mix_ref, wv_ref, wo_ref, wq_ref, wk_ref, field_ref, cot_ref, top_ref = refs[:8]
-    mine_ref, other_ref, half_ref = refs[8:]
+    mix_ref, wv_ref, wo_ref, wq_ref, wk_ref, field_ref, cot_ref, top_ref, out_ref = refs
     cells = field_ref.shape[0] // WIDTH
     low_f, low_c = join_low(lows, cells)
     wide = low_f.shape[1]
@@ -422,12 +423,7 @@
         return mul_left(found[:WIDTH] + found[WIDTH:], right)
 
     found = pull(wq_ref[...], left_f, cot_ref[...]) + pull(wk_ref[...], left_c, field_ref[...])
-    half = found.shape[1] // 2
-    half_ref[0] = found[:, :half]
-    half_ref[1] = found[:, half:]
-    core = lax.axis_index("gx") & 1
-    mine_ref[...] = half_ref[core].astype(jnp.bfloat16)
-    other_ref[...] = half_ref[core ^ 1].astype(jnp.bfloat16)
+    out_ref[...] = found.astype(jnp.bfloat16)
 
 
 def put_cells(ref, total):
@@ -489,11 +485,14 @@
     out_ref[...] = mul(left, keyset) + cot_ref[...].astype(jnp.float32)
 
 
-def final_kernel(places, mine_ref, other_ref, feat_ref, base_ref, plane_ref, out_ref, data_ref,
-                 half_ref, semaphores):
+def final_kernel(places, *refs):
+    parts, refs = refs[:-6], refs[-6:]
+    feat_ref, base_ref, plane_ref, out_ref, data_ref, semaphores = refs
     depth = base_ref.shape[1]
     _, rows_x, rows_y, _ = data_ref.shape
-    found = join_halves(half_ref, mine_ref, other_ref)
+    found = parts[0][...].astype(jnp.float32)
+    for part in parts[1:]:
+        found = found + part[...].astype(jnp.float32)
     normed = feat_ref[0:WIDTH, :]
     inverse = feat_ref[WIDTH : WIDTH + 1, :]
     found = inverse * (found - normed * jnp.mean(found * normed, axis=0, keepdims=True))
@@ -629,13 +628,14 @@
         (w_value, w_out, qk_weight),
         flops=cube // 8,
     )
-    total = run(
-        add_core_kernel,
-        [like((WIDTH + cells, half), f32)],
-        (sums[0], swap(sums[1], "gx", span_x, 1)),
-    )
-    for level in range(1, span_x.bit_length() - 1):
-        (total,) = taken(add_kernel, (total, swap(total, "gx", span_x, 1 << level)), last=True)
+    total, other = sums
+    for level in range(span_x.bit_length() - 1):
+        step = 1 << level
+        total = run(
+            functools.partial(add_beside_kernel, step),
+            [like((WIDTH + cells, half), f32)],
+            (total, swap(total if level else other, "gx", span_x, step)),
+        )
     totals = taken(add_kernel, swaps(total, "gy", span_y))
     totals, cots, wz = lax.optimization_barrier((totals, cots, wz))
     mine = run(
@@ -661,15 +661,14 @@
     (low,) = taken(stack_kernel, swaps(send, "gy", span_y), last=True)
     first, *others = swaps(low, "gx", span_x, False)
     lows = (first,) + tuple(reversed(others))
-    pulled = like((WIDTH, half), bf16)
-    top, mine, other = run(
+    pulled = like((WIDTH, depth), bf16)
+    top, total = run(
         functools.partial(mix_kernel, factor_z, span_x),
-        [like((2, cells, wide), f32), pulled, pulled],
+        [like((2, cells, wide), f32), pulled],
         lows + (mix, wv, wo, wq, wk, cols, cots),
         flops=cube,
-        scratch=[halves],
-    )
-    total = run(add_pull_kernel, [pulled], (mine, swap(other, "gx", span_x, 1)))
+    )
+    total = run(add_pull_kernel, [pulled], (total, swap(total, "gx", span_x, 1)))
     base = run(base_kernel, [like((rows, depth), f32)], (top, wv, both, cots), flops=cube)
     total, base = lax.optimization_barrier((total, base))
     for level in range(1, span_x.bit_length() - 1):
@@ -684,15 +683,12 @@
         flops=2 * cube,
     )
     total, layer_output, plane = lax.optimization_barrier((total, layer_output, plane))
-    total = run(
-        add_pull_kernel, [like(pulled.shape, f32)], swaps(total, "gy", span_y, False)
-    )
     field_grad = run(
         functools.partial(final_kernel, grid_x * grid_y),
         [like(field.shape, bf16)],
-        (total, swap(total, "gx", span_x, 1), feat_z, base, plane),
+        swaps(total, "gy", span_y, False) + (feat_z, base, plane),
         target=pltpu.HBM,
-        scratch=[chunked[0], halves, chunked[1]],
+        scratch=chunked,
     )
     return (layer_output, field_grad)
 

time: 51.6 us -> 50.7 us (0.983)
  waiting for transfers between devices: 19.4 us -> 18.6 us
    ppermute x18 -> x17, waiting for transfers between devices: 19.4 us -> 18.6 us  [swap(): return lax.ppermute(part, axis, [(i, i ^ step) for i in range(size)])]
    ppermute x18 -> x17, starting transfers between devices: 20 us -> 19.9 us  [swap(): return lax.ppermute(part, axis, [(i, i ^ step) for i in range(size)])]
    pallas_call x21 -> x20, Pallas kernels: 11.1 us -> 11.2 us  [run(): pl.pallas_call(kernel, out_shape=tuple(outs), in_specs=[pl.BlockSpec(memo...]
  transfers between devices with their start and end apart: 18 -> 17, of which waited for: 14 -> 13; matrix products, arithmetic and copies ran while one was open for 0% -> 0% of each run, Pallas kernels for 12% -> 12%
where the time goes in v13:
time: 50.7 us; the launch traced here: 50.5 us
  starting transfers between devices  19.9 us (39%)
  waiting for transfers between devices  18.6 us (37%)
  Pallas kernels  11.2 us (22%)
  between operations  0.76 us (1%)
    ppermute x17, starting transfers between devices, swap(): return lax.ppermute(part, axis, [(i, i ^ step) for i in range(size)])  19.9 us
    ppermute x17, waiting for transfers between devices, swap(): return lax.ppermute(part, axis, [(i, i ^ step) for i in range(size)])  18.6 us
    pallas_call x20, Pallas kernels, run(): pl.pallas_call(kernel, out_shape=tuple(outs), in_specs=[pl.BlockSpec(memo...  11.2 us
  transfers between devices with their start and end apart: 17, of which 13 were waited for; matrix products, arithmetic and copies ran while one was open for 0% of the time, Pallas kernels for 12%

profile of v13, /device:TPU:0, one launch (start us, length us, event | category | flops | bytes accessed | tf_op | source)
XLA Modules:
  0.0 50.5 jit_solution(17525544954039455800)
XLA Ops:
  0.6 1.8 %shard_map.77 = (f32[72,256]{1,0:T(8,128)S(1)}, f32[72,256]{1,0:T(8,128)S(1)}, bf16[512,512]{1,0:T(8,128)(2,1)S(1)}) custom-call(bf16[64,2,4,512]{3,2,1,0:T(4,128)(2,1)} %field_ref.1), custom_call_target="tpu_custom_call" | custom-call | flops 67108864 | bytes 1196032 | tf_op jit(solution)/shard_map/pallas_call | solution.py:550
  2.4 0.5 %collective-permute-start = (f32[72,256]{1,0:T(8,128)S(1)}, f32[72,256]{1,0:T(8,128)S(1)}, u32[]{:S(2)}, u32[]{:S(2)}) collective-permute-start(f32[72,256]{1,0:T(8,128)S(1)} %get-tuple-element.28), channel_id=1, source_target_pairs={{0,4},{4,0},{8,12},{12,8},{1,5},{5,1},{9,13},{13,9},{2,6},{6,2},{1... | collective-permute-start | bytes 221192 | tf_op jit(solution)/shard_map/ppermute | solution.py:27
  2.9 0.9 %collective-permute-done.other_ref = f32[72,256]{1,0:T(8,128)S(1)} collective-permute-done((f32[72,256]{1,0:T(8,128)S(1)}, f32[72,256]{1,0:T(8,128)S(1)}, u32[]{:S(2)}, u32[]{:S(2)}) %collective-permute-start) | collective-permute-done | bytes 73760 | tf_op jit(solution)/shard_map/ppermute | solution.py:27
  3.9 2.9 %collective-permute-start.1 = (f32[72,256]{1,0:T(8,128)S(1)}, f32[72,256]{1,0:T(8,128)S(1)}, u32[]{:S(2)}, u32[]{:S(2)}) collective-permute-start(f32[72,256]{1,0:T(8,128)S(1)} %shard_map.78.mine_ref), channel_id=1, source_target_pairs={{0,8},{4,12},{8,0},{12,4},{1,9},{5,13},{9,1},{13,5},{2,10},{6,14},... | collective-permute-start | bytes 221192 | tf_op jit(solution)/shard_map/ppermute | solution.py:27
  6.8 2.6 %collective-permute-done.1.other_ref = f32[72,256]{1,0:T(8,128)S(1)} collective-permute-done((f32[72,256]{1,0:T(8,128)S(1)}, f32[72,256]{1,0:T(8,128)S(1)}, u32[]{:S(2)}, u32[]{:S(2)}) %collective-permute-start.1) | collective-permute-done | bytes 73760 | tf_op jit(solution)/shard_map/ppermute | solution.py:27
  9.4 3.9 %collective-permute-start.2 = (f32[72,256]{1,0:T(8,128)S(1)}, f32[72,256]{1,0:T(8,128)S(1)}, u32[]{:S(2)}, u32[]{:S(2)}) collective-permute-start(f32[72,256]{1,0:T(8,128)S(1)} %shard_map.79.refs_0_), channel_id=1, source_target_pairs={{0,3},{1,2},{2,1},{3,0},{4,7},{5,6},{6,5},{7,4},{8,11},{9,10},{10,... | collective-permute-start | bytes 221192 | tf_op jit(solution)/shard_map/ppermute | solution.py:27
  13.4 0.6 %collective-permute-start.4 = (f32[72,256]{1,0:T(8,128)S(1)}, f32[72,256]{1,0:T(8,128)S(1)}, u32[]{:S(2)}, u32[]{:S(2)}) collective-permute-start(f32[72,256]{1,0:T(8,128)S(1)} %shard_map.79.refs_0_), channel_id=1, source_target_pairs={{0,1},{1,0},{2,3},{3,2},{4,5},{5,4},{6,7},{7,6},{8,9},{9,8},{10,11... | collective-permute-start | bytes 221192 | tf_op jit(solution)/shard_map/ppermute | solution.py:27
  14.3 1.2 %shard_map.82.cot_ref.refs_10_ = bf16[512,512]{1,0:T(8,128)(2,1)S(1)} custom-call(bf16[64,2,4,512]{3,2,1,0:T(4,128)(2,1)} %cot_ref.1), custom_call_target="tpu_custom_call" | custom-call | flops 268435456 | bytes 1048576 | tf_op jit(solution)/shard_map/pallas_call | solution.py:550
  15.4 0.8 %collective-permute-done.2.refs_1_ = f32[72,256]{1,0:T(8,128)S(1)} collective-permute-done((f32[72,256]{1,0:T(8,128)S(1)}, f32[72,256]{1,0:T(8,128)S(1)}, u32[]{:S(2)}, u32[]{:S(2)}) %collective-permute-start.2) | collective-permute-done | bytes 73760 | tf_op jit(solution)/shard_map/ppermute | solution.py:27
  16.3 2.8 %collective-permute-done.3.refs_1_ = f32[72,256]{1,0:T(8,128)S(1)} collective-permute-done((f32[72,256]{1,0:T(8,128)S(1)}, f32[72,256]{1,0:T(8,128)S(1)}, u32[]{:S(2)}, u32[]{:S(2)}) %collective-permute-start.3) | collective-permute-done | bytes 73760 | tf_op jit(solution)/shard_map/ppermute | solution.py:27
  19.2 1.3 %collective-permute-done.5.other_ref = f32[72,256]{1,0:T(8,128)S(1)} collective-permute-done((f32[72,256]{1,0:T(8,128)S(1)}, f32[72,256]{1,0:T(8,128)S(1)}, u32[]{:S(2)}, u32[]{:S(2)}) %collective-permute-start.5) | collective-permute-done | bytes 73760 | tf_op jit(solution)/shard_map/ppermute | solution.py:27
  20.5 1.0 %shard_map.85 = (bf16[16,512]{1,0:T(8,128)(2,1)S(1)}, bf16[128,512]{1,0:T(8,128)(2,1)S(1)}, f32[72,512]{1,0:T(8,128)S(1)}) custom-call(f32[72,256]{1,0:T(8,128)S(1)} %shard_map.84.mine_ref, f32[72,256]{1,0:T(8,128)S(1)} %collective-permute-done.5.other_ref, f32[128,64]{1,0:T(8,128)S(1)} %get-tuple-element.32.wz_ref, ...), custom_call_target="tpu_custom_call" | custom-call | flops 536870912 | bytes 1785856 | tf_op jit(solution)/shard_map/pallas_call | solution.py:550
  21.5 2.7 %collective-permute-start.6 = (bf16[16,512]{1,0:T(8,128)(2,1)S(1)}, bf16[16,512]{1,0:T(8,128)(2,1)S(1)}, u32[]{:S(2)}, u32[]{:S(2)}) collective-permute-start(bf16[16,512]{1,0:T(8,128)(2,1)S(1)} %get-tuple-element.37.refs_0_), channel_id=1, source_target_pairs={{0,3},{1,2},{2,1},{3,0},{4,7},{5,6},{6,5},{7,4},{8,11},{9,10},{10,... | collective-permute-start | bytes 49160 | tf_op jit(solution)/shard_map/ppermute | solution.py:27
  24.2 1.8 %collective-permute-start.8 = (bf16[16,512]{1,0:T(8,128)(2,1)S(1)}, bf16[16,512]{1,0:T(8,128)(2,1)S(1)}, u32[]{:S(2)}, u32[]{:S(2)}) collective-permute-start(bf16[16,512]{1,0:T(8,128)(2,1)S(1)} %get-tuple-element.37.refs_0_), channel_id=1, source_target_pairs={{0,1},{1,0},{2,3},{3,2},{4,5},{5,4},{6,7},{7,6},{8,9},{9,8},{10,11... | collective-permute-start | bytes 49160 | tf_op jit(solution)/shard_map/ppermute | solution.py:27
  25.9 1.1 %collective-permute-done.6.refs_1_ = bf16[16,512]{1,0:T(8,128)(2,1)S(1)} collective-permute-done((bf16[16,512]{1,0:T(8,128)(2,1)S(1)}, bf16[16,512]{1,0:T(8,128)(2,1)S(1)}, u32[]{:S(2)}, u32[]{:S(2)}) %collective-permute-start.6) | collective-permute-done | bytes 16416 | tf_op jit(solution)/shard_map/ppermute | solution.py:27
  27.1 1.7 %collective-permute-done.7.refs_1_ = bf16[16,512]{1,0:T(8,128)(2,1)S(1)} collective-permute-done((bf16[16,512]{1,0:T(8,128)(2,1)S(1)}, bf16[16,512]{1,0:T(8,128)(2,1)S(1)}, u32[]{:S(2)}, u32[]{:S(2)}) %collective-permute-start.7) | collective-permute-done | bytes 16416 | tf_op jit(solution)/shard_map/ppermute | solution.py:27
  28.9 1.4 %collective-permute-start.10 = (bf16[64,512]{1,0:T(8,128)(2,1)S(1)}, bf16[64,512]{1,0:T(8,128)(2,1)S(1)}, u32[]{:S(2)}, u32[]{:S(2)}) collective-permute-start(bf16[64,512]{1,0:T(8,128)(2,1)S(1)} %shard_map.88.refs_0_), channel_id=1, source_target_pairs={{0,8},{4,12},{8,0},{12,4},{1,9},{5,13},{9,1},{13,5},{2,10},{6,14},... | collective-permute-start | bytes 196616 | tf_op jit(solution)/shard_map/ppermute | solution.py:27
  30.3 0.5 collective-permute-start.9
  30.8 1.5 %shard_map.89 = (f32[2,64,128]{2,1,0:T(8,128)S(1)}, f32[8,128,64]{2,1,0:T(8,128)S(1)}, f32[2,1024,128]{2,1,0:T(8,128)S(1)}) custom-call(f32[88,256]{1,0:T(8,128)S(1)} %shard_map.81.refs_0_, f32[72,256]{1,0:T(8,128)S(1)} %collective-permute-done.4.refs_1_, bf16[2,128,128]{2,1,0:T(8,128)(2,1)S(1)} %copy-done.1, f32[3,2,64,64]{3,2,1,0:T(8,128)S(1)} %copy-done), custom_call_target="tpu_custom_call" | custom-call | flops 134217728 | bytes 1703936 | tf_op jit(solution)/shard_map/pallas_call | solution.py:550
  32.3 1.0 %collective-permute-done.11.refs_3_ = bf16[64,512]{1,0:T(8,128)(2,1)S(1)} collective-permute-done((bf16[64,512]{1,0:T(8,128)(2,1)S(1)}, bf16[64,512]{1,0:T(8,128)(2,1)S(1)}, u32[]{:S(2)}, u32[]{:S(2)}) %collective-permute-start.11) | collective-permute-done | bytes 65568 | tf_op jit(solution)/shard_map/ppermute | solution.py:27
  33.3 1.1 %collective-permute-done.10.refs_2_ = bf16[64,512]{1,0:T(8,128)(2,1)S(1)} collective-permute-done((bf16[64,512]{1,0:T(8,128)(2,1)S(1)}, bf16[64,512]{1,0:T(8,128)(2,1)S(1)}, u32[]{:S(2)}, u32[]{:S(2)}) %collective-permute-start.10) | collective-permute-done | bytes 65568 | tf_op jit(solution)/shard_map/ppermute | solution.py:27
  34.4 1.0 %shard_map.90 = (f32[2,8,512]{2,1,0:T(8,128)S(1)}, bf16[64,512]{1,0:T(8,128)(2,1)S(1)}) custom-call(bf16[64,512]{1,0:T(8,128)(2,1)S(1)} %shard_map.88.refs_0_, bf16[64,512]{1,0:T(8,128)(2,1)S(1)} %collective-permute-done.9.refs_1_, bf16[64,512]{1,0:T(8,128)(2,1)S(1)} %collective-permute-done.10.refs_2_, bf16[64,512]{1,0:T(8,128)(2,1)S(1)} %collective-permute-done.11.refs_3_, ...), custom_call_target="tpu_custom_call" | custom-call | flops 268435456 | bytes 1998848 | tf_op jit(solution)/shard_map/pallas_call | solution.py:550
  36.1 0.7 %collective-permute-done.12.refs_1_ = bf16[64,512]{1,0:T(8,128)(2,1)S(1)} collective-permute-done((bf16[64,512]{1,0:T(8,128)(2,1)S(1)}, bf16[64,512]{1,0:T(8,128)(2,1)S(1)}, u32[]{:S(2)}, u32[]{:S(2)}) %collective-permute-start.12) | collective-permute-done | bytes 65568 | tf_op jit(solution)/shard_map/ppermute | solution.py:27
  36.8 0.9 %collective-permute-start.13 = (bf16[64,512]{1,0:T(8,128)(2,1)S(1)}, bf16[64,512]{1,0:T(8,128)(2,1)S(1)}, u32[]{:S(2)}, u32[]{:S(2)}) collective-permute-start(bf16[64,512]{1,0:T(8,128)(2,1)S(1)} %shard_map.91.refs_0_), channel_id=1, source_target_pairs={{0,8},{4,12},{8,0},{12,4},{1,9},{5,13},{9,1},{13,5},{2,10},{6,14},... | collective-permute-start | bytes 196616 | tf_op jit(solution)/shard_map/ppermute | solution.py:27
  37.6 1.2 %shard_map.94 = bf16[64,2,4,512]{3,2,1,0:T(4,128)(2,1)} custom-call(f32[2,8,512]{2,1,0:T(8,128)S(1)} %get-tuple-element.42.top_ref, f32[64,512]{1,0:T(8,128)S(1)} %get-tuple-element.36.wo_ref.refs_6_, bf16[128,512]{1,0:T(8,128)(2,1)S(1)} %get-tuple-element.43.both_ref, bf16[512,512]{1,0:T(8,128)(2,1)S(1)} %get-tuple-element.33.field_ref.refs_9_), custom_call_target="tpu_custom_call" | custom-call | flops 268435456 | bytes 1343488 | tf_op jit(solution)/shard_map/pallas_call | solution.py:550
  38.9 1.6 %shard_map.95.refs_6_ = f32[512,128]{1,0:T(8,128)S(1)} custom-call(bf16[64,512]{1,0:T(8,128)(2,1)S(1)} %shard_map.88.refs_0_, bf16[64,512]{1,0:T(8,128)(2,1)S(1)} %collective-permute-done.9.refs_1_, bf16[64,512]{1,0:T(8,128)(2,1)S(1)} %collective-permute-done.10.refs_2_, bf16[64,512]{1,0:T(8,128)(2,1)S(1)} %collective-permute-done.11.refs_3_, ...), custom_call_target="tpu_custom_call" | custom-call | flops 536870912 | bytes 1998848 | tf_op jit(solution)/shard_map/pallas_call | solution.py:550
  40.5 0.6 %collective-permute-done.13.refs_1_ = bf16[64,512]{1,0:T(8,128)(2,1)S(1)} collective-permute-done((bf16[64,512]{1,0:T(8,128)(2,1)S(1)}, bf16[64,512]{1,0:T(8,128)(2,1)S(1)}, u32[]{:S(2)}, u32[]{:S(2)}) %collective-permute-start.13) | collective-permute-done | bytes 65568 | tf_op jit(solution)/shard_map/ppermute | solution.py:27
  41.1 1.2 %collective-permute-start.16 = (bf16[64,512]{1,0:T(8,128)(2,1)S(1)}, bf16[64,512]{1,0:T(8,128)(2,1)S(1)}, u32[]{:S(2)}, u32[]{:S(2)}) collective-permute-start(bf16[64,512]{1,0:T(8,128)(2,1)S(1)} %shard_map.93.refs_0_), channel_id=1, source_target_pairs={{0,1},{1,0},{2,3},{3,2},{4,5},{5,4},{6,7},{7,6},{8,9},{9,8},{10,11... | collective-permute-start | bytes 196616 | tf_op jit(solution)/shard_map/ppermute | solution.py:27
  42.3 1.1 %collective-permute-start.15 = (bf16[64,512]{1,0:T(8,128)(2,1)S(1)}, bf16[64,512]{1,0:T(8,128)(2,1)S(1)}, u32[]{:S(2)}, u32[]{:S(2)}) collective-permute-start(bf16[64,512]{1,0:T(8,128)(2,1)S(1)} %shard_map.93.refs_0_), channel_id=1, source_target_pairs={{0,2},{1,3},{2,0},{3,1},{4,6},{5,7},{6,4},{7,5},{8,10},{9,11},{10,... | collective-permute-start | bytes 196616 | tf_op jit(solution)/shard_map/ppermute | solution.py:27
  43.3 2.2 %collective-permute-start.14 = (bf16[64,512]{1,0:T(8,128)(2,1)S(1)}, bf16[64,512]{1,0:T(8,128)(2,1)S(1)}, u32[]{:S(2)}, u32[]{:S(2)}) collective-permute-start(bf16[64,512]{1,0:T(8,128)(2,1)S(1)} %shard_map.93.refs_0_), channel_id=1, source_target_pairs={{0,3},{1,2},{2,1},{3,0},{4,7},{5,6},{6,5},{7,4},{8,11},{9,10},{10,... | collective-permute-start | bytes 196616 | tf_op jit(solution)/shard_map/ppermute | solution.py:27
  46.0 3.6 %collective-permute-done.15.refs_2_ = bf16[64,512]{1,0:T(8,128)(2,1)S(1)} collective-permute-done((bf16[64,512]{1,0:T(8,128)(2,1)S(1)}, bf16[64,512]{1,0:T(8,128)(2,1)S(1)}, u32[]{:S(2)}, u32[]{:S(2)}) %collective-permute-start.15) | collective-permute-done | bytes 65568 | tf_op jit(solution)/shard_map/ppermute | solution.py:27
  49.6 0.9 %shard_map.96 = bf16[64,2,4,512]{3,2,1,0:T(4,128)(2,1)} custom-call(bf16[64,512]{1,0:T(8,128)(2,1)S(1)} %shard_map.93.refs_0_, bf16[64,512]{1,0:T(8,128)(2,1)S(1)} %collective-permute-done.14.refs_1_, bf16[64,512]{1,0:T(8,128)(2,1)S(1)} %collective-permute-done.15.refs_2_, bf16[64,512]{1,0:T(8,128)(2,1)S(1)} %collective-permute-done.16.refs_3_, ...), custom_call_target="tpu_custom_call" | custom-call | bytes 2244608 | tf_op jit(solution)/shard_map/pallas_call | solution.py:550
  (30 shorter events, 1.6 us)
Async XLA Ops:
  2.4 1.4 %collective-permute-start = (f32[72,256]{1,0:T(8,128)S(1)}, f32[72,256]{1,0:T(8,128)S(1)}, u32[]{:S(2)}, u32[]{:S(2)}) collective-permute-start(f32[72,256]{1,0:T(8,128)S(1)} %get-tuple-element.28), channel_id=1, source_target_pairs={{0,4},{4,0},{8,12},{12,8},{1,5},{5,1},{9,13},{13,9},{2,6},{6,2},{1... | collective-permute-start | bytes 221192 | tf_op jit(solution)/shard_map/ppermute | solution.py:27
  3.9 10.1 %copy-start = (f32[3,2,64,64]{3,2,1,0:T(8,128)S(1)}, f32[3,2,64,64]{3,2,1,0:T(8,128)}, u32[]{:S(2)}) copy-start(f32[3,2,64,64]{3,2,1,0:T(8,128)} %refs_7_.1) | copy-start | bytes 294916
  3.9 10.1 %copy-start.2 = (bf16[64,64]{1,0:T(8,128)(2,1)S(1)}, bf16[64,64]{1,0:T(8,128)(2,1)}, u32[]{:S(2)}) copy-start(bf16[64,64]{1,0:T(8,128)(2,1)} %wv_ref.1) | copy-start | bytes 24580
  3.9 10.1 %copy-start.3 = (bf16[64,64]{1,0:T(8,128)(2,1)S(1)}, bf16[64,64]{1,0:T(8,128)(2,1)}, u32[]{:S(2)}) copy-start(bf16[64,64]{1,0:T(8,128)(2,1)} %wo_ref.1) | copy-start | bytes 24580
  3.9 5.5 %collective-permute-start.1 = (f32[72,256]{1,0:T(8,128)S(1)}, f32[72,256]{1,0:T(8,128)S(1)}, u32[]{:S(2)}, u32[]{:S(2)}) collective-permute-start(f32[72,256]{1,0:T(8,128)S(1)} %shard_map.78.mine_ref), channel_id=1, source_target_pairs={{0,8},{4,12},{8,0},{12,4},{1,9},{5,13},{9,1},{13,5},{2,10},{6,14},... | collective-permute-start | bytes 221192 | tf_op jit(solution)/shard_map/ppermute | solution.py:27
  9.4 6.8 %collective-permute-start.2 = (f32[72,256]{1,0:T(8,128)S(1)}, f32[72,256]{1,0:T(8,128)S(1)}, u32[]{:S(2)}, u32[]{:S(2)}) collective-permute-start(f32[72,256]{1,0:T(8,128)S(1)} %shard_map.79.refs_0_), channel_id=1, source_target_pairs={{0,3},{1,2},{2,1},{3,0},{4,7},{5,6},{6,5},{7,4},{8,11},{9,10},{10,... | collective-permute-start | bytes 221192 | tf_op jit(solution)/shard_map/ppermute | solution.py:27
  13.4 5.7 %collective-permute-start.3 = (f32[72,256]{1,0:T(8,128)S(1)}, f32[72,256]{1,0:T(8,128)S(1)}, u32[]{:S(2)}, u32[]{:S(2)}) collective-permute-start(f32[72,256]{1,0:T(8,128)S(1)} %shard_map.79.refs_0_), channel_id=1, source_target_pairs={{0,2},{1,3},{2,0},{3,1},{4,6},{5,7},{6,4},{7,5},{8,10},{9,11},{10,... | collective-permute-start | bytes 221192 | tf_op jit(solution)/shard_map/ppermute | solution.py:27
  13.4 5.7 %collective-permute-start.4 = (f32[72,256]{1,0:T(8,128)S(1)}, f32[72,256]{1,0:T(8,128)S(1)}, u32[]{:S(2)}, u32[]{:S(2)}) collective-permute-start(f32[72,256]{1,0:T(8,128)S(1)} %shard_map.79.refs_0_), channel_id=1, source_target_pairs={{0,1},{1,0},{2,3},{3,2},{4,5},{5,4},{6,7},{7,6},{8,9},{9,8},{10,11... | collective-permute-start | bytes 221192 | tf_op jit(solution)/shard_map/ppermute | solution.py:27
  19.1 1.3 %collective-permute-start.5 = (f32[72,256]{1,0:T(8,128)S(1)}, f32[72,256]{1,0:T(8,128)S(1)}, u32[]{:S(2)}, u32[]{:S(2)}) collective-permute-start(f32[72,256]{1,0:T(8,128)S(1)} %shard_map.84.mine_ref), channel_id=1, source_target_pairs={{0,4},{4,0},{8,12},{12,8},{1,5},{5,1},{9,13},{13,9},{2,6},{6,2},{1... | collective-permute-start | bytes 221192 | tf_op jit(solution)/shard_map/ppermute | solution.py:27
  21.5 5.6 %collective-permute-start.6 = (bf16[16,512]{1,0:T(8,128)(2,1)S(1)}, bf16[16,512]{1,0:T(8,128)(2,1)S(1)}, u32[]{:S(2)}, u32[]{:S(2)}) collective-permute-start(bf16[16,512]{1,0:T(8,128)(2,1)S(1)} %get-tuple-element.37.refs_0_), channel_id=1, source_target_pairs={{0,3},{1,2},{2,1},{3,0},{4,7},{5,6},{6,5},{7,4},{8,11},{9,10},{10,... | collective-permute-start | bytes 49160 | tf_op jit(solution)/shard_map/ppermute | solution.py:27
  24.2 4.6 %collective-permute-start.7 = (bf16[16,512]{1,0:T(8,128)(2,1)S(1)}, bf16[16,512]{1,0:T(8,128)(2,1)S(1)}, u32[]{:S(2)}, u32[]{:S(2)}) collective-permute-start(bf16[16,512]{1,0:T(8,128)(2,1)S(1)} %get-tuple-element.37.refs_0_), channel_id=1, source_target_pairs={{0,2},{1,3},{2,0},{3,1},{4,6},{5,7},{6,4},{7,5},{8,10},{9,11},{10,... | collective-permute-start | bytes 49160 | tf_op jit(solution)/shard_map/ppermute | solution.py:27
  24.2 4.6 %collective-permute-start.8 = (bf16[16,512]{1,0:T(8,128)(2,1)S(1)}, bf16[16,512]{1,0:T(8,128)(2,1)S(1)}, u32[]{:S(2)}, u32[]{:S(2)}) collective-permute-start(bf16[16,512]{1,0:T(8,128)(2,1)S(1)} %get-tuple-element.37.refs_0_), channel_id=1, source_target_pairs={{0,1},{1,0},{2,3},{3,2},{4,5},{5,4},{6,7},{7,6},{8,9},{9,8},{10,11... | collective-permute-start | bytes 49160 | tf_op jit(solution)/shard_map/ppermute | solution.py:27
  28.8 2.0 %copy-start.1 = (bf16[2,128,128]{2,1,0:T(8,128)(2,1)S(1)}, bf16[2,128,128]{2,1,0:T(8,128)(2,1)}, u32[]{:S(2)}) copy-start(bf16[2,128,128]{2,1,0:T(8,128)(2,1)} %constant.2.clone.refs_2_.refs_6_) | copy-start | bytes 196612
  28.8 4.5 %collective-permute-start.11 = (bf16[64,512]{1,0:T(8,128)(2,1)S(1)}, bf16[64,512]{1,0:T(8,128)(2,1)S(1)}, u32[]{:S(2)}, u32[]{:S(2)}) collective-permute-start(bf16[64,512]{1,0:T(8,128)(2,1)S(1)} %shard_map.88.refs_0_), channel_id=1, source_target_pairs={{0,12},{4,8},{8,4},{12,0},{1,13},{5,9},{9,5},{13,1},{2,14},{6,10},... | collective-permute-start | bytes 196616 | tf_op jit(solution)/shard_map/ppermute | solution.py:27
  28.9 5.5 %collective-permute-start.10 = (bf16[64,512]{1,0:T(8,128)(2,1)S(1)}, bf16[64,512]{1,0:T(8,128)(2,1)S(1)}, u32[]{:S(2)}, u32[]{:S(2)}) collective-permute-start(bf16[64,512]{1,0:T(8,128)(2,1)S(1)} %shard_map.88.refs_0_), channel_id=1, source_target_pairs={{0,8},{4,12},{8,0},{12,4},{1,9},{5,13},{9,1},{13,5},{2,10},{6,14},... | collective-permute-start | bytes 196616 | tf_op jit(solution)/shard_map/ppermute | solution.py:27
  30.3 4.1 %collective-permute-start.9 = (bf16[64,512]{1,0:T(8,128)(2,1)S(1)}, bf16[64,512]{1,0:T(8,128)(2,1)S(1)}, u32[]{:S(2)}, u32[]{:S(2)}) collective-permute-start(bf16[64,512]{1,0:T(8,128)(2,1)S(1)} %shard_map.88.refs_0_), channel_id=1, source_target_pairs={{0,4},{4,0},{8,12},{12,8},{1,5},{5,1},{9,13},{13,9},{2,6},{6,2},{1... | collective-permute-start | bytes 196616 | tf_op jit(solution)/shard_map/ppermute | solution.py:27
  35.4 1.3 %collective-permute-start.12 = (bf16[64,512]{1,0:T(8,128)(2,1)S(1)}, bf16[64,512]{1,0:T(8,128)(2,1)S(1)}, u32[]{:S(2)}, u32[]{:S(2)}) collective-permute-start(bf16[64,512]{1,0:T(8,128)(2,1)S(1)} %get-tuple-element.41.refs_0_), channel_id=1, source_target_pairs={{0,4},{4,0},{8,12},{12,8},{1,5},{5,1},{9,13},{13,9},{2,6},{6,2},{1... | collective-permute-start | bytes 196616 | tf_op jit(solution)/shard_map/ppermute | solution.py:27
  36.8 4.3 %collective-permute-start.13 = (bf16[64,512]{1,0:T(8,128)(2,1)S(1)}, bf16[64,512]{1,0:T(8,128)(2,1)S(1)}, u32[]{:S(2)}, u32[]{:S(2)}) collective-permute-start(bf16[64,512]{1,0:T(8,128)(2,1)S(1)} %shard_map.91.refs_0_), channel_id=1, source_target_pairs={{0,8},{4,12},{8,0},{12,4},{1,9},{5,13},{9,1},{13,5},{2,10},{6,14},... | collective-permute-start | bytes 196616 | tf_op jit(solution)/shard_map/ppermute | solution.py:27
  41.1 4.8 %collective-permute-start.16 = (bf16[64,512]{1,0:T(8,128)(2,1)S(1)}, bf16[64,512]{1,0:T(8,128)(2,1)S(1)}, u32[]{:S(2)}, u32[]{:S(2)}) collective-permute-start(bf16[64,512]{1,0:T(8,128)(2,1)S(1)} %shard_map.93.refs_0_), channel_id=1, source_target_pairs={{0,1},{1,0},{2,3},{3,2},{4,5},{5,4},{6,7},{7,6},{8,9},{9,8},{10,11... | collective-permute-start | bytes 196616 | tf_op jit(solution)/shard_map/ppermute | solution.py:27
  42.3 7.3 %collective-permute-start.15 = (bf16[64,512]{1,0:T(8,128)(2,1)S(1)}, bf16[64,512]{1,0:T(8,128)(2,1)S(1)}, u32[]{:S(2)}, u32[]{:S(2)}) collective-permute-start(bf16[64,512]{1,0:T(8,128)(2,1)S(1)} %shard_map.93.refs_0_), channel_id=1, source_target_pairs={{0,2},{1,3},{2,0},{3,1},{4,6},{5,7},{6,4},{7,5},{8,10},{9,11},{10,... | collective-permute-start | bytes 196616 | tf_op jit(solution)/shard_map/ppermute | solution.py:27
  43.3 6.2 %collective-permute-start.14 = (bf16[64,512]{1,0:T(8,128)(2,1)S(1)}, bf16[64,512]{1,0:T(8,128)(2,1)S(1)}, u32[]{:S(2)}, u32[]{:S(2)}) collective-permute-start(bf16[64,512]{1,0:T(8,128)(2,1)S(1)} %shard_map.93.refs_0_), channel_id=1, source_target_pairs={{0,3},{1,2},{2,1},{3,0},{4,7},{5,6},{6,5},{7,4},{8,11},{9,10},{10,... | collective-permute-start | bytes 196616 | tf_op jit(solution)/shard_map/ppermute | solution.py:27

commit v14 on v13

--- a/solution.py
+++ b/solution.py
@@ -255,21 +255,23 @@
     own = jnp.zeros((cells, LANES), jnp.float32)
     pick = number((size, size * cells), 1) // cells == number((size, size * cells), 0)
     pick = pick.astype(jnp.bfloat16)
-    ones = jnp.ones((depth, LANES), jnp.bfloat16)
     for index, copy in enumerate(copies):
         copy.wait()
         rows = slice(index * size, (index + 1) * size)
         data = data_ref[rows].astype(jnp.float32)
         data = jnp.concatenate([data[:, at_x] for at_x in range(rows_x)], axis=1)
+        lanes = data[..., :LANES]
+        for start in range(LANES, depth, LANES):
+            lanes = lanes + data[..., start : start + LANES]
+        row_sums = jnp.sum(lanes, axis=2, keepdims=True)
+        shape = lanes.shape
+        mine = number(shape, 0) + index * size == number(shape, 2)
+        own = own + jnp.sum(jnp.where(mine, row_sums, 0.0), axis=0)
         data = data.reshape(size * cells, depth).astype(jnp.bfloat16)
         cols_ref[index * size * cells : (index + 1) * size * cells, :] = data
         part = mul(pick, data)
         half_ref[0, rows, :] = part[:, : depth // 2]
         half_ref[1, rows, :] = part[:, depth // 2 :]
-        row_sums = mul(data, ones).reshape(size, cells, LANES)
-        shape = row_sums.shape
-        mine = number(shape, 0) + index * size == number(shape, 2)
-        own = own + jnp.sum(jnp.where(mine, row_sums, 0.0), axis=0)
     for step, out in enumerate(outs):
         out[0:WIDTH, :] = half_ref[(lax.axis_index("gx") & 1) ^ step]
         out[WIDTH:, :] = jnp.concatenate([own] * (depth // 2 // LANES), axis=1)

time: 50.7 us -> 50.5 us (level)
  no operation moved by 1% of the time
where the time goes in v14:
time: 50.5 us; the launch traced here: 50.3 us
  starting transfers between devices  19.9 us (39%)
  waiting for transfers between devices  18.6 us (37%)
  Pallas kernels  11 us (22%)
  between operations  0.76 us (2%)
    ppermute x17, starting transfers between devices, swap(): return lax.ppermute(part, axis, [(i, i ^ step) for i in range(size)])  19.9 us
    ppermute x17, waiting for transfers between devices, swap(): return lax.ppermute(part, axis, [(i, i ^ step) for i in range(size)])  18.6 us
    pallas_call x20, Pallas kernels, run(): pl.pallas_call(kernel, out_shape=tuple(outs), in_specs=[pl.BlockSpec(memo...  11 us
  transfers between devices with their start and end apart: 17, of which 13 were waited for; matrix products, arithmetic and copies ran while one was open for 0% of the time, Pallas kernels for 12%

profile of v14, /device:TPU:0, one launch (start us, length us, event | category | flops | bytes accessed | tf_op | source)
XLA Modules:
  0.0 50.3 jit_solution(12374122305292652021)
XLA Ops:
  0.6 1.6 %shard_map.77 = (f32[72,256]{1,0:T(8,128)S(1)}, f32[72,256]{1,0:T(8,128)S(1)}, bf16[512,512]{1,0:T(8,128)(2,1)S(1)}) custom-call(bf16[64,2,4,512]{3,2,1,0:T(4,128)(2,1)} %field_ref.1), custom_call_target="tpu_custom_call" | custom-call | flops 67108864 | bytes 1196032 | tf_op jit(solution)/shard_map/pallas_call | solution.py:552
  2.2 0.5 %collective-permute-start = (f32[72,256]{1,0:T(8,128)S(1)}, f32[72,256]{1,0:T(8,128)S(1)}, u32[]{:S(2)}, u32[]{:S(2)}) collective-permute-start(f32[72,256]{1,0:T(8,128)S(1)} %get-tuple-element.28), channel_id=1, source_target_pairs={{0,4},{4,0},{8,12},{12,8},{1,5},{5,1},{9,13},{13,9},{2,6},{6,2},{1... | collective-permute-start | bytes 221192 | tf_op jit(solution)/shard_map/ppermute | solution.py:27
  2.7 0.9 %collective-permute-done.other_ref = f32[72,256]{1,0:T(8,128)S(1)} collective-permute-done((f32[72,256]{1,0:T(8,128)S(1)}, f32[72,256]{1,0:T(8,128)S(1)}, u32[]{:S(2)}, u32[]{:S(2)}) %collective-permute-start) | collective-permute-done | bytes 73760 | tf_op jit(solution)/shard_map/ppermute | solution.py:27
  3.7 2.9 %collective-permute-start.1 = (f32[72,256]{1,0:T(8,128)S(1)}, f32[72,256]{1,0:T(8,128)S(1)}, u32[]{:S(2)}, u32[]{:S(2)}) collective-permute-start(f32[72,256]{1,0:T(8,128)S(1)} %shard_map.78.mine_ref), channel_id=1, source_target_pairs={{0,8},{4,12},{8,0},{12,4},{1,9},{5,13},{9,1},{13,5},{2,10},{6,14},... | collective-permute-start | bytes 221192 | tf_op jit(solution)/shard_map/ppermute | solution.py:27
  6.6 2.6 %collective-permute-done.1.other_ref = f32[72,256]{1,0:T(8,128)S(1)} collective-permute-done((f32[72,256]{1,0:T(8,128)S(1)}, f32[72,256]{1,0:T(8,128)S(1)}, u32[]{:S(2)}, u32[]{:S(2)}) %collective-permute-start.1) | collective-permute-done | bytes 73760 | tf_op jit(solution)/shard_map/ppermute | solution.py:27
  9.2 3.9 %collective-permute-start.2 = (f32[72,256]{1,0:T(8,128)S(1)}, f32[72,256]{1,0:T(8,128)S(1)}, u32[]{:S(2)}, u32[]{:S(2)}) collective-permute-start(f32[72,256]{1,0:T(8,128)S(1)} %shard_map.79.refs_0_), channel_id=1, source_target_pairs={{0,3},{1,2},{2,1},{3,0},{4,7},{5,6},{6,5},{7,4},{8,11},{9,10},{10,... | collective-permute-start | bytes 221192 | tf_op jit(solution)/shard_map/ppermute | solution.py:27
  13.1 0.6 %collective-permute-start.4 = (f32[72,256]{1,0:T(8,128)S(1)}, f32[72,256]{1,0:T(8,128)S(1)}, u32[]{:S(2)}, u32[]{:S(2)}) collective-permute-start(f32[72,256]{1,0:T(8,128)S(1)} %shard_map.79.refs_0_), channel_id=1, source_target_pairs={{0,1},{1,0},{2,3},{3,2},{4,5},{5,4},{6,7},{7,6},{8,9},{9,8},{10,11... | collective-permute-start | bytes 221192 | tf_op jit(solution)/shard_map/ppermute | solution.py:27
  14.0 1.2 %shard_map.82.cot_ref.refs_10_ = bf16[512,512]{1,0:T(8,128)(2,1)S(1)} custom-call(bf16[64,2,4,512]{3,2,1,0:T(4,128)(2,1)} %cot_ref.1), custom_call_target="tpu_custom_call" | custom-call | flops 268435456 | bytes 1048576 | tf_op jit(solution)/shard_map/pallas_call | solution.py:552
  15.2 0.8 %collective-permute-done.2.refs_1_ = f32[72,256]{1,0:T(8,128)S(1)} collective-permute-done((f32[72,256]{1,0:T(8,128)S(1)}, f32[72,256]{1,0:T(8,128)S(1)}, u32[]{:S(2)}, u32[]{:S(2)}) %collective-permute-start.2) | collective-permute-done | bytes 73760 | tf_op jit(solution)/shard_map/ppermute | solution.py:27
  16.0 2.8 %collective-permute-done.3.refs_1_ = f32[72,256]{1,0:T(8,128)S(1)} collective-permute-done((f32[72,256]{1,0:T(8,128)S(1)}, f32[72,256]{1,0:T(8,128)S(1)}, u32[]{:S(2)}, u32[]{:S(2)}) %collective-permute-start.3) | collective-permute-done | bytes 73760 | tf_op jit(solution)/shard_map/ppermute | solution.py:27
  19.0 1.3 %collective-permute-done.5.other_ref = f32[72,256]{1,0:T(8,128)S(1)} collective-permute-done((f32[72,256]{1,0:T(8,128)S(1)}, f32[72,256]{1,0:T(8,128)S(1)}, u32[]{:S(2)}, u32[]{:S(2)}) %collective-permute-start.5) | collective-permute-done | bytes 73760 | tf_op jit(solution)/shard_map/ppermute | solution.py:27
  20.2 1.0 %shard_map.85 = (bf16[16,512]{1,0:T(8,128)(2,1)S(1)}, bf16[128,512]{1,0:T(8,128)(2,1)S(1)}, f32[72,512]{1,0:T(8,128)S(1)}) custom-call(f32[72,256]{1,0:T(8,128)S(1)} %shard_map.84.mine_ref, f32[72,256]{1,0:T(8,128)S(1)} %collective-permute-done.5.other_ref, f32[128,64]{1,0:T(8,128)S(1)} %get-tuple-element.32.wz_ref, ...), custom_call_target="tpu_custom_call" | custom-call | flops 536870912 | bytes 1785856 | tf_op jit(solution)/shard_map/pallas_call | solution.py:552
  21.2 2.7 %collective-permute-start.6 = (bf16[16,512]{1,0:T(8,128)(2,1)S(1)}, bf16[16,512]{1,0:T(8,128)(2,1)S(1)}, u32[]{:S(2)}, u32[]{:S(2)}) collective-permute-start(bf16[16,512]{1,0:T(8,128)(2,1)S(1)} %get-tuple-element.37.refs_0_), channel_id=1, source_target_pairs={{0,3},{1,2},{2,1},{3,0},{4,7},{5,6},{6,5},{7,4},{8,11},{9,10},{10,... | collective-permute-start | bytes 49160 | tf_op jit(solution)/shard_map/ppermute | solution.py:27
  23.9 1.8 %collective-permute-start.8 = (bf16[16,512]{1,0:T(8,128)(2,1)S(1)}, bf16[16,512]{1,0:T(8,128)(2,1)S(1)}, u32[]{:S(2)}, u32[]{:S(2)}) collective-permute-start(bf16[16,512]{1,0:T(8,128)(2,1)S(1)} %get-tuple-element.37.refs_0_), channel_id=1, source_target_pairs={{0,1},{1,0},{2,3},{3,2},{4,5},{5,4},{6,7},{7,6},{8,9},{9,8},{10,11... | collective-permute-start | bytes 49160 | tf_op jit(solution)/shard_map/ppermute | solution.py:27
  25.7 1.1 %collective-permute-done.6.refs_1_ = bf16[16,512]{1,0:T(8,128)(2,1)S(1)} collective-permute-done((bf16[16,512]{1,0:T(8,128)(2,1)S(1)}, bf16[16,512]{1,0:T(8,128)(2,1)S(1)}, u32[]{:S(2)}, u32[]{:S(2)}) %collective-permute-start.6) | collective-permute-done | bytes 16416 | tf_op jit(solution)/shard_map/ppermute | solution.py:27
  26.8 1.7 %collective-permute-done.7.refs_1_ = bf16[16,512]{1,0:T(8,128)(2,1)S(1)} collective-permute-done((bf16[16,512]{1,0:T(8,128)(2,1)S(1)}, bf16[16,512]{1,0:T(8,128)(2,1)S(1)}, u32[]{:S(2)}, u32[]{:S(2)}) %collective-permute-start.7) | collective-permute-done | bytes 16416 | tf_op jit(solution)/shard_map/ppermute | solution.py:27
  28.7 1.4 %collective-permute-start.10 = (bf16[64,512]{1,0:T(8,128)(2,1)S(1)}, bf16[64,512]{1,0:T(8,128)(2,1)S(1)}, u32[]{:S(2)}, u32[]{:S(2)}) collective-permute-start(bf16[64,512]{1,0:T(8,128)(2,1)S(1)} %shard_map.88.refs_0_), channel_id=1, source_target_pairs={{0,8},{4,12},{8,0},{12,4},{1,9},{5,13},{9,1},{13,5},{2,10},{6,14},... | collective-permute-start | bytes 196616 | tf_op jit(solution)/shard_map/ppermute | solution.py:27
  30.0 0.5 collective-permute-start.9
  30.5 1.5 %shard_map.89 = (f32[2,64,128]{2,1,0:T(8,128)S(1)}, f32[8,128,64]{2,1,0:T(8,128)S(1)}, f32[2,1024,128]{2,1,0:T(8,128)S(1)}) custom-call(f32[88,256]{1,0:T(8,128)S(1)} %shard_map.81.refs_0_, f32[72,256]{1,0:T(8,128)S(1)} %collective-permute-done.4.refs_1_, bf16[2,128,128]{2,1,0:T(8,128)(2,1)S(1)} %copy-done.1, f32[3,2,64,64]{3,2,1,0:T(8,128)S(1)} %copy-done), custom_call_target="tpu_custom_call" | custom-call | flops 134217728 | bytes 1703936 | tf_op jit(solution)/shard_map/pallas_call | solution.py:552
  32.0 1.0 %collective-permute-done.11.refs_3_ = bf16[64,512]{1,0:T(8,128)(2,1)S(1)} collective-permute-done((bf16[64,512]{1,0:T(8,128)(2,1)S(1)}, bf16[64,512]{1,0:T(8,128)(2,1)S(1)}, u32[]{:S(2)}, u32[]{:S(2)}) %collective-permute-start.11) | collective-permute-done | bytes 65568 | tf_op jit(solution)/shard_map/ppermute | solution.py:27
  33.0 1.1 %collective-permute-done.10.refs_2_ = bf16[64,512]{1,0:T(8,128)(2,1)S(1)} collective-permute-done((bf16[64,512]{1,0:T(8,128)(2,1)S(1)}, bf16[64,512]{1,0:T(8,128)(2,1)S(1)}, u32[]{:S(2)}, u32[]{:S(2)}) %collective-permute-start.10) | collective-permute-done | bytes 65568 | tf_op jit(solution)/shard_map/ppermute | solution.py:27
  34.1 1.0 %shard_map.90 = (f32[2,8,512]{2,1,0:T(8,128)S(1)}, bf16[64,512]{1,0:T(8,128)(2,1)S(1)}) custom-call(bf16[64,512]{1,0:T(8,128)(2,1)S(1)} %shard_map.88.refs_0_, bf16[64,512]{1,0:T(8,128)(2,1)S(1)} %collective-permute-done.9.refs_1_, bf16[64,512]{1,0:T(8,128)(2,1)S(1)} %collective-permute-done.10.refs_2_, bf16[64,512]{1,0:T(8,128)(2,1)S(1)} %collective-permute-done.11.refs_3_, ...), custom_call_target="tpu_custom_call" | custom-call | flops 268435456 | bytes 1998848 | tf_op jit(solution)/shard_map/pallas_call | solution.py:552
  35.8 0.7 %collective-permute-done.12.refs_1_ = bf16[64,512]{1,0:T(8,128)(2,1)S(1)} collective-permute-done((bf16[64,512]{1,0:T(8,128)(2,1)S(1)}, bf16[64,512]{1,0:T(8,128)(2,1)S(1)}, u32[]{:S(2)}, u32[]{:S(2)}) %collective-permute-start.12) | collective-permute-done | bytes 65568 | tf_op jit(solution)/shard_map/ppermute | solution.py:27
  36.5 0.9 %collective-permute-start.13 = (bf16[64,512]{1,0:T(8,128)(2,1)S(1)}, bf16[64,512]{1,0:T(8,128)(2,1)S(1)}, u32[]{:S(2)}, u32[]{:S(2)}) collective-permute-start(bf16[64,512]{1,0:T(8,128)(2,1)S(1)} %shard_map.91.refs_0_), channel_id=1, source_target_pairs={{0,8},{4,12},{8,0},{12,4},{1,9},{5,13},{9,1},{13,5},{2,10},{6,14},... | collective-permute-start | bytes 196616 | tf_op jit(solution)/shard_map/ppermute | solution.py:27
  37.4 1.2 %shard_map.94 = bf16[64,2,4,512]{3,2,1,0:T(4,128)(2,1)} custom-call(f32[2,8,512]{2,1,0:T(8,128)S(1)} %get-tuple-element.42.top_ref, f32[64,512]{1,0:T(8,128)S(1)} %get-tuple-element.36.wo_ref.refs_6_, bf16[128,512]{1,0:T(8,128)(2,1)S(1)} %get-tuple-element.43.both_ref, bf16[512,512]{1,0:T(8,128)(2,1)S(1)} %get-tuple-element.33.field_ref.refs_9_), custom_call_target="tpu_custom_call" | custom-call | flops 268435456 | bytes 1343488 | tf_op jit(solution)/shard_map/pallas_call | solution.py:552
  38.7 1.6 %shard_map.95.refs_6_ = f32[512,128]{1,0:T(8,128)S(1)} custom-call(bf16[64,512]{1,0:T(8,128)(2,1)S(1)} %shard_map.88.refs_0_, bf16[64,512]{1,0:T(8,128)(2,1)S(1)} %collective-permute-done.9.refs_1_, bf16[64,512]{1,0:T(8,128)(2,1)S(1)} %collective-permute-done.10.refs_2_, bf16[64,512]{1,0:T(8,128)(2,1)S(1)} %collective-permute-done.11.refs_3_, ...), custom_call_target="tpu_custom_call" | custom-call | flops 536870912 | bytes 1998848 | tf_op jit(solution)/shard_map/pallas_call | solution.py:552
  40.3 0.6 %collective-permute-done.13.refs_1_ = bf16[64,512]{1,0:T(8,128)(2,1)S(1)} collective-permute-done((bf16[64,512]{1,0:T(8,128)(2,1)S(1)}, bf16[64,512]{1,0:T(8,128)(2,1)S(1)}, u32[]{:S(2)}, u32[]{:S(2)}) %collective-permute-start.13) | collective-permute-done | bytes 65568 | tf_op jit(solution)/shard_map/ppermute | solution.py:27
  40.9 1.2 %collective-permute-start.16 = (bf16[64,512]{1,0:T(8,128)(2,1)S(1)}, bf16[64,512]{1,0:T(8,128)(2,1)S(1)}, u32[]{:S(2)}, u32[]{:S(2)}) collective-permute-start(bf16[64,512]{1,0:T(8,128)(2,1)S(1)} %shard_map.93.refs_0_), channel_id=1, source_target_pairs={{0,1},{1,0},{2,3},{3,2},{4,5},{5,4},{6,7},{7,6},{8,9},{9,8},{10,11... | collective-permute-start | bytes 196616 | tf_op jit(solution)/shard_map/ppermute | solution.py:27
  42.0 1.1 %collective-permute-start.15 = (bf16[64,512]{1,0:T(8,128)(2,1)S(1)}, bf16[64,512]{1,0:T(8,128)(2,1)S(1)}, u32[]{:S(2)}, u32[]{:S(2)}) collective-permute-start(bf16[64,512]{1,0:T(8,128)(2,1)S(1)} %shard_map.93.refs_0_), channel_id=1, source_target_pairs={{0,2},{1,3},{2,0},{3,1},{4,6},{5,7},{6,4},{7,5},{8,10},{9,11},{10,... | collective-permute-start | bytes 196616 | tf_op jit(solution)/shard_map/ppermute | solution.py:27
  43.1 2.2 %collective-permute-start.14 = (bf16[64,512]{1,0:T(8,128)(2,1)S(1)}, bf16[64,512]{1,0:T(8,128)(2,1)S(1)}, u32[]{:S(2)}, u32[]{:S(2)}) collective-permute-start(bf16[64,512]{1,0:T(8,128)(2,1)S(1)} %shard_map.93.refs_0_), channel_id=1, source_target_pairs={{0,3},{1,2},{2,1},{3,0},{4,7},{5,6},{6,5},{7,4},{8,11},{9,10},{10,... | collective-permute-start | bytes 196616 | tf_op jit(solution)/shard_map/ppermute | solution.py:27
  45.7 3.6 %collective-permute-done.15.refs_2_ = bf16[64,512]{1,0:T(8,128)(2,1)S(1)} collective-permute-done((bf16[64,512]{1,0:T(8,128)(2,1)S(1)}, bf16[64,512]{1,0:T(8,128)(2,1)S(1)}, u32[]{:S(2)}, u32[]{:S(2)}) %collective-permute-start.15) | collective-permute-done | bytes 65568 | tf_op jit(solution)/shard_map/ppermute | solution.py:27
  49.4 0.9 %shard_map.96 = bf16[64,2,4,512]{3,2,1,0:T(4,128)(2,1)} custom-call(bf16[64,512]{1,0:T(8,128)(2,1)S(1)} %shard_map.93.refs_0_, bf16[64,512]{1,0:T(8,128)(2,1)S(1)} %collective-permute-done.14.refs_1_, bf16[64,512]{1,0:T(8,128)(2,1)S(1)} %collective-permute-done.15.refs_2_, bf16[64,512]{1,0:T(8,128)(2,1)S(1)} %collective-permute-done.16.refs_3_, ...), custom_call_target="tpu_custom_call" | custom-call | bytes 2244608 | tf_op jit(solution)/shard_map/pallas_call | solution.py:552
  (30 shorter events, 1.6 us)
Async XLA Ops:
  2.2 1.4 %collective-permute-start = (f32[72,256]{1,0:T(8,128)S(1)}, f32[72,256]{1,0:T(8,128)S(1)}, u32[]{:S(2)}, u32[]{:S(2)}) collective-permute-start(f32[72,256]{1,0:T(8,128)S(1)} %get-tuple-element.28), channel_id=1, source_target_pairs={{0,4},{4,0},{8,12},{12,8},{1,5},{5,1},{9,13},{13,9},{2,6},{6,2},{1... | collective-permute-start | bytes 221192 | tf_op jit(solution)/shard_map/ppermute | solution.py:27
  3.6 10.1 %copy-start = (f32[3,2,64,64]{3,2,1,0:T(8,128)S(1)}, f32[3,2,64,64]{3,2,1,0:T(8,128)}, u32[]{:S(2)}) copy-start(f32[3,2,64,64]{3,2,1,0:T(8,128)} %refs_7_.1) | copy-start | bytes 294916
  3.7 10.1 %copy-start.2 = (bf16[64,64]{1,0:T(8,128)(2,1)S(1)}, bf16[64,64]{1,0:T(8,128)(2,1)}, u32[]{:S(2)}) copy-start(bf16[64,64]{1,0:T(8,128)(2,1)} %wv_ref.1) | copy-start | bytes 24580
  3.7 10.1 %copy-start.3 = (bf16[64,64]{1,0:T(8,128)(2,1)S(1)}, bf16[64,64]{1,0:T(8,128)(2,1)}, u32[]{:S(2)}) copy-start(bf16[64,64]{1,0:T(8,128)(2,1)} %wo_ref.1) | copy-start | bytes 24580
  3.7 5.5 %collective-permute-start.1 = (f32[72,256]{1,0:T(8,128)S(1)}, f32[72,256]{1,0:T(8,128)S(1)}, u32[]{:S(2)}, u32[]{:S(2)}) collective-permute-start(f32[72,256]{1,0:T(8,128)S(1)} %shard_map.78.mine_ref), channel_id=1, source_target_pairs={{0,8},{4,12},{8,0},{12,4},{1,9},{5,13},{9,1},{13,5},{2,10},{6,14},... | collective-permute-start | bytes 221192 | tf_op jit(solution)/shard_map/ppermute | solution.py:27
  9.2 6.8 %collective-permute-start.2 = (f32[72,256]{1,0:T(8,128)S(1)}, f32[72,256]{1,0:T(8,128)S(1)}, u32[]{:S(2)}, u32[]{:S(2)}) collective-permute-start(f32[72,256]{1,0:T(8,128)S(1)} %shard_map.79.refs_0_), channel_id=1, source_target_pairs={{0,3},{1,2},{2,1},{3,0},{4,7},{5,6},{6,5},{7,4},{8,11},{9,10},{10,... | collective-permute-start | bytes 221192 | tf_op jit(solution)/shard_map/ppermute | solution.py:27
  13.1 5.7 %collective-permute-start.3 = (f32[72,256]{1,0:T(8,128)S(1)}, f32[72,256]{1,0:T(8,128)S(1)}, u32[]{:S(2)}, u32[]{:S(2)}) collective-permute-start(f32[72,256]{1,0:T(8,128)S(1)} %shard_map.79.refs_0_), channel_id=1, source_target_pairs={{0,2},{1,3},{2,0},{3,1},{4,6},{5,7},{6,4},{7,5},{8,10},{9,11},{10,... | collective-permute-start | bytes 221192 | tf_op jit(solution)/shard_map/ppermute | solution.py:27
  13.1 5.7 %collective-permute-start.4 = (f32[72,256]{1,0:T(8,128)S(1)}, f32[72,256]{1,0:T(8,128)S(1)}, u32[]{:S(2)}, u32[]{:S(2)}) collective-permute-start(f32[72,256]{1,0:T(8,128)S(1)} %shard_map.79.refs_0_), channel_id=1, source_target_pairs={{0,1},{1,0},{2,3},{3,2},{4,5},{5,4},{6,7},{7,6},{8,9},{9,8},{10,11... | collective-permute-start | bytes 221192 | tf_op jit(solution)/shard_map/ppermute | solution.py:27
  18.9 1.3 %collective-permute-start.5 = (f32[72,256]{1,0:T(8,128)S(1)}, f32[72,256]{1,0:T(8,128)S(1)}, u32[]{:S(2)}, u32[]{:S(2)}) collective-permute-start(f32[72,256]{1,0:T(8,128)S(1)} %shard_map.84.mine_ref), channel_id=1, source_target_pairs={{0,4},{4,0},{8,12},{12,8},{1,5},{5,1},{9,13},{13,9},{2,6},{6,2},{1... | collective-permute-start | bytes 221192 | tf_op jit(solution)/shard_map/ppermute | solution.py:27
  21.2 5.6 %collective-permute-start.6 = (bf16[16,512]{1,0:T(8,128)(2,1)S(1)}, bf16[16,512]{1,0:T(8,128)(2,1)S(1)}, u32[]{:S(2)}, u32[]{:S(2)}) collective-permute-start(bf16[16,512]{1,0:T(8,128)(2,1)S(1)} %get-tuple-element.37.refs_0_), channel_id=1, source_target_pairs={{0,3},{1,2},{2,1},{3,0},{4,7},{5,6},{6,5},{7,4},{8,11},{9,10},{10,... | collective-permute-start | bytes 49160 | tf_op jit(solution)/shard_map/ppermute | solution.py:27
  23.9 4.6 %collective-permute-start.7 = (bf16[16,512]{1,0:T(8,128)(2,1)S(1)}, bf16[16,512]{1,0:T(8,128)(2,1)S(1)}, u32[]{:S(2)}, u32[]{:S(2)}) collective-permute-start(bf16[16,512]{1,0:T(8,128)(2,1)S(1)} %get-tuple-element.37.refs_0_), channel_id=1, source_target_pairs={{0,2},{1,3},{2,0},{3,1},{4,6},{5,7},{6,4},{7,5},{8,10},{9,11},{10,... | collective-permute-start | bytes 49160 | tf_op jit(solution)/shard_map/ppermute | solution.py:27
  23.9 4.6 %collective-permute-start.8 = (bf16[16,512]{1,0:T(8,128)(2,1)S(1)}, bf16[16,512]{1,0:T(8,128)(2,1)S(1)}, u32[]{:S(2)}, u32[]{:S(2)}) collective-permute-start(bf16[16,512]{1,0:T(8,128)(2,1)S(1)} %get-tuple-element.37.refs_0_), channel_id=1, source_target_pairs={{0,1},{1,0},{2,3},{3,2},{4,5},{5,4},{6,7},{7,6},{8,9},{9,8},{10,11... | collective-permute-start | bytes 49160 | tf_op jit(solution)/shard_map/ppermute | solution.py:27
  28.6 2.0 %copy-start.1 = (bf16[2,128,128]{2,1,0:T(8,128)(2,1)S(1)}, bf16[2,128,128]{2,1,0:T(8,128)(2,1)}, u32[]{:S(2)}) copy-start(bf16[2,128,128]{2,1,0:T(8,128)(2,1)} %constant.2.clone.refs_2_.refs_6_) | copy-start | bytes 196612
  28.6 4.5 %collective-permute-start.11 = (bf16[64,512]{1,0:T(8,128)(2,1)S(1)}, bf16[64,512]{1,0:T(8,128)(2,1)S(1)}, u32[]{:S(2)}, u32[]{:S(2)}) collective-permute-start(bf16[64,512]{1,0:T(8,128)(2,1)S(1)} %shard_map.88.refs_0_), channel_id=1, source_target_pairs={{0,12},{4,8},{8,4},{12,0},{1,13},{5,9},{9,5},{13,1},{2,14},{6,10},... | collective-permute-start | bytes 196616 | tf_op jit(solution)/shard_map/ppermute | solution.py:27
  28.7 5.5 %collective-permute-start.10 = (bf16[64,512]{1,0:T(8,128)(2,1)S(1)}, bf16[64,512]{1,0:T(8,128)(2,1)S(1)}, u32[]{:S(2)}, u32[]{:S(2)}) collective-permute-start(bf16[64,512]{1,0:T(8,128)(2,1)S(1)} %shard_map.88.refs_0_), channel_id=1, source_target_pairs={{0,8},{4,12},{8,0},{12,4},{1,9},{5,13},{9,1},{13,5},{2,10},{6,14},... | collective-permute-start | bytes 196616 | tf_op jit(solution)/shard_map/ppermute | solution.py:27
  30.0 4.1 %collective-permute-start.9 = (bf16[64,512]{1,0:T(8,128)(2,1)S(1)}, bf16[64,512]{1,0:T(8,128)(2,1)S(1)}, u32[]{:S(2)}, u32[]{:S(2)}) collective-permute-start(bf16[64,512]{1,0:T(8,128)(2,1)S(1)} %shard_map.88.refs_0_), channel_id=1, source_target_pairs={{0,4},{4,0},{8,12},{12,8},{1,5},{5,1},{9,13},{13,9},{2,6},{6,2},{1... | collective-permute-start | bytes 196616 | tf_op jit(solution)/shard_map/ppermute | solution.py:27
  35.2 1.3 %collective-permute-start.12 = (bf16[64,512]{1,0:T(8,128)(2,1)S(1)}, bf16[64,512]{1,0:T(8,128)(2,1)S(1)}, u32[]{:S(2)}, u32[]{:S(2)}) collective-permute-start(bf16[64,512]{1,0:T(8,128)(2,1)S(1)} %get-tuple-element.41.refs_0_), channel_id=1, source_target_pairs={{0,4},{4,0},{8,12},{12,8},{1,5},{5,1},{9,13},{13,9},{2,6},{6,2},{1... | collective-permute-start | bytes 196616 | tf_op jit(solution)/shard_map/ppermute | solution.py:27
  36.5 4.3 %collective-permute-start.13 = (bf16[64,512]{1,0:T(8,128)(2,1)S(1)}, bf16[64,512]{1,0:T(8,128)(2,1)S(1)}, u32[]{:S(2)}, u32[]{:S(2)}) collective-permute-start(bf16[64,512]{1,0:T(8,128)(2,1)S(1)} %shard_map.91.refs_0_), channel_id=1, source_target_pairs={{0,8},{4,12},{8,0},{12,4},{1,9},{5,13},{9,1},{13,5},{2,10},{6,14},... | collective-permute-start | bytes 196616 | tf_op jit(solution)/shard_map/ppermute | solution.py:27
  40.9 4.8 %collective-permute-start.16 = (bf16[64,512]{1,0:T(8,128)(2,1)S(1)}, bf16[64,512]{1,0:T(8,128)(2,1)S(1)}, u32[]{:S(2)}, u32[]{:S(2)}) collective-permute-start(bf16[64,512]{1,0:T(8,128)(2,1)S(1)} %shard_map.93.refs_0_), channel_id=1, source_target_pairs={{0,1},{1,0},{2,3},{3,2},{4,5},{5,4},{6,7},{7,6},{8,9},{9,8},{10,11... | collective-permute-start | bytes 196616 | tf_op jit(solution)/shard_map/ppermute | solution.py:27
  42.0 7.3 %collective-permute-start.15 = (bf16[64,512]{1,0:T(8,128)(2,1)S(1)}, bf16[64,512]{1,0:T(8,128)(2,1)S(1)}, u32[]{:S(2)}, u32[]{:S(2)}) collective-permute-start(bf16[64,512]{1,0:T(8,128)(2,1)S(1)} %shard_map.93.refs_0_), channel_id=1, source_target_pairs={{0,2},{1,3},{2,0},{3,1},{4,6},{5,7},{6,4},{7,5},{8,10},{9,11},{10,... | collective-permute-start | bytes 196616 | tf_op jit(solution)/shard_map/ppermute | solution.py:27
  43.1 6.2 %collective-permute-start.14 = (bf16[64,512]{1,0:T(8,128)(2,1)S(1)}, bf16[64,512]{1,0:T(8,128)(2,1)S(1)}, u32[]{:S(2)}, u32[]{:S(2)}) collective-permute-start(bf16[64,512]{1,0:T(8,128)(2,1)S(1)} %shard_map.93.refs_0_), channel_id=1, source_target_pairs={{0,3},{1,2},{2,1},{3,0},{4,7},{5,6},{6,5},{7,4},{8,11},{9,10},{10,... | collective-permute-start | bytes 196616 | tf_op jit(solution)/shard_map/ppermute | solution.py:27

commit v15 on v14

--- a/solution.py
+++ b/solution.py
@@ -277,19 +277,6 @@
         out[WIDTH:, :] = jnp.concatenate([own] * (depth // 2 // LANES), axis=1)
 
 
-def add_kernel(*refs):
-    parts, out_ref = refs[:-1], refs[-1]
-    total = parts[0][0:WIDTH, :]
-    for part in parts[1:]:
-        total = total + part[0:WIDTH, :]
-    out_ref[0:WIDTH, :] = total
-    start = WIDTH
-    for part in parts:
-        more = part.shape[0] - WIDTH
-        out_ref[start : start + more, :] = part[WIDTH:, :]
-        start += more
-
-
 def add_beside_kernel(known, mine_ref, other_ref, out_ref):
     out_ref[0:WIDTH, :] = mine_ref[0:WIDTH, :] + other_ref[0:WIDTH, :]
     lanes = known * WIDTH
@@ -298,6 +285,21 @@
     if rest > 0:
         rows.append(jnp.zeros((rows[0].shape[0], rest), jnp.float32))
     out_ref[WIDTH:, :] = jnp.concatenate(rows, axis=1)
+
+
+def narrow_kernel(total_ref, out_ref):
+    out_ref[0:WIDTH, :] = total_ref[0:WIDTH, :].astype(jnp.bfloat16)
+    high, low = split(total_ref[WIDTH:, :])
+    out_ref[WIDTH:, :] = jnp.concatenate([high, low], axis=0)
+
+
+def add_narrow_kernel(found_ref, part_ref, out_ref):
+    known = found_ref.shape[0]
+    part = part_ref[...].astype(jnp.float32)
+    cells = (part.shape[0] - WIDTH) // 2
+    out_ref[0:WIDTH, :] = found_ref[0:WIDTH, :] + part[0:WIDTH]
+    out_ref[WIDTH:known, :] = found_ref[WIDTH:, :]
+    out_ref[known:, :] = part[WIDTH : WIDTH + cells] + part[WIDTH + cells :]
 
 
 def stack_kernel(*refs):
@@ -638,7 +640,11 @@
             [like((WIDTH + cells, half), f32)],
             (total, swap(total if level else other, "gx", span_x, step)),
         )
-    totals = taken(add_kernel, swaps(total, "gy", span_y))
+    sent = run(narrow_kernel, [like((WIDTH + 2 * cells, half), bf16)], (total,))
+    for part in swaps(sent, "gy", span_y)[1:]:
+        shape = (total.shape[0] + cells, half)
+        total = run(add_narrow_kernel, [like(shape, f32)], (total, part))
+    totals = (total,)
     totals, cots, wz = lax.optimization_barrier((totals, cots, wz))
     mine = run(
         functools.partial(factor_kernel, grid_x * grid_y),

time: 50.5 us -> 49.7 us (0.984)
  waiting for transfers between devices: 18.6 us -> 18 us
    ppermute x17, waiting for transfers between devices: 18.6 us -> 18 us  [swap(): return lax.ppermute(part, axis, [(i, i ^ step) for i in range(size)])]
    pallas_call x20 -> x22, Pallas kernels: 11 us -> 11 us  [run(): pl.pallas_call(kernel, out_shape=tuple(outs), in_specs=[pl.BlockSpec(memo...]
  transfers between devices with their start and end apart: 17 -> 17, of which waited for: 13 -> 14; matrix products, arithmetic and copies ran while one was open for 0% -> 0% of each run, Pallas kernels for 12% -> 13%
where the time goes in v15:
time: 49.7 us; the launch traced here: 49.5 us
  starting transfers between devices  19.7 us (40%)
  waiting for transfers between devices  18 us (36%)
  Pallas kernels  11 us (22%)
  between operations  0.77 us (2%)
    ppermute x17, starting transfers between devices, swap(): return lax.ppermute(part, axis, [(i, i ^ step) for i in range(size)])  19.7 us
    ppermute x17, waiting for transfers between devices, swap(): return lax.ppermute(part, axis, [(i, i ^ step) for i in range(size)])  18 us
    pallas_call x22, Pallas kernels, run(): pl.pallas_call(kernel, out_shape=tuple(outs), in_specs=[pl.BlockSpec(memo...  11 us
  transfers between devices with their start and end apart: 17, of which 14 were waited for; matrix products, arithmetic and copies ran while one was open for 0% of the time, Pallas kernels for 13%

profile of v15, /device:TPU:0, one launch (start us, length us, event | category | flops | bytes accessed | tf_op | source)
XLA Modules:
  0.0 49.5 jit_solution(5006111455922345135)
XLA Ops:
  0.6 1.6 %shard_map.77 = (f32[72,256]{1,0:T(8,128)S(1)}, f32[72,256]{1,0:T(8,128)S(1)}, bf16[512,512]{1,0:T(8,128)(2,1)S(1)}) custom-call(bf16[64,2,4,512]{3,2,1,0:T(4,128)(2,1)} %field_ref.1), custom_call_target="tpu_custom_call" | custom-call | flops 67108864 | bytes 1196032 | tf_op jit(solution)/shard_map/pallas_call | solution.py:554
  2.2 0.5 %collective-permute-start = (f32[72,256]{1,0:T(8,128)S(1)}, f32[72,256]{1,0:T(8,128)S(1)}, u32[]{:S(2)}, u32[]{:S(2)}) collective-permute-start(f32[72,256]{1,0:T(8,128)S(1)} %get-tuple-element.27), channel_id=1, source_target_pairs={{0,4},{4,0},{8,12},{12,8},{1,5},{5,1},{9,13},{13,9},{2,6},{6,2},{1... | collective-permute-start | bytes 221192 | tf_op jit(solution)/shard_map/ppermute | solution.py:27
  2.7 0.9 %collective-permute-done.other_ref = f32[72,256]{1,0:T(8,128)S(1)} collective-permute-done((f32[72,256]{1,0:T(8,128)S(1)}, f32[72,256]{1,0:T(8,128)S(1)}, u32[]{:S(2)}, u32[]{:S(2)}) %collective-permute-start) | collective-permute-done | bytes 73760 | tf_op jit(solution)/shard_map/ppermute | solution.py:27
  3.7 2.9 %collective-permute-start.1 = (f32[72,256]{1,0:T(8,128)S(1)}, f32[72,256]{1,0:T(8,128)S(1)}, u32[]{:S(2)}, u32[]{:S(2)}) collective-permute-start(f32[72,256]{1,0:T(8,128)S(1)} %shard_map.78.mine_ref), channel_id=1, source_target_pairs={{0,8},{4,12},{8,0},{12,4},{1,9},{5,13},{9,1},{13,5},{2,10},{6,14},... | collective-permute-start | bytes 221192 | tf_op jit(solution)/shard_map/ppermute | solution.py:27
  6.6 2.6 %collective-permute-done.1.other_ref = f32[72,256]{1,0:T(8,128)S(1)} collective-permute-done((f32[72,256]{1,0:T(8,128)S(1)}, f32[72,256]{1,0:T(8,128)S(1)}, u32[]{:S(2)}, u32[]{:S(2)}) %collective-permute-start.1) | collective-permute-done | bytes 73760 | tf_op jit(solution)/shard_map/ppermute | solution.py:27
  9.2 3.9 %collective-permute-start.2 = (bf16[80,256]{1,0:T(8,128)(2,1)S(1)}, bf16[80,256]{1,0:T(8,128)(2,1)S(1)}, u32[]{:S(2)}, u32[]{:S(2)}) collective-permute-start(bf16[80,256]{1,0:T(8,128)(2,1)S(1)} %shard_map.80), channel_id=1, source_target_pairs={{0,3},{1,2},{2,1},{3,0},{4,7},{5,6},{6,5},{7,4},{8,11},{9,10},{10,... | collective-permute-start | bytes 122888 | tf_op jit(solution)/shard_map/ppermute | solution.py:27
  13.2 0.6 %collective-permute-start.4 = (bf16[80,256]{1,0:T(8,128)(2,1)S(1)}, bf16[80,256]{1,0:T(8,128)(2,1)S(1)}, u32[]{:S(2)}, u32[]{:S(2)}) collective-permute-start(bf16[80,256]{1,0:T(8,128)(2,1)S(1)} %shard_map.80), channel_id=1, source_target_pairs={{0,1},{1,0},{2,3},{3,2},{4,5},{5,4},{6,7},{7,6},{8,9},{9,8},{10,11... | collective-permute-start | bytes 122888 | tf_op jit(solution)/shard_map/ppermute | solution.py:27
  14.1 1.2 %shard_map.84.cot_ref.refs_10_ = bf16[512,512]{1,0:T(8,128)(2,1)S(1)} custom-call(bf16[64,2,4,512]{3,2,1,0:T(4,128)(2,1)} %cot_ref.1), custom_call_target="tpu_custom_call" | custom-call | flops 268435456 | bytes 1048576 | tf_op jit(solution)/shard_map/pallas_call | solution.py:554
  15.4 2.7 %collective-permute-done.3.part_ref = bf16[80,256]{1,0:T(8,128)(2,1)S(1)} collective-permute-done((bf16[80,256]{1,0:T(8,128)(2,1)S(1)}, bf16[80,256]{1,0:T(8,128)(2,1)S(1)}, u32[]{:S(2)}, u32[]{:S(2)}) %collective-permute-start.3) | collective-permute-done | bytes 40992 | tf_op jit(solution)/shard_map/ppermute | solution.py:27
  18.2 1.3 %collective-permute-done.5.other_ref = f32[72,256]{1,0:T(8,128)S(1)} collective-permute-done((f32[72,256]{1,0:T(8,128)S(1)}, f32[72,256]{1,0:T(8,128)S(1)}, u32[]{:S(2)}, u32[]{:S(2)}) %collective-permute-start.5) | collective-permute-done | bytes 73760 | tf_op jit(solution)/shard_map/ppermute | solution.py:27
  19.5 1.0 %shard_map.87 = (bf16[16,512]{1,0:T(8,128)(2,1)S(1)}, bf16[128,512]{1,0:T(8,128)(2,1)S(1)}, f32[72,512]{1,0:T(8,128)S(1)}) custom-call(f32[72,256]{1,0:T(8,128)S(1)} %shard_map.86.mine_ref, f32[72,256]{1,0:T(8,128)S(1)} %collective-permute-done.5.other_ref, f32[128,64]{1,0:T(8,128)S(1)} %get-tuple-element.30.wz_ref, ...), custom_call_target="tpu_custom_call" | custom-call | flops 536870912 | bytes 1785856 | tf_op jit(solution)/shard_map/pallas_call | solution.py:554
  20.5 1.5 %collective-permute-start.6 = (bf16[16,512]{1,0:T(8,128)(2,1)S(1)}, bf16[16,512]{1,0:T(8,128)(2,1)S(1)}, u32[]{:S(2)}, u32[]{:S(2)}) collective-permute-start(bf16[16,512]{1,0:T(8,128)(2,1)S(1)} %get-tuple-element.35.refs_0_), channel_id=1, source_target_pairs={{0,3},{1,2},{2,1},{3,0},{4,7},{5,6},{6,5},{7,4},{8,11},{9,10},{10,... | collective-permute-start | bytes 49160 | tf_op jit(solution)/shard_map/ppermute | solution.py:27
  22.0 0.6 %collective-permute-start.7 = (bf16[16,512]{1,0:T(8,128)(2,1)S(1)}, bf16[16,512]{1,0:T(8,128)(2,1)S(1)}, u32[]{:S(2)}, u32[]{:S(2)}) collective-permute-start(bf16[16,512]{1,0:T(8,128)(2,1)S(1)} %get-tuple-element.35.refs_0_), channel_id=1, source_target_pairs={{0,2},{1,3},{2,0},{3,1},{4,6},{5,7},{6,4},{7,5},{8,10},{9,11},{10,... | collective-permute-start | bytes 49160 | tf_op jit(solution)/shard_map/ppermute | solution.py:27
  22.6 2.3 %collective-permute-start.8 = (bf16[16,512]{1,0:T(8,128)(2,1)S(1)}, bf16[16,512]{1,0:T(8,128)(2,1)S(1)}, u32[]{:S(2)}, u32[]{:S(2)}) collective-permute-start(bf16[16,512]{1,0:T(8,128)(2,1)S(1)} %get-tuple-element.35.refs_0_), channel_id=1, source_target_pairs={{0,1},{1,0},{2,3},{3,2},{4,5},{5,4},{6,7},{7,6},{8,9},{9,8},{10,11... | collective-permute-start | bytes 49160 | tf_op jit(solution)/shard_map/ppermute | solution.py:27
  24.9 1.3 %collective-permute-done.6.refs_1_ = bf16[16,512]{1,0:T(8,128)(2,1)S(1)} collective-permute-done((bf16[16,512]{1,0:T(8,128)(2,1)S(1)}, bf16[16,512]{1,0:T(8,128)(2,1)S(1)}, u32[]{:S(2)}, u32[]{:S(2)}) %collective-permute-start.6) | collective-permute-done | bytes 16416 | tf_op jit(solution)/shard_map/ppermute | solution.py:27
  26.9 1.4 %collective-permute-start.10 = (bf16[64,512]{1,0:T(8,128)(2,1)S(1)}, bf16[64,512]{1,0:T(8,128)(2,1)S(1)}, u32[]{:S(2)}, u32[]{:S(2)}) collective-permute-start(bf16[64,512]{1,0:T(8,128)(2,1)S(1)} %shard_map.90.refs_0_), channel_id=1, source_target_pairs={{0,8},{4,12},{8,0},{12,4},{1,9},{5,13},{9,1},{13,5},{2,10},{6,14},... | collective-permute-start | bytes 196616 | tf_op jit(solution)/shard_map/ppermute | solution.py:27
  28.7 1.5 %shard_map.91 = (f32[2,64,128]{2,1,0:T(8,128)S(1)}, f32[8,128,64]{2,1,0:T(8,128)S(1)}, f32[2,1024,128]{2,1,0:T(8,128)S(1)}) custom-call(f32[96,256]{1,0:T(8,128)S(1)} %shard_map.83.refs_0_, bf16[2,128,128]{2,1,0:T(8,128)(2,1)S(1)} %copy-done.1, f32[3,2,64,64]{3,2,1,0:T(8,128)S(1)} %copy-done), custom_call_target="tpu_custom_call" | custom-call | flops 134217728 | bytes 1638400 | tf_op jit(solution)/shard_map/pallas_call | solution.py:554
  30.2 1.0 %collective-permute-done.11.refs_3_ = bf16[64,512]{1,0:T(8,128)(2,1)S(1)} collective-permute-done((bf16[64,512]{1,0:T(8,128)(2,1)S(1)}, bf16[64,512]{1,0:T(8,128)(2,1)S(1)}, u32[]{:S(2)}, u32[]{:S(2)}) %collective-permute-start.11) | collective-permute-done | bytes 65568 | tf_op jit(solution)/shard_map/ppermute | solution.py:27
  31.1 1.4 %collective-permute-done.10.refs_2_ = bf16[64,512]{1,0:T(8,128)(2,1)S(1)} collective-permute-done((bf16[64,512]{1,0:T(8,128)(2,1)S(1)}, bf16[64,512]{1,0:T(8,128)(2,1)S(1)}, u32[]{:S(2)}, u32[]{:S(2)}) %collective-permute-start.10) | collective-permute-done | bytes 65568 | tf_op jit(solution)/shard_map/ppermute | solution.py:27
  32.6 1.0 %shard_map.92 = (f32[2,8,512]{2,1,0:T(8,128)S(1)}, bf16[64,512]{1,0:T(8,128)(2,1)S(1)}) custom-call(bf16[64,512]{1,0:T(8,128)(2,1)S(1)} %shard_map.90.refs_0_, bf16[64,512]{1,0:T(8,128)(2,1)S(1)} %collective-permute-done.9.refs_1_, bf16[64,512]{1,0:T(8,128)(2,1)S(1)} %collective-permute-done.10.refs_2_, bf16[64,512]{1,0:T(8,128)(2,1)S(1)} %collective-permute-done.11.refs_3_, ...), custom_call_target="tpu_custom_call" | custom-call | flops 268435456 | bytes 1998848 | tf_op jit(solution)/shard_map/pallas_call | solution.py:554
  33.8 0.4 shard_map.94.refs_5_
  34.2 0.7 %collective-permute-done.12.refs_1_ = bf16[64,512]{1,0:T(8,128)(2,1)S(1)} collective-permute-done((bf16[64,512]{1,0:T(8,128)(2,1)S(1)}, bf16[64,512]{1,0:T(8,128)(2,1)S(1)}, u32[]{:S(2)}, u32[]{:S(2)}) %collective-permute-start.12) | collective-permute-done | bytes 65568 | tf_op jit(solution)/shard_map/ppermute | solution.py:27
  35.0 0.7 %collective-permute-start.13 = (bf16[64,512]{1,0:T(8,128)(2,1)S(1)}, bf16[64,512]{1,0:T(8,128)(2,1)S(1)}, u32[]{:S(2)}, u32[]{:S(2)}) collective-permute-start(bf16[64,512]{1,0:T(8,128)(2,1)S(1)} %shard_map.93.refs_0_), channel_id=1, source_target_pairs={{0,8},{4,12},{8,0},{12,4},{1,9},{5,13},{9,1},{13,5},{2,10},{6,14},... | collective-permute-start | bytes 196616 | tf_op jit(solution)/shard_map/ppermute | solution.py:27
  35.7 1.2 %shard_map.96 = bf16[64,2,4,512]{3,2,1,0:T(4,128)(2,1)} custom-call(f32[2,8,512]{2,1,0:T(8,128)S(1)} %get-tuple-element.40.top_ref, f32[64,512]{1,0:T(8,128)S(1)} %get-tuple-element.34.wo_ref.refs_6_, bf16[128,512]{1,0:T(8,128)(2,1)S(1)} %get-tuple-element.41.both_ref, bf16[512,512]{1,0:T(8,128)(2,1)S(1)} %get-tuple-element.31.field_ref.refs_9_), custom_call_target="tpu_custom_call" | custom-call | flops 268435456 | bytes 1343488 | tf_op jit(solution)/shard_map/pallas_call | solution.py:554
  37.0 1.6 %shard_map.97.refs_6_ = f32[512,128]{1,0:T(8,128)S(1)} custom-call(bf16[64,512]{1,0:T(8,128)(2,1)S(1)} %shard_map.90.refs_0_, bf16[64,512]{1,0:T(8,128)(2,1)S(1)} %collective-permute-done.9.refs_1_, bf16[64,512]{1,0:T(8,128)(2,1)S(1)} %collective-permute-done.10.refs_2_, bf16[64,512]{1,0:T(8,128)(2,1)S(1)} %collective-permute-done.11.refs_3_, ...), custom_call_target="tpu_custom_call" | custom-call | flops 536870912 | bytes 1998848 | tf_op jit(solution)/shard_map/pallas_call | solution.py:554
  38.6 0.7 %collective-permute-done.13.refs_1_ = bf16[64,512]{1,0:T(8,128)(2,1)S(1)} collective-permute-done((bf16[64,512]{1,0:T(8,128)(2,1)S(1)}, bf16[64,512]{1,0:T(8,128)(2,1)S(1)}, u32[]{:S(2)}, u32[]{:S(2)}) %collective-permute-start.13) | collective-permute-done | bytes 65568 | tf_op jit(solution)/shard_map/ppermute | solution.py:27
  39.3 1.9 %collective-permute-start.16 = (bf16[64,512]{1,0:T(8,128)(2,1)S(1)}, bf16[64,512]{1,0:T(8,128)(2,1)S(1)}, u32[]{:S(2)}, u32[]{:S(2)}) collective-permute-start(bf16[64,512]{1,0:T(8,128)(2,1)S(1)} %shard_map.95.refs_0_), channel_id=1, source_target_pairs={{0,1},{1,0},{2,3},{3,2},{4,5},{5,4},{6,7},{7,6},{8,9},{9,8},{10,11... | collective-permute-start | bytes 196616 | tf_op jit(solution)/shard_map/ppermute | solution.py:27
  41.3 1.1 %collective-permute-start.15 = (bf16[64,512]{1,0:T(8,128)(2,1)S(1)}, bf16[64,512]{1,0:T(8,128)(2,1)S(1)}, u32[]{:S(2)}, u32[]{:S(2)}) collective-permute-start(bf16[64,512]{1,0:T(8,128)(2,1)S(1)} %shard_map.95.refs_0_), channel_id=1, source_target_pairs={{0,2},{1,3},{2,0},{3,1},{4,6},{5,7},{6,4},{7,5},{8,10},{9,11},{10,... | collective-permute-start | bytes 196616 | tf_op jit(solution)/shard_map/ppermute | solution.py:27
  42.4 1.4 %collective-permute-start.14 = (bf16[64,512]{1,0:T(8,128)(2,1)S(1)}, bf16[64,512]{1,0:T(8,128)(2,1)S(1)}, u32[]{:S(2)}, u32[]{:S(2)}) collective-permute-start(bf16[64,512]{1,0:T(8,128)(2,1)S(1)} %shard_map.95.refs_0_), channel_id=1, source_target_pairs={{0,3},{1,2},{2,1},{3,0},{4,7},{5,6},{6,5},{7,4},{8,11},{9,10},{10,... | collective-permute-start | bytes 196616 | tf_op jit(solution)/shard_map/ppermute | solution.py:27
  43.8 3.9 %collective-permute-done.15.refs_2_ = bf16[64,512]{1,0:T(8,128)(2,1)S(1)} collective-permute-done((bf16[64,512]{1,0:T(8,128)(2,1)S(1)}, bf16[64,512]{1,0:T(8,128)(2,1)S(1)}, u32[]{:S(2)}, u32[]{:S(2)}) %collective-permute-start.15) | collective-permute-done | bytes 65568 | tf_op jit(solution)/shard_map/ppermute | solution.py:27
  47.7 0.9 %collective-permute-done.14.refs_1_ = bf16[64,512]{1,0:T(8,128)(2,1)S(1)} collective-permute-done((bf16[64,512]{1,0:T(8,128)(2,1)S(1)}, bf16[64,512]{1,0:T(8,128)(2,1)S(1)}, u32[]{:S(2)}, u32[]{:S(2)}) %collective-permute-start.14) | collective-permute-done | bytes 65568 | tf_op jit(solution)/shard_map/ppermute | solution.py:27
  48.5 0.9 %shard_map.98 = bf16[64,2,4,512]{3,2,1,0:T(4,128)(2,1)} custom-call(bf16[64,512]{1,0:T(8,128)(2,1)S(1)} %shard_map.95.refs_0_, bf16[64,512]{1,0:T(8,128)(2,1)S(1)} %collective-permute-done.14.refs_1_, bf16[64,512]{1,0:T(8,128)(2,1)S(1)} %collective-permute-done.15.refs_2_, bf16[64,512]{1,0:T(8,128)(2,1)S(1)} %collective-permute-done.16.refs_3_, ...), custom_call_target="tpu_custom_call" | custom-call | bytes 2244608 | tf_op jit(solution)/shard_map/pallas_call | solution.py:554
  (32 shorter events, 1.8 us)
Async XLA Ops:
  2.2 1.4 %collective-permute-start = (f32[72,256]{1,0:T(8,128)S(1)}, f32[72,256]{1,0:T(8,128)S(1)}, u32[]{:S(2)}, u32[]{:S(2)}) collective-permute-start(f32[72,256]{1,0:T(8,128)S(1)} %get-tuple-element.27), channel_id=1, source_target_pairs={{0,4},{4,0},{8,12},{12,8},{1,5},{5,1},{9,13},{13,9},{2,6},{6,2},{1... | collective-permute-start | bytes 221192 | tf_op jit(solution)/shard_map/ppermute | solution.py:27
  3.7 10.1 %copy-start = (f32[3,2,64,64]{3,2,1,0:T(8,128)S(1)}, f32[3,2,64,64]{3,2,1,0:T(8,128)}, u32[]{:S(2)}) copy-start(f32[3,2,64,64]{3,2,1,0:T(8,128)} %refs_7_.1) | copy-start | bytes 294916
  3.7 5.4 %collective-permute-start.1 = (f32[72,256]{1,0:T(8,128)S(1)}, f32[72,256]{1,0:T(8,128)S(1)}, u32[]{:S(2)}, u32[]{:S(2)}) collective-permute-start(f32[72,256]{1,0:T(8,128)S(1)} %shard_map.78.mine_ref), channel_id=1, source_target_pairs={{0,8},{4,12},{8,0},{12,4},{1,9},{5,13},{9,1},{13,5},{2,10},{6,14},... | collective-permute-start | bytes 221192 | tf_op jit(solution)/shard_map/ppermute | solution.py:27
  9.2 4.6 %copy-start.2 = (bf16[64,64]{1,0:T(8,128)(2,1)S(1)}, bf16[64,64]{1,0:T(8,128)(2,1)}, u32[]{:S(2)}) copy-start(bf16[64,64]{1,0:T(8,128)(2,1)} %wv_ref.1) | copy-start | bytes 24580
  9.2 4.6 %copy-start.3 = (bf16[64,64]{1,0:T(8,128)(2,1)S(1)}, bf16[64,64]{1,0:T(8,128)(2,1)}, u32[]{:S(2)}) copy-start(bf16[64,64]{1,0:T(8,128)(2,1)} %wo_ref.1) | copy-start | bytes 24580
  9.2 6.1 %collective-permute-start.2 = (bf16[80,256]{1,0:T(8,128)(2,1)S(1)}, bf16[80,256]{1,0:T(8,128)(2,1)S(1)}, u32[]{:S(2)}, u32[]{:S(2)}) collective-permute-start(bf16[80,256]{1,0:T(8,128)(2,1)S(1)} %shard_map.80), channel_id=1, source_target_pairs={{0,3},{1,2},{2,1},{3,0},{4,7},{5,6},{6,5},{7,4},{8,11},{9,10},{10,... | collective-permute-start | bytes 122888 | tf_op jit(solution)/shard_map/ppermute | solution.py:27
  13.2 4.9 %collective-permute-start.3 = (bf16[80,256]{1,0:T(8,128)(2,1)S(1)}, bf16[80,256]{1,0:T(8,128)(2,1)S(1)}, u32[]{:S(2)}, u32[]{:S(2)}) collective-permute-start(bf16[80,256]{1,0:T(8,128)(2,1)S(1)} %shard_map.80), channel_id=1, source_target_pairs={{0,2},{1,3},{2,0},{3,1},{4,6},{5,7},{6,4},{7,5},{8,10},{9,11},{10,... | collective-permute-start | bytes 122888 | tf_op jit(solution)/shard_map/ppermute | solution.py:27
  13.2 4.9 %collective-permute-start.4 = (bf16[80,256]{1,0:T(8,128)(2,1)S(1)}, bf16[80,256]{1,0:T(8,128)(2,1)S(1)}, u32[]{:S(2)}, u32[]{:S(2)}) collective-permute-start(bf16[80,256]{1,0:T(8,128)(2,1)S(1)} %shard_map.80), channel_id=1, source_target_pairs={{0,1},{1,0},{2,3},{3,2},{4,5},{5,4},{6,7},{7,6},{8,9},{9,8},{10,11... | collective-permute-start | bytes 122888 | tf_op jit(solution)/shard_map/ppermute | solution.py:27
  18.1 1.3 %collective-permute-start.5 = (f32[72,256]{1,0:T(8,128)S(1)}, f32[72,256]{1,0:T(8,128)S(1)}, u32[]{:S(2)}, u32[]{:S(2)}) collective-permute-start(f32[72,256]{1,0:T(8,128)S(1)} %shard_map.86.mine_ref), channel_id=1, source_target_pairs={{0,4},{4,0},{8,12},{12,8},{1,5},{5,1},{9,13},{13,9},{2,6},{6,2},{1... | collective-permute-start | bytes 221192 | tf_op jit(solution)/shard_map/ppermute | solution.py:27
  20.5 5.8 %collective-permute-start.6 = (bf16[16,512]{1,0:T(8,128)(2,1)S(1)}, bf16[16,512]{1,0:T(8,128)(2,1)S(1)}, u32[]{:S(2)}, u32[]{:S(2)}) collective-permute-start(bf16[16,512]{1,0:T(8,128)(2,1)S(1)} %get-tuple-element.35.refs_0_), channel_id=1, source_target_pairs={{0,3},{1,2},{2,1},{3,0},{4,7},{5,6},{6,5},{7,4},{8,11},{9,10},{10,... | collective-permute-start | bytes 49160 | tf_op jit(solution)/shard_map/ppermute | solution.py:27
  22.0 4.7 %collective-permute-start.7 = (bf16[16,512]{1,0:T(8,128)(2,1)S(1)}, bf16[16,512]{1,0:T(8,128)(2,1)S(1)}, u32[]{:S(2)}, u32[]{:S(2)}) collective-permute-start(bf16[16,512]{1,0:T(8,128)(2,1)S(1)} %get-tuple-element.35.refs_0_), channel_id=1, source_target_pairs={{0,2},{1,3},{2,0},{3,1},{4,6},{5,7},{6,4},{7,5},{8,10},{9,11},{10,... | collective-permute-start | bytes 49160 | tf_op jit(solution)/shard_map/ppermute | solution.py:27
  22.6 4.2 %collective-permute-start.8 = (bf16[16,512]{1,0:T(8,128)(2,1)S(1)}, bf16[16,512]{1,0:T(8,128)(2,1)S(1)}, u32[]{:S(2)}, u32[]{:S(2)}) collective-permute-start(bf16[16,512]{1,0:T(8,128)(2,1)S(1)} %get-tuple-element.35.refs_0_), channel_id=1, source_target_pairs={{0,1},{1,0},{2,3},{3,2},{4,5},{5,4},{6,7},{7,6},{8,9},{9,8},{10,11... | collective-permute-start | bytes 49160 | tf_op jit(solution)/shard_map/ppermute | solution.py:27
  26.6 2.0 %copy-start.1 = (bf16[2,128,128]{2,1,0:T(8,128)(2,1)S(1)}, bf16[2,128,128]{2,1,0:T(8,128)(2,1)}, u32[]{:S(2)}) copy-start(bf16[2,128,128]{2,1,0:T(8,128)(2,1)} %constant.2.clone.refs_1_.refs_6_) | copy-start | bytes 196612
  26.8 4.3 %collective-permute-start.11 = (bf16[64,512]{1,0:T(8,128)(2,1)S(1)}, bf16[64,512]{1,0:T(8,128)(2,1)S(1)}, u32[]{:S(2)}, u32[]{:S(2)}) collective-permute-start(bf16[64,512]{1,0:T(8,128)(2,1)S(1)} %shard_map.90.refs_0_), channel_id=1, source_target_pairs={{0,12},{4,8},{8,4},{12,0},{1,13},{5,9},{9,5},{13,1},{2,14},{6,10},... | collective-permute-start | bytes 196616 | tf_op jit(solution)/shard_map/ppermute | solution.py:27
  26.9 5.7 %collective-permute-start.10 = (bf16[64,512]{1,0:T(8,128)(2,1)S(1)}, bf16[64,512]{1,0:T(8,128)(2,1)S(1)}, u32[]{:S(2)}, u32[]{:S(2)}) collective-permute-start(bf16[64,512]{1,0:T(8,128)(2,1)S(1)} %shard_map.90.refs_0_), channel_id=1, source_target_pairs={{0,8},{4,12},{8,0},{12,4},{1,9},{5,13},{9,1},{13,5},{2,10},{6,14},... | collective-permute-start | bytes 196616 | tf_op jit(solution)/shard_map/ppermute | solution.py:27
  28.4 4.2 %collective-permute-start.9 = (bf16[64,512]{1,0:T(8,128)(2,1)S(1)}, bf16[64,512]{1,0:T(8,128)(2,1)S(1)}, u32[]{:S(2)}, u32[]{:S(2)}) collective-permute-start(bf16[64,512]{1,0:T(8,128)(2,1)S(1)} %shard_map.90.refs_0_), channel_id=1, source_target_pairs={{0,4},{4,0},{8,12},{12,8},{1,5},{5,1},{9,13},{13,9},{2,6},{6,2},{1... | collective-permute-start | bytes 196616 | tf_op jit(solution)/shard_map/ppermute | solution.py:27
  33.6 1.3 %collective-permute-start.12 = (bf16[64,512]{1,0:T(8,128)(2,1)S(1)}, bf16[64,512]{1,0:T(8,128)(2,1)S(1)}, u32[]{:S(2)}, u32[]{:S(2)}) collective-permute-start(bf16[64,512]{1,0:T(8,128)(2,1)S(1)} %get-tuple-element.39.refs_0_), channel_id=1, source_target_pairs={{0,4},{4,0},{8,12},{12,8},{1,5},{5,1},{9,13},{13,9},{2,6},{6,2},{1... | collective-permute-start | bytes 196616 | tf_op jit(solution)/shard_map/ppermute | solution.py:27
  35.0 4.3 %collective-permute-start.13 = (bf16[64,512]{1,0:T(8,128)(2,1)S(1)}, bf16[64,512]{1,0:T(8,128)(2,1)S(1)}, u32[]{:S(2)}, u32[]{:S(2)}) collective-permute-start(bf16[64,512]{1,0:T(8,128)(2,1)S(1)} %shard_map.93.refs_0_), channel_id=1, source_target_pairs={{0,8},{4,12},{8,0},{12,4},{1,9},{5,13},{9,1},{13,5},{2,10},{6,14},... | collective-permute-start | bytes 196616 | tf_op jit(solution)/shard_map/ppermute | solution.py:27
  39.3 4.5 %collective-permute-start.16 = (bf16[64,512]{1,0:T(8,128)(2,1)S(1)}, bf16[64,512]{1,0:T(8,128)(2,1)S(1)}, u32[]{:S(2)}, u32[]{:S(2)}) collective-permute-start(bf16[64,512]{1,0:T(8,128)(2,1)S(1)} %shard_map.95.refs_0_), channel_id=1, source_target_pairs={{0,1},{1,0},{2,3},{3,2},{4,5},{5,4},{6,7},{7,6},{8,9},{9,8},{10,11... | collective-permute-start | bytes 196616 | tf_op jit(solution)/shard_map/ppermute | solution.py:27
  41.3 6.4 %collective-permute-start.15 = (bf16[64,512]{1,0:T(8,128)(2,1)S(1)}, bf16[64,512]{1,0:T(8,128)(2,1)S(1)}, u32[]{:S(2)}, u32[]{:S(2)}) collective-permute-start(bf16[64,512]{1,0:T(8,128)(2,1)S(1)} %shard_map.95.refs_0_), channel_id=1, source_target_pairs={{0,2},{1,3},{2,0},{3,1},{4,6},{5,7},{6,4},{7,5},{8,10},{9,11},{10,... | collective-permute-start | bytes 196616 | tf_op jit(solution)/shard_map/ppermute | solution.py:27
  42.4 6.2 %collective-permute-start.14 = (bf16[64,512]{1,0:T(8,128)(2,1)S(1)}, bf16[64,512]{1,0:T(8,128)(2,1)S(1)}, u32[]{:S(2)}, u32[]{:S(2)}) collective-permute-start(bf16[64,512]{1,0:T(8,128)(2,1)S(1)} %shard_map.95.refs_0_), channel_id=1, source_target_pairs={{0,3},{1,2},{2,1},{3,0},{4,7},{5,6},{6,5},{7,4},{8,11},{9,10},{10,... | collective-permute-start | bytes 196616 | tf_op jit(solution)/shard_map/ppermute | solution.py:27

commit v16 on v15

--- a/solution.py
+++ b/solution.py
@@ -404,7 +404,8 @@
 
 def mix_kernel(factor, spans, *refs):
     lows, refs = refs[:spans], refs[spans:]
-    mix_ref, wv_ref, wo_ref, wq_ref, wk_ref, field_ref, cot_ref, top_ref, out_ref = refs
+    mix_ref, wv_ref, wo_ref, wq_ref, wk_ref, field_ref, cot_ref, top_ref = refs[:8]
+    mine_ref, other_ref, half_ref = refs[8:]
     cells = field_ref.shape[0] // WIDTH
     low_f, low_c = join_low(lows, cells)
     wide = low_f.shape[1]
@@ -427,7 +428,12 @@
         return mul_left(found[:WIDTH] + found[WIDTH:], right)
 
     found = pull(wq_ref[...], left_f, cot_ref[...]) + pull(wk_ref[...], left_c, field_ref[...])
-    out_ref[...] = found.astype(jnp.bfloat16)
+    half = found.shape[1] // 2
+    half_ref[0] = found[:, :half]
+    half_ref[1] = found[:, half:]
+    core = lax.axis_index("gx") & 1
+    mine_ref[...] = half_ref[core].astype(jnp.bfloat16)
+    other_ref[...] = half_ref[core ^ 1].astype(jnp.bfloat16)
 
 
 def put_cells(ref, total):
@@ -489,14 +495,11 @@
     out_ref[...] = mul(left, keyset) + cot_ref[...].astype(jnp.float32)
 
 
-def final_kernel(places, *refs):
-    parts, refs = refs[:-6], refs[-6:]
-    feat_ref, base_ref, plane_ref, out_ref, data_ref, semaphores = refs
+def final_kernel(places, mine_ref, other_ref, feat_ref, base_ref, plane_ref, out_ref, data_ref,
+                 half_ref, semaphores):
     depth = base_ref.shape[1]
     _, rows_x, rows_y, _ = data_ref.shape
-    found = parts[0][...].astype(jnp.float32)
-    for part in parts[1:]:
-        found = found + part[...].astype(jnp.float32)
+    found = join_halves(half_ref, mine_ref, other_ref)
     normed = feat_ref[0:WIDTH, :]
     inverse = feat_ref[WIDTH : WIDTH + 1, :]
     found = inverse * (found - normed * jnp.mean(found * normed, axis=0, keepdims=True))
@@ -669,34 +672,39 @@
     (low,) = taken(stack_kernel, swaps(send, "gy", span_y), last=True)
     first, *others = swaps(low, "gx", span_x, False)
     lows = (first,) + tuple(reversed(others))
-    pulled = like((WIDTH, depth), bf16)
-    top, total = run(
+    pulled = like((WIDTH, half), bf16)
+    top, mine, other = run(
         functools.partial(mix_kernel, factor_z, span_x),
-        [like((2, cells, wide), f32), pulled],
+        [like((2, cells, wide), f32), pulled, pulled],
         lows + (mix, wv, wo, wq, wk, cols, cots),
         flops=cube,
-    )
-    total = run(add_pull_kernel, [pulled], (total, swap(total, "gx", span_x, 1)))
+        scratch=[halves],
+    )
+    total = run(add_pull_kernel, [pulled], (mine, swap(other, "gx", span_x, 1)))
     base = run(base_kernel, [like((rows, depth), f32)], (top, wv, both, cots), flops=cube)
     total, base = lax.optimization_barrier((total, base))
     for level in range(1, span_x.bit_length() - 1):
         total = run(add_pull_kernel, [pulled], (total, swap(total, "gx", span_x, 1 << level)))
-    layer_output = run(
-        output_kernel, [like(field.shape, bf16)], (top, wo, both, cols), flops=cube
-    )
     plane = run(
         functools.partial(gram_kernel, cells, lengths, factor_z),
         [like((rows, LANES), f32)],
         lows + (feat, full, same, qk_weight),
         flops=2 * cube,
     )
-    total, layer_output, plane = lax.optimization_barrier((total, layer_output, plane))
+    total, plane = lax.optimization_barrier((total, plane))
+    layer_output = run(
+        output_kernel, [like(field.shape, bf16)], (top, wo, both, cols), flops=cube
+    )
+    total = run(
+        add_pull_kernel, [like(pulled.shape, f32)], swaps(total, "gy", span_y, False)
+    )
+    total, layer_output = lax.optimization_barrier((total, layer_output))
     field_grad = run(
         functools.partial(final_kernel, grid_x * grid_y),
         [like(field.shape, bf16)],
-        swaps(total, "gy", span_y, False) + (feat_z, base, plane),
+        (total, swap(total, "gx", span_x, 1), feat_z, base, plane),
         target=pltpu.HBM,
-        scratch=chunked,
+        scratch=[chunked[0], halves, chunked[1]],
     )
     return (layer_output, field_grad)
 

time: 49.7 us -> 50.2 us (1.010)
    ppermute x17 -> x18, waiting for transfers between devices: 18 us -> 18.4 us  [swap(): return lax.ppermute(part, axis, [(i, i ^ step) for i in range(size)])]
    ppermute x17 -> x18, starting transfers between devices: 19.7 us -> 19.7 us  [swap(): return lax.ppermute(part, axis, [(i, i ^ step) for i in range(size)])]
    pallas_call x22 -> x23, Pallas kernels: 11 us -> 11.1 us  [run(): pl.pallas_call(kernel, out_shape=tuple(outs), in_specs=[pl.BlockSpec(memo...]
  transfers between devices with their start and end apart: 17 -> 18, of which waited for: 14 -> 15; matrix products, arithmetic and copies ran while one was open for 0% -> 0% of each run, Pallas kernels for 13% -> 13%
where the time goes in v16:
time: 50.2 us; the launch traced here: 50 us
  starting transfers between devices  19.7 us (39%)
  waiting for transfers between devices  18.4 us (37%)
  Pallas kernels  11.1 us (22%)
  between operations  0.79 us (2%)
    ppermute x18, starting transfers between devices, swap(): return lax.ppermute(part, axis, [(i, i ^ step) for i in range(size)])  19.7 us
    ppermute x18, waiting for transfers between devices, swap(): return lax.ppermute(part, axis, [(i, i ^ step) for i in range(size)])  18.4 us
    pallas_call x23, Pallas kernels, run(): pl.pallas_call(kernel, out_shape=tuple(outs), in_specs=[pl.BlockSpec(memo...  11.1 us
  transfers between devices with their start and end apart: 18, of which 15 were waited for; matrix products, arithmetic and copies ran while one was open for 0% of the time, Pallas kernels for 13%

profile of v16, /device:TPU:0, one launch (start us, length us, event | category | flops | bytes accessed | tf_op | source)
XLA Modules:
  0.0 50.0 jit_solution(8320522772868527056)
XLA Ops:
  0.6 1.6 %shard_map.77 = (f32[72,256]{1,0:T(8,128)S(1)}, f32[72,256]{1,0:T(8,128)S(1)}, bf16[512,512]{1,0:T(8,128)(2,1)S(1)}) custom-call(bf16[64,2,4,512]{3,2,1,0:T(4,128)(2,1)} %field_ref.1), custom_call_target="tpu_custom_call" | custom-call | flops 67108864 | bytes 1196032 | tf_op jit(solution)/shard_map/pallas_call | solution.py:557
  2.2 0.5 %collective-permute-start = (f32[72,256]{1,0:T(8,128)S(1)}, f32[72,256]{1,0:T(8,128)S(1)}, u32[]{:S(2)}, u32[]{:S(2)}) collective-permute-start(f32[72,256]{1,0:T(8,128)S(1)} %get-tuple-element.29), channel_id=1, source_target_pairs={{0,4},{4,0},{8,12},{12,8},{1,5},{5,1},{9,13},{13,9},{2,6},{6,2},{1... | collective-permute-start | bytes 221192 | tf_op jit(solution)/shard_map/ppermute | solution.py:27
  2.7 0.9 %collective-permute-done.other_ref = f32[72,256]{1,0:T(8,128)S(1)} collective-permute-done((f32[72,256]{1,0:T(8,128)S(1)}, f32[72,256]{1,0:T(8,128)S(1)}, u32[]{:S(2)}, u32[]{:S(2)}) %collective-permute-start) | collective-permute-done | bytes 73760 | tf_op jit(solution)/shard_map/ppermute | solution.py:27
  3.7 2.9 %collective-permute-start.1 = (f32[72,256]{1,0:T(8,128)S(1)}, f32[72,256]{1,0:T(8,128)S(1)}, u32[]{:S(2)}, u32[]{:S(2)}) collective-permute-start(f32[72,256]{1,0:T(8,128)S(1)} %shard_map.78.mine_ref), channel_id=1, source_target_pairs={{0,8},{4,12},{8,0},{12,4},{1,9},{5,13},{9,1},{13,5},{2,10},{6,14},... | collective-permute-start | bytes 221192 | tf_op jit(solution)/shard_map/ppermute | solution.py:27
  6.6 2.6 %collective-permute-done.1.other_ref = f32[72,256]{1,0:T(8,128)S(1)} collective-permute-done((f32[72,256]{1,0:T(8,128)S(1)}, f32[72,256]{1,0:T(8,128)S(1)}, u32[]{:S(2)}, u32[]{:S(2)}) %collective-permute-start.1) | collective-permute-done | bytes 73760 | tf_op jit(solution)/shard_map/ppermute | solution.py:27
  9.2 3.9 %collective-permute-start.2 = (bf16[80,256]{1,0:T(8,128)(2,1)S(1)}, bf16[80,256]{1,0:T(8,128)(2,1)S(1)}, u32[]{:S(2)}, u32[]{:S(2)}) collective-permute-start(bf16[80,256]{1,0:T(8,128)(2,1)S(1)} %shard_map.80), channel_id=1, source_target_pairs={{0,3},{1,2},{2,1},{3,0},{4,7},{5,6},{6,5},{7,4},{8,11},{9,10},{10,... | collective-permute-start | bytes 122888 | tf_op jit(solution)/shard_map/ppermute | solution.py:27
  13.2 0.6 %collective-permute-start.4 = (bf16[80,256]{1,0:T(8,128)(2,1)S(1)}, bf16[80,256]{1,0:T(8,128)(2,1)S(1)}, u32[]{:S(2)}, u32[]{:S(2)}) collective-permute-start(bf16[80,256]{1,0:T(8,128)(2,1)S(1)} %shard_map.80), channel_id=1, source_target_pairs={{0,1},{1,0},{2,3},{3,2},{4,5},{5,4},{6,7},{7,6},{8,9},{9,8},{10,11... | collective-permute-start | bytes 122888 | tf_op jit(solution)/shard_map/ppermute | solution.py:27
  14.1 1.2 %shard_map.84.cot_ref.refs_10_ = bf16[512,512]{1,0:T(8,128)(2,1)S(1)} custom-call(bf16[64,2,4,512]{3,2,1,0:T(4,128)(2,1)} %cot_ref.1), custom_call_target="tpu_custom_call" | custom-call | flops 268435456 | bytes 1048576 | tf_op jit(solution)/shard_map/pallas_call | solution.py:557
  15.4 2.7 %collective-permute-done.3.part_ref = bf16[80,256]{1,0:T(8,128)(2,1)S(1)} collective-permute-done((bf16[80,256]{1,0:T(8,128)(2,1)S(1)}, bf16[80,256]{1,0:T(8,128)(2,1)S(1)}, u32[]{:S(2)}, u32[]{:S(2)}) %collective-permute-start.3) | collective-permute-done | bytes 40992 | tf_op jit(solution)/shard_map/ppermute | solution.py:27
  18.2 1.3 %collective-permute-done.5.other_ref = f32[72,256]{1,0:T(8,128)S(1)} collective-permute-done((f32[72,256]{1,0:T(8,128)S(1)}, f32[72,256]{1,0:T(8,128)S(1)}, u32[]{:S(2)}, u32[]{:S(2)}) %collective-permute-start.5) | collective-permute-done | bytes 73760 | tf_op jit(solution)/shard_map/ppermute | solution.py:27
  19.5 1.0 %shard_map.87 = (bf16[16,512]{1,0:T(8,128)(2,1)S(1)}, bf16[128,512]{1,0:T(8,128)(2,1)S(1)}, f32[72,512]{1,0:T(8,128)S(1)}) custom-call(f32[72,256]{1,0:T(8,128)S(1)} %shard_map.86.mine_ref, f32[72,256]{1,0:T(8,128)S(1)} %collective-permute-done.5.other_ref, f32[128,64]{1,0:T(8,128)S(1)} %get-tuple-element.32.wz_ref, ...), custom_call_target="tpu_custom_call" | custom-call | flops 536870912 | bytes 1785856 | tf_op jit(solution)/shard_map/pallas_call | solution.py:557
  20.5 1.5 %collective-permute-start.6 = (bf16[16,512]{1,0:T(8,128)(2,1)S(1)}, bf16[16,512]{1,0:T(8,128)(2,1)S(1)}, u32[]{:S(2)}, u32[]{:S(2)}) collective-permute-start(bf16[16,512]{1,0:T(8,128)(2,1)S(1)} %get-tuple-element.37.refs_0_), channel_id=1, source_target_pairs={{0,3},{1,2},{2,1},{3,0},{4,7},{5,6},{6,5},{7,4},{8,11},{9,10},{10,... | collective-permute-start | bytes 49160 | tf_op jit(solution)/shard_map/ppermute | solution.py:27
  22.0 0.6 %collective-permute-start.7 = (bf16[16,512]{1,0:T(8,128)(2,1)S(1)}, bf16[16,512]{1,0:T(8,128)(2,1)S(1)}, u32[]{:S(2)}, u32[]{:S(2)}) collective-permute-start(bf16[16,512]{1,0:T(8,128)(2,1)S(1)} %get-tuple-element.37.refs_0_), channel_id=1, source_target_pairs={{0,2},{1,3},{2,0},{3,1},{4,6},{5,7},{6,4},{7,5},{8,10},{9,11},{10,... | collective-permute-start | bytes 49160 | tf_op jit(solution)/shard_map/ppermute | solution.py:27
  22.6 2.3 %collective-permute-start.8 = (bf16[16,512]{1,0:T(8,128)(2,1)S(1)}, bf16[16,512]{1,0:T(8,128)(2,1)S(1)}, u32[]{:S(2)}, u32[]{:S(2)}) collective-permute-start(bf16[16,512]{1,0:T(8,128)(2,1)S(1)} %get-tuple-element.37.refs_0_), channel_id=1, source_target_pairs={{0,1},{1,0},{2,3},{3,2},{4,5},{5,4},{6,7},{7,6},{8,9},{9,8},{10,11... | collective-permute-start | bytes 49160 | tf_op jit(solution)/shard_map/ppermute | solution.py:27
  24.9 1.3 %collective-permute-done.6.refs_1_ = bf16[16,512]{1,0:T(8,128)(2,1)S(1)} collective-permute-done((bf16[16,512]{1,0:T(8,128)(2,1)S(1)}, bf16[16,512]{1,0:T(8,128)(2,1)S(1)}, u32[]{:S(2)}, u32[]{:S(2)}) %collective-permute-start.6) | collective-permute-done | bytes 16416 | tf_op jit(solution)/shard_map/ppermute | solution.py:27
  26.9 1.4 %collective-permute-start.10 = (bf16[64,512]{1,0:T(8,128)(2,1)S(1)}, bf16[64,512]{1,0:T(8,128)(2,1)S(1)}, u32[]{:S(2)}, u32[]{:S(2)}) collective-permute-start(bf16[64,512]{1,0:T(8,128)(2,1)S(1)} %shard_map.90.refs_0_), channel_id=1, source_target_pairs={{0,8},{4,12},{8,0},{12,4},{1,9},{5,13},{9,1},{13,5},{2,10},{6,14},... | collective-permute-start | bytes 196616 | tf_op jit(solution)/shard_map/ppermute | solution.py:27
  28.7 1.5 %shard_map.91 = (f32[2,64,128]{2,1,0:T(8,128)S(1)}, f32[8,128,64]{2,1,0:T(8,128)S(1)}, f32[2,1024,128]{2,1,0:T(8,128)S(1)}) custom-call(f32[96,256]{1,0:T(8,128)S(1)} %shard_map.83.refs_0_, bf16[2,128,128]{2,1,0:T(8,128)(2,1)S(1)} %copy-done.1, f32[3,2,64,64]{3,2,1,0:T(8,128)S(1)} %copy-done), custom_call_target="tpu_custom_call" | custom-call | flops 134217728 | bytes 1638400 | tf_op jit(solution)/shard_map/pallas_call | solution.py:557
  30.2 1.0 %collective-permute-done.11.refs_3_ = bf16[64,512]{1,0:T(8,128)(2,1)S(1)} collective-permute-done((bf16[64,512]{1,0:T(8,128)(2,1)S(1)}, bf16[64,512]{1,0:T(8,128)(2,1)S(1)}, u32[]{:S(2)}, u32[]{:S(2)}) %collective-permute-start.11) | collective-permute-done | bytes 65568 | tf_op jit(solution)/shard_map/ppermute | solution.py:27
  31.1 1.4 %collective-permute-done.10.refs_2_ = bf16[64,512]{1,0:T(8,128)(2,1)S(1)} collective-permute-done((bf16[64,512]{1,0:T(8,128)(2,1)S(1)}, bf16[64,512]{1,0:T(8,128)(2,1)S(1)}, u32[]{:S(2)}, u32[]{:S(2)}) %collective-permute-start.10) | collective-permute-done | bytes 65568 | tf_op jit(solution)/shard_map/ppermute | solution.py:27
  32.6 1.1 %shard_map.92 = (f32[2,8,512]{2,1,0:T(8,128)S(1)}, bf16[64,256]{1,0:T(8,128)(2,1)S(1)}, bf16[64,256]{1,0:T(8,128)(2,1)S(1)}) custom-call(bf16[64,512]{1,0:T(8,128)(2,1)S(1)} %shard_map.90.refs_0_, bf16[64,512]{1,0:T(8,128)(2,1)S(1)} %collective-permute-done.9.refs_1_, bf16[64,512]{1,0:T(8,128)(2,1)S(1)} %collective-permute-done.10.refs_2_, ...), custom_call_target="tpu_custom_call" | custom-call | flops 268435456 | bytes 1998848 | tf_op jit(solution)/shard_map/pallas_call | solution.py:557
  34.3 0.7 %collective-permute-done.12.refs_1_ = bf16[64,256]{1,0:T(8,128)(2,1)S(1)} collective-permute-done((bf16[64,256]{1,0:T(8,128)(2,1)S(1)}, bf16[64,256]{1,0:T(8,128)(2,1)S(1)}, u32[]{:S(2)}, u32[]{:S(2)}) %collective-permute-start.12) | collective-permute-done | bytes 32800 | tf_op jit(solution)/shard_map/ppermute | solution.py:27
  35.0 0.7 %collective-permute-start.13 = (bf16[64,256]{1,0:T(8,128)(2,1)S(1)}, bf16[64,256]{1,0:T(8,128)(2,1)S(1)}, u32[]{:S(2)}, u32[]{:S(2)}) collective-permute-start(bf16[64,256]{1,0:T(8,128)(2,1)S(1)} %shard_map.93.refs_0_), channel_id=1, source_target_pairs={{0,8},{4,12},{8,0},{12,4},{1,9},{5,13},{9,1},{13,5},{2,10},{6,14},... | collective-permute-start | bytes 98312 | tf_op jit(solution)/shard_map/ppermute | solution.py:27
  35.7 1.6 %shard_map.96.plane_ref = f32[512,128]{1,0:T(8,128)S(1)} custom-call(bf16[64,512]{1,0:T(8,128)(2,1)S(1)} %shard_map.90.refs_0_, bf16[64,512]{1,0:T(8,128)(2,1)S(1)} %collective-permute-done.9.refs_1_, bf16[64,512]{1,0:T(8,128)(2,1)S(1)} %collective-permute-done.10.refs_2_, bf16[64,512]{1,0:T(8,128)(2,1)S(1)} %collective-permute-done.11.refs_3_, ...), custom_call_target="tpu_custom_call" | custom-call | flops 536870912 | bytes 1998848 | tf_op jit(solution)/shard_map/pallas_call | solution.py:557
  37.3 1.6 %collective-permute-done.13.refs_1_ = bf16[64,256]{1,0:T(8,128)(2,1)S(1)} collective-permute-done((bf16[64,256]{1,0:T(8,128)(2,1)S(1)}, bf16[64,256]{1,0:T(8,128)(2,1)S(1)}, u32[]{:S(2)}, u32[]{:S(2)}) %collective-permute-start.13) | collective-permute-done | bytes 32800 | tf_op jit(solution)/shard_map/ppermute | solution.py:27
  39.0 1.9 %collective-permute-start.16 = (bf16[64,256]{1,0:T(8,128)(2,1)S(1)}, bf16[64,256]{1,0:T(8,128)(2,1)S(1)}, u32[]{:S(2)}, u32[]{:S(2)}) collective-permute-start(bf16[64,256]{1,0:T(8,128)(2,1)S(1)} %shard_map.95.refs_0_), channel_id=1, source_target_pairs={{0,1},{1,0},{2,3},{3,2},{4,5},{5,4},{6,7},{7,6},{8,9},{9,8},{10,11... | collective-permute-start | bytes 98312 | tf_op jit(solution)/shard_map/ppermute | solution.py:27
  40.9 1.1 %collective-permute-start.15 = (bf16[64,256]{1,0:T(8,128)(2,1)S(1)}, bf16[64,256]{1,0:T(8,128)(2,1)S(1)}, u32[]{:S(2)}, u32[]{:S(2)}) collective-permute-start(bf16[64,256]{1,0:T(8,128)(2,1)S(1)} %shard_map.95.refs_0_), channel_id=1, source_target_pairs={{0,2},{1,3},{2,0},{3,1},{4,6},{5,7},{6,4},{7,5},{8,10},{9,11},{10,... | collective-permute-start | bytes 98312 | tf_op jit(solution)/shard_map/ppermute | solution.py:27
  42.0 1.4 %collective-permute-start.14 = (bf16[64,256]{1,0:T(8,128)(2,1)S(1)}, bf16[64,256]{1,0:T(8,128)(2,1)S(1)}, u32[]{:S(2)}, u32[]{:S(2)}) collective-permute-start(bf16[64,256]{1,0:T(8,128)(2,1)S(1)} %shard_map.95.refs_0_), channel_id=1, source_target_pairs={{0,3},{1,2},{2,1},{3,0},{4,7},{5,6},{6,5},{7,4},{8,11},{9,10},{10,... | collective-permute-start | bytes 98312 | tf_op jit(solution)/shard_map/ppermute | solution.py:27
  43.4 1.3 %shard_map.98 = bf16[64,2,4,512]{3,2,1,0:T(4,128)(2,1)} custom-call(f32[2,8,512]{2,1,0:T(8,128)S(1)} %get-tuple-element.43.top_ref, f32[64,512]{1,0:T(8,128)S(1)} %get-tuple-element.36.wo_ref.refs_6_, bf16[128,512]{1,0:T(8,128)(2,1)S(1)} %get-tuple-element.44.both_ref, bf16[512,512]{1,0:T(8,128)(2,1)S(1)} %get-tuple-element.33.field_ref.refs_9_), custom_call_target="tpu_custom_call" | custom-call | flops 268435456 | bytes 1343488 | tf_op jit(solution)/shard_map/pallas_call | solution.py:557
  44.7 1.2 %collective-permute-done.15.refs_2_ = bf16[64,256]{1,0:T(8,128)(2,1)S(1)} collective-permute-done((bf16[64,256]{1,0:T(8,128)(2,1)S(1)}, bf16[64,256]{1,0:T(8,128)(2,1)S(1)}, u32[]{:S(2)}, u32[]{:S(2)}) %collective-permute-start.15) | collective-permute-done | bytes 32800 | tf_op jit(solution)/shard_map/ppermute | solution.py:27
  45.9 1.8 %collective-permute-done.14.refs_1_ = bf16[64,256]{1,0:T(8,128)(2,1)S(1)} collective-permute-done((bf16[64,256]{1,0:T(8,128)(2,1)S(1)}, bf16[64,256]{1,0:T(8,128)(2,1)S(1)}, u32[]{:S(2)}, u32[]{:S(2)}) %collective-permute-start.14) | collective-permute-done | bytes 32800 | tf_op jit(solution)/shard_map/ppermute | solution.py:27
  47.8 1.2 %collective-permute-done.17.other_ref = f32[64,256]{1,0:T(8,128)S(1)} collective-permute-done((f32[64,256]{1,0:T(8,128)S(1)}, f32[64,256]{1,0:T(8,128)S(1)}, u32[]{:S(2)}, u32[]{:S(2)}) %collective-permute-start.17) | collective-permute-done | bytes 65568 | tf_op jit(solution)/shard_map/ppermute | solution.py:27
  49.0 1.0 %shard_map.99 = bf16[64,2,4,512]{3,2,1,0:T(4,128)(2,1)} custom-call(f32[64,256]{1,0:T(8,128)S(1)} %shard_map.97.mine_ref, f32[64,256]{1,0:T(8,128)S(1)} %collective-permute-done.17.other_ref, f32[72,512]{1,0:T(8,128)S(1)} %get-tuple-element.51.feat_ref, f32[512,512]{1,0:T(8,128)S(1)} %shard_map.94.base_ref, f32[512,128]{1,0:T(8,128)S(1)} %shard_map.96.plane_ref), custom_call_target="tpu_custom_call" | custom-call | bytes 2113536 | tf_op jit(solution)/shard_map/pallas_call | solution.py:557
  (35 shorter events, 2.3 us)
Async XLA Ops:
  2.2 1.4 %collective-permute-start = (f32[72,256]{1,0:T(8,128)S(1)}, f32[72,256]{1,0:T(8,128)S(1)}, u32[]{:S(2)}, u32[]{:S(2)}) collective-permute-start(f32[72,256]{1,0:T(8,128)S(1)} %get-tuple-element.29), channel_id=1, source_target_pairs={{0,4},{4,0},{8,12},{12,8},{1,5},{5,1},{9,13},{13,9},{2,6},{6,2},{1... | collective-permute-start | bytes 221192 | tf_op jit(solution)/shard_map/ppermute | solution.py:27
  3.7 10.1 %copy-start = (f32[3,2,64,64]{3,2,1,0:T(8,128)S(1)}, f32[3,2,64,64]{3,2,1,0:T(8,128)}, u32[]{:S(2)}) copy-start(f32[3,2,64,64]{3,2,1,0:T(8,128)} %refs_7_.1) | copy-start | bytes 294916
  3.7 5.4 %collective-permute-start.1 = (f32[72,256]{1,0:T(8,128)S(1)}, f32[72,256]{1,0:T(8,128)S(1)}, u32[]{:S(2)}, u32[]{:S(2)}) collective-permute-start(f32[72,256]{1,0:T(8,128)S(1)} %shard_map.78.mine_ref), channel_id=1, source_target_pairs={{0,8},{4,12},{8,0},{12,4},{1,9},{5,13},{9,1},{13,5},{2,10},{6,14},... | collective-permute-start | bytes 221192 | tf_op jit(solution)/shard_map/ppermute | solution.py:27
  9.2 4.6 %copy-start.2 = (bf16[64,64]{1,0:T(8,128)(2,1)S(1)}, bf16[64,64]{1,0:T(8,128)(2,1)}, u32[]{:S(2)}) copy-start(bf16[64,64]{1,0:T(8,128)(2,1)} %wv_ref.1) | copy-start | bytes 24580
  9.2 4.6 %copy-start.3 = (bf16[64,64]{1,0:T(8,128)(2,1)S(1)}, bf16[64,64]{1,0:T(8,128)(2,1)}, u32[]{:S(2)}) copy-start(bf16[64,64]{1,0:T(8,128)(2,1)} %wo_ref.1) | copy-start | bytes 24580
  9.2 6.1 %collective-permute-start.2 = (bf16[80,256]{1,0:T(8,128)(2,1)S(1)}, bf16[80,256]{1,0:T(8,128)(2,1)S(1)}, u32[]{:S(2)}, u32[]{:S(2)}) collective-permute-start(bf16[80,256]{1,0:T(8,128)(2,1)S(1)} %shard_map.80), channel_id=1, source_target_pairs={{0,3},{1,2},{2,1},{3,0},{4,7},{5,6},{6,5},{7,4},{8,11},{9,10},{10,... | collective-permute-start | bytes 122888 | tf_op jit(solution)/shard_map/ppermute | solution.py:27
  13.2 4.9 %collective-permute-start.3 = (bf16[80,256]{1,0:T(8,128)(2,1)S(1)}, bf16[80,256]{1,0:T(8,128)(2,1)S(1)}, u32[]{:S(2)}, u32[]{:S(2)}) collective-permute-start(bf16[80,256]{1,0:T(8,128)(2,1)S(1)} %shard_map.80), channel_id=1, source_target_pairs={{0,2},{1,3},{2,0},{3,1},{4,6},{5,7},{6,4},{7,5},{8,10},{9,11},{10,... | collective-permute-start | bytes 122888 | tf_op jit(solution)/shard_map/ppermute | solution.py:27
  13.2 4.9 %collective-permute-start.4 = (bf16[80,256]{1,0:T(8,128)(2,1)S(1)}, bf16[80,256]{1,0:T(8,128)(2,1)S(1)}, u32[]{:S(2)}, u32[]{:S(2)}) collective-permute-start(bf16[80,256]{1,0:T(8,128)(2,1)S(1)} %shard_map.80), channel_id=1, source_target_pairs={{0,1},{1,0},{2,3},{3,2},{4,5},{5,4},{6,7},{7,6},{8,9},{9,8},{10,11... | collective-permute-start | bytes 122888 | tf_op jit(solution)/shard_map/ppermute | solution.py:27
  18.1 1.3 %collective-permute-start.5 = (f32[72,256]{1,0:T(8,128)S(1)}, f32[72,256]{1,0:T(8,128)S(1)}, u32[]{:S(2)}, u32[]{:S(2)}) collective-permute-start(f32[72,256]{1,0:T(8,128)S(1)} %shard_map.86.mine_ref), channel_id=1, source_target_pairs={{0,4},{4,0},{8,12},{12,8},{1,5},{5,1},{9,13},{13,9},{2,6},{6,2},{1... | collective-permute-start | bytes 221192 | tf_op jit(solution)/shard_map/ppermute | solution.py:27
  20.5 5.8 %collective-permute-start.6 = (bf16[16,512]{1,0:T(8,128)(2,1)S(1)}, bf16[16,512]{1,0:T(8,128)(2,1)S(1)}, u32[]{:S(2)}, u32[]{:S(2)}) collective-permute-start(bf16[16,512]{1,0:T(8,128)(2,1)S(1)} %get-tuple-element.37.refs_0_), channel_id=1, source_target_pairs={{0,3},{1,2},{2,1},{3,0},{4,7},{5,6},{6,5},{7,4},{8,11},{9,10},{10,... | collective-permute-start | bytes 49160 | tf_op jit(solution)/shard_map/ppermute | solution.py:27
  22.0 4.7 %collective-permute-start.7 = (bf16[16,512]{1,0:T(8,128)(2,1)S(1)}, bf16[16,512]{1,0:T(8,128)(2,1)S(1)}, u32[]{:S(2)}, u32[]{:S(2)}) collective-permute-start(bf16[16,512]{1,0:T(8,128)(2,1)S(1)} %get-tuple-element.37.refs_0_), channel_id=1, source_target_pairs={{0,2},{1,3},{2,0},{3,1},{4,6},{5,7},{6,4},{7,5},{8,10},{9,11},{10,... | collective-permute-start | bytes 49160 | tf_op jit(solution)/shard_map/ppermute | solution.py:27
  22.6 4.2 %collective-permute-start.8 = (bf16[16,512]{1,0:T(8,128)(2,1)S(1)}, bf16[16,512]{1,0:T(8,128)(2,1)S(1)}, u32[]{:S(2)}, u32[]{:S(2)}) collective-permute-start(bf16[16,512]{1,0:T(8,128)(2,1)S(1)} %get-tuple-element.37.refs_0_), channel_id=1, source_target_pairs={{0,1},{1,0},{2,3},{3,2},{4,5},{5,4},{6,7},{7,6},{8,9},{9,8},{10,11... | collective-permute-start | bytes 49160 | tf_op jit(solution)/shard_map/ppermute | solution.py:27
  26.6 2.0 %copy-start.1 = (bf16[2,128,128]{2,1,0:T(8,128)(2,1)S(1)}, bf16[2,128,128]{2,1,0:T(8,128)(2,1)}, u32[]{:S(2)}) copy-start(bf16[2,128,128]{2,1,0:T(8,128)(2,1)} %constant.2.clone.refs_1_.refs_6_) | copy-start | bytes 196612
  26.8 4.3 %collective-permute-start.11 = (bf16[64,512]{1,0:T(8,128)(2,1)S(1)}, bf16[64,512]{1,0:T(8,128)(2,1)S(1)}, u32[]{:S(2)}, u32[]{:S(2)}) collective-permute-start(bf16[64,512]{1,0:T(8,128)(2,1)S(1)} %shard_map.90.refs_0_), channel_id=1, source_target_pairs={{0,12},{4,8},{8,4},{12,0},{1,13},{5,9},{9,5},{13,1},{2,14},{6,10},... | collective-permute-start | bytes 196616 | tf_op jit(solution)/shard_map/ppermute | solution.py:27
  26.9 5.7 %collective-permute-start.10 = (bf16[64,512]{1,0:T(8,128)(2,1)S(1)}, bf16[64,512]{1,0:T(8,128)(2,1)S(1)}, u32[]{:S(2)}, u32[]{:S(2)}) collective-permute-start(bf16[64,512]{1,0:T(8,128)(2,1)S(1)} %shard_map.90.refs_0_), channel_id=1, source_target_pairs={{0,8},{4,12},{8,0},{12,4},{1,9},{5,13},{9,1},{13,5},{2,10},{6,14},... | collective-permute-start | bytes 196616 | tf_op jit(solution)/shard_map/ppermute | solution.py:27
  28.4 4.2 %collective-permute-start.9 = (bf16[64,512]{1,0:T(8,128)(2,1)S(1)}, bf16[64,512]{1,0:T(8,128)(2,1)S(1)}, u32[]{:S(2)}, u32[]{:S(2)}) collective-permute-start(bf16[64,512]{1,0:T(8,128)(2,1)S(1)} %shard_map.90.refs_0_), channel_id=1, source_target_pairs={{0,4},{4,0},{8,12},{12,8},{1,5},{5,1},{9,13},{13,9},{2,6},{6,2},{1... | collective-permute-start | bytes 196616 | tf_op jit(solution)/shard_map/ppermute | solution.py:27
  33.7 1.3 %collective-permute-start.12 = (bf16[64,256]{1,0:T(8,128)(2,1)S(1)}, bf16[64,256]{1,0:T(8,128)(2,1)S(1)}, u32[]{:S(2)}, u32[]{:S(2)}) collective-permute-start(bf16[64,256]{1,0:T(8,128)(2,1)S(1)} %get-tuple-element.42), channel_id=1, source_target_pairs={{0,4},{4,0},{8,12},{12,8},{1,5},{5,1},{9,13},{13,9},{2,6},{6,2},{1... | collective-permute-start | bytes 98312 | tf_op jit(solution)/shard_map/ppermute | solution.py:27
  35.0 4.0 %collective-permute-start.13 = (bf16[64,256]{1,0:T(8,128)(2,1)S(1)}, bf16[64,256]{1,0:T(8,128)(2,1)S(1)}, u32[]{:S(2)}, u32[]{:S(2)}) collective-permute-start(bf16[64,256]{1,0:T(8,128)(2,1)S(1)} %shard_map.93.refs_0_), channel_id=1, source_target_pairs={{0,8},{4,12},{8,0},{12,4},{1,9},{5,13},{9,1},{13,5},{2,10},{6,14},... | collective-permute-start | bytes 98312 | tf_op jit(solution)/shard_map/ppermute | solution.py:27
  39.0 5.7 %collective-permute-start.16 = (bf16[64,256]{1,0:T(8,128)(2,1)S(1)}, bf16[64,256]{1,0:T(8,128)(2,1)S(1)}, u32[]{:S(2)}, u32[]{:S(2)}) collective-permute-start(bf16[64,256]{1,0:T(8,128)(2,1)S(1)} %shard_map.95.refs_0_), channel_id=1, source_target_pairs={{0,1},{1,0},{2,3},{3,2},{4,5},{5,4},{6,7},{7,6},{8,9},{9,8},{10,11... | collective-permute-start | bytes 98312 | tf_op jit(solution)/shard_map/ppermute | solution.py:27
  40.9 5.0 %collective-permute-start.15 = (bf16[64,256]{1,0:T(8,128)(2,1)S(1)}, bf16[64,256]{1,0:T(8,128)(2,1)S(1)}, u32[]{:S(2)}, u32[]{:S(2)}) collective-permute-start(bf16[64,256]{1,0:T(8,128)(2,1)S(1)} %shard_map.95.refs_0_), channel_id=1, source_target_pairs={{0,2},{1,3},{2,0},{3,1},{4,6},{5,7},{6,4},{7,5},{8,10},{9,11},{10,... | collective-permute-start | bytes 98312 | tf_op jit(solution)/shard_map/ppermute | solution.py:27
  42.0 5.7 %collective-permute-start.14 = (bf16[64,256]{1,0:T(8,128)(2,1)S(1)}, bf16[64,256]{1,0:T(8,128)(2,1)S(1)}, u32[]{:S(2)}, u32[]{:S(2)}) collective-permute-start(bf16[64,256]{1,0:T(8,128)(2,1)S(1)} %shard_map.95.refs_0_), channel_id=1, source_target_pairs={{0,3},{1,2},{2,1},{3,0},{4,7},{5,6},{6,5},{7,4},{8,11},{9,10},{10,... | collective-permute-start | bytes 98312 | tf_op jit(solution)/shard_map/ppermute | solution.py:27
  47.7 1.3 %collective-permute-start.17 = (f32[64,256]{1,0:T(8,128)S(1)}, f32[64,256]{1,0:T(8,128)S(1)}, u32[]{:S(2)}, u32[]{:S(2)}) collective-permute-start(f32[64,256]{1,0:T(8,128)S(1)} %shard_map.97.mine_ref), channel_id=1, source_target_pairs={{0,4},{4,0},{8,12},{12,8},{1,5},{5,1},{9,13},{13,9},{2,6},{6,2},{1... | collective-permute-start | bytes 196616 | tf_op jit(solution)/shard_map/ppermute | solution.py:27

commit v17 on v15

--- a/solution.py
+++ b/solution.py
@@ -483,15 +483,17 @@
     out_ref[...] = mul_left(own.reshape(-1, WIDTH), jnp.ones((WIDTH, LANES), jnp.bfloat16))
 
 
-def base_kernel(top_ref, wv_ref, both_ref, cot_ref, out_ref):
+def base_kernel(top_ref, wv_ref, both_ref, cot_ref, plane_ref, out_ref):
     keyset = expand(both_ref[...].astype(jnp.float32)[WIDTH:])
     left = spread(wv_ref[...], top_ref[1])
-    out_ref[...] = mul(left, keyset) + cot_ref[...].astype(jnp.float32)
+    found = mul(left, keyset) + cot_ref[...].astype(jnp.float32)
+    columns = found.shape[1] // LANES
+    out_ref[...] = found + jnp.concatenate([plane_ref[...]] * columns, axis=1)
 
 
 def final_kernel(places, *refs):
-    parts, refs = refs[:-6], refs[-6:]
-    feat_ref, base_ref, plane_ref, out_ref, data_ref, semaphores = refs
+    parts, refs = refs[:-5], refs[-5:]
+    feat_ref, base_ref, out_ref, data_ref, semaphores = refs
     depth = base_ref.shape[1]
     _, rows_x, rows_y, _ = data_ref.shape
     found = parts[0][...].astype(jnp.float32)
@@ -508,8 +510,6 @@
     for index in range(chunks):
         rows = slice(index * size, (index + 1) * size)
         base = base_ref[index * size * cells : (index + 1) * size * cells, :]
-        plane = plane_ref[index * size * cells : (index + 1) * size * cells, :]
-        base = base + jnp.concatenate([plane] * (depth // LANES), axis=1)
         total = base.reshape(size, cells, depth) + found[rows][:, None, :]
         for at_x in range(rows_x):
             part = total[:, at_x * rows_y : (at_x + 1) * rows_y, :]
@@ -587,7 +587,7 @@
 
     half = depth // 2
     halves = pltpu.VMEM((2, WIDTH, half), f32)
-    chunked = [pltpu.VMEM(field.shape, bf16), pltpu.SemaphoreType.DMA((4,))]
+    chunked = [pltpu.VMEM(field.shape, bf16), pltpu.SemaphoreType.DMA((8,))]
     factor_z = 1.0 / math.sqrt(HEAD_DIM * depth)
     cube = rows * wide * depth * 2
 
@@ -677,8 +677,6 @@
         flops=cube,
     )
     total = run(add_pull_kernel, [pulled], (total, swap(total, "gx", span_x, 1)))
-    base = run(base_kernel, [like((rows, depth), f32)], (top, wv, both, cots), flops=cube)
-    total, base = lax.optimization_barrier((total, base))
     for level in range(1, span_x.bit_length() - 1):
         total = run(add_pull_kernel, [pulled], (total, swap(total, "gx", span_x, 1 << level)))
     layer_output = run(
@@ -690,11 +688,12 @@
         lows + (feat, full, same, qk_weight),
         flops=2 * cube,
     )
-    total, layer_output, plane = lax.optimization_barrier((total, layer_output, plane))
+    total, plane = lax.optimization_barrier((total, plane))
+    base = run(base_kernel, [like((rows, depth), f32)], (top, wv, both, cots, plane), flops=cube)
     field_grad = run(
         functools.partial(final_kernel, grid_x * grid_y),
         [like(field.shape, bf16)],
-        swaps(total, "gy", span_y, False) + (feat_z, base, plane),
+        swaps(total, "gy", span_y, False) + (feat_z, base),
         target=pltpu.HBM,
         scratch=chunked,
     )

time: 49.7 us -> 50.1 us (level)
  no operation moved by 1% of the time
where the time goes in v17:
time: 50.1 us; the launch traced here: 49.9 us
  starting transfers between devices  19.7 us (39%)
  waiting for transfers between devices  18 us (36%)
  Pallas kernels  11.4 us (23%)
  between operations  0.78 us (2%)
    ppermute x17, starting transfers between devices, swap(): return lax.ppermute(part, axis, [(i, i ^ step) for i in range(size)])  19.7 us
    ppermute x17, waiting for transfers between devices, swap(): return lax.ppermute(part, axis, [(i, i ^ step) for i in range(size)])  18 us
    pallas_call x22, Pallas kernels, run(): pl.pallas_call(kernel, out_shape=tuple(outs), in_specs=[pl.BlockSpec(memo...  11.4 us
  transfers between devices with their start and end apart: 17, of which 14 were waited for; matrix products, arithmetic and copies ran while one was open for 0% of the time, Pallas kernels for 13%

profile of v17, /device:TPU:0, one launch (start us, length us, event | category | flops | bytes accessed | tf_op | source)
XLA Modules:
  0.0 49.9 jit_solution(5273518070242217956)
XLA Ops:
  0.6 2.0 %shard_map.77 = (f32[72,256]{1,0:T(8,128)S(1)}, f32[72,256]{1,0:T(8,128)S(1)}, bf16[512,512]{1,0:T(8,128)(2,1)S(1)}) custom-call(bf16[64,2,4,512]{3,2,1,0:T(4,128)(2,1)} %field_ref.1), custom_call_target="tpu_custom_call" | custom-call | flops 67108864 | bytes 1196032 | tf_op jit(solution)/shard_map/pallas_call | solution.py:554
  2.6 0.5 %collective-permute-start = (f32[72,256]{1,0:T(8,128)S(1)}, f32[72,256]{1,0:T(8,128)S(1)}, u32[]{:S(2)}, u32[]{:S(2)}) collective-permute-start(f32[72,256]{1,0:T(8,128)S(1)} %get-tuple-element.24), channel_id=1, source_target_pairs={{0,4},{4,0},{8,12},{12,8},{1,5},{5,1},{9,13},{13,9},{2,6},{6,2},{1... | collective-permute-start | bytes 221192 | tf_op jit(solution)/shard_map/ppermute | solution.py:27
  3.2 0.9 %collective-permute-done.other_ref = f32[72,256]{1,0:T(8,128)S(1)} collective-permute-done((f32[72,256]{1,0:T(8,128)S(1)}, f32[72,256]{1,0:T(8,128)S(1)}, u32[]{:S(2)}, u32[]{:S(2)}) %collective-permute-start) | collective-permute-done | bytes 73760 | tf_op jit(solution)/shard_map/ppermute | solution.py:27
  4.2 2.9 %collective-permute-start.1 = (f32[72,256]{1,0:T(8,128)S(1)}, f32[72,256]{1,0:T(8,128)S(1)}, u32[]{:S(2)}, u32[]{:S(2)}) collective-permute-start(f32[72,256]{1,0:T(8,128)S(1)} %shard_map.78.mine_ref), channel_id=1, source_target_pairs={{0,8},{4,12},{8,0},{12,4},{1,9},{5,13},{9,1},{13,5},{2,10},{6,14},... | collective-permute-start | bytes 221192 | tf_op jit(solution)/shard_map/ppermute | solution.py:27
  7.0 2.6 %collective-permute-done.1.other_ref = f32[72,256]{1,0:T(8,128)S(1)} collective-permute-done((f32[72,256]{1,0:T(8,128)S(1)}, f32[72,256]{1,0:T(8,128)S(1)}, u32[]{:S(2)}, u32[]{:S(2)}) %collective-permute-start.1) | collective-permute-done | bytes 73760 | tf_op jit(solution)/shard_map/ppermute | solution.py:27
  9.7 3.9 %collective-permute-start.2 = (bf16[80,256]{1,0:T(8,128)(2,1)S(1)}, bf16[80,256]{1,0:T(8,128)(2,1)S(1)}, u32[]{:S(2)}, u32[]{:S(2)}) collective-permute-start(bf16[80,256]{1,0:T(8,128)(2,1)S(1)} %shard_map.80), channel_id=1, source_target_pairs={{0,3},{1,2},{2,1},{3,0},{4,7},{5,6},{6,5},{7,4},{8,11},{9,10},{10,... | collective-permute-start | bytes 122888 | tf_op jit(solution)/shard_map/ppermute | solution.py:27
  13.6 0.6 %collective-permute-start.4 = (bf16[80,256]{1,0:T(8,128)(2,1)S(1)}, bf16[80,256]{1,0:T(8,128)(2,1)S(1)}, u32[]{:S(2)}, u32[]{:S(2)}) collective-permute-start(bf16[80,256]{1,0:T(8,128)(2,1)S(1)} %shard_map.80), channel_id=1, source_target_pairs={{0,1},{1,0},{2,3},{3,2},{4,5},{5,4},{6,7},{7,6},{8,9},{9,8},{10,11... | collective-permute-start | bytes 122888 | tf_op jit(solution)/shard_map/ppermute | solution.py:27
  14.5 1.1 %shard_map.84.cot_ref.refs_10_ = bf16[512,512]{1,0:T(8,128)(2,1)S(1)} custom-call(bf16[64,2,4,512]{3,2,1,0:T(4,128)(2,1)} %cot_ref.1), custom_call_target="tpu_custom_call" | custom-call | flops 268435456 | bytes 1048576 | tf_op jit(solution)/shard_map/pallas_call | solution.py:554
  15.8 2.7 %collective-permute-done.3.part_ref = bf16[80,256]{1,0:T(8,128)(2,1)S(1)} collective-permute-done((bf16[80,256]{1,0:T(8,128)(2,1)S(1)}, bf16[80,256]{1,0:T(8,128)(2,1)S(1)}, u32[]{:S(2)}, u32[]{:S(2)}) %collective-permute-start.3) | collective-permute-done | bytes 40992 | tf_op jit(solution)/shard_map/ppermute | solution.py:27
  18.7 1.3 %collective-permute-done.5.other_ref = f32[72,256]{1,0:T(8,128)S(1)} collective-permute-done((f32[72,256]{1,0:T(8,128)S(1)}, f32[72,256]{1,0:T(8,128)S(1)}, u32[]{:S(2)}, u32[]{:S(2)}) %collective-permute-start.5) | collective-permute-done | bytes 73760 | tf_op jit(solution)/shard_map/ppermute | solution.py:27
  19.9 1.0 %shard_map.87 = (bf16[16,512]{1,0:T(8,128)(2,1)S(1)}, bf16[128,512]{1,0:T(8,128)(2,1)S(1)}, f32[72,512]{1,0:T(8,128)S(1)}) custom-call(f32[72,256]{1,0:T(8,128)S(1)} %shard_map.86.mine_ref, f32[72,256]{1,0:T(8,128)S(1)} %collective-permute-done.5.other_ref, f32[128,64]{1,0:T(8,128)S(1)} %get-tuple-element.27.wz_ref, ...), custom_call_target="tpu_custom_call" | custom-call | flops 536870912 | bytes 1785856 | tf_op jit(solution)/shard_map/pallas_call | solution.py:554
  20.9 1.5 %collective-permute-start.6 = (bf16[16,512]{1,0:T(8,128)(2,1)S(1)}, bf16[16,512]{1,0:T(8,128)(2,1)S(1)}, u32[]{:S(2)}, u32[]{:S(2)}) collective-permute-start(bf16[16,512]{1,0:T(8,128)(2,1)S(1)} %get-tuple-element.32.refs_0_), channel_id=1, source_target_pairs={{0,3},{1,2},{2,1},{3,0},{4,7},{5,6},{6,5},{7,4},{8,11},{9,10},{10,... | collective-permute-start | bytes 49160 | tf_op jit(solution)/shard_map/ppermute | solution.py:27
  22.4 0.6 %collective-permute-start.7 = (bf16[16,512]{1,0:T(8,128)(2,1)S(1)}, bf16[16,512]{1,0:T(8,128)(2,1)S(1)}, u32[]{:S(2)}, u32[]{:S(2)}) collective-permute-start(bf16[16,512]{1,0:T(8,128)(2,1)S(1)} %get-tuple-element.32.refs_0_), channel_id=1, source_target_pairs={{0,2},{1,3},{2,0},{3,1},{4,6},{5,7},{6,4},{7,5},{8,10},{9,11},{10,... | collective-permute-start | bytes 49160 | tf_op jit(solution)/shard_map/ppermute | solution.py:27
  23.1 2.3 %collective-permute-start.8 = (bf16[16,512]{1,0:T(8,128)(2,1)S(1)}, bf16[16,512]{1,0:T(8,128)(2,1)S(1)}, u32[]{:S(2)}, u32[]{:S(2)}) collective-permute-start(bf16[16,512]{1,0:T(8,128)(2,1)S(1)} %get-tuple-element.32.refs_0_), channel_id=1, source_target_pairs={{0,1},{1,0},{2,3},{3,2},{4,5},{5,4},{6,7},{7,6},{8,9},{9,8},{10,11... | collective-permute-start | bytes 49160 | tf_op jit(solution)/shard_map/ppermute | solution.py:27
  25.4 1.3 %collective-permute-done.6.refs_1_ = bf16[16,512]{1,0:T(8,128)(2,1)S(1)} collective-permute-done((bf16[16,512]{1,0:T(8,128)(2,1)S(1)}, bf16[16,512]{1,0:T(8,128)(2,1)S(1)}, u32[]{:S(2)}, u32[]{:S(2)}) %collective-permute-start.6) | collective-permute-done | bytes 16416 | tf_op jit(solution)/shard_map/ppermute | solution.py:27
  27.3 1.4 %collective-permute-start.10 = (bf16[64,512]{1,0:T(8,128)(2,1)S(1)}, bf16[64,512]{1,0:T(8,128)(2,1)S(1)}, u32[]{:S(2)}, u32[]{:S(2)}) collective-permute-start(bf16[64,512]{1,0:T(8,128)(2,1)S(1)} %shard_map.90.refs_0_), channel_id=1, source_target_pairs={{0,8},{4,12},{8,0},{12,4},{1,9},{5,13},{9,1},{13,5},{2,10},{6,14},... | collective-permute-start | bytes 196616 | tf_op jit(solution)/shard_map/ppermute | solution.py:27
  29.1 1.5 %shard_map.91 = (f32[2,64,128]{2,1,0:T(8,128)S(1)}, f32[8,128,64]{2,1,0:T(8,128)S(1)}, f32[2,1024,128]{2,1,0:T(8,128)S(1)}) custom-call(f32[96,256]{1,0:T(8,128)S(1)} %shard_map.83.refs_0_, bf16[2,128,128]{2,1,0:T(8,128)(2,1)S(1)} %copy-done.1, f32[3,2,64,64]{3,2,1,0:T(8,128)S(1)} %copy-done), custom_call_target="tpu_custom_call" | custom-call | flops 134217728 | bytes 1638400 | tf_op jit(solution)/shard_map/pallas_call | solution.py:554
  30.6 1.0 %collective-permute-done.11.refs_3_ = bf16[64,512]{1,0:T(8,128)(2,1)S(1)} collective-permute-done((bf16[64,512]{1,0:T(8,128)(2,1)S(1)}, bf16[64,512]{1,0:T(8,128)(2,1)S(1)}, u32[]{:S(2)}, u32[]{:S(2)}) %collective-permute-start.11) | collective-permute-done | bytes 65568 | tf_op jit(solution)/shard_map/ppermute | solution.py:27
  31.6 1.4 %collective-permute-done.10.refs_2_ = bf16[64,512]{1,0:T(8,128)(2,1)S(1)} collective-permute-done((bf16[64,512]{1,0:T(8,128)(2,1)S(1)}, bf16[64,512]{1,0:T(8,128)(2,1)S(1)}, u32[]{:S(2)}, u32[]{:S(2)}) %collective-permute-start.10) | collective-permute-done | bytes 65568 | tf_op jit(solution)/shard_map/ppermute | solution.py:27
  33.0 1.0 %shard_map.92 = (f32[2,8,512]{2,1,0:T(8,128)S(1)}, bf16[64,512]{1,0:T(8,128)(2,1)S(1)}) custom-call(bf16[64,512]{1,0:T(8,128)(2,1)S(1)} %shard_map.90.refs_0_, bf16[64,512]{1,0:T(8,128)(2,1)S(1)} %collective-permute-done.9.refs_1_, bf16[64,512]{1,0:T(8,128)(2,1)S(1)} %collective-permute-done.10.refs_2_, bf16[64,512]{1,0:T(8,128)(2,1)S(1)} %collective-permute-done.11.refs_3_, ...), custom_call_target="tpu_custom_call" | custom-call | flops 268435456 | bytes 1998848 | tf_op jit(solution)/shard_map/pallas_call | solution.py:554
  34.2 1.2 %collective-permute-done.12.refs_1_ = bf16[64,512]{1,0:T(8,128)(2,1)S(1)} collective-permute-done((bf16[64,512]{1,0:T(8,128)(2,1)S(1)}, bf16[64,512]{1,0:T(8,128)(2,1)S(1)}, u32[]{:S(2)}, u32[]{:S(2)}) %collective-permute-start.12) | collective-permute-done | bytes 65568 | tf_op jit(solution)/shard_map/ppermute | solution.py:27
  35.4 0.7 %collective-permute-start.13 = (bf16[64,512]{1,0:T(8,128)(2,1)S(1)}, bf16[64,512]{1,0:T(8,128)(2,1)S(1)}, u32[]{:S(2)}, u32[]{:S(2)}) collective-permute-start(bf16[64,512]{1,0:T(8,128)(2,1)S(1)} %shard_map.94.refs_0_), channel_id=1, source_target_pairs={{0,8},{4,12},{8,0},{12,4},{1,9},{5,13},{9,1},{13,5},{2,10},{6,14},... | collective-permute-start | bytes 196616 | tf_op jit(solution)/shard_map/ppermute | solution.py:27
  36.2 1.6 %shard_map.96.plane_ref = f32[512,128]{1,0:T(8,128)S(1)} custom-call(bf16[64,512]{1,0:T(8,128)(2,1)S(1)} %shard_map.90.refs_0_, bf16[64,512]{1,0:T(8,128)(2,1)S(1)} %collective-permute-done.9.refs_1_, bf16[64,512]{1,0:T(8,128)(2,1)S(1)} %collective-permute-done.10.refs_2_, bf16[64,512]{1,0:T(8,128)(2,1)S(1)} %collective-permute-done.11.refs_3_, ...), custom_call_target="tpu_custom_call" | custom-call | flops 536870912 | bytes 1998848 | tf_op jit(solution)/shard_map/pallas_call | solution.py:554
  37.8 2.0 %collective-permute-done.13.refs_1_ = bf16[64,512]{1,0:T(8,128)(2,1)S(1)} collective-permute-done((bf16[64,512]{1,0:T(8,128)(2,1)S(1)}, bf16[64,512]{1,0:T(8,128)(2,1)S(1)}, u32[]{:S(2)}, u32[]{:S(2)}) %collective-permute-start.13) | collective-permute-done | bytes 65568 | tf_op jit(solution)/shard_map/ppermute | solution.py:27
  39.8 1.9 %collective-permute-start.16 = (bf16[64,512]{1,0:T(8,128)(2,1)S(1)}, bf16[64,512]{1,0:T(8,128)(2,1)S(1)}, u32[]{:S(2)}, u32[]{:S(2)}) collective-permute-start(bf16[64,512]{1,0:T(8,128)(2,1)S(1)} %shard_map.95.refs_0_), channel_id=1, source_target_pairs={{0,1},{1,0},{2,3},{3,2},{4,5},{5,4},{6,7},{7,6},{8,9},{9,8},{10,11... | collective-permute-start | bytes 196616 | tf_op jit(solution)/shard_map/ppermute | solution.py:27
  41.7 1.1 %collective-permute-start.15 = (bf16[64,512]{1,0:T(8,128)(2,1)S(1)}, bf16[64,512]{1,0:T(8,128)(2,1)S(1)}, u32[]{:S(2)}, u32[]{:S(2)}) collective-permute-start(bf16[64,512]{1,0:T(8,128)(2,1)S(1)} %shard_map.95.refs_0_), channel_id=1, source_target_pairs={{0,2},{1,3},{2,0},{3,1},{4,6},{5,7},{6,4},{7,5},{8,10},{9,11},{10,... | collective-permute-start | bytes 196616 | tf_op jit(solution)/shard_map/ppermute | solution.py:27
  42.8 1.4 %collective-permute-start.14 = (bf16[64,512]{1,0:T(8,128)(2,1)S(1)}, bf16[64,512]{1,0:T(8,128)(2,1)S(1)}, u32[]{:S(2)}, u32[]{:S(2)}) collective-permute-start(bf16[64,512]{1,0:T(8,128)(2,1)S(1)} %shard_map.95.refs_0_), channel_id=1, source_target_pairs={{0,3},{1,2},{2,1},{3,0},{4,7},{5,6},{6,5},{7,4},{8,11},{9,10},{10,... | collective-permute-start | bytes 196616 | tf_op jit(solution)/shard_map/ppermute | solution.py:27
  44.2 1.3 %shard_map.93 = bf16[64,2,4,512]{3,2,1,0:T(4,128)(2,1)} custom-call(f32[2,8,512]{2,1,0:T(8,128)S(1)} %get-tuple-element.36.top_ref, f32[64,512]{1,0:T(8,128)S(1)} %get-tuple-element.31.wo_ref.refs_6_, bf16[128,512]{1,0:T(8,128)(2,1)S(1)} %get-tuple-element.37.both_ref, bf16[512,512]{1,0:T(8,128)(2,1)S(1)} %get-tuple-element.28.field_ref.refs_9_), custom_call_target="tpu_custom_call" | custom-call | flops 268435456 | bytes 1343488 | tf_op jit(solution)/shard_map/pallas_call | solution.py:554
  45.5 0.5 shard_map.97.refs_5_
  46.0 2.0 %collective-permute-done.15.refs_2_ = bf16[64,512]{1,0:T(8,128)(2,1)S(1)} collective-permute-done((bf16[64,512]{1,0:T(8,128)(2,1)S(1)}, bf16[64,512]{1,0:T(8,128)(2,1)S(1)}, u32[]{:S(2)}, u32[]{:S(2)}) %collective-permute-start.15) | collective-permute-done | bytes 65568 | tf_op jit(solution)/shard_map/ppermute | solution.py:27
  47.9 1.0 %collective-permute-done.14.refs_1_ = bf16[64,512]{1,0:T(8,128)(2,1)S(1)} collective-permute-done((bf16[64,512]{1,0:T(8,128)(2,1)S(1)}, bf16[64,512]{1,0:T(8,128)(2,1)S(1)}, u32[]{:S(2)}, u32[]{:S(2)}) %collective-permute-start.14) | collective-permute-done | bytes 65568 | tf_op jit(solution)/shard_map/ppermute | solution.py:27
  49.0 0.9 %shard_map.98 = bf16[64,2,4,512]{3,2,1,0:T(4,128)(2,1)} custom-call(bf16[64,512]{1,0:T(8,128)(2,1)S(1)} %shard_map.95.refs_0_, bf16[64,512]{1,0:T(8,128)(2,1)S(1)} %collective-permute-done.14.refs_1_, bf16[64,512]{1,0:T(8,128)(2,1)S(1)} %collective-permute-done.15.refs_2_, bf16[64,512]{1,0:T(8,128)(2,1)S(1)} %collective-permute-done.16.refs_3_, ...), custom_call_target="tpu_custom_call" | custom-call | bytes 1982464 | tf_op jit(solution)/shard_map/pallas_call | solution.py:554
  (32 shorter events, 1.8 us)
Async XLA Ops:
  2.6 1.4 %collective-permute-start = (f32[72,256]{1,0:T(8,128)S(1)}, f32[72,256]{1,0:T(8,128)S(1)}, u32[]{:S(2)}, u32[]{:S(2)}) collective-permute-start(f32[72,256]{1,0:T(8,128)S(1)} %get-tuple-element.24), channel_id=1, source_target_pairs={{0,4},{4,0},{8,12},{12,8},{1,5},{5,1},{9,13},{13,9},{2,6},{6,2},{1... | collective-permute-start | bytes 221192 | tf_op jit(solution)/shard_map/ppermute | solution.py:27
  4.1 10.1 %copy-start = (f32[3,2,64,64]{3,2,1,0:T(8,128)S(1)}, f32[3,2,64,64]{3,2,1,0:T(8,128)}, u32[]{:S(2)}) copy-start(f32[3,2,64,64]{3,2,1,0:T(8,128)} %refs_7_.1) | copy-start | bytes 294916
  4.2 5.4 %collective-permute-start.1 = (f32[72,256]{1,0:T(8,128)S(1)}, f32[72,256]{1,0:T(8,128)S(1)}, u32[]{:S(2)}, u32[]{:S(2)}) collective-permute-start(f32[72,256]{1,0:T(8,128)S(1)} %shard_map.78.mine_ref), channel_id=1, source_target_pairs={{0,8},{4,12},{8,0},{12,4},{1,9},{5,13},{9,1},{13,5},{2,10},{6,14},... | collective-permute-start | bytes 221192 | tf_op jit(solution)/shard_map/ppermute | solution.py:27
  9.6 4.6 %copy-start.2 = (bf16[64,64]{1,0:T(8,128)(2,1)S(1)}, bf16[64,64]{1,0:T(8,128)(2,1)}, u32[]{:S(2)}) copy-start(bf16[64,64]{1,0:T(8,128)(2,1)} %wv_ref.1) | copy-start | bytes 24580
  9.6 4.6 %copy-start.3 = (bf16[64,64]{1,0:T(8,128)(2,1)S(1)}, bf16[64,64]{1,0:T(8,128)(2,1)}, u32[]{:S(2)}) copy-start(bf16[64,64]{1,0:T(8,128)(2,1)} %wo_ref.1) | copy-start | bytes 24580
  9.7 6.1 %collective-permute-start.2 = (bf16[80,256]{1,0:T(8,128)(2,1)S(1)}, bf16[80,256]{1,0:T(8,128)(2,1)S(1)}, u32[]{:S(2)}, u32[]{:S(2)}) collective-permute-start(bf16[80,256]{1,0:T(8,128)(2,1)S(1)} %shard_map.80), channel_id=1, source_target_pairs={{0,3},{1,2},{2,1},{3,0},{4,7},{5,6},{6,5},{7,4},{8,11},{9,10},{10,... | collective-permute-start | bytes 122888 | tf_op jit(solution)/shard_map/ppermute | solution.py:27
  13.6 4.9 %collective-permute-start.3 = (bf16[80,256]{1,0:T(8,128)(2,1)S(1)}, bf16[80,256]{1,0:T(8,128)(2,1)S(1)}, u32[]{:S(2)}, u32[]{:S(2)}) collective-permute-start(bf16[80,256]{1,0:T(8,128)(2,1)S(1)} %shard_map.80), channel_id=1, source_target_pairs={{0,2},{1,3},{2,0},{3,1},{4,6},{5,7},{6,4},{7,5},{8,10},{9,11},{10,... | collective-permute-start | bytes 122888 | tf_op jit(solution)/shard_map/ppermute | solution.py:27
  13.6 4.9 %collective-permute-start.4 = (bf16[80,256]{1,0:T(8,128)(2,1)S(1)}, bf16[80,256]{1,0:T(8,128)(2,1)S(1)}, u32[]{:S(2)}, u32[]{:S(2)}) collective-permute-start(bf16[80,256]{1,0:T(8,128)(2,1)S(1)} %shard_map.80), channel_id=1, source_target_pairs={{0,1},{1,0},{2,3},{3,2},{4,5},{5,4},{6,7},{7,6},{8,9},{9,8},{10,11... | collective-permute-start | bytes 122888 | tf_op jit(solution)/shard_map/ppermute | solution.py:27
  18.6 1.3 %collective-permute-start.5 = (f32[72,256]{1,0:T(8,128)S(1)}, f32[72,256]{1,0:T(8,128)S(1)}, u32[]{:S(2)}, u32[]{:S(2)}) collective-permute-start(f32[72,256]{1,0:T(8,128)S(1)} %shard_map.86.mine_ref), channel_id=1, source_target_pairs={{0,4},{4,0},{8,12},{12,8},{1,5},{5,1},{9,13},{13,9},{2,6},{6,2},{1... | collective-permute-start | bytes 221192 | tf_op jit(solution)/shard_map/ppermute | solution.py:27
  20.9 5.8 %collective-permute-start.6 = (bf16[16,512]{1,0:T(8,128)(2,1)S(1)}, bf16[16,512]{1,0:T(8,128)(2,1)S(1)}, u32[]{:S(2)}, u32[]{:S(2)}) collective-permute-start(bf16[16,512]{1,0:T(8,128)(2,1)S(1)} %get-tuple-element.32.refs_0_), channel_id=1, source_target_pairs={{0,3},{1,2},{2,1},{3,0},{4,7},{5,6},{6,5},{7,4},{8,11},{9,10},{10,... | collective-permute-start | bytes 49160 | tf_op jit(solution)/shard_map/ppermute | solution.py:27
  22.4 4.6 %collective-permute-start.7 = (bf16[16,512]{1,0:T(8,128)(2,1)S(1)}, bf16[16,512]{1,0:T(8,128)(2,1)S(1)}, u32[]{:S(2)}, u32[]{:S(2)}) collective-permute-start(bf16[16,512]{1,0:T(8,128)(2,1)S(1)} %get-tuple-element.32.refs_0_), channel_id=1, source_target_pairs={{0,2},{1,3},{2,0},{3,1},{4,6},{5,7},{6,4},{7,5},{8,10},{9,11},{10,... | collective-permute-start | bytes 49160 | tf_op jit(solution)/shard_map/ppermute | solution.py:27
  23.1 4.2 %collective-permute-start.8 = (bf16[16,512]{1,0:T(8,128)(2,1)S(1)}, bf16[16,512]{1,0:T(8,128)(2,1)S(1)}, u32[]{:S(2)}, u32[]{:S(2)}) collective-permute-start(bf16[16,512]{1,0:T(8,128)(2,1)S(1)} %get-tuple-element.32.refs_0_), channel_id=1, source_target_pairs={{0,1},{1,0},{2,3},{3,2},{4,5},{5,4},{6,7},{7,6},{8,9},{9,8},{10,11... | collective-permute-start | bytes 49160 | tf_op jit(solution)/shard_map/ppermute | solution.py:27
  27.1 2.0 %copy-start.1 = (bf16[2,128,128]{2,1,0:T(8,128)(2,1)S(1)}, bf16[2,128,128]{2,1,0:T(8,128)(2,1)}, u32[]{:S(2)}) copy-start(bf16[2,128,128]{2,1,0:T(8,128)(2,1)} %constant.2.clone.refs_1_.refs_6_) | copy-start | bytes 196612
  27.2 4.3 %collective-permute-start.11 = (bf16[64,512]{1,0:T(8,128)(2,1)S(1)}, bf16[64,512]{1,0:T(8,128)(2,1)S(1)}, u32[]{:S(2)}, u32[]{:S(2)}) collective-permute-start(bf16[64,512]{1,0:T(8,128)(2,1)S(1)} %shard_map.90.refs_0_), channel_id=1, source_target_pairs={{0,12},{4,8},{8,4},{12,0},{1,13},{5,9},{9,5},{13,1},{2,14},{6,10},... | collective-permute-start | bytes 196616 | tf_op jit(solution)/shard_map/ppermute | solution.py:27
  27.3 5.7 %collective-permute-start.10 = (bf16[64,512]{1,0:T(8,128)(2,1)S(1)}, bf16[64,512]{1,0:T(8,128)(2,1)S(1)}, u32[]{:S(2)}, u32[]{:S(2)}) collective-permute-start(bf16[64,512]{1,0:T(8,128)(2,1)S(1)} %shard_map.90.refs_0_), channel_id=1, source_target_pairs={{0,8},{4,12},{8,0},{12,4},{1,9},{5,13},{9,1},{13,5},{2,10},{6,14},... | collective-permute-start | bytes 196616 | tf_op jit(solution)/shard_map/ppermute | solution.py:27
  28.8 4.2 %collective-permute-start.9 = (bf16[64,512]{1,0:T(8,128)(2,1)S(1)}, bf16[64,512]{1,0:T(8,128)(2,1)S(1)}, u32[]{:S(2)}, u32[]{:S(2)}) collective-permute-start(bf16[64,512]{1,0:T(8,128)(2,1)S(1)} %shard_map.90.refs_0_), channel_id=1, source_target_pairs={{0,4},{4,0},{8,12},{12,8},{1,5},{5,1},{9,13},{13,9},{2,6},{6,2},{1... | collective-permute-start | bytes 196616 | tf_op jit(solution)/shard_map/ppermute | solution.py:27
  34.1 1.3 %collective-permute-start.12 = (bf16[64,512]{1,0:T(8,128)(2,1)S(1)}, bf16[64,512]{1,0:T(8,128)(2,1)S(1)}, u32[]{:S(2)}, u32[]{:S(2)}) collective-permute-start(bf16[64,512]{1,0:T(8,128)(2,1)S(1)} %get-tuple-element.38.refs_0_), channel_id=1, source_target_pairs={{0,4},{4,0},{8,12},{12,8},{1,5},{5,1},{9,13},{13,9},{2,6},{6,2},{1... | collective-permute-start | bytes 196616 | tf_op jit(solution)/shard_map/ppermute | solution.py:27
  35.4 4.3 %collective-permute-start.13 = (bf16[64,512]{1,0:T(8,128)(2,1)S(1)}, bf16[64,512]{1,0:T(8,128)(2,1)S(1)}, u32[]{:S(2)}, u32[]{:S(2)}) collective-permute-start(bf16[64,512]{1,0:T(8,128)(2,1)S(1)} %shard_map.94.refs_0_), channel_id=1, source_target_pairs={{0,8},{4,12},{8,0},{12,4},{1,9},{5,13},{9,1},{13,5},{2,10},{6,14},... | collective-permute-start | bytes 196616 | tf_op jit(solution)/shard_map/ppermute | solution.py:27
  39.8 6.2 %collective-permute-start.16 = (bf16[64,512]{1,0:T(8,128)(2,1)S(1)}, bf16[64,512]{1,0:T(8,128)(2,1)S(1)}, u32[]{:S(2)}, u32[]{:S(2)}) collective-permute-start(bf16[64,512]{1,0:T(8,128)(2,1)S(1)} %shard_map.95.refs_0_), channel_id=1, source_target_pairs={{0,1},{1,0},{2,3},{3,2},{4,5},{5,4},{6,7},{7,6},{8,9},{9,8},{10,11... | collective-permute-start | bytes 196616 | tf_op jit(solution)/shard_map/ppermute | solution.py:27
  41.7 6.2 %collective-permute-start.15 = (bf16[64,512]{1,0:T(8,128)(2,1)S(1)}, bf16[64,512]{1,0:T(8,128)(2,1)S(1)}, u32[]{:S(2)}, u32[]{:S(2)}) collective-permute-start(bf16[64,512]{1,0:T(8,128)(2,1)S(1)} %shard_map.95.refs_0_), channel_id=1, source_target_pairs={{0,2},{1,3},{2,0},{3,1},{4,6},{5,7},{6,4},{7,5},{8,10},{9,11},{10,... | collective-permute-start | bytes 196616 | tf_op jit(solution)/shard_map/ppermute | solution.py:27
  42.8 6.2 %collective-permute-start.14 = (bf16[64,512]{1,0:T(8,128)(2,1)S(1)}, bf16[64,512]{1,0:T(8,128)(2,1)S(1)}, u32[]{:S(2)}, u32[]{:S(2)}) collective-permute-start(bf16[64,512]{1,0:T(8,128)(2,1)S(1)} %shard_map.95.refs_0_), channel_id=1, source_target_pairs={{0,3},{1,2},{2,1},{3,0},{4,7},{5,6},{6,5},{7,4},{8,11},{9,10},{10,... | collective-permute-start | bytes 196616 | tf_op jit(solution)/shard_map/ppermute | solution.py:27

commit v18 on v17

--- a/solution.py
+++ b/solution.py
@@ -587,7 +587,7 @@
 
     half = depth // 2
     halves = pltpu.VMEM((2, WIDTH, half), f32)
-    chunked = [pltpu.VMEM(field.shape, bf16), pltpu.SemaphoreType.DMA((8,))]
+    chunked = [pltpu.VMEM(field.shape, bf16), pltpu.SemaphoreType.DMA((4,))]
     factor_z = 1.0 / math.sqrt(HEAD_DIM * depth)
     cube = rows * wide * depth * 2
 

time: 50.1 us -> 49.6 us (0.990)
  no operation moved by 1% of the time
where the time goes in v18:
time: 49.6 us; the launch traced here: 49.5 us
  starting transfers between devices  19.7 us (40%)
  waiting for transfers between devices  18 us (36%)
  Pallas kernels  11 us (22%)
  between operations  0.78 us (2%)
    ppermute x17, starting transfers between devices, swap(): return lax.ppermute(part, axis, [(i, i ^ step) for i in range(size)])  19.7 us
    ppermute x17, waiting for transfers between devices, swap(): return lax.ppermute(part, axis, [(i, i ^ step) for i in range(size)])  18 us
    pallas_call x22, Pallas kernels, run(): pl.pallas_call(kernel, out_shape=tuple(outs), in_specs=[pl.BlockSpec(memo...  11 us
  transfers between devices with their start and end apart: 17, of which 14 were waited for; matrix products, arithmetic and copies ran while one was open for 0% of the time, Pallas kernels for 13%

profile of v18, /device:TPU:0, one launch (start us, length us, event | category | flops | bytes accessed | tf_op | source)
XLA Modules:
  0.0 49.5 jit_solution(15139667735482828892)
XLA Ops:
  0.6 1.6 %shard_map.77 = (f32[72,256]{1,0:T(8,128)S(1)}, f32[72,256]{1,0:T(8,128)S(1)}, bf16[512,512]{1,0:T(8,128)(2,1)S(1)}) custom-call(bf16[64,2,4,512]{3,2,1,0:T(4,128)(2,1)} %field_ref.1), custom_call_target="tpu_custom_call" | custom-call | flops 67108864 | bytes 1196032 | tf_op jit(solution)/shard_map/pallas_call | solution.py:554
  2.2 0.5 %collective-permute-start = (f32[72,256]{1,0:T(8,128)S(1)}, f32[72,256]{1,0:T(8,128)S(1)}, u32[]{:S(2)}, u32[]{:S(2)}) collective-permute-start(f32[72,256]{1,0:T(8,128)S(1)} %get-tuple-element.24), channel_id=1, source_target_pairs={{0,4},{4,0},{8,12},{12,8},{1,5},{5,1},{9,13},{13,9},{2,6},{6,2},{1... | collective-permute-start | bytes 221192 | tf_op jit(solution)/shard_map/ppermute | solution.py:27
  2.7 0.9 %collective-permute-done.other_ref = f32[72,256]{1,0:T(8,128)S(1)} collective-permute-done((f32[72,256]{1,0:T(8,128)S(1)}, f32[72,256]{1,0:T(8,128)S(1)}, u32[]{:S(2)}, u32[]{:S(2)}) %collective-permute-start) | collective-permute-done | bytes 73760 | tf_op jit(solution)/shard_map/ppermute | solution.py:27
  3.7 2.9 %collective-permute-start.1 = (f32[72,256]{1,0:T(8,128)S(1)}, f32[72,256]{1,0:T(8,128)S(1)}, u32[]{:S(2)}, u32[]{:S(2)}) collective-permute-start(f32[72,256]{1,0:T(8,128)S(1)} %shard_map.78.mine_ref), channel_id=1, source_target_pairs={{0,8},{4,12},{8,0},{12,4},{1,9},{5,13},{9,1},{13,5},{2,10},{6,14},... | collective-permute-start | bytes 221192 | tf_op jit(solution)/shard_map/ppermute | solution.py:27
  6.6 2.6 %collective-permute-done.1.other_ref = f32[72,256]{1,0:T(8,128)S(1)} collective-permute-done((f32[72,256]{1,0:T(8,128)S(1)}, f32[72,256]{1,0:T(8,128)S(1)}, u32[]{:S(2)}, u32[]{:S(2)}) %collective-permute-start.1) | collective-permute-done | bytes 73760 | tf_op jit(solution)/shard_map/ppermute | solution.py:27
  9.2 3.9 %collective-permute-start.2 = (bf16[80,256]{1,0:T(8,128)(2,1)S(1)}, bf16[80,256]{1,0:T(8,128)(2,1)S(1)}, u32[]{:S(2)}, u32[]{:S(2)}) collective-permute-start(bf16[80,256]{1,0:T(8,128)(2,1)S(1)} %shard_map.80), channel_id=1, source_target_pairs={{0,3},{1,2},{2,1},{3,0},{4,7},{5,6},{6,5},{7,4},{8,11},{9,10},{10,... | collective-permute-start | bytes 122888 | tf_op jit(solution)/shard_map/ppermute | solution.py:27
  13.2 0.6 %collective-permute-start.4 = (bf16[80,256]{1,0:T(8,128)(2,1)S(1)}, bf16[80,256]{1,0:T(8,128)(2,1)S(1)}, u32[]{:S(2)}, u32[]{:S(2)}) collective-permute-start(bf16[80,256]{1,0:T(8,128)(2,1)S(1)} %shard_map.80), channel_id=1, source_target_pairs={{0,1},{1,0},{2,3},{3,2},{4,5},{5,4},{6,7},{7,6},{8,9},{9,8},{10,11... | collective-permute-start | bytes 122888 | tf_op jit(solution)/shard_map/ppermute | solution.py:27
  14.1 1.2 %shard_map.84.cot_ref.refs_10_ = bf16[512,512]{1,0:T(8,128)(2,1)S(1)} custom-call(bf16[64,2,4,512]{3,2,1,0:T(4,128)(2,1)} %cot_ref.1), custom_call_target="tpu_custom_call" | custom-call | flops 268435456 | bytes 1048576 | tf_op jit(solution)/shard_map/pallas_call | solution.py:554
  15.4 2.7 %collective-permute-done.3.part_ref = bf16[80,256]{1,0:T(8,128)(2,1)S(1)} collective-permute-done((bf16[80,256]{1,0:T(8,128)(2,1)S(1)}, bf16[80,256]{1,0:T(8,128)(2,1)S(1)}, u32[]{:S(2)}, u32[]{:S(2)}) %collective-permute-start.3) | collective-permute-done | bytes 40992 | tf_op jit(solution)/shard_map/ppermute | solution.py:27
  18.2 1.3 %collective-permute-done.5.other_ref = f32[72,256]{1,0:T(8,128)S(1)} collective-permute-done((f32[72,256]{1,0:T(8,128)S(1)}, f32[72,256]{1,0:T(8,128)S(1)}, u32[]{:S(2)}, u32[]{:S(2)}) %collective-permute-start.5) | collective-permute-done | bytes 73760 | tf_op jit(solution)/shard_map/ppermute | solution.py:27
  19.5 1.0 %shard_map.87 = (bf16[16,512]{1,0:T(8,128)(2,1)S(1)}, bf16[128,512]{1,0:T(8,128)(2,1)S(1)}, f32[72,512]{1,0:T(8,128)S(1)}) custom-call(f32[72,256]{1,0:T(8,128)S(1)} %shard_map.86.mine_ref, f32[72,256]{1,0:T(8,128)S(1)} %collective-permute-done.5.other_ref, f32[128,64]{1,0:T(8,128)S(1)} %get-tuple-element.27.wz_ref, ...), custom_call_target="tpu_custom_call" | custom-call | flops 536870912 | bytes 1785856 | tf_op jit(solution)/shard_map/pallas_call | solution.py:554
  20.5 1.5 %collective-permute-start.6 = (bf16[16,512]{1,0:T(8,128)(2,1)S(1)}, bf16[16,512]{1,0:T(8,128)(2,1)S(1)}, u32[]{:S(2)}, u32[]{:S(2)}) collective-permute-start(bf16[16,512]{1,0:T(8,128)(2,1)S(1)} %get-tuple-element.32.refs_0_), channel_id=1, source_target_pairs={{0,3},{1,2},{2,1},{3,0},{4,7},{5,6},{6,5},{7,4},{8,11},{9,10},{10,... | collective-permute-start | bytes 49160 | tf_op jit(solution)/shard_map/ppermute | solution.py:27
  22.0 0.6 %collective-permute-start.7 = (bf16[16,512]{1,0:T(8,128)(2,1)S(1)}, bf16[16,512]{1,0:T(8,128)(2,1)S(1)}, u32[]{:S(2)}, u32[]{:S(2)}) collective-permute-start(bf16[16,512]{1,0:T(8,128)(2,1)S(1)} %get-tuple-element.32.refs_0_), channel_id=1, source_target_pairs={{0,2},{1,3},{2,0},{3,1},{4,6},{5,7},{6,4},{7,5},{8,10},{9,11},{10,... | collective-permute-start | bytes 49160 | tf_op jit(solution)/shard_map/ppermute | solution.py:27
  22.6 2.3 %collective-permute-start.8 = (bf16[16,512]{1,0:T(8,128)(2,1)S(1)}, bf16[16,512]{1,0:T(8,128)(2,1)S(1)}, u32[]{:S(2)}, u32[]{:S(2)}) collective-permute-start(bf16[16,512]{1,0:T(8,128)(2,1)S(1)} %get-tuple-element.32.refs_0_), channel_id=1, source_target_pairs={{0,1},{1,0},{2,3},{3,2},{4,5},{5,4},{6,7},{7,6},{8,9},{9,8},{10,11... | collective-permute-start | bytes 49160 | tf_op jit(solution)/shard_map/ppermute | solution.py:27
  24.9 1.3 %collective-permute-done.6.refs_1_ = bf16[16,512]{1,0:T(8,128)(2,1)S(1)} collective-permute-done((bf16[16,512]{1,0:T(8,128)(2,1)S(1)}, bf16[16,512]{1,0:T(8,128)(2,1)S(1)}, u32[]{:S(2)}, u32[]{:S(2)}) %collective-permute-start.6) | collective-permute-done | bytes 16416 | tf_op jit(solution)/shard_map/ppermute | solution.py:27
  26.9 1.4 %collective-permute-start.10 = (bf16[64,512]{1,0:T(8,128)(2,1)S(1)}, bf16[64,512]{1,0:T(8,128)(2,1)S(1)}, u32[]{:S(2)}, u32[]{:S(2)}) collective-permute-start(bf16[64,512]{1,0:T(8,128)(2,1)S(1)} %shard_map.90.refs_0_), channel_id=1, source_target_pairs={{0,8},{4,12},{8,0},{12,4},{1,9},{5,13},{9,1},{13,5},{2,10},{6,14},... | collective-permute-start | bytes 196616 | tf_op jit(solution)/shard_map/ppermute | solution.py:27
  28.7 1.5 %shard_map.91 = (f32[2,64,128]{2,1,0:T(8,128)S(1)}, f32[8,128,64]{2,1,0:T(8,128)S(1)}, f32[2,1024,128]{2,1,0:T(8,128)S(1)}) custom-call(f32[96,256]{1,0:T(8,128)S(1)} %shard_map.83.refs_0_, bf16[2,128,128]{2,1,0:T(8,128)(2,1)S(1)} %copy-done.1, f32[3,2,64,64]{3,2,1,0:T(8,128)S(1)} %copy-done), custom_call_target="tpu_custom_call" | custom-call | flops 134217728 | bytes 1638400 | tf_op jit(solution)/shard_map/pallas_call | solution.py:554
  30.2 1.0 %collective-permute-done.11.refs_3_ = bf16[64,512]{1,0:T(8,128)(2,1)S(1)} collective-permute-done((bf16[64,512]{1,0:T(8,128)(2,1)S(1)}, bf16[64,512]{1,0:T(8,128)(2,1)S(1)}, u32[]{:S(2)}, u32[]{:S(2)}) %collective-permute-start.11) | collective-permute-done | bytes 65568 | tf_op jit(solution)/shard_map/ppermute | solution.py:27
  31.1 1.4 %collective-permute-done.10.refs_2_ = bf16[64,512]{1,0:T(8,128)(2,1)S(1)} collective-permute-done((bf16[64,512]{1,0:T(8,128)(2,1)S(1)}, bf16[64,512]{1,0:T(8,128)(2,1)S(1)}, u32[]{:S(2)}, u32[]{:S(2)}) %collective-permute-start.10) | collective-permute-done | bytes 65568 | tf_op jit(solution)/shard_map/ppermute | solution.py:27
  32.6 1.0 %shard_map.92 = (f32[2,8,512]{2,1,0:T(8,128)S(1)}, bf16[64,512]{1,0:T(8,128)(2,1)S(1)}) custom-call(bf16[64,512]{1,0:T(8,128)(2,1)S(1)} %shard_map.90.refs_0_, bf16[64,512]{1,0:T(8,128)(2,1)S(1)} %collective-permute-done.9.refs_1_, bf16[64,512]{1,0:T(8,128)(2,1)S(1)} %collective-permute-done.10.refs_2_, bf16[64,512]{1,0:T(8,128)(2,1)S(1)} %collective-permute-done.11.refs_3_, ...), custom_call_target="tpu_custom_call" | custom-call | flops 268435456 | bytes 1998848 | tf_op jit(solution)/shard_map/pallas_call | solution.py:554
  33.8 1.2 %collective-permute-done.12.refs_1_ = bf16[64,512]{1,0:T(8,128)(2,1)S(1)} collective-permute-done((bf16[64,512]{1,0:T(8,128)(2,1)S(1)}, bf16[64,512]{1,0:T(8,128)(2,1)S(1)}, u32[]{:S(2)}, u32[]{:S(2)}) %collective-permute-start.12) | collective-permute-done | bytes 65568 | tf_op jit(solution)/shard_map/ppermute | solution.py:27
  35.0 0.7 %collective-permute-start.13 = (bf16[64,512]{1,0:T(8,128)(2,1)S(1)}, bf16[64,512]{1,0:T(8,128)(2,1)S(1)}, u32[]{:S(2)}, u32[]{:S(2)}) collective-permute-start(bf16[64,512]{1,0:T(8,128)(2,1)S(1)} %shard_map.94.refs_0_), channel_id=1, source_target_pairs={{0,8},{4,12},{8,0},{12,4},{1,9},{5,13},{9,1},{13,5},{2,10},{6,14},... | collective-permute-start | bytes 196616 | tf_op jit(solution)/shard_map/ppermute | solution.py:27
  35.7 1.6 %shard_map.96.plane_ref = f32[512,128]{1,0:T(8,128)S(1)} custom-call(bf16[64,512]{1,0:T(8,128)(2,1)S(1)} %shard_map.90.refs_0_, bf16[64,512]{1,0:T(8,128)(2,1)S(1)} %collective-permute-done.9.refs_1_, bf16[64,512]{1,0:T(8,128)(2,1)S(1)} %collective-permute-done.10.refs_2_, bf16[64,512]{1,0:T(8,128)(2,1)S(1)} %collective-permute-done.11.refs_3_, ...), custom_call_target="tpu_custom_call" | custom-call | flops 536870912 | bytes 1998848 | tf_op jit(solution)/shard_map/pallas_call | solution.py:554
  37.4 2.0 %collective-permute-done.13.refs_1_ = bf16[64,512]{1,0:T(8,128)(2,1)S(1)} collective-permute-done((bf16[64,512]{1,0:T(8,128)(2,1)S(1)}, bf16[64,512]{1,0:T(8,128)(2,1)S(1)}, u32[]{:S(2)}, u32[]{:S(2)}) %collective-permute-start.13) | collective-permute-done | bytes 65568 | tf_op jit(solution)/shard_map/ppermute | solution.py:27
  39.3 1.9 %collective-permute-start.16 = (bf16[64,512]{1,0:T(8,128)(2,1)S(1)}, bf16[64,512]{1,0:T(8,128)(2,1)S(1)}, u32[]{:S(2)}, u32[]{:S(2)}) collective-permute-start(bf16[64,512]{1,0:T(8,128)(2,1)S(1)} %shard_map.95.refs_0_), channel_id=1, source_target_pairs={{0,1},{1,0},{2,3},{3,2},{4,5},{5,4},{6,7},{7,6},{8,9},{9,8},{10,11... | collective-permute-start | bytes 196616 | tf_op jit(solution)/shard_map/ppermute | solution.py:27
  41.3 1.1 %collective-permute-start.15 = (bf16[64,512]{1,0:T(8,128)(2,1)S(1)}, bf16[64,512]{1,0:T(8,128)(2,1)S(1)}, u32[]{:S(2)}, u32[]{:S(2)}) collective-permute-start(bf16[64,512]{1,0:T(8,128)(2,1)S(1)} %shard_map.95.refs_0_), channel_id=1, source_target_pairs={{0,2},{1,3},{2,0},{3,1},{4,6},{5,7},{6,4},{7,5},{8,10},{9,11},{10,... | collective-permute-start | bytes 196616 | tf_op jit(solution)/shard_map/ppermute | solution.py:27
  42.4 1.4 %collective-permute-start.14 = (bf16[64,512]{1,0:T(8,128)(2,1)S(1)}, bf16[64,512]{1,0:T(8,128)(2,1)S(1)}, u32[]{:S(2)}, u32[]{:S(2)}) collective-permute-start(bf16[64,512]{1,0:T(8,128)(2,1)S(1)} %shard_map.95.refs_0_), channel_id=1, source_target_pairs={{0,3},{1,2},{2,1},{3,0},{4,7},{5,6},{6,5},{7,4},{8,11},{9,10},{10,... | collective-permute-start | bytes 196616 | tf_op jit(solution)/shard_map/ppermute | solution.py:27
  43.8 1.3 %shard_map.93 = bf16[64,2,4,512]{3,2,1,0:T(4,128)(2,1)} custom-call(f32[2,8,512]{2,1,0:T(8,128)S(1)} %get-tuple-element.36.top_ref, f32[64,512]{1,0:T(8,128)S(1)} %get-tuple-element.31.wo_ref.refs_6_, bf16[128,512]{1,0:T(8,128)(2,1)S(1)} %get-tuple-element.37.both_ref, bf16[512,512]{1,0:T(8,128)(2,1)S(1)} %get-tuple-element.28.field_ref.refs_9_), custom_call_target="tpu_custom_call" | custom-call | flops 268435456 | bytes 1343488 | tf_op jit(solution)/shard_map/pallas_call | solution.py:554
  45.0 0.5 shard_map.97.refs_5_
  45.5 2.0 %collective-permute-done.15.refs_2_ = bf16[64,512]{1,0:T(8,128)(2,1)S(1)} collective-permute-done((bf16[64,512]{1,0:T(8,128)(2,1)S(1)}, bf16[64,512]{1,0:T(8,128)(2,1)S(1)}, u32[]{:S(2)}, u32[]{:S(2)}) %collective-permute-start.15) | collective-permute-done | bytes 65568 | tf_op jit(solution)/shard_map/ppermute | solution.py:27
  47.5 1.0 %collective-permute-done.14.refs_1_ = bf16[64,512]{1,0:T(8,128)(2,1)S(1)} collective-permute-done((bf16[64,512]{1,0:T(8,128)(2,1)S(1)}, bf16[64,512]{1,0:T(8,128)(2,1)S(1)}, u32[]{:S(2)}, u32[]{:S(2)}) %collective-permute-start.14) | collective-permute-done | bytes 65568 | tf_op jit(solution)/shard_map/ppermute | solution.py:27
  48.6 0.9 %shard_map.98 = bf16[64,2,4,512]{3,2,1,0:T(4,128)(2,1)} custom-call(bf16[64,512]{1,0:T(8,128)(2,1)S(1)} %shard_map.95.refs_0_, bf16[64,512]{1,0:T(8,128)(2,1)S(1)} %collective-permute-done.14.refs_1_, bf16[64,512]{1,0:T(8,128)(2,1)S(1)} %collective-permute-done.15.refs_2_, bf16[64,512]{1,0:T(8,128)(2,1)S(1)} %collective-permute-done.16.refs_3_, ...), custom_call_target="tpu_custom_call" | custom-call | bytes 1982464 | tf_op jit(solution)/shard_map/pallas_call | solution.py:554
  (32 shorter events, 1.8 us)
Async XLA Ops:
  2.2 1.4 %collective-permute-start = (f32[72,256]{1,0:T(8,128)S(1)}, f32[72,256]{1,0:T(8,128)S(1)}, u32[]{:S(2)}, u32[]{:S(2)}) collective-permute-start(f32[72,256]{1,0:T(8,128)S(1)} %get-tuple-element.24), channel_id=1, source_target_pairs={{0,4},{4,0},{8,12},{12,8},{1,5},{5,1},{9,13},{13,9},{2,6},{6,2},{1... | collective-permute-start | bytes 221192 | tf_op jit(solution)/shard_map/ppermute | solution.py:27
  3.7 10.1 %copy-start = (f32[3,2,64,64]{3,2,1,0:T(8,128)S(1)}, f32[3,2,64,64]{3,2,1,0:T(8,128)}, u32[]{:S(2)}) copy-start(f32[3,2,64,64]{3,2,1,0:T(8,128)} %refs_7_.1) | copy-start | bytes 294916
  3.7 5.4 %collective-permute-start.1 = (f32[72,256]{1,0:T(8,128)S(1)}, f32[72,256]{1,0:T(8,128)S(1)}, u32[]{:S(2)}, u32[]{:S(2)}) collective-permute-start(f32[72,256]{1,0:T(8,128)S(1)} %shard_map.78.mine_ref), channel_id=1, source_target_pairs={{0,8},{4,12},{8,0},{12,4},{1,9},{5,13},{9,1},{13,5},{2,10},{6,14},... | collective-permute-start | bytes 221192 | tf_op jit(solution)/shard_map/ppermute | solution.py:27
  9.2 4.6 %copy-start.2 = (bf16[64,64]{1,0:T(8,128)(2,1)S(1)}, bf16[64,64]{1,0:T(8,128)(2,1)}, u32[]{:S(2)}) copy-start(bf16[64,64]{1,0:T(8,128)(2,1)} %wv_ref.1) | copy-start | bytes 24580
  9.2 4.6 %copy-start.3 = (bf16[64,64]{1,0:T(8,128)(2,1)S(1)}, bf16[64,64]{1,0:T(8,128)(2,1)}, u32[]{:S(2)}) copy-start(bf16[64,64]{1,0:T(8,128)(2,1)} %wo_ref.1) | copy-start | bytes 24580
  9.2 6.1 %collective-permute-start.2 = (bf16[80,256]{1,0:T(8,128)(2,1)S(1)}, bf16[80,256]{1,0:T(8,128)(2,1)S(1)}, u32[]{:S(2)}, u32[]{:S(2)}) collective-permute-start(bf16[80,256]{1,0:T(8,128)(2,1)S(1)} %shard_map.80), channel_id=1, source_target_pairs={{0,3},{1,2},{2,1},{3,0},{4,7},{5,6},{6,5},{7,4},{8,11},{9,10},{10,... | collective-permute-start | bytes 122888 | tf_op jit(solution)/shard_map/ppermute | solution.py:27
  13.2 4.9 %collective-permute-start.3 = (bf16[80,256]{1,0:T(8,128)(2,1)S(1)}, bf16[80,256]{1,0:T(8,128)(2,1)S(1)}, u32[]{:S(2)}, u32[]{:S(2)}) collective-permute-start(bf16[80,256]{1,0:T(8,128)(2,1)S(1)} %shard_map.80), channel_id=1, source_target_pairs={{0,2},{1,3},{2,0},{3,1},{4,6},{5,7},{6,4},{7,5},{8,10},{9,11},{10,... | collective-permute-start | bytes 122888 | tf_op jit(solution)/shard_map/ppermute | solution.py:27
  13.2 4.9 %collective-permute-start.4 = (bf16[80,256]{1,0:T(8,128)(2,1)S(1)}, bf16[80,256]{1,0:T(8,128)(2,1)S(1)}, u32[]{:S(2)}, u32[]{:S(2)}) collective-permute-start(bf16[80,256]{1,0:T(8,128)(2,1)S(1)} %shard_map.80), channel_id=1, source_target_pairs={{0,1},{1,0},{2,3},{3,2},{4,5},{5,4},{6,7},{7,6},{8,9},{9,8},{10,11... | collective-permute-start | bytes 122888 | tf_op jit(solution)/shard_map/ppermute | solution.py:27
  18.1 1.3 %collective-permute-start.5 = (f32[72,256]{1,0:T(8,128)S(1)}, f32[72,256]{1,0:T(8,128)S(1)}, u32[]{:S(2)}, u32[]{:S(2)}) collective-permute-start(f32[72,256]{1,0:T(8,128)S(1)} %shard_map.86.mine_ref), channel_id=1, source_target_pairs={{0,4},{4,0},{8,12},{12,8},{1,5},{5,1},{9,13},{13,9},{2,6},{6,2},{1... | collective-permute-start | bytes 221192 | tf_op jit(solution)/shard_map/ppermute | solution.py:27
  20.5 5.8 %collective-permute-start.6 = (bf16[16,512]{1,0:T(8,128)(2,1)S(1)}, bf16[16,512]{1,0:T(8,128)(2,1)S(1)}, u32[]{:S(2)}, u32[]{:S(2)}) collective-permute-start(bf16[16,512]{1,0:T(8,128)(2,1)S(1)} %get-tuple-element.32.refs_0_), channel_id=1, source_target_pairs={{0,3},{1,2},{2,1},{3,0},{4,7},{5,6},{6,5},{7,4},{8,11},{9,10},{10,... | collective-permute-start | bytes 49160 | tf_op jit(solution)/shard_map/ppermute | solution.py:27
  22.0 4.7 %collective-permute-start.7 = (bf16[16,512]{1,0:T(8,128)(2,1)S(1)}, bf16[16,512]{1,0:T(8,128)(2,1)S(1)}, u32[]{:S(2)}, u32[]{:S(2)}) collective-permute-start(bf16[16,512]{1,0:T(8,128)(2,1)S(1)} %get-tuple-element.32.refs_0_), channel_id=1, source_target_pairs={{0,2},{1,3},{2,0},{3,1},{4,6},{5,7},{6,4},{7,5},{8,10},{9,11},{10,... | collective-permute-start | bytes 49160 | tf_op jit(solution)/shard_map/ppermute | solution.py:27
  22.6 4.2 %collective-permute-start.8 = (bf16[16,512]{1,0:T(8,128)(2,1)S(1)}, bf16[16,512]{1,0:T(8,128)(2,1)S(1)}, u32[]{:S(2)}, u32[]{:S(2)}) collective-permute-start(bf16[16,512]{1,0:T(8,128)(2,1)S(1)} %get-tuple-element.32.refs_0_), channel_id=1, source_target_pairs={{0,1},{1,0},{2,3},{3,2},{4,5},{5,4},{6,7},{7,6},{8,9},{9,8},{10,11... | collective-permute-start | bytes 49160 | tf_op jit(solution)/shard_map/ppermute | solution.py:27
  26.6 2.0 %copy-start.1 = (bf16[2,128,128]{2,1,0:T(8,128)(2,1)S(1)}, bf16[2,128,128]{2,1,0:T(8,128)(2,1)}, u32[]{:S(2)}) copy-start(bf16[2,128,128]{2,1,0:T(8,128)(2,1)} %constant.2.clone.refs_1_.refs_6_) | copy-start | bytes 196612
  26.8 4.3 %collective-permute-start.11 = (bf16[64,512]{1,0:T(8,128)(2,1)S(1)}, bf16[64,512]{1,0:T(8,128)(2,1)S(1)}, u32[]{:S(2)}, u32[]{:S(2)}) collective-permute-start(bf16[64,512]{1,0:T(8,128)(2,1)S(1)} %shard_map.90.refs_0_), channel_id=1, source_target_pairs={{0,12},{4,8},{8,4},{12,0},{1,13},{5,9},{9,5},{13,1},{2,14},{6,10},... | collective-permute-start | bytes 196616 | tf_op jit(solution)/shard_map/ppermute | solution.py:27
  26.9 5.7 %collective-permute-start.10 = (bf16[64,512]{1,0:T(8,128)(2,1)S(1)}, bf16[64,512]{1,0:T(8,128)(2,1)S(1)}, u32[]{:S(2)}, u32[]{:S(2)}) collective-permute-start(bf16[64,512]{1,0:T(8,128)(2,1)S(1)} %shard_map.90.refs_0_), channel_id=1, source_target_pairs={{0,8},{4,12},{8,0},{12,4},{1,9},{5,13},{9,1},{13,5},{2,10},{6,14},... | collective-permute-start | bytes 196616 | tf_op jit(solution)/shard_map/ppermute | solution.py:27
  28.4 4.2 %collective-permute-start.9 = (bf16[64,512]{1,0:T(8,128)(2,1)S(1)}, bf16[64,512]{1,0:T(8,128)(2,1)S(1)}, u32[]{:S(2)}, u32[]{:S(2)}) collective-permute-start(bf16[64,512]{1,0:T(8,128)(2,1)S(1)} %shard_map.90.refs_0_), channel_id=1, source_target_pairs={{0,4},{4,0},{8,12},{12,8},{1,5},{5,1},{9,13},{13,9},{2,6},{6,2},{1... | collective-permute-start | bytes 196616 | tf_op jit(solution)/shard_map/ppermute | solution.py:27
  33.6 1.3 %collective-permute-start.12 = (bf16[64,512]{1,0:T(8,128)(2,1)S(1)}, bf16[64,512]{1,0:T(8,128)(2,1)S(1)}, u32[]{:S(2)}, u32[]{:S(2)}) collective-permute-start(bf16[64,512]{1,0:T(8,128)(2,1)S(1)} %get-tuple-element.38.refs_0_), channel_id=1, source_target_pairs={{0,4},{4,0},{8,12},{12,8},{1,5},{5,1},{9,13},{13,9},{2,6},{6,2},{1... | collective-permute-start | bytes 196616 | tf_op jit(solution)/shard_map/ppermute | solution.py:27
  35.0 4.3 %collective-permute-start.13 = (bf16[64,512]{1,0:T(8,128)(2,1)S(1)}, bf16[64,512]{1,0:T(8,128)(2,1)S(1)}, u32[]{:S(2)}, u32[]{:S(2)}) collective-permute-start(bf16[64,512]{1,0:T(8,128)(2,1)S(1)} %shard_map.94.refs_0_), channel_id=1, source_target_pairs={{0,8},{4,12},{8,0},{12,4},{1,9},{5,13},{9,1},{13,5},{2,10},{6,14},... | collective-permute-start | bytes 196616 | tf_op jit(solution)/shard_map/ppermute | solution.py:27
  39.3 6.2 %collective-permute-start.16 = (bf16[64,512]{1,0:T(8,128)(2,1)S(1)}, bf16[64,512]{1,0:T(8,128)(2,1)S(1)}, u32[]{:S(2)}, u32[]{:S(2)}) collective-permute-start(bf16[64,512]{1,0:T(8,128)(2,1)S(1)} %shard_map.95.refs_0_), channel_id=1, source_target_pairs={{0,1},{1,0},{2,3},{3,2},{4,5},{5,4},{6,7},{7,6},{8,9},{9,8},{10,11... | collective-permute-start | bytes 196616 | tf_op jit(solution)/shard_map/ppermute | solution.py:27
  41.3 6.2 %collective-permute-start.15 = (bf16[64,512]{1,0:T(8,128)(2,1)S(1)}, bf16[64,512]{1,0:T(8,128)(2,1)S(1)}, u32[]{:S(2)}, u32[]{:S(2)}) collective-permute-start(bf16[64,512]{1,0:T(8,128)(2,1)S(1)} %shard_map.95.refs_0_), channel_id=1, source_target_pairs={{0,2},{1,3},{2,0},{3,1},{4,6},{5,7},{6,4},{7,5},{8,10},{9,11},{10,... | collective-permute-start | bytes 196616 | tf_op jit(solution)/shard_map/ppermute | solution.py:27
  42.4 6.2 %collective-permute-start.14 = (bf16[64,512]{1,0:T(8,128)(2,1)S(1)}, bf16[64,512]{1,0:T(8,128)(2,1)S(1)}, u32[]{:S(2)}, u32[]{:S(2)}) collective-permute-start(bf16[64,512]{1,0:T(8,128)(2,1)S(1)} %shard_map.95.refs_0_), channel_id=1, source_target_pairs={{0,3},{1,2},{2,1},{3,0},{4,7},{5,6},{6,5},{7,4},{8,11},{9,10},{10,... | collective-permute-start | bytes 196616 | tf_op jit(solution)/shard_map/ppermute | solution.py:27
